TPU v7x, 128 devices: a whole 4x4x4 slice. The times are simulated.
128 devices in a mesh: dp: 16 (over z_hi, y, core), mp: 8 (over z_lo, x).
Axes of the slice: x: 4, y: 4, z: 4 (z_hi: 2, z_lo: 2; z = z_hi * 2 + z_lo), core: 2. Of those that a mesh axis runs over, the one named last changes fastest.
Arguments:
- prefix_input: bfloat16 [16, 1536, 1152], P('dp', 'mp'), may hold values from -6 to 6
- action_input: bfloat16 [16, 96, 1024], P('dp', 'mp'), may hold values from -6 to 6
- prefix_cotangent: bfloat16 [16, 1536, 1152], P('dp', 'mp'), may hold values from -6 to 6
- action_cotangent: bfloat16 [16, 96, 1024], P('dp', 'mp'), may hold values from -6 to 6
- prefix_lengths: int32 [16, 2], P('dp'), may hold values from 1 to 1152, as said below
- mixture: int32 [16, 2], P('dp'), may hold values from 8 to 64
- cut_points: int32 [9], replicated, may hold values from 0 to 4096, as said below
- prefix_query: bfloat16 [1152, 1024], P(('dp', 'mp')), may hold values from -0.1875 to 0.1875
- prefix_key: bfloat16 [1152, 256], P(('dp', 'mp')), may hold values from -0.1875 to 0.1875
- prefix_value: bfloat16 [1152, 256], P(('dp', 'mp')), may hold values from -0.1875 to 0.1875
- prefix_out: bfloat16 [1024, 1152], P(('dp', 'mp')), may hold values from -3 to 3
- prefix_first_gain: bfloat16 [1152], P(('dp', 'mp')), may hold values from 0.099609375 to 1.8984375
- prefix_second_gain: bfloat16 [1152], P(('dp', 'mp')), may hold values from 0.099609375 to 1.8984375
- action_query: bfloat16 [1024, 1024], P(('dp', 'mp')), may hold values from -0.1875 to 0.1875
- action_key: bfloat16 [1024, 256], P(('dp', 'mp')), may hold values from -0.1875 to 0.1875
- action_value: bfloat16 [1024, 256], P(('dp', 'mp')), may hold values from -0.1875 to 0.1875
- action_out: bfloat16 [1024, 1024], P(('dp', 'mp')), may hold values from -3 to 3
- action_first_gain: bfloat16 [1024], P(('dp', 'mp')), may hold values from 0.099609375 to 1.8984375
- action_second_gain: bfloat16 [1024], P(('dp', 'mp')), may hold values from 0.099609375 to 1.8984375
- prefix_gate: bfloat16 [1152, 6912], P(None, 'mp'), may hold values from -0.1875 to 0.1875
- prefix_up: bfloat16 [1152, 6912], P(None, 'mp'), may hold values from -0.1875 to 0.1875
- prefix_down: bfloat16 [6912, 1152], P('mp'), may hold values from -0.078125 to 0.078125
- action_gate: bfloat16 [8, 1024, 1024], P('mp'), may hold values from -0.1875 to 0.1875
- action_up: bfloat16 [8, 1024, 1024], P('mp'), may hold values from -0.1875 to 0.1875
- action_down: bfloat16 [8, 1024, 1024], P('mp'), may hold values from -0.25 to 0.25
Outputs:
- prefix_output: bfloat16 [16, 1536, 1152], P('dp', 'mp')
- action_output: bfloat16 [16, 96, 1024], P('dp', 'mp')
- prefix_input_gradient: bfloat16 [16, 1536, 1152], P('dp', 'mp')
- action_input_gradient: bfloat16 [16, 96, 1024], P('dp', 'mp')
- prefix_query_gradient: float32 [1152, 1024], P(('dp', 'mp'))
- prefix_key_gradient: float32 [1152, 256], P(('dp', 'mp'))
- prefix_value_gradient: float32 [1152, 256], P(('dp', 'mp'))
- prefix_out_gradient: float32 [1024, 1152], P(('dp', 'mp'))
- prefix_first_gradient: float32 [1152], P(('dp', 'mp'))
- prefix_second_gradient: float32 [1152], P(('dp', 'mp'))
- action_query_gradient: float32 [1024, 1024], P(('dp', 'mp'))
- action_key_gradient: float32 [1024, 256], P(('dp', 'mp'))
- action_value_gradient: float32 [1024, 256], P(('dp', 'mp'))
- action_out_gradient: float32 [1024, 1024], P(('dp', 'mp'))
- action_first_gradient: float32 [1024], P(('dp', 'mp'))
- action_second_gradient: float32 [1024], P(('dp', 'mp'))
- prefix_gate_gradient: float32 [1152, 6912], P(None, 'mp')
- prefix_up_gradient: float32 [1152, 6912], P(None, 'mp')
- prefix_down_gradient: float32 [6912, 1152], P('mp')
- action_gate_gradient: float32 [8, 1024, 1024], P('mp')
- action_up_gradient: float32 [8, 1024, 1024], P('mp')
- action_down_gradient: float32 [8, 1024, 1024], P('mp')
Inputs may be any that keep to these rules, and one draw needn't show every extreme that they name: `prefix_lengths`: each row sums to 1536; exactly one entry of each row is 1152. cut_points[0] = 0, cut_points[8] = 4096, rising, multiples of 128; each difference cut_points[j+1] - cut_points[j] is at most 1024, reached by exactly one j in every draw.
All inputs are finite; a program needn't handle non-finite values.
Results may differ from a plain program's by a relative error of at most 0.024.
Values may be sent and summed in bfloat16 or wider, within the bound.
No kernel may reach another device: no remote copies, remote signals or barrier semaphores. Data moves between devices by JAX's collectives and lax.ppermute only.
A program may use at most 256 MiB of HBM per device.

v0:
```python
import jax
import jax.numpy as jnp
from jax import lax
from jax.sharding import PartitionSpec as P

ACT_LEN = 48


epsilon = 1e-06
mix_denominator = 32.0
rope_base = 10000.0


def normalize(inputs, gain_vector):
    return (
        inputs
        * lax.rsqrt(jnp.mean(inputs * inputs, axis=-1, keepdims=True) + epsilon)
        * gain_vector
    )


def rotate(inputs, position):
    half_size = inputs.shape[-1] // 2
    frequency = rope_base ** (-jnp.arange(half_size, dtype=jnp.float32) / half_size)
    angles = position.astype(jnp.float32)[:, None] * frequency[None, :]
    cosine = jnp.cos(angles)[:, None, :]
    sine_table = jnp.sin(angles)[:, None, :]
    first_half = inputs[..., :half_size]
    second_half = inputs[..., half_size:]
    return jnp.concatenate(
        [
            first_half * cosine - second_half * sine_table,
            second_half * cosine + first_half * sine_table,
        ],
        axis=-1,
    )


def gelu_tanh(inputs):
    return jax.nn.gelu(inputs, approximate=True)


def item_tables(lengths, prefix_total, action_total, item_count, action_length):
    ends_at = jnp.cumsum(lengths)
    starts_at = ends_at - lengths
    prefix_rows = jnp.arange(prefix_total, dtype=jnp.int32)
    prefix_item = jnp.sum((prefix_rows[:, None] >= ends_at[None, :]).astype(jnp.int32), axis=1)
    item_ids = jnp.arange(item_count, dtype=jnp.int32)
    prefix_pick = prefix_item[:, None] == item_ids[None, :]
    prefix_place = prefix_rows - jnp.sum(jnp.where(prefix_pick, starts_at[None, :], 0), axis=1)
    action_rows = jnp.arange(action_total, dtype=jnp.int32)
    action_item = action_rows // action_length
    action_pick = action_item[:, None] == item_ids[None, :]
    action_place = (
        jnp.sum(jnp.where(action_pick, lengths[None, :], 0), axis=1) + action_rows % action_length
    )
    return (prefix_item, prefix_place, prefix_pick, action_item, action_place, action_pick)


def stream_front(inputs, full_set, place):
    query_weight, key_weight, value_weight = (full_set[0], full_set[1], full_set[2])
    row_count = inputs.shape[0]
    head_size = key_weight.shape[1]
    normed_value, normed_pull = jax.vjp(normalize, inputs, full_set[4].astype(jnp.float32))
    first_normed = normed_value.astype(jnp.bfloat16)
    query_raw = jnp.dot(first_normed, query_weight, preferred_element_type=jnp.float32)
    key_raw = jnp.dot(first_normed, key_weight, preferred_element_type=jnp.float32)
    value_raw = jnp.dot(first_normed, value_weight, preferred_element_type=jnp.float32)

    def query_turn(raw_rows):
        return rotate(raw_rows.reshape(row_count, -1, head_size), place) * head_size ** (-0.5)

    def key_turn(raw_rows):
        return rotate(raw_rows.reshape(row_count, 1, head_size), place)[:, 0, :]

    queries, query_pull = jax.vjp(query_turn, query_raw)
    key_rows, key_pull = jax.vjp(key_turn, key_raw)
    stacked = jnp.stack([key_rows.astype(jnp.bfloat16), value_raw.astype(jnp.bfloat16)], axis=1)
    return (first_normed, normed_pull, queries.astype(jnp.bfloat16), query_pull, key_pull, stacked)


def masked_scores(queries, key_rows, visible):
    scores = jnp.einsum("qhd,kd->hqk", queries, key_rows, preferred_element_type=jnp.float32)
    return jnp.where(visible[None], scores, -1e30)


def stream_middle(inputs, context, full_set):
    hidden_state = inputs + jnp.dot(context, full_set[3], preferred_element_type=jnp.float32)
    second_value, second_pull = jax.vjp(normalize, hidden_state, full_set[5].astype(jnp.float32))
    return (hidden_state, second_value.astype(jnp.bfloat16), second_pull)


def feed_forward(rows_in, gate_weight, up_weight, down_weight, valid):
    gate_values = jnp.dot(rows_in, gate_weight, preferred_element_type=jnp.float32)
    up_values = jnp.dot(rows_in, up_weight, preferred_element_type=jnp.float32)
    activated, gelu_pull = jax.vjp(gelu_tanh, gate_values)
    product = (activated * up_values * valid).astype(jnp.bfloat16)
    partial_sum = jnp.dot(product, down_weight, preferred_element_type=jnp.float32)
    return (partial_sum, (up_values, activated, gelu_pull, product))


def feed_backward(seed_rows, gate_weight, up_weight, down_weight, valid, saved):
    up_values, activated, gelu_pull, product = saved
    product_delta = jnp.dot(seed_rows, down_weight.T, preferred_element_type=jnp.float32) * valid
    gate_delta = gelu_pull(product_delta * up_values)[0].astype(jnp.bfloat16)
    up_delta = (product_delta * activated).astype(jnp.bfloat16)
    rows_delta = jnp.dot(gate_delta, gate_weight.T, preferred_element_type=jnp.float32)
    rows_delta = rows_delta + jnp.dot(up_delta, up_weight.T, preferred_element_type=jnp.float32)
    return (rows_delta, gate_delta, up_delta)


def feed_weight_grads(rows_in, seed_rows, product, gate_delta, up_delta):
    return (
        jnp.dot(rows_in.T, gate_delta, preferred_element_type=jnp.float32),
        jnp.dot(rows_in.T, up_delta, preferred_element_type=jnp.float32),
        jnp.dot(product.T, seed_rows, preferred_element_type=jnp.float32),
    )


def stream_back(inputs_front, full_set, query_delta, key_value_delta, hidden_delta):
    first_normed, normed_pull, query_pull, key_pull = inputs_front
    query_raw_delta = query_pull(query_delta)[0].astype(jnp.bfloat16)
    key_raw_delta = key_pull(key_value_delta[:, 0, :])[0].astype(jnp.bfloat16)
    value_raw_delta = key_value_delta[:, 1, :].astype(jnp.bfloat16)
    query_grad = jnp.dot(first_normed.T, query_raw_delta, preferred_element_type=jnp.float32)
    key_grad = jnp.dot(first_normed.T, key_raw_delta, preferred_element_type=jnp.float32)
    value_grad = jnp.dot(first_normed.T, value_raw_delta, preferred_element_type=jnp.float32)
    normed_delta = jnp.dot(query_raw_delta, full_set[0].T, preferred_element_type=jnp.float32)
    normed_delta = normed_delta + jnp.dot(
        key_raw_delta, full_set[1].T, preferred_element_type=jnp.float32
    )
    normed_delta = normed_delta + jnp.dot(
        value_raw_delta, full_set[2].T, preferred_element_type=jnp.float32
    )
    input_delta, first_gain_delta = normed_pull(normed_delta)
    return (
        (hidden_delta + input_delta).astype(jnp.bfloat16),
        query_grad,
        key_grad,
        value_grad,
        first_gain_delta,
    )


def on_device(
    prefix_input,
    action_input,
    prefix_cotangent,
    action_cotangent,
    prefix_lengths,
    mixture,
    cut_points,
    prefix_query,
    prefix_key,
    prefix_value,
    prefix_out,
    prefix_first_gain,
    prefix_second_gain,
    action_query,
    action_key,
    action_value,
    action_out,
    action_first_gain,
    action_second_gain,
    prefix_gate,
    prefix_up,
    prefix_down,
    action_gate,
    action_up,
    action_down,
):
    shard_index = lax.axis_index("mp")
    group_ways = lax.axis_size("mp")
    prefix_count = prefix_input.shape[1]
    action_count = action_input.shape[1]
    head_size = prefix_key.shape[1]
    head_count = prefix_query.shape[1] // head_size
    item_count = prefix_lengths.shape[1]
    slot_width = action_gate.shape[2]
    group_prefix = prefix_count * group_ways
    group_action = action_count * group_ways
    lengths = prefix_lengths[0]
    tables = item_tables(lengths, group_prefix, group_action, item_count, ACT_LEN)
    own_prefix = shard_index * prefix_count
    own_action = shard_index * action_count
    prefix_place = lax.dynamic_slice_in_dim(tables[1], own_prefix, prefix_count)
    action_place = lax.dynamic_slice_in_dim(tables[4], own_action, action_count)
    prefix_pick = lax.dynamic_slice_in_dim(tables[2], own_prefix, prefix_count)
    action_pick = lax.dynamic_slice_in_dim(tables[5], own_action, action_count)
    query_item = jnp.concatenate(
        [
            lax.dynamic_slice_in_dim(tables[0], own_prefix, prefix_count),
            lax.dynamic_slice_in_dim(tables[3], own_action, action_count),
        ],
        axis=0,
    )
    key_item = jnp.concatenate([tables[0], tables[3]], axis=0)
    query_action = jnp.concatenate(
        [jnp.zeros((prefix_count,), jnp.bool_), jnp.ones((action_count,), jnp.bool_)], axis=0
    )
    key_action = jnp.concatenate(
        [jnp.zeros((group_prefix,), jnp.bool_), jnp.ones((group_action,), jnp.bool_)], axis=0
    )
    visible = (query_item[:, None] == key_item[None, :]) & (
        query_action[:, None] | ~key_action[None, :]
    )
    gathered = (
        lax.all_gather(prefix_query, ("dp", "mp"), axis=0, tiled=True),
        lax.all_gather(prefix_key, ("dp", "mp"), axis=0, tiled=True),
        lax.all_gather(prefix_value, ("dp", "mp"), axis=0, tiled=True),
        lax.all_gather(prefix_out, ("dp", "mp"), axis=0, tiled=True),
        lax.all_gather(prefix_first_gain, ("dp", "mp"), axis=0, tiled=True),
        lax.all_gather(prefix_second_gain, ("dp", "mp"), axis=0, tiled=True),
        lax.all_gather(action_query, ("dp", "mp"), axis=0, tiled=True),
        lax.all_gather(action_key, ("dp", "mp"), axis=0, tiled=True),
        lax.all_gather(action_value, ("dp", "mp"), axis=0, tiled=True),
        lax.all_gather(action_out, ("dp", "mp"), axis=0, tiled=True),
        lax.all_gather(action_first_gain, ("dp", "mp"), axis=0, tiled=True),
        lax.all_gather(action_second_gain, ("dp", "mp"), axis=0, tiled=True),
    )
    prefix_full = gathered[:6]
    action_full = gathered[6:]
    prefix_x = prefix_input[0].astype(jnp.float32)
    action_x = action_input[0].astype(jnp.float32)
    prefix_front = stream_front(prefix_x, prefix_full, prefix_place)
    action_front = stream_front(action_x, action_full, action_place)
    prefix_kv, action_kv = (
        lax.all_gather(prefix_front[5], "mp", axis=0, tiled=True),
        lax.all_gather(action_front[5], "mp", axis=0, tiled=True),
    )
    key_value_all = jnp.concatenate([prefix_kv, action_kv], axis=0)
    queries_all = jnp.concatenate([prefix_front[2], action_front[2]], axis=0)
    query_rows = queries_all.shape[0]
    scores = masked_scores(queries_all, key_value_all[:, 0, :], visible)
    row_top = jnp.max(scores, axis=-1, keepdims=True)
    shifted = jnp.exp(scores - row_top)
    row_total = jnp.sum(shifted, axis=-1, keepdims=True)
    probs = shifted / row_total
    log_total = row_top + jnp.log(row_total)
    context = (
        jnp.einsum(
            "hqk,kd->qhd",
            probs.astype(jnp.bfloat16),
            key_value_all[:, 1, :],
            preferred_element_type=jnp.float32,
        )
        .astype(jnp.bfloat16)
        .reshape(query_rows, head_count * head_size)
    )
    prefix_context = context[:prefix_count]
    action_context = context[prefix_count:]
    prefix_hidden, prefix_second, prefix_second_pull = stream_middle(
        prefix_x, prefix_context, prefix_full
    )
    action_hidden, action_second, action_second_pull = stream_middle(
        action_x, action_context, action_full
    )
    prefix_rows_in, action_rows_in = (
        lax.all_gather(prefix_second, "mp", axis=0, tiled=True),
        lax.all_gather(action_second, "mp", axis=0, tiled=True),
    )
    cut_pair = lax.dynamic_slice_in_dim(cut_points, shard_index, 2)
    action_valid = (jnp.arange(slot_width, dtype=jnp.int32) < cut_pair[1] - cut_pair[0]).astype(
        jnp.float32
    )[None, :]
    prefix_partial, prefix_saved = feed_forward(
        prefix_rows_in, prefix_gate, prefix_up, prefix_down, 1.0
    )
    action_partial, action_saved = feed_forward(
        action_rows_in, action_gate[0], action_up[0], action_down[0], action_valid
    )
    prefix_sum, action_sum = (
        lax.psum_scatter(
            prefix_partial.astype(jnp.bfloat16), "mp", scatter_dimension=0, tiled=True
        ).astype(jnp.float32),
        lax.psum_scatter(
            action_partial.astype(jnp.bfloat16), "mp", scatter_dimension=0, tiled=True
        ).astype(jnp.float32),
    )
    prefix_output = (prefix_hidden + prefix_sum).astype(jnp.bfloat16)[None]
    action_output = (action_hidden + action_sum).astype(jnp.bfloat16)[None]
    share_value = mixture[0].astype(jnp.float32) / mix_denominator
    prefix_seed = (
        prefix_cotangent[0].astype(jnp.float32)
        * jnp.sum(jnp.where(prefix_pick, share_value[None, :], 0.0), axis=1)[:, None]
    )
    action_seed = (
        action_cotangent[0].astype(jnp.float32)
        * jnp.sum(jnp.where(action_pick, share_value[None, :], 0.0), axis=1)[:, None]
    )
    prefix_seed_rows, action_seed_rows = (
        lax.all_gather(prefix_seed.astype(jnp.bfloat16), "mp", axis=0, tiled=True),
        lax.all_gather(action_seed.astype(jnp.bfloat16), "mp", axis=0, tiled=True),
    )
    prefix_rows_delta, prefix_gate_delta, prefix_up_delta = feed_backward(
        prefix_seed_rows, prefix_gate, prefix_up, prefix_down, 1.0, prefix_saved
    )
    action_rows_delta, action_gate_delta, action_up_delta = feed_backward(
        action_seed_rows, action_gate[0], action_up[0], action_down[0], action_valid, action_saved
    )
    prefix_mlp = feed_weight_grads(
        prefix_rows_in, prefix_seed_rows, prefix_saved[3], prefix_gate_delta, prefix_up_delta
    )
    action_mlp = feed_weight_grads(
        action_rows_in, action_seed_rows, action_saved[3], action_gate_delta, action_up_delta
    )
    summed = (
        lax.psum(prefix_mlp[0].astype(jnp.bfloat16), "dp").astype(jnp.float32),
        lax.psum(prefix_mlp[1].astype(jnp.bfloat16), "dp").astype(jnp.float32),
        lax.psum(prefix_mlp[2].astype(jnp.bfloat16), "dp").astype(jnp.float32),
        lax.psum(action_mlp[0].astype(jnp.bfloat16), "dp").astype(jnp.float32),
        lax.psum(action_mlp[1].astype(jnp.bfloat16), "dp").astype(jnp.float32),
        lax.psum(action_mlp[2].astype(jnp.bfloat16), "dp").astype(jnp.float32),
    )
    prefix_mlp = summed[:3]
    action_mlp = summed[3:]
    prefix_second_delta, action_second_delta = (
        lax.psum_scatter(
            prefix_rows_delta.astype(jnp.bfloat16), "mp", scatter_dimension=0, tiled=True
        ).astype(jnp.float32),
        lax.psum_scatter(
            action_rows_delta.astype(jnp.bfloat16), "mp", scatter_dimension=0, tiled=True
        ).astype(jnp.float32),
    )
    prefix_hidden_part, prefix_second_grad = prefix_second_pull(prefix_second_delta)
    action_hidden_part, action_second_grad = action_second_pull(action_second_delta)
    prefix_hidden_delta = prefix_seed + prefix_hidden_part
    action_hidden_delta = action_seed + action_hidden_part
    prefix_hidden_low = prefix_hidden_delta.astype(jnp.bfloat16)
    action_hidden_low = action_hidden_delta.astype(jnp.bfloat16)
    prefix_out_grad = jnp.dot(
        prefix_context.T, prefix_hidden_low, preferred_element_type=jnp.float32
    )
    action_out_grad = jnp.dot(
        action_context.T, action_hidden_low, preferred_element_type=jnp.float32
    )
    context_delta = jnp.concatenate(
        [
            jnp.dot(prefix_hidden_low, prefix_full[3].T, preferred_element_type=jnp.float32),
            jnp.dot(action_hidden_low, action_full[3].T, preferred_element_type=jnp.float32),
        ],
        axis=0,
    )
    context_delta = context_delta.astype(jnp.bfloat16).reshape(query_rows, head_count, head_size)
    scores_again = masked_scores(queries_all, key_value_all[:, 0, :], visible)
    probs_again = jnp.exp(scores_again - log_total)
    probs_low = probs_again.astype(jnp.bfloat16)
    probs_delta = jnp.einsum(
        "qhd,kd->hqk", context_delta, key_value_all[:, 1, :], preferred_element_type=jnp.float32
    )
    row_dot = jnp.sum(probs_again * probs_delta, axis=-1, keepdims=True)
    score_delta = (probs_again * (probs_delta - row_dot)).astype(jnp.bfloat16)
    queries_delta = jnp.einsum(
        "hqk,kd->qhd", score_delta, key_value_all[:, 0, :], preferred_element_type=jnp.float32
    )
    keys_delta = jnp.einsum(
        "hqk,qhd->kd", score_delta, queries_all, preferred_element_type=jnp.float32
    )
    values_delta = jnp.einsum(
        "hqk,qhd->kd", probs_low, context_delta, preferred_element_type=jnp.float32
    )
    key_value_delta = jnp.stack([keys_delta, values_delta], axis=1)
    prefix_kv_delta, action_kv_delta = (
        lax.psum_scatter(
            key_value_delta[:group_prefix].astype(jnp.bfloat16),
            "mp",
            scatter_dimension=0,
            tiled=True,
        ).astype(jnp.float32),
        lax.psum_scatter(
            key_value_delta[group_prefix:].astype(jnp.bfloat16),
            "mp",
            scatter_dimension=0,
            tiled=True,
        ).astype(jnp.float32),
    )
    prefix_back = stream_back(
        (prefix_front[0], prefix_front[1], prefix_front[3], prefix_front[4]),
        prefix_full,
        queries_delta[:prefix_count],
        prefix_kv_delta,
        prefix_hidden_delta,
    )
    action_back = stream_back(
        (action_front[0], action_front[1], action_front[3], action_front[4]),
        action_full,
        queries_delta[prefix_count:],
        action_kv_delta,
        action_hidden_delta,
    )
    weight_sums = (
        lax.psum_scatter(prefix_back[1], ("dp", "mp"), scatter_dimension=0, tiled=True),
        lax.psum_scatter(prefix_back[2], ("dp", "mp"), scatter_dimension=0, tiled=True),
        lax.psum_scatter(prefix_back[3], ("dp", "mp"), scatter_dimension=0, tiled=True),
        lax.psum_scatter(prefix_out_grad, ("dp", "mp"), scatter_dimension=0, tiled=True),
        lax.psum_scatter(prefix_back[4], ("dp", "mp"), scatter_dimension=0, tiled=True),
        lax.psum_scatter(prefix_second_grad, ("dp", "mp"), scatter_dimension=0, tiled=True),
        lax.psum_scatter(action_back[1], ("dp", "mp"), scatter_dimension=0, tiled=True),
        lax.psum_scatter(action_back[2], ("dp", "mp"), scatter_dimension=0, tiled=True),
        lax.psum_scatter(action_back[3], ("dp", "mp"), scatter_dimension=0, tiled=True),
        lax.psum_scatter(action_out_grad, ("dp", "mp"), scatter_dimension=0, tiled=True),
        lax.psum_scatter(action_back[4], ("dp", "mp"), scatter_dimension=0, tiled=True),
        lax.psum_scatter(action_second_grad, ("dp", "mp"), scatter_dimension=0, tiled=True),
    )
    return (
        prefix_output,
        action_output,
        prefix_back[0][None],
        action_back[0][None],
        weight_sums[0],
        weight_sums[1],
        weight_sums[2],
        weight_sums[3],
        weight_sums[4],
        weight_sums[5],
        weight_sums[6],
        weight_sums[7],
        weight_sums[8],
        weight_sums[9],
        weight_sums[10],
        weight_sums[11],
        prefix_mlp[0],
        prefix_mlp[1],
        prefix_mlp[2],
        action_mlp[0][None],
        action_mlp[1][None],
        action_mlp[2][None],
    )


def solution(mesh):
    return jax.shard_map(
        on_device,
        mesh=mesh,
        in_specs=(
            P("dp", "mp", None),
            P("dp", "mp", None),
            P("dp", "mp", None),
            P("dp", "mp", None),
            P("dp", None),
            P("dp", None),
            P(),
            P(("dp", "mp"), None),
            P(("dp", "mp"), None),
            P(("dp", "mp"), None),
            P(("dp", "mp"), None),
            P(("dp", "mp")),
            P(("dp", "mp")),
            P(("dp", "mp"), None),
            P(("dp", "mp"), None),
            P(("dp", "mp"), None),
            P(("dp", "mp"), None),
            P(("dp", "mp")),
            P(("dp", "mp")),
            P(None, "mp"),
            P(None, "mp"),
            P("mp", None),
            P("mp", None, None),
            P("mp", None, None),
            P("mp", None, None),
        ),
        out_specs=(
            P("dp", "mp", None),
            P("dp", "mp", None),
            P("dp", "mp", None),
            P("dp", "mp", None),
            P(("dp", "mp"), None),
            P(("dp", "mp"), None),
            P(("dp", "mp"), None),
            P(("dp", "mp"), None),
            P(("dp", "mp")),
            P(("dp", "mp")),
            P(("dp", "mp"), None),
            P(("dp", "mp"), None),
            P(("dp", "mp"), None),
            P(("dp", "mp"), None),
            P(("dp", "mp")),
            P(("dp", "mp")),
            P(None, "mp"),
            P(None, "mp"),
            P("mp", None),
            P("mp", None, None),
            P("mp", None, None),
            P("mp", None, None),
        ),
        check_vma=False,
    )
```

profile of v0, /device:TPU:0, one launch (start us, length us, event | category | flops | bytes accessed | tf_op | source)
XLA Modules:
  0.0 5265.6 jit_solution(5375686029905920845)
XLA Ops:
  12.4 68.5 %all-reduce.27 = (bf16[1152]{0:T(1024)(128)(2,1)S(1)}, bf16[1024]{0:T(1024)(128)(2,1)S(1)}, bf16[1152]{0:T(1024)(128)(2,1)S(1)}, bf16[1024]{0:T(1024)(128)(2,1)}) all-reduce(bf16[1152]{0:T(1024)(128)(2,1)S(1)} %dynamic-update-slice, bf16[1024]{0:T(1024)(128)(2,1)S(1)} %dynamic-update-slice.1, ...), channel_id=1, replica_groups=mesh['dp'=16,'mp'=8] {'dp','mp'}, use_global_device_ids=true, to_apply=%add.8 | all-reduce | flops 4352 | bytes 17408
  82.1 337.8 %all-gather.1 = bf16[128,9,256]{2,1,0:T(8,128)(2,1)} all-gather(bf16[1,9,256]{2,1,0:T(8,128)(2,1)} %bitcast.338), channel_id=1, replica_groups=mesh['dp'=16,'mp'=8] {'dp','mp'}, dimensions={0}, use_global_device_ids=true | all-gather | bytes 594432 | tf_op jit(solution)/shard_map/all_gather | solution.py:210
  421.4 335.7 %all-gather = bf16[128,9,256]{2,1,0:T(8,128)(2,1)} all-gather(bf16[1,9,256]{2,1,0:T(8,128)(2,1)S(1)} %bitcast.339), channel_id=1, replica_groups=mesh['dp'=16,'mp'=8] {'dp','mp'}, dimensions={0}, use_global_device_ids=true | all-gather | bytes 594432 | tf_op jit(solution)/shard_map/all_gather | solution.py:209
  765.8 314.8 %all_gather.60 = bf16[1024,256]{1,0:T(8,128)(2,1)S(1)} all-gather(bf16[8,256]{1,0:T(8,128)(2,1)S(1)} %copy-done.83), channel_id=1, replica_groups=mesh['dp'=16,'mp'=8] {'dp','mp'}, dimensions={0}, use_global_device_ids=true | all-gather | bytes 528384 | tf_op jit(solution)/shard_map/all_gather | solution.py:216
  1080.6 312.8 %all_gather.59 = bf16[1024,256]{1,0:T(8,128)(2,1)S(1)} all-gather(bf16[8,256]{1,0:T(8,128)(2,1)S(1)} %copy-done.84), channel_id=1, replica_groups=mesh['dp'=16,'mp'=8] {'dp','mp'}, dimensions={0}, use_global_device_ids=true | all-gather | bytes 528384 | tf_op jit(solution)/shard_map/all_gather | solution.py:215
  1394.1 28.4 all_gather.61
  1435.7 5.5 reshape.619
  1456.8 253.8 %all-gather.17.cloned.1.call-done = bf16[1024,1152]{1,0:T(8,128)(2,1)} async-done(((bf16[8,1152]{1,0:T(8,128)(2,1)}), bf16[1024,1152]{1,0:T(8,128)(2,1)}) %all-gather.17.cloned.1.call-update) | async-done | bytes 2359312 | tf_op jit(solution)/shard_map/all_gather | solution.py:211
  1719.5 42.6 all-gather.19.cloned.1.call-done
  1762.1 8.7 fusion.210
  1770.9 5.7 fusion.211
  1776.6 33.5 all-gather.23.cloned.1.call-done
  1810.1 12.7 multiply_convert_fusion
  1827.2 5.8 fusion.2
  1833.2 8.3 convolution_convert_fusion
  1842.8 30.5 all-gather.4
  1882.1 226.9 %all-gather.21.cloned.1.call-done = bf16[1024,1024]{1,0:T(8,128)(2,1)} async-done(((bf16[8,1024]{1,0:T(8,128)(2,1)}), bf16[1024,1024]{1,0:T(8,128)(2,1)}) %all-gather.21.cloned.1.call-update) | async-done | bytes 2097168 | tf_op jit(solution)/shard_map/all_gather | solution.py:217
  2112.5 32.1 all-gather.3
  2153.6 23.1 fusion.207
  2180.9 6.1 collective-permute-start.3
  2199.4 16.1 reduce-scatter.12.cloned.1.call-done
  2218.9 4.9 fusion.3
  2249.0 7.7 convolution_convert_fusion.3
  2267.1 5.1 reduce-scatter.16.cloned.1.call-done
  2280.0 65.3 %all-reduce.34.cloned.1.call-done = bf16[96,2,256]{2,1,0:T(2,128)(2,1)} async-done(((bf16[96,2,256]{2,1,0:T(2,128)(2,1)}), bf16[96,2,256]{2,1,0:T(2,128)(2,1)}) %all-reduce.34.cloned.1.call-update) | async-done | bytes 98320
  2361.0 72.4 %all-reduce.25 = (f32[1152]{0:T(1024)S(1)}, f32[1152]{0:T(1024)S(1)}, f32[1024]{0:T(1024)S(1)}, f32[1024]{0:T(1024)S(1)}) all-reduce(f32[1152]{0:T(1024)S(1)} %get-tuple-element.24, f32[1152]{0:T(1024)S(1)} %copy-done.55, f32[1024]{0:T(1024)S(1)} %get-tuple-element.28, ...), channel_id=12, replica_groups=mesh['dp'=16,'mp'=8] {'dp','mp'}, use_global_device_ids=true, to_apply=%region_28.29.clone | all-reduce | flops 4352 | bytes 34816
  2436.7 91.2 %all-reduce.38.cloned.1.call-done = (bf16[1152,864]{0,1:T(8,128)(2,1)}, bf16[1152,864]{0,1:T(8,128)(2,1)}, bf16[864,1152]{1,0:T(8,128)(2,1)}, bf16[1,1024,1024]{...) async-done(((bf16[1152,864]{0,1:T(8,128)(2,1)}, bf16[1152,864]{0,1:T(8,128)(2,1)}, bf16[864,1152]{1,0:T(8,128)(2,1)}, ...) | async-done | bytes 12263440 | tf_op jit(solution)/shard_map/psum | solution.py:308
  2544.6 156.5 %all-reduce.36.cloned.1.call-done = (f32[1152,1024]{1,0:T(8,128)}, f32[1152,256]{1,0:T(8,128)}, f32[1152,256]{1,0:T(8,128)}, f32[1024,1152]{1,0:T(8,128)}) async-done(((f32[1152,1024]{1,0:T(8,128)}, f32[1152,256]{1,0:T(8,128)}, f32[1152,256]{1,0:T(8,128)}, f32[1024,1152]{1,0:T(8,128)}), (f32[1152,1024]{1,0:T(8,128)}, f32[1152,256]{1,0:T(8,128)}, f32[1152,256]{1,0:T(8,128)}, ...) | async-done | bytes 11796496
  2705.4 640.2 %reduce-scatter.24.cloned.1.call-done = f32[8,1024]{1,0:T(8,128)} async-done(((f32[1024,1024]{1,0:T(8,128)}), f32[8,1024]{1,0:T(8,128)}) %reduce-scatter.24.cloned.1.call-update) | async-done | bytes 32784 | tf_op jit(solution)/shard_map/reduce_scatter | solution.py:401
  3345.6 636.4 %reduce-scatter.20.cloned.1.call-done = f32[8,256]{1,0:T(8,128)} async-done(((f32[1024,256]{1,0:T(8,128)}), f32[8,256]{1,0:T(8,128)}) %reduce-scatter.20.cloned.1.call-update) | async-done | bytes 8208 | tf_op jit(solution)/shard_map/reduce_scatter | solution.py:399
  3981.9 636.3 %reduce-scatter.22.cloned.1.call-done = f32[8,256]{1,0:T(8,128)} async-done(((f32[1024,256]{1,0:T(8,128)}), f32[8,256]{1,0:T(8,128)}) %reduce-scatter.22.cloned.1.call-update) | async-done | bytes 8208 | tf_op jit(solution)/shard_map/reduce_scatter | solution.py:400
  4618.3 640.3 %reduce-scatter.18.cloned.1.call-done = f32[8,1024]{1,0:T(8,128)} async-done(((f32[1024,1024]{1,0:T(8,128)}), f32[8,1024]{1,0:T(8,128)}) %reduce-scatter.18.cloned.1.call-update) | async-done | bytes 32784 | tf_op jit(solution)/shard_map/reduce_scatter | solution.py:398
  (422 shorter events, 181.1 us)
Async XLA Ops:
  7.2 2141.4 %copy-start = (bf16[1,1024,1024]{2,1,0:T(8,128)(2,1)S(1)}, bf16[1,1024,1024]{2,1,0:T(8,128)(2,1)}, u32[]{:S(2)}) copy-start(bf16[1,1024,1024]{2,1,0:T(8,128)(2,1)} %param.47) | copy-start | bytes 6291460
  7.2 1418.2 %all-gather.13.cloned.1.call-start = ((), (), s32[]{:S(2)}) async-start(), calls=%async_computation.7 | async-start | bytes 1769472 | tf_op jit(solution)/shard_map/all_gather | solution.py:228
  7.3 1386.6 %copy-start.61 = (f32[128]{0:T(128)}, f32[128]{0:T(128)S(1)}, u32[]{:S(2)}) copy-start(f32[128]{0:T(128)S(1)} %multiply_power_fusion) | copy-start | bytes 1540
  80.9 1364.6 %copy-start.39 = (f32[1152]{0:T(1024)}, f32[1152]{0:T(1024)S(1)}, u32[]{:S(2)}) copy-start(f32[1152]{0:T(1024)S(1)} %convert_element_type.291) | copy-start | bytes 13828
  82.1 677.3 %copy-start.72 = (f32[192]{0:T(256)}, f32[192]{0:T(256)S(1)}, u32[]{:S(2)}) copy-start(f32[192]{0:T(256)S(1)} %fusion.66) | copy-start | bytes 2308
  82.1 1363.4 %copy-start.53 = (f32[192]{0:T(256)}, f32[192]{0:T(256)S(1)}, u32[]{:S(2)}) copy-start(f32[192]{0:T(256)S(1)} %fusion.185) | copy-start | bytes 2308
  82.1 677.3 %copy-start.3 = (bf16[1,192,1152]{2,1,0:T(8,128)(2,1)S(1)}, bf16[1,192,1152]{2,1,0:T(8,128)(2,1)}, u32[]{:S(2)}) copy-start(bf16[1,192,1152]{2,1,0:T(8,128)(2,1)} %param.25) | copy-start | bytes 1327108
  763.0 665.8 %all-gather.15.cloned.1.call-start = ((), (), s32[]{:S(2)}) async-start(), calls=%async_computation.8 | async-start | bytes 2113536 | tf_op jit(solution)/shard_map/all_gather | solution.py:214
  763.8 671.9 %all-gather.25.cloned.1.call-start = ((), (), s32[]{:S(2)}) async-start(), calls=%async_computation.20 | async-start | bytes 4227072 | tf_op jit(solution)/shard_map/all_gather | solution.py:208
  764.5 946.1 %all-gather.17.cloned.1.call-start = ((), (), s32[]{:S(2)}) async-start(), calls=%async_computation.9 | async-start | bytes 2377728 | tf_op jit(solution)/shard_map/all_gather | solution.py:211
  765.1 997.1 %all-gather.19.cloned.1.call-start = ((), (), s32[]{:S(2)}) async-start(), calls=%async_computation.10 | async-start | bytes 3981312 | tf_op jit(solution)/shard_map/all_gather | solution.py:259
  765.3 667.5 %copy-start.44 = (f32[1024]{0:T(1024)}, f32[1024]{0:T(1024)S(1)}, u32[]{:S(2)}) copy-start(f32[1024]{0:T(1024)S(1)} %convert_element_type.298) | copy-start | bytes 12292
  765.5 667.3 %copy-start.58 = (f32[12]{0:T(128)}, f32[12]{0:T(128)S(1)}, u32[]{:S(2)}) copy-start(f32[12]{0:T(128)S(1)} %fusion.189) | copy-start | bytes 148
  765.8 669.2 %copy-start.49 = (f32[12,128]{1,0:T(8,128)}, f32[12,128]{1,0:T(8,128)S(1)}, u32[]{:S(2)}) copy-start(f32[12,128]{1,0:T(8,128)S(1)} %get-tuple-element.82) | copy-start | bytes 18436
  765.8 669.2 %copy-start.51 = (f32[12,128]{1,0:T(8,128)}, f32[12,128]{1,0:T(8,128)S(1)}, u32[]{:S(2)}) copy-start(f32[12,128]{1,0:T(8,128)S(1)} %get-tuple-element.83) | copy-start | bytes 18436
  1715.3 94.8 %all-gather.23.cloned.1.call-start = ((), (), s32[]{:S(2)}) async-start(), calls=%async_computation.13 | async-start | bytes 3981312 | tf_op jit(solution)/shard_map/all_gather | solution.py:292
  1718.7 390.4 %all-gather.21.cloned.1.call-start = ((), (), s32[]{:S(2)}) async-start(), calls=%async_computation.12 | async-start | bytes 2113536 | tf_op jit(solution)/shard_map/all_gather | solution.py:217
  1719.4 478.0 %reduce-scatter.14.cloned.1.call-start = ((), (), s32[]{:S(2)}) async-start(), calls=%async_computation.14 | async-start | bytes 3981312 | tf_op jit(solution)/shard_map/reduce_scatter | solution.py:318
  1833.0 382.5 %reduce-scatter.12.cloned.1.call-start = ((), (), s32[]{:S(2)}) async-start(), calls=%async_computation.11 | async-start | bytes 3981312 | tf_op jit(solution)/shard_map/reduce_scatter | solution.py:273
  1841.6 430.5 %reduce-scatter.16.cloned.1.call-start = ((), (), s32[]{:S(2)}) async-start(), calls=%async_computation.15 | async-start | bytes 1769472 | tf_op jit(solution)/shard_map/reduce_scatter | solution.py:364
  2176.8 13.1 collective-permute-start.2
  2178.9 12.4 collective-permute-start
  2180.9 9.0 collective-permute-start.3
  2187.0 4.2 collective-permute-start.1
  2230.1 115.1 %all-reduce.34.cloned.1.call-start = ((), (), s32[]{:S(2)}) async-start(), calls=%async_computation.21 | async-start | bytes 196608
  2249.0 279.0 %all-reduce.38.cloned.1.call-start = ((), (), s32[]{:S(2)}) async-start(), calls=%async_computation.23 | async-start | bytes 24526848 | tf_op jit(solution)/shard_map/psum | solution.py:308
  2256.8 444.2 %all-reduce.36.cloned.1.call-start = ((), (), s32[]{:S(2)}) async-start(), calls=%async_computation.22 | async-start | bytes 23592960
  2276.5 1069.0 %reduce-scatter.24.cloned.1.call-start = ((), (), s32[]{:S(2)}) async-start(), calls=%async_computation.19 | async-start | bytes 4227072 | tf_op jit(solution)/shard_map/reduce_scatter | solution.py:401
  2279.3 1702.6 %reduce-scatter.20.cloned.1.call-start = ((), (), s32[]{:S(2)}) async-start(), calls=%async_computation.17 | async-start | bytes 1056768 | tf_op jit(solution)/shard_map/reduce_scatter | solution.py:399
  2347.6 2270.6 %reduce-scatter.22.cloned.1.call-start = ((), (), s32[]{:S(2)}) async-start(), calls=%async_computation.18 | async-start | bytes 1056768 | tf_op jit(solution)/shard_map/reduce_scatter | solution.py:400
  2349.4 2909.2 %reduce-scatter.18.cloned.1.call-start = ((), (), s32[]{:S(2)}) async-start(), calls=%async_computation.16 | async-start | bytes 4227072 | tf_op jit(solution)/shard_map/reduce_scatter | solution.py:398
  2542.1 2716.4 %copy-start.1 = (bf16[1,1024,1024]{2,1,0:T(8,128)(2,1)S(1)}, bf16[1,1024,1024]{2,1,0:T(8,128)(2,1)}, u32[]{:S(2)}) copy-start(bf16[1,1024,1024]{2,1,0:T(8,128)(2,1)} %param.47) | copy-start | bytes 6291460
  (96 other events, 5441.1 us)
Sparse Core Ops, SparseCore 0:
  763.1 35.9 all-gather.12
  800.8 298.6 all-gather.14
  1101.2 306.8 all-gather.24
  1409.7 300.9 all-gather.16
  1715.5 46.6 all-gather.18
  1764.2 45.8 all-gather.22
  1811.8 297.2 all-gather.20
  2112.1 52.4 reduce-scatter.13
  2167.7 47.7 reduce-scatter.11
  2230.3 41.8 reduce-scatter.15
  2275.2 70.0 all-reduce.33
  2349.0 178.9 all-reduce.37
  2533.6 167.4 all-reduce.35
  2703.8 641.6 reduce-scatter.23
  3348.4 633.4 reduce-scatter.19
  3984.7 633.5 reduce-scatter.21
  4621.1 637.3 reduce-scatter.17
where the time goes:
time: 5270 us
  waiting for transfers between devices  3450 us (65%)
  blocking collectives  1560 us (30%)
  matrix products  136 us (3%)
    reduce_scatter x1, waiting for transfers between devices, on_device(): lax.psum_scatter(action_back[1], ('dp', 'mp'), scatter_dimension=0, tiled...  640 us
    reduce_scatter x1, waiting for transfers between devices, on_device(): lax.psum_scatter(action_out_grad, ('dp', 'mp'), scatter_dimension=0, tile...  640 us
    reduce_scatter x1, waiting for transfers between devices, on_device(): lax.psum_scatter(action_back[2], ('dp', 'mp'), scatter_dimension=0, tiled...  636 us
    reduce_scatter x1, waiting for transfers between devices, on_device(): lax.psum_scatter(action_back[3], ('dp', 'mp'), scatter_dimension=0, tiled...  636 us
    all_gather x1, blocking collectives, on_device(): lax.all_gather(prefix_value, ('dp', 'mp'), axis=0, tiled=True)  338 us
    all_gather x1, blocking collectives, on_device(): lax.all_gather(prefix_key, ('dp', 'mp'), axis=0, tiled=True)  336 us
    all_gather x1, blocking collectives, on_device(): lax.all_gather(action_value, ('dp', 'mp'), axis=0, tiled=True)  315 us
    all_gather x1, blocking collectives, on_device(): lax.all_gather(action_key, ('dp', 'mp'), axis=0, tiled=True)  313 us
  transfers between devices with their start and end apart: 21, of which 14 were waited for; matrix products, arithmetic and copies ran while one was open for 4% of the time, Pallas kernels for 0%

commit v1 on v0

v1 whole, which is shorter than its diff:
```python
import jax
import jax.numpy as jnp
from jax import lax
from jax.sharding import PartitionSpec as P

ACT_LEN = 48
EPSILON = 1e-06
ROPE_BASE = 10000.0
HEADS = 4
HD = 256
PREF = 192
ACT = 12
ACT_PAD = 16
BLOCK = PREF + ACT_PAD
N_MP = 8
bf16 = jnp.bfloat16
f32 = jnp.float32


def mp_swap(array, step):
    return lax.ppermute(array, "mp", [(i, i ^ step) for i in range(N_MP)])


def dp_swap(array, step):
    return lax.ppermute(array, "dp", [(i, i ^ step) for i in range(16)])


def yz_swap(array, step):
    return dp_swap(array, (step >> 2) * 8 + (step & 3) * 2)


def core_swap(array):
    return dp_swap(array, 1)


ORDER = (4, 1, 3, 6, 2, 5, 7)


def dot(a, b):
    return jnp.dot(a, b, preferred_element_type=f32)


def dot_t(a, b):
    return lax.dot_general(a, b, (((1,), (1,)), ((), ())), preferred_element_type=f32)


def t_dot(a, b):
    return lax.dot_general(a, b, (((0,), (0,)), ((), ())), preferred_element_type=f32)


def inverse_rms(rows):
    return lax.rsqrt(jnp.mean(rows * rows, axis=-1, keepdims=True) + EPSILON)


def normalize_back(rows, scale, gain, delta):
    a = delta * gain
    return scale * (a - rows * (scale * scale) * jnp.mean(a * rows, axis=-1, keepdims=True))


def rotate(rows, cosine, sine):
    half = HD // 2
    first, second = rows[:, :half], rows[:, half:]
    return jnp.concatenate(
        [first * cosine - second * sine, second * cosine + first * sine], axis=1
    )


def unrotate(rows, cosine, sine):
    return rotate(rows, cosine, -sine)


def angle_tables(place):
    half = HD // 2
    frequency = ROPE_BASE ** (-jnp.arange(half, dtype=f32) / half)
    angles = place.astype(f32)[:, None] * frequency[None, :]
    return jnp.cos(angles), jnp.sin(angles)


def gather_mp(array, index, order=ORDER):
    out = jnp.zeros((N_MP,) + array.shape, array.dtype)
    out = lax.dynamic_update_index_in_dim(out, array, index, 0)
    for step in order:
        out = lax.dynamic_update_index_in_dim(out, mp_swap(array, step), index ^ step, 0)
    return out


def gather_yz(array, index, order=ORDER):
    out = jnp.zeros((8,) + array.shape, array.dtype)
    out = lax.dynamic_update_index_in_dim(out, array, index, 0)
    for step in order:
        out = lax.dynamic_update_index_in_dim(out, yz_swap(array, step), index ^ step, 0)
    return out


def gather_core(array, core):
    other = core_swap(array)
    low = jnp.where(core == 0, array, other)
    high = jnp.where(core == 0, other, array)
    return jnp.stack([low, high], axis=1)


def scatter_sum(pieces, index, swap, order=ORDER):
    total = lax.dynamic_index_in_dim(pieces, index, 0, keepdims=False).astype(f32)
    for step in order:
        piece = lax.dynamic_index_in_dim(pieces, index ^ step, 0, keepdims=False)
        total = total + swap(piece, step).astype(f32)
    return total


def gelu_parts(gate):
    c0 = 0.7978845608028654
    c1 = 0.044715
    square = gate * gate
    tanh = jnp.tanh(c0 * gate * (1.0 + c1 * square))
    half = 0.5 * (1.0 + tanh)
    slope = half + 0.5 * gate * (1.0 - tanh * tanh) * c0 * (1.0 + 3.0 * c1 * square)
    return gate * half, slope


def feed_chunk(rows, seed, gate_weight, up_weight, down_weight, valid):
    gate = dot(rows, gate_weight)
    up = dot(rows, up_weight)
    active, slope = gelu_parts(gate)
    product_delta = dot_t(seed, down_weight)
    if valid is not None:
        active = active * valid
        product_delta = product_delta * valid
    product = (active * up).astype(bf16)
    gate_delta = (product_delta * up * slope).astype(bf16)
    up_delta = (product_delta * active).astype(bf16)
    rows_delta = dot_t(gate_delta, gate_weight) + dot_t(up_delta, up_weight)
    partial = dot(product, down_weight)
    return product, gate_delta, up_delta, rows_delta.astype(bf16), partial.astype(bf16)


def pad_action(rows):
    return jnp.pad(rows, ((0, ACT_PAD - ACT), (0, 0)))


def block_of(prefix_rows, action_rows):
    width = prefix_rows.shape[1] - action_rows.shape[1]
    return jnp.concatenate([prefix_rows, jnp.pad(action_rows, ((0, 0), (0, width)))], axis=0)


def on_device(
    prefix_input,
    action_input,
    prefix_cotangent,
    action_cotangent,
    prefix_lengths,
    mixture,
    cut_points,
    prefix_query,
    prefix_key,
    prefix_value,
    prefix_out,
    prefix_first_gain,
    prefix_second_gain,
    action_query,
    action_key,
    action_value,
    action_out,
    action_first_gain,
    action_second_gain,
    prefix_gate,
    prefix_up,
    prefix_down,
    action_gate,
    action_up,
    action_down,
):
    mp = lax.axis_index("mp")
    dp = lax.axis_index("dp")
    core = dp & 1
    yz = (dp >> 3) * 4 + ((dp >> 1) & 3)
    D = prefix_input.shape[2]
    DA = action_input.shape[2]

    lengths = prefix_lengths[0]
    first_length = lengths[0]
    prefix_rows = jnp.arange(N_MP * PREF, dtype=jnp.int32)
    prefix_item = (prefix_rows >= first_length).astype(jnp.int32)
    prefix_place = prefix_rows - jnp.where(prefix_item == 1, first_length, 0)
    slot = jnp.arange(N_MP * ACT_PAD, dtype=jnp.int32)
    slot_real = (slot % ACT_PAD) < ACT
    action_rows = (slot // ACT_PAD) * ACT + slot % ACT_PAD
    action_item = (action_rows >= ACT_LEN).astype(jnp.int32)
    action_place = jnp.where(action_item == 1, lengths[1], first_length) + action_rows % ACT_LEN
    action_item = jnp.where(slot_real, action_item, 2)
    key_item = jnp.concatenate([prefix_item, action_item])
    key_is_action = jnp.concatenate(
        [jnp.zeros((N_MP * PREF,), jnp.bool_), jnp.ones((N_MP * ACT_PAD,), jnp.bool_)]
    )
    own_prefix_item = lax.dynamic_slice_in_dim(prefix_item, mp * PREF, PREF)
    own_action_item = lax.dynamic_slice_in_dim(action_item, mp * ACT_PAD, ACT_PAD)
    own_item = jnp.concatenate([own_prefix_item, own_action_item])
    own_is_action = jnp.concatenate(
        [jnp.zeros((PREF,), jnp.bool_), jnp.ones((ACT_PAD,), jnp.bool_)]
    )
    visible = (own_item[:, None] == key_item[None, :]) & (
        own_is_action[:, None] | ~key_is_action[None, :]
    )
    all_place = jnp.concatenate([prefix_place, action_place])
    key_cos, key_sin = angle_tables(all_place)
    own_place = jnp.concatenate(
        [
            lax.dynamic_slice_in_dim(prefix_place, mp * PREF, PREF),
            lax.dynamic_slice_in_dim(action_place, mp * ACT_PAD, ACT_PAD),
        ]
    )
    own_cos, own_sin = angle_tables(own_place)

    own_action = pad_action(action_input[0])
    own_block = block_of(prefix_input[0], own_action)
    x_all = lax.all_gather(own_block, "mp", axis=0, tiled=False)

    share = mixture[0].astype(f32) / 32.0
    prefix_seed = prefix_cotangent[0].astype(f32) * jnp.where(
        own_prefix_item == 1, share[1], share[0]
    )[:, None]
    action_seed = pad_action(action_cotangent[0]).astype(f32) * jnp.where(
        own_action_item == 1, share[1], share[0]
    )[:, None]
    seed_block = block_of(prefix_seed.astype(bf16), action_seed.astype(bf16))
    seed_block, _ = lax.optimization_barrier((seed_block, x_all[0, :8, :128]))
    seed_all = lax.all_gather(seed_block, "mp", axis=0, tiled=False)

    def column_block(first, second):
        return jnp.pad(jnp.stack([first, second], axis=1), ((0, 0), (0, 126)))

    pack_d = jnp.concatenate(
        [
            prefix_key,
            prefix_value,
            column_block(prefix_first_gain, prefix_second_gain),
            prefix_query,
        ],
        axis=1,
    )
    pack_a = jnp.concatenate(
        [
            action_key,
            action_value,
            column_block(action_first_gain, action_second_gain),
            action_query,
            prefix_out,
            action_out,
        ],
        axis=1,
    )
    pack = jnp.concatenate([pack_d, jnp.pad(pack_a, ((0, 1), (0, 0)))], axis=1)
    wide = pack_d.shape[1]
    near = gather_mp(pack, mp)
    near_d = near[:, :, :wide].reshape(72, wide)
    near_a = near[:, :8, wide:].reshape(64, pack_a.shape[1])
    kv_pack = jnp.concatenate([near_d[:, :640], near_a[:, :640]], axis=0)
    q_pack = jnp.concatenate([near_d[:, 640:], near_a[:, 640:1664]], axis=0)
    o_pack = near_a[:, 1664:]
    kv_full = gather_core(gather_yz(kv_pack, yz), core)
    q_full = gather_core(gather_yz(q_pack, yz), core)
    o_full = gather_core(gather_yz(o_pack, yz), core)
    kv_d = kv_full[:, :, :72].reshape(D, 640)
    kv_a = kv_full[:, :, 72:].reshape(DA, 640)
    wkv_d, wkv_a = kv_d[:, :512], kv_a[:, :512]
    wq_d = q_full[:, :, :72].reshape(D, 1024)
    wq_a = q_full[:, :, 72:].reshape(DA, 1024)
    wo_d = o_full[..., :D].reshape(1024, D)
    wo_a = o_full[..., D:].reshape(1024, DA)
    gains_d = kv_d[:, 512:].T.astype(f32)
    gains_a = kv_a[:, 512:].T.astype(f32)
    first_gain_d, second_gain_d = gains_d[0:1], gains_d[1:2]
    first_gain_a, second_gain_a = gains_a[0:1], gains_a[1:2]

    all_x_d = x_all[:, :PREF].reshape(N_MP * PREF, D).astype(f32)
    all_x_a = x_all[:, PREF:, :DA].reshape(N_MP * ACT_PAD, DA).astype(f32)
    all_normed_d = (all_x_d * inverse_rms(all_x_d) * first_gain_d).astype(bf16)
    all_normed_a = (all_x_a * inverse_rms(all_x_a) * first_gain_a).astype(bf16)
    kv_raw = jnp.concatenate([dot(all_normed_d, wkv_d), dot(all_normed_a, wkv_a)], axis=0)
    keys = rotate(kv_raw[:, :HD], key_cos, key_sin).astype(bf16)
    values = kv_raw[:, HD:].astype(bf16)

    x_d = prefix_input[0].astype(f32)
    x_a = own_action.astype(f32)
    rms_d, rms_a = inverse_rms(x_d), inverse_rms(x_a)
    normed_d = (x_d * rms_d * first_gain_d).astype(bf16)
    normed_a = (x_a * rms_a * first_gain_a).astype(bf16)
    query_raw = jnp.concatenate([dot(normed_d, wq_d), dot(normed_a, wq_a)], axis=0)
    queries = jnp.concatenate(
        [
            (rotate(query_raw[:, h * HD : (h + 1) * HD], own_cos, own_sin) * HD**-0.5)
            for h in range(HEADS)
        ],
        axis=0,
    ).astype(bf16)

    mask = visible[None]
    scores = dot_t(queries, keys).reshape(HEADS, BLOCK, -1)
    scores = jnp.where(mask, scores, -1e30)
    top = jnp.max(scores, axis=-1, keepdims=True)
    shifted = jnp.exp(scores - top)
    probs = shifted / jnp.sum(shifted, axis=-1, keepdims=True)
    probs_low = probs.astype(bf16).reshape(HEADS * BLOCK, -1)
    context_rows = dot(probs_low, values).astype(bf16)
    context = jnp.concatenate(
        [context_rows[h * BLOCK : (h + 1) * BLOCK] for h in range(HEADS)], axis=1
    )
    context_d, context_a = context[:PREF], context[PREF:]

    hidden_d = x_d + dot(context_d, wo_d)
    real = (jnp.arange(ACT_PAD) < ACT)[:, None]
    hidden_a = jnp.where(real, x_a + dot(context_a, wo_a), 0.0)
    scale_d, scale_a = inverse_rms(hidden_d), inverse_rms(hidden_a)
    second_d = (hidden_d * scale_d * second_gain_d).astype(bf16)
    second_a = (hidden_a * scale_a * second_gain_a).astype(bf16)

    second_block = block_of(second_d, second_a)
    cut_pair = lax.dynamic_slice_in_dim(cut_points, mp, 2)
    valid = (jnp.arange(action_gate.shape[2], dtype=jnp.int32) < cut_pair[1] - cut_pair[0]).astype(
        f32
    )[None, :]
    steps = (0,) + ORDER
    blocks = {0: second_block}
    for k in ORDER:
        blocks[k] = mp_swap(second_block, k)
    seeds = {k: lax.dynamic_index_in_dim(seed_all, mp ^ k, 0, keepdims=False) for k in steps}
    done = {}
    for k in steps:
        done[k] = feed_chunk(
            blocks[k][:PREF], seeds[k][:PREF], prefix_gate, prefix_up, prefix_down, None
        )
    rows_a = jnp.concatenate([blocks[k][PREF:, :DA] for k in steps], axis=0)
    seeds_a = jnp.concatenate([seeds[k][PREF:, :DA] for k in steps], axis=0)
    done_a = feed_chunk(rows_a, seeds_a, action_gate[0], action_up[0], action_down[0], valid)

    def rows_for(item, which):
        k = steps[item]
        return block_of(done[k][which], done_a[which][item * ACT_PAD : (item + 1) * ACT_PAD])

    delta_total = rows_for(0, 3).astype(f32)
    for item in range(1, N_MP):
        delta_total = delta_total + mp_swap(rows_for(item, 3), steps[item]).astype(f32)
    out_total = rows_for(0, 4).astype(f32)
    for item in range(1, N_MP):
        out_total = out_total + mp_swap(rows_for(item, 4), steps[item]).astype(f32)
    prefix_output = (hidden_d + out_total[:PREF]).astype(bf16)[None]
    action_output = (hidden_a + out_total[PREF:, :DA])[:ACT].astype(bf16)[None]

    rows_d = jnp.concatenate([blocks[k][:PREF] for k in steps], axis=0)
    seeds_d = jnp.concatenate([seeds[k][:PREF] for k in steps], axis=0)
    product_d, gate_delta_d, up_delta_d = (
        jnp.concatenate([done[k][i] for k in steps], axis=0) for i in range(3)
    )
    mlp = (
        t_dot(rows_d, gate_delta_d),
        t_dot(rows_d, up_delta_d),
        t_dot(product_d, seeds_d),
        t_dot(rows_a, done_a[1]),
        t_dot(rows_a, done_a[2]),
        t_dot(done_a[0], seeds_a),
    )
    mlp = tuple(lax.psum(g.astype(bf16), "dp").astype(f32) for g in mlp)

    delta_d, delta_a = delta_total[:PREF], delta_total[PREF:, :DA]
    hidden_delta_d = prefix_seed + normalize_back(hidden_d, scale_d, second_gain_d, delta_d)
    hidden_delta_a = action_seed + normalize_back(hidden_a, scale_a, second_gain_a, delta_a)
    ones_d = jnp.ones((PREF, 128), bf16)
    ones_a = jnp.ones((ACT_PAD, 128), bf16)
    second_term_d = t_dot((delta_d * hidden_d * scale_d).astype(bf16), ones_d)
    second_term_a = t_dot((delta_a * hidden_a * scale_a).astype(bf16), ones_a)
    low_d, low_a = hidden_delta_d.astype(bf16), hidden_delta_a.astype(bf16)
    out_grad_d = t_dot(context_d, low_d)
    out_grad_a = t_dot(context_a, low_a)
    context_delta = jnp.concatenate([dot_t(low_d, wo_d), dot_t(low_a, wo_a)], axis=0).astype(bf16)
    context_delta = jnp.concatenate(
        [context_delta[:, h * HD : (h + 1) * HD] for h in range(HEADS)], axis=0
    )

    probs_delta = dot_t(context_delta, values).reshape(HEADS, BLOCK, -1)
    row_dot = jnp.sum(probs * probs_delta, axis=-1, keepdims=True)
    score_delta = (probs * (probs_delta - row_dot)).astype(bf16).reshape(HEADS * BLOCK, -1)
    queries_delta = dot(score_delta, keys)
    keys_delta = t_dot(score_delta, queries)
    values_delta = t_dot(probs_low, context_delta)
    query_raw_delta = jnp.concatenate(
        [
            unrotate(queries_delta[h * BLOCK : (h + 1) * BLOCK], own_cos, own_sin) * HD**-0.5
            for h in range(HEADS)
        ],
        axis=1,
    ).astype(bf16)
    key_raw_delta = unrotate(keys_delta, key_cos, key_sin)
    kv_delta = jnp.concatenate([key_raw_delta, values_delta], axis=1).astype(bf16)
    kv_pieces = jnp.concatenate(
        [
            kv_delta[: N_MP * PREF].reshape(N_MP, PREF, 512),
            kv_delta[N_MP * PREF :].reshape(N_MP, ACT_PAD, 512),
        ],
        axis=1,
    )
    kv_own = scatter_sum(kv_pieces, mp, mp_swap).astype(bf16)

    q_grad_d = t_dot(normed_d, query_raw_delta[:PREF])
    q_grad_a = t_dot(normed_a, query_raw_delta[PREF:])
    kv_grad_d = t_dot(all_normed_d, kv_delta[: N_MP * PREF])
    kv_grad_a = t_dot(all_normed_a, kv_delta[N_MP * PREF :])

    def split(array):
        return array.astype(bf16).reshape(8, 2, -1, array.shape[1])

    o_grads = split(jnp.concatenate([out_grad_d, out_grad_a], axis=1))
    q_grads = jnp.concatenate(
        [
            split(jnp.concatenate([q_grad_d, second_term_d], axis=1)),
            split(jnp.concatenate([q_grad_a, second_term_a], axis=1)),
        ],
        axis=2,
    )
    kv_grads = jnp.concatenate([split(kv_grad_d), split(kv_grad_a)], axis=2)

    def reduce_far(pieces):
        mine = lax.dynamic_index_in_dim(pieces, core, 1, keepdims=False)
        theirs = lax.dynamic_index_in_dim(pieces, 1 - core, 1, keepdims=False)
        summed = (mine.astype(f32) + core_swap(theirs).astype(f32)).astype(bf16)
        return scatter_sum(summed, yz, yz_swap)

    o_near = reduce_far(o_grads)
    q_near = reduce_far(q_grads)
    kv_near = reduce_far(kv_grads)
    last_d = jnp.concatenate([q_near[:72], kv_near[:72]], axis=1).astype(bf16)
    last_a = jnp.concatenate([q_near[72:], kv_near[72:], o_near], axis=1).astype(bf16)
    last = jnp.concatenate(
        [
            last_d.reshape(N_MP, 9, -1),
            jnp.pad(last_a.reshape(N_MP, 8, -1), ((0, 0), (0, 1), (0, 0))),
        ],
        axis=2,
    )
    last = scatter_sum(last, mp, mp_swap)
    w_d = last_d.shape[1]
    grads_d, grads_a = last[:, :w_d], last[:8, w_d:]

    def split_grads(grads, query, key, value, gain):
        query_grad = grads[:, :1024]
        second = grads[:, 1024]
        key_grad = grads[:, 1152:1408]
        value_grad = grads[:, 1408:1664]
        first = (
            jnp.sum(query_grad * query.astype(f32), axis=1)
            + jnp.sum(key_grad * key.astype(f32), axis=1)
            + jnp.sum(value_grad * value.astype(f32), axis=1)
        ) / gain.astype(f32)
        return query_grad, key_grad, value_grad, first, second

    gd = split_grads(grads_d, prefix_query, prefix_key, prefix_value, prefix_first_gain)
    ga = split_grads(grads_a, action_query, action_key, action_value, action_first_gain)
    prefix_out_grad = grads_a[:, 1664 : 1664 + D]
    action_out_grad = grads_a[:, 1664 + D :]

    first_delta_d = dot_t(query_raw_delta[:PREF], wq_d) + dot_t(kv_own[:PREF], wkv_d)
    first_delta_a = dot_t(query_raw_delta[PREF:], wq_a) + dot_t(kv_own[PREF:], wkv_a)
    input_d = hidden_delta_d + normalize_back(x_d, rms_d, first_gain_d, first_delta_d)
    input_a = hidden_delta_a + normalize_back(x_a, rms_a, first_gain_a, first_delta_a)

    return (
        prefix_output,
        action_output,
        input_d.astype(bf16)[None],
        input_a[:ACT].astype(bf16)[None],
        gd[0],
        gd[1],
        gd[2],
        prefix_out_grad,
        gd[3],
        gd[4],
        ga[0],
        ga[1],
        ga[2],
        action_out_grad,
        ga[3],
        ga[4],
        mlp[0],
        mlp[1],
        mlp[2],
        mlp[3][None],
        mlp[4][None],
        mlp[5][None],
    )


def solution(mesh):
    rows = P("dp", "mp", None)
    both = P(("dp", "mp"), None)
    vector = P(("dp", "mp"))
    slots = P("mp", None, None)
    return jax.shard_map(
        on_device,
        mesh=mesh,
        in_specs=(rows,) * 4
        + (P("dp", None), P("dp", None), P())
        + (both,) * 4
        + (vector,) * 2
        + (both,) * 4
        + (vector,) * 2
        + (P(None, "mp"), P(None, "mp"), P("mp", None))
        + (slots,) * 3,
        out_specs=(rows,) * 4
        + (both,) * 4
        + (vector,) * 2
        + (both,) * 4
        + (vector,) * 2
        + (P(None, "mp"), P(None, "mp"), P("mp", None))
        + (slots,) * 3,
        check_vma=False,
    )
```

time: 5270 us -> 806 us (0.15)
  waiting for transfers between devices: 3450 us -> 304 us
  blocking collectives: 1560 us -> 0 us
  starting transfers between devices: 13.7 us -> 158 us
  other arithmetic: 46.3 us -> 120 us
    reduce_scatter x7 -> x0, waiting for transfers between devices: 2570 us -> none  [the longest x1 640 us: on_device(): lax.psum_scatter(action_back[1], ('dp', 'mp'), scatter_dimension=0, tiled...]
    all_gather x7 -> x0, blocking collectives: 1390 us -> none  [the longest x1 338 us: on_device(): lax.all_gather(prefix_value, ('dp', 'mp'), axis=0, tiled=True)]
    all_gather x7 -> x2, waiting for transfers between devices: 557 us -> 0.01 us  [the longest x1 0.01 us: on_device(): seed_all = lax.all_gather(seed_block, 'mp', axis=0, tiled=False)]
    ppermute x0 -> x90, waiting for transfers between devices: none -> 304 us  [the longest x42 173 us: mp_swap(): return lax.ppermute(array, 'mp', [(i, i ^ step) for i in range(N_MP)])]
    unnamed x23 -> x3, waiting for transfers between devices: 226 us -> 0.05 us
    unnamed x3 -> x0, blocking collectives: 164 us -> none
    ppermute x0 -> x90, starting transfers between devices: none -> 158 us  [the longest x48 84 us: dp_swap(): return lax.ppermute(array, 'dp', [(i, i ^ step) for i in range(16)])]
    psum x1, waiting for transfers between devices: 91.2 us -> 0.01 us  [on_device(): mlp = tuple((lax.psum(g.astype(bf16), 'dp').astype(f32) for g in mlp))]
  transfers between devices with their start and end apart: 21 -> 93, of which waited for: 14 -> 36; matrix products, arithmetic and copies ran while one was open for 4% -> 27% of each run, Pallas kernels for 0% -> 0%
where the time goes in v1:
time: 806 us; the launch traced here: 795 us
  waiting for transfers between devices  304 us (38%)
  starting transfers between devices  158 us (20%)
  matrix products  126 us (16%)
  other arithmetic  120 us (15%)
  local copies, waits for them, and re-layouts  68.8 us (9%)
  between operations  18.1 us (2%)
    ppermute x42, waiting for transfers between devices, mp_swap(): return lax.ppermute(array, 'mp', [(i, i ^ step) for i in range(N_MP)])  173 us
    ppermute x48, waiting for transfers between devices, dp_swap(): return lax.ppermute(array, 'dp', [(i, i ^ step) for i in range(16)])  131 us
    ppermute x48, starting transfers between devices, dp_swap(): return lax.ppermute(array, 'dp', [(i, i ^ step) for i in range(16)])  84 us
    ppermute x42, starting transfers between devices, mp_swap(): return lax.ppermute(array, 'mp', [(i, i ^ step) for i in range(N_MP)])  73.8 us
    dot_general x35, matrix products, dot(): return jnp.dot(a, b, preferred_element_type=f32)  51.7 us
    dot_general x16, matrix products, t_dot(): lax.dot_general(a, b, (((0,), (0,)), ((), ())), preferred_element_type=f32)  38.6 us
    dot_general x35, matrix products, dot_t(): lax.dot_general(a, b, (((1,), (1,)), ((), ())), preferred_element_type=f32)  35.4 us
    unnamed x367, local copies, waits for them, and re-layouts  31 us
  transfers between devices with their start and end apart: 93, of which 36 were waited for; matrix products, arithmetic and copies ran while one was open for 27% of the time, Pallas kernels for 0%

profile of v1, /device:TPU:0, one launch (start us, length us, event | category | flops | bytes accessed | tf_op | source)
XLA Modules:
  0.0 794.9 jit_solution(5956941735902404746)
XLA Ops:
  57.6 4.8 collective-permute-done.6
  78.9 12.8 %collective-permute-done.7 = bf16[136,640]{1,0:T(8,128)(2,1)S(1)} collective-permute-done((bf16[136,640]{1,0:T(8,128)(2,1)S(1)}, bf16[136,640]{1,0:T(8,128)(2,1)S(1)}, u32[]{:S(2)}, u32[]{:S(2)}) %collective-permute-start.7) | collective-permute-done | bytes 174112 | tf_op jit(solution)/shard_map/ppermute | solution.py:25
  95.2 7.5 collective-permute-done.9
  103.9 4.4 collective-permute-done.10
  113.3 10.2 %collective-permute-done.12 = bf16[136,640]{1,0:T(8,128)(2,1)S(1)} collective-permute-done((bf16[136,640]{1,0:T(8,128)(2,1)S(1)}, bf16[136,640]{1,0:T(8,128)(2,1)S(1)}, u32[]{:S(2)}, u32[]{:S(2)}) %collective-permute-start.12) | collective-permute-done | bytes 174112 | tf_op jit(solution)/shard_map/ppermute | solution.py:25
  129.0 26.1 %collective-permute-done.23 = bf16[64,2176]{1,0:T(8,128)(2,1)S(1)} collective-permute-done((bf16[64,2176]{1,0:T(8,128)(2,1)S(1)}, bf16[64,2176]{1,0:T(8,128)(2,1)S(1)}, u32[]{:S(2)}, u32[]{:S(2)}) %collective-permute-start.23) | collective-permute-done | bytes 278560 | tf_op jit(solution)/shard_map/ppermute | solution.py:25
  156.5 7.1 collective-permute-done.24
  166.4 6.2 collective-permute-done.25
  185.9 6.0 collective-permute-done.20
  194.2 10.4 %collective-permute-done.21 = bf16[136,1024]{1,0:T(8,128)(2,1)S(1)} collective-permute-done((bf16[136,1024]{1,0:T(8,128)(2,1)S(1)}, bf16[136,1024]{1,0:T(8,128)(2,1)S(1)}, u32[]{:S(2)}, u32[]{:S(2)}) %collective-permute-start.21) | collective-permute-done | bytes 278560 | tf_op jit(solution)/shard_map/ppermute | solution.py:25
  205.2 5.0 collective-permute-done.28
  224.0 5.6 slice_convert_fusion
  230.5 5.5 fusion.1
  239.0 4.2 fusion.72
  243.4 4.2 fusion.116
  292.6 6.9 collective-permute-done.33
  301.8 15.8 %collective-permute-done.36 = bf16[208,1152]{1,0:T(8,128)(2,1)S(1)} collective-permute-done((bf16[208,1152]{1,0:T(8,128)(2,1)}, bf16[208,1152]{1,0:T(8,128)(2,1)S(1)}, u32[]{:S(2)}, u32[]{:S(2)}) %collective-permute-start.36) | collective-permute-done | bytes 479264 | tf_op jit(solution)/shard_map/ppermute | solution.py:21
  356.2 5.1 convolution_convert_fusion.2
  361.3 5.1 convolution_convert_fusion.3
  400.4 5.0 convolution_convert_fusion.1
  428.5 26.6 %collective-permute-done.50 = bf16[208,1152]{1,0:T(8,128)(2,1)S(1)} collective-permute-done((bf16[208,1152]{1,0:T(8,128)(2,1)S(1)}, bf16[208,1152]{1,0:T(8,128)(2,1)S(1)}, u32[]{:S(2)}, u32[]{:S(2)}) %collective-permute-start.50) | collective-permute-done | bytes 479264 | tf_op jit(solution)/shard_map/ppermute | solution.py:21
  462.1 60.5 %collective-permute-done.38 = bf16[208,1152]{1,0:T(8,128)(2,1)S(1)} collective-permute-done((bf16[208,1152]{1,0:T(8,128)(2,1)S(1)}, bf16[208,1152]{1,0:T(8,128)(2,1)S(1)}, u32[]{:S(2)}, u32[]{:S(2)}) %collective-permute-start.38) | collective-permute-done | bytes 479264 | tf_op jit(solution)/shard_map/ppermute | solution.py:21
  522.7 5.0 collective-permute-start.43
  530.5 18.2 %collective-permute-done.43 = bf16[208,1152]{1,0:T(8,128)(2,1)S(1)} collective-permute-done((bf16[208,1152]{1,0:T(8,128)(2,1)S(1)}, bf16[208,1152]{1,0:T(8,128)(2,1)S(1)}, u32[]{:S(2)}, u32[]{:S(2)}) %collective-permute-start.43) | collective-permute-done | bytes 479264 | tf_op jit(solution)/shard_map/ppermute | solution.py:21
  562.6 4.4 fusion.112
  608.0 20.8 %collective-permute-done.52 = bf16[208,512]{1,0:T(8,128)(2,1)} collective-permute-done((bf16[208,512]{1,0:T(8,128)(2,1)}, bf16[208,512]{1,0:T(8,128)(2,1)}, u32[]{:S(2)}, u32[]{:S(2)}) %collective-permute-start.52) | collective-permute-done | bytes 213024 | tf_op jit(solution)/shard_map/ppermute | solution.py:21
  634.8 5.7 collective-permute-done.57
  688.5 4.1 collective-permute-done.76
  698.3 4.6 collective-permute-done.78
  716.5 7.8 collective-permute-done.60
  731.0 10.1 %collective-permute-done.65 = bf16[136,1152]{1,0:T(8,128)(2,1)S(1)} collective-permute-done((bf16[136,1152]{1,0:T(8,128)(2,1)S(1)}, bf16[136,1152]{1,0:T(8,128)(2,1)S(1)}, u32[]{:S(2)}, u32[]{:S(2)}) %collective-permute-start.65) | collective-permute-done | bytes 313376 | tf_op jit(solution)/shard_map/ppermute | solution.py:25
  772.0 4.2 broadcast_in_dim.288
  (829 shorter events, 447.0 us)
Async XLA Ops:
  7.2 216.8 %all-gather.5.cloned.1.call-start = ((), (), s32[]{:S(2)}) async-start(), calls=%async_computation | async-start | bytes 4313088 | tf_op jit(solution)/shard_map/all_gather | solution.py:215
  10.8 257.6 %all-gather.7.cloned.1.call-start = ((), (), s32[]{:S(2)}) async-start(), calls=%async_computation.1 | async-start | bytes 4313088 | tf_op jit(solution)/shard_map/all_gather | solution.py:226
  24.0 28.8 %collective-permute-start.4 = (bf16[9,5504]{1,0:T(8,128)(2,1)S(1)}, bf16[9,5504]{1,0:T(8,128)(2,1)S(1)}, u32[]{:S(2)}, u32[]{:S(2)}) collective-permute-start(bf16[9,5504]{1,0:T(8,128)(2,1)S(1)} %constant_dynamic-update-slice_fusion.6), channel_id=1, source_target_pairs={{0,2},{1,3},{2,0},{3,1},{4,6},{5,7},{6,4},{7,5},{8,10},{9,11},{10,... | collective-permute-start | bytes 297224 | tf_op jit(solution)/shard_map/ppermute | solution.py:21
  34.7 737.3 %all-reduce.28.cloned.1.call-start = ((), (), s32[]{:S(2)}) async-start(), calls=%async_computation.2 | async-start | bytes 24526848 | tf_op jit(solution)/shard_map/psum | solution.py:361
  68.4 106.0 %collective-permute-start.15 = (bf16[136,1024]{1,0:T(8,128)(2,1)S(1)}, bf16[136,1024]{1,0:T(8,128)(2,1)S(1)}, u32[]{:S(2)}, u32[]{:S(2)}) collective-permute-start(bf16[136,1024]{1,0:T(8,128)(2,1)S(1)} %pad_maximum_fusion.13), channel_id=1, source_target_pairs={{0,64},{8,72},{16,80},{24,88},{32,96},{40,104},{48,112},{56,120},{... | collective-permute-start | bytes 835592 | tf_op jit(solution)/shard_map/ppermute | solution.py:25
  72.1 104.0 %collective-permute-start.16 = (bf16[136,1024]{1,0:T(8,128)(2,1)S(1)}, bf16[136,1024]{1,0:T(8,128)(2,1)S(1)}, u32[]{:S(2)}, u32[]{:S(2)}) collective-permute-start(bf16[136,1024]{1,0:T(8,128)(2,1)S(1)} %pad_maximum_fusion.13), channel_id=1, source_target_pairs={{0,16},{8,24},{16,0},{24,8},{32,48},{40,56},{48,32},{56,40},{64,80... | collective-permute-start | bytes 835592 | tf_op jit(solution)/shard_map/ppermute | solution.py:25
  73.7 105.6 %collective-permute-start.17 = (bf16[136,1024]{1,0:T(8,128)(2,1)S(1)}, bf16[136,1024]{1,0:T(8,128)(2,1)S(1)}, u32[]{:S(2)}, u32[]{:S(2)}) collective-permute-start(bf16[136,1024]{1,0:T(8,128)(2,1)S(1)} %pad_maximum_fusion.13), channel_id=1, source_target_pairs={{0,48},{8,56},{16,32},{24,40},{32,16},{40,24},{48,0},{56,8},{64,11... | collective-permute-start | bytes 835592 | tf_op jit(solution)/shard_map/ppermute | solution.py:25
  123.5 31.5 %collective-permute-start.23 = (bf16[64,2176]{1,0:T(8,128)(2,1)S(1)}, bf16[64,2176]{1,0:T(8,128)(2,1)S(1)}, u32[]{:S(2)}, u32[]{:S(2)}) collective-permute-start(bf16[64,2176]{1,0:T(8,128)(2,1)S(1)} %slice.674), channel_id=1, source_target_pairs={{0,64},{8,72},{16,80},{24,88},{32,96},{40,104},{48,112},{56,120},{... | collective-permute-start | bytes 835592 | tf_op jit(solution)/shard_map/ppermute | solution.py:25
  126.3 54.7 %collective-permute-start.18 = (bf16[136,1024]{1,0:T(8,128)(2,1)S(1)}, bf16[136,1024]{1,0:T(8,128)(2,1)S(1)}, u32[]{:S(2)}, u32[]{:S(2)}) collective-permute-start(bf16[136,1024]{1,0:T(8,128)(2,1)S(1)} %pad_maximum_fusion.13), channel_id=1, source_target_pairs={{0,96},{8,104},{16,112},{24,120},{32,64},{40,72},{48,80},{56,88},{... | collective-permute-start | bytes 835592 | tf_op jit(solution)/shard_map/ppermute | solution.py:25
  176.1 28.4 %collective-permute-start.21 = (bf16[136,1024]{1,0:T(8,128)(2,1)S(1)}, bf16[136,1024]{1,0:T(8,128)(2,1)S(1)}, u32[]{:S(2)}, u32[]{:S(2)}) collective-permute-start(bf16[136,1024]{1,0:T(8,128)(2,1)S(1)} %pad_maximum_fusion.13), channel_id=1, source_target_pairs={{0,112},{8,120},{16,96},{24,104},{32,80},{40,88},{48,64},{56,72},{... | collective-permute-start | bytes 835592 | tf_op jit(solution)/shard_map/ppermute | solution.py:25
  263.6 35.9 %collective-permute-start.33 = (bf16[208,1152]{1,0:T(8,128)(2,1)}, bf16[208,1152]{1,0:T(8,128)(2,1)}, u32[]{:S(2)}, u32[]{:S(2)}) collective-permute-start(bf16[208,1152]{1,0:T(8,128)(2,1)} %fusion.148), channel_id=1, source_target_pairs={{0,3},{1,2},{2,1},{3,0},{4,7},{5,6},{6,5},{7,4},{8,11},{9,10},{10,... | collective-permute-start | bytes 1437704 | tf_op jit(solution)/shard_map/ppermute | solution.py:21
  264.1 36.2 %collective-permute-start.34 = (bf16[208,1152]{1,0:T(8,128)(2,1)}, bf16[208,1152]{1,0:T(8,128)(2,1)}, u32[]{:S(2)}, u32[]{:S(2)}) collective-permute-start(bf16[208,1152]{1,0:T(8,128)(2,1)} %fusion.148), channel_id=1, source_target_pairs={{0,6},{1,7},{2,4},{3,5},{4,2},{5,3},{6,0},{7,1},{8,14},{9,15},{10,... | collective-permute-start | bytes 1437704 | tf_op jit(solution)/shard_map/ppermute | solution.py:21
  267.6 33.4 %collective-permute-start.35 = (bf16[208,1152]{1,0:T(8,128)(2,1)}, bf16[208,1152]{1,0:T(8,128)(2,1)}, u32[]{:S(2)}, u32[]{:S(2)}) collective-permute-start(bf16[208,1152]{1,0:T(8,128)(2,1)} %fusion.148), channel_id=1, source_target_pairs={{0,2},{1,3},{2,0},{3,1},{4,6},{5,7},{6,4},{7,5},{8,10},{9,11},{10,... | collective-permute-start | bytes 1437704 | tf_op jit(solution)/shard_map/ppermute | solution.py:21
  286.2 31.4 %collective-permute-start.36 = (bf16[208,1152]{1,0:T(8,128)(2,1)}, bf16[208,1152]{1,0:T(8,128)(2,1)S(1)}, u32[]{:S(2)}, u32[]{:S(2)}) collective-permute-start(bf16[208,1152]{1,0:T(8,128)(2,1)} %fusion.148), channel_id=1, source_target_pairs={{0,5},{1,4},{2,7},{3,6},{4,1},{5,0},{6,3},{7,2},{8,13},{9,12},{10,... | collective-permute-start | bytes 1437704 | tf_op jit(solution)/shard_map/ppermute | solution.py:21
  289.2 28.5 %collective-permute-start.37 = (bf16[208,1152]{1,0:T(8,128)(2,1)}, bf16[208,1152]{1,0:T(8,128)(2,1)S(1)}, u32[]{:S(2)}, u32[]{:S(2)}) collective-permute-start(bf16[208,1152]{1,0:T(8,128)(2,1)} %fusion.148), channel_id=1, source_target_pairs={{0,7},{1,6},{2,5},{3,4},{4,3},{5,2},{6,1},{7,0},{8,15},{9,14},{10,... | collective-permute-start | bytes 1437704 | tf_op jit(solution)/shard_map/ppermute | solution.py:21
  381.9 39.5 %collective-permute-start.45 = (bf16[208,1152]{1,0:T(8,128)(2,1)}, bf16[208,1152]{1,0:T(8,128)(2,1)}, u32[]{:S(2)}, u32[]{:S(2)}) collective-permute-start(bf16[208,1152]{1,0:T(8,128)(2,1)} %fusion.158), channel_id=1, source_target_pairs={{0,4},{1,5},{2,6},{3,7},{4,0},{5,1},{6,2},{7,3},{8,12},{9,13},{10,... | collective-permute-start | bytes 1437704 | tf_op jit(solution)/shard_map/ppermute | solution.py:21
  385.6 37.5 %collective-permute-start.46 = (bf16[208,1152]{1,0:T(8,128)(2,1)}, bf16[208,1152]{1,0:T(8,128)(2,1)}, u32[]{:S(2)}, u32[]{:S(2)}) collective-permute-start(bf16[208,1152]{1,0:T(8,128)(2,1)} %fusion.159), channel_id=1, source_target_pairs={{0,1},{1,0},{2,3},{3,2},{4,5},{5,4},{6,7},{7,6},{8,9},{9,8},{10,11... | collective-permute-start | bytes 1437704 | tf_op jit(solution)/shard_map/ppermute | solution.py:21
  388.2 37.6 %collective-permute-start.47 = (bf16[208,1152]{1,0:T(8,128)(2,1)}, bf16[208,1152]{1,0:T(8,128)(2,1)}, u32[]{:S(2)}, u32[]{:S(2)}) collective-permute-start(bf16[208,1152]{1,0:T(8,128)(2,1)} %fusion.160), channel_id=1, source_target_pairs={{0,3},{1,2},{2,1},{3,0},{4,7},{5,6},{6,5},{7,4},{8,11},{9,10},{10,... | collective-permute-start | bytes 1437704 | tf_op jit(solution)/shard_map/ppermute | solution.py:21
  391.1 36.2 %collective-permute-start.48 = (bf16[208,1152]{1,0:T(8,128)(2,1)}, bf16[208,1152]{1,0:T(8,128)(2,1)}, u32[]{:S(2)}, u32[]{:S(2)}) collective-permute-start(bf16[208,1152]{1,0:T(8,128)(2,1)} %fusion.161), channel_id=1, source_target_pairs={{0,6},{1,7},{2,4},{3,5},{4,2},{5,3},{6,0},{7,1},{8,14},{9,15},{10,... | collective-permute-start | bytes 1437704 | tf_op jit(solution)/shard_map/ppermute | solution.py:21
  396.2 31.5 %collective-permute-start.49 = (bf16[208,1152]{1,0:T(8,128)(2,1)}, bf16[208,1152]{1,0:T(8,128)(2,1)}, u32[]{:S(2)}, u32[]{:S(2)}) collective-permute-start(bf16[208,1152]{1,0:T(8,128)(2,1)} %fusion.162), channel_id=1, source_target_pairs={{0,2},{1,3},{2,0},{3,1},{4,6},{5,7},{6,4},{7,5},{8,10},{9,11},{10,... | collective-permute-start | bytes 1437704 | tf_op jit(solution)/shard_map/ppermute | solution.py:21
  421.5 33.6 %collective-permute-start.50 = (bf16[208,1152]{1,0:T(8,128)(2,1)S(1)}, bf16[208,1152]{1,0:T(8,128)(2,1)S(1)}, u32[]{:S(2)}, u32[]{:S(2)}) collective-permute-start(bf16[208,1152]{1,0:T(8,128)(2,1)S(1)} %copy-done.85), channel_id=1, source_target_pairs={{0,5},{1,4},{2,7},{3,6},{4,1},{5,0},{6,3},{7,2},{8,13},{9,12},{10,... | collective-permute-start | bytes 1437704 | tf_op jit(solution)/shard_map/ppermute | solution.py:21
  423.2 34.4 %collective-permute-start.51 = (bf16[208,1152]{1,0:T(8,128)(2,1)S(1)}, bf16[208,1152]{1,0:T(8,128)(2,1)S(1)}, u32[]{:S(2)}, u32[]{:S(2)}) collective-permute-start(bf16[208,1152]{1,0:T(8,128)(2,1)S(1)} %fusion.164), channel_id=1, source_target_pairs={{0,7},{1,6},{2,5},{3,4},{4,3},{5,2},{6,1},{7,0},{8,15},{9,14},{10,... | collective-permute-start | bytes 1437704 | tf_op jit(solution)/shard_map/ppermute | solution.py:21
  425.8 96.9 %collective-permute-start.38 = (bf16[208,1152]{1,0:T(8,128)(2,1)S(1)}, bf16[208,1152]{1,0:T(8,128)(2,1)S(1)}, u32[]{:S(2)}, u32[]{:S(2)}) collective-permute-start(bf16[208,1152]{1,0:T(8,128)(2,1)S(1)} %copy-done.84), channel_id=1, source_target_pairs={{0,4},{1,5},{2,6},{3,7},{4,0},{5,1},{6,2},{7,3},{8,12},{9,13},{10,... | collective-permute-start | bytes 1437704 | tf_op jit(solution)/shard_map/ppermute | solution.py:21
  427.4 100.3 %collective-permute-start.39 = (bf16[208,1152]{1,0:T(8,128)(2,1)S(1)}, bf16[208,1152]{1,0:T(8,128)(2,1)S(1)}, u32[]{:S(2)}, u32[]{:S(2)}) collective-permute-start(bf16[208,1152]{1,0:T(8,128)(2,1)S(1)} %copy-done.83), channel_id=1, source_target_pairs={{0,1},{1,0},{2,3},{3,2},{4,5},{5,4},{6,7},{7,6},{8,9},{9,8},{10,11... | collective-permute-start | bytes 1437704 | tf_op jit(solution)/shard_map/ppermute | solution.py:21
  427.8 102.7 %collective-permute-start.40 = (bf16[208,1152]{1,0:T(8,128)(2,1)S(1)}, bf16[208,1152]{1,0:T(8,128)(2,1)S(1)}, u32[]{:S(2)}, u32[]{:S(2)}) collective-permute-start(bf16[208,1152]{1,0:T(8,128)(2,1)S(1)} %copy-done.82), channel_id=1, source_target_pairs={{0,3},{1,2},{2,1},{3,0},{4,7},{5,6},{6,5},{7,4},{8,11},{9,10},{10,... | collective-permute-start | bytes 1437704 | tf_op jit(solution)/shard_map/ppermute | solution.py:21
  455.0 75.4 %collective-permute-start.41 = (bf16[208,1152]{1,0:T(8,128)(2,1)S(1)}, bf16[208,1152]{1,0:T(8,128)(2,1)S(1)}, u32[]{:S(2)}, u32[]{:S(2)}) collective-permute-start(bf16[208,1152]{1,0:T(8,128)(2,1)S(1)} %copy-done.81), channel_id=1, source_target_pairs={{0,6},{1,7},{2,4},{3,5},{4,2},{5,3},{6,0},{7,1},{8,14},{9,15},{10,... | collective-permute-start | bytes 1437704 | tf_op jit(solution)/shard_map/ppermute | solution.py:21
  457.6 72.9 %collective-permute-start.42 = (bf16[208,1152]{1,0:T(8,128)(2,1)S(1)}, bf16[208,1152]{1,0:T(8,128)(2,1)S(1)}, u32[]{:S(2)}, u32[]{:S(2)}) collective-permute-start(bf16[208,1152]{1,0:T(8,128)(2,1)S(1)} %copy-done.80), channel_id=1, source_target_pairs={{0,2},{1,3},{2,0},{3,1},{4,6},{5,7},{6,4},{7,5},{8,10},{9,11},{10,... | collective-permute-start | bytes 1437704 | tf_op jit(solution)/shard_map/ppermute | solution.py:21
  587.2 41.5 %collective-permute-start.52 = (bf16[208,512]{1,0:T(8,128)(2,1)}, bf16[208,512]{1,0:T(8,128)(2,1)}, u32[]{:S(2)}, u32[]{:S(2)}) collective-permute-start(bf16[208,512]{1,0:T(8,128)(2,1)} %get-tuple-element.138), channel_id=1, source_target_pairs={{0,4},{1,5},{2,6},{3,7},{4,0},{5,1},{6,2},{7,3},{8,12},{9,13},{10,... | collective-permute-start | bytes 638984 | tf_op jit(solution)/shard_map/ppermute | solution.py:21
  588.0 42.2 %collective-permute-start.53 = (bf16[208,512]{1,0:T(8,128)(2,1)}, bf16[208,512]{1,0:T(8,128)(2,1)}, u32[]{:S(2)}, u32[]{:S(2)}) collective-permute-start(bf16[208,512]{1,0:T(8,128)(2,1)} %get-tuple-element.139), channel_id=1, source_target_pairs={{0,1},{1,0},{2,3},{3,2},{4,5},{5,4},{6,7},{7,6},{8,9},{9,8},{10,11... | collective-permute-start | bytes 638984 | tf_op jit(solution)/shard_map/ppermute | solution.py:21
  590.4 43.8 %collective-permute-start.54 = (bf16[208,512]{1,0:T(8,128)(2,1)}, bf16[208,512]{1,0:T(8,128)(2,1)}, u32[]{:S(2)}, u32[]{:S(2)}) collective-permute-start(bf16[208,512]{1,0:T(8,128)(2,1)} %get-tuple-element.140), channel_id=1, source_target_pairs={{0,3},{1,2},{2,1},{3,0},{4,7},{5,6},{6,5},{7,4},{8,11},{9,10},{10,... | collective-permute-start | bytes 638984 | tf_op jit(solution)/shard_map/ppermute | solution.py:21
  591.2 43.0 %collective-permute-start.55 = (bf16[208,512]{1,0:T(8,128)(2,1)}, bf16[208,512]{1,0:T(8,128)(2,1)}, u32[]{:S(2)}, u32[]{:S(2)}) collective-permute-start(bf16[208,512]{1,0:T(8,128)(2,1)} %get-tuple-element.141), channel_id=1, source_target_pairs={{0,6},{1,7},{2,4},{3,5},{4,2},{5,3},{6,0},{7,1},{8,14},{9,15},{10,... | collective-permute-start | bytes 638984 | tf_op jit(solution)/shard_map/ppermute | solution.py:21
  592.8 42.0 %collective-permute-start.56 = (bf16[208,512]{1,0:T(8,128)(2,1)}, bf16[208,512]{1,0:T(8,128)(2,1)}, u32[]{:S(2)}, u32[]{:S(2)}) collective-permute-start(bf16[208,512]{1,0:T(8,128)(2,1)} %get-tuple-element.142), channel_id=1, source_target_pairs={{0,2},{1,3},{2,0},{3,1},{4,6},{5,7},{6,4},{7,5},{8,10},{9,11},{10,... | collective-permute-start | bytes 638984 | tf_op jit(solution)/shard_map/ppermute | solution.py:21
  (226 other events, 4050.6 us)
Sparse Core Ops, SparseCore 0:
  10.9 69.1 all-gather.4
  81.7 66.4 all-gather.6
  418.1 211.7 all-reduce.27

commit v2 on v1

v2 whole, which is shorter than its diff:
```python
import functools

import jax
import jax.numpy as jnp
import numpy as np
from jax import lax
from jax.experimental import pallas as pl
from jax.experimental.pallas import tpu as pltpu
from jax.sharding import PartitionSpec as P

ACT_LEN = 48
EPSILON = 1e-06
ROPE_BASE = 10000.0
HEADS = 4
HD = 256
PREF = 192
ACT = 12
ACT_PAD = 16
BLOCK = PREF + ACT_PAD
N_MP = 8
HALF_A = 96
HALF_B = BLOCK - HALF_A
HIDDEN_PAD = 896
VMEM_FEED = 50
bf16 = jnp.bfloat16
f32 = jnp.float32
ANY = pl.BlockSpec(memory_space=pl.ANY)
SMEM = pl.BlockSpec(memory_space=pltpu.SMEM)
VMEM = pl.BlockSpec(memory_space=pltpu.VMEM)
ARRIVALS = (
    ((0, 0), (0, 1)),
    ((1, 0), (1, 1)),
    ((3, 0), (3, 1)),
    ((4, 0), (4, 1)),
    ((5, 0), (7, 0)),
    ((2, 0), (5, 1)),
    ((2, 1), (7, 1)),
    ((6, 0),),
    ((6, 1),),
)
PARTS = tuple(part for parts in ARRIVALS for part in parts)
ROW_BLOCK = np.concatenate([np.full((HALF_A, HALF_B)[h], k) for k, h in PARTS]).astype(np.int32)
ROW_ID = np.concatenate(
    [np.arange(HALF_A) if h == 0 else np.arange(HALF_A, BLOCK) for _, h in PARTS]
).astype(np.int32)


def mp_swap(array, step):
    return lax.ppermute(array, "mp", [(i, i ^ step) for i in range(N_MP)])


def dp_swap(array, step):
    return lax.ppermute(array, "dp", [(i, i ^ step) for i in range(16)])


def yz_swap(array, step):
    return dp_swap(array, (step >> 2) * 8 + (step & 3) * 2)


def core_swap(array):
    return dp_swap(array, 1)


def where_parts(first, arrays, sizes):
    where = {}
    for i in range(arrays):
        at = 0
        for k, h in ARRIVALS[first + i]:
            where[k, h] = (i, at)
            at += sizes[h]
    return where


def fence_kernel(*refs):
    pass


def fence(array, *after):
    return pl.pallas_call(
        fence_kernel,
        in_specs=[pl.BlockSpec(memory_space=pl.ANY)] * (1 + len(after)),
        out_specs=pl.BlockSpec(memory_space=pl.ANY),
        out_shape=jax.ShapeDtypeStruct(array.shape, array.dtype),
        input_output_aliases={0: 0},
        cost_estimate=pl.CostEstimate(flops=0, bytes_accessed=0, transcendentals=0),
        name="fence",
    )(array, *after)


def join(*parts):
    return jnp.concatenate(parts, axis=0)


def add_low(*parts):
    total = parts[0].astype(f32)
    for part in parts[1:]:
        total = total + part.astype(f32)
    return total.astype(bf16)


def held(array, after):
    return fence(array, *after) if after else array


def relay_gather(a, b, swap, during=None, hold=None):
    na, nb = a.shape[0], b.shape[0]
    during = during or (lambda stage, arrived, sends: ())
    hold = hold or {}
    own = held(join(a, b), hold.get(1, ()))
    s1, s3, s4 = swap(own, 1), swap(own, 3), swap(own, 4)
    after = during(1, (own,), (own,)) + hold.get(2, ())
    sends = (join(s1[:na], s3[:na]), join(s3[:na], s4[na:]), join(s1[na:], s4[na:]))
    sends = tuple(held(x, after) for x in sends)
    zz, v1, v3 = swap(sends[0], 4), swap(sends[1], 1), swap(sends[2], 3)
    after = during(2, (s1, s3, s4), sends) + hold.get(3, ())
    sends = (held(zz[na:], after), held(v1[na:], after))
    z2a, z2b = swap(sends[0], 1), swap(sends[1], 3)
    during(3, (zz, v1, v3), sends)
    return own, s1, s3, s4, zz, v1, v3, z2a, z2b


def relay_scatter(pa, pb, swap, hold=None, sent=None):
    na, nb = pa[0].shape[0], pb[0].shape[0]
    hold = hold or {}
    sent = {} if sent is None else sent
    get = lambda stage: hold[stage]() if stage in hold else ()
    after = get(1)
    sent[1] = (held(pa[6], after), held(pb[6], after))
    r1, r3 = swap(sent[1][0], 1), swap(sent[1][1], 3)
    p7a = add_low(pa[7], r1)
    p5b = add_low(pb[5], r3)
    after = get(2)
    sends = (join(pa[5], p7a), join(pa[2], p5b), join(pb[2], pb[7]))
    sent[2] = tuple(held(x, after) for x in sends)
    zz, v1, v3 = swap(sent[2][0], 4), swap(sent[2][1], 1), swap(sent[2][2], 3)
    p1 = join(add_low(pa[1], zz[:na]), add_low(pb[1], v3[:nb]))
    p3 = join(add_low(pa[3], zz[na:], v1[:na]), pb[3])
    p4 = join(pa[4], add_low(pb[4], v1[na:], v3[nb:]))
    after = get(3)
    sent[3] = tuple(held(x, after) for x in (p1, p3, p4))
    s1, s3, s4 = swap(sent[3][0], 1), swap(sent[3][1], 3), swap(sent[3][2], 4)
    return pa[0], pb[0], s1, s3, s4


def total_of(pieces):
    pa, pb, s1, s3, s4 = pieces
    na = pa.shape[0]
    total_a = pa.astype(f32) + s1[:na].astype(f32) + s3[:na].astype(f32) + s4[:na].astype(f32)
    total_b = pb.astype(f32) + s1[na:].astype(f32) + s3[na:].astype(f32) + s4[na:].astype(f32)
    return total_a, total_b


def ring_scatter(pieces, swap, hold=None, sent=None):
    n = pieces[0].shape[0]
    hold = hold or {}
    near = [join(pieces[j], pieces[j ^ 4]) for j in range(4)]
    near[1:] = [held(x, hold.get(1, ())) for x in near[1:]]
    if sent is not None:
        sent += near[1:]
    total = near[0].astype(f32)
    for j in (1, 3, 2):
        total = total + swap(near[j], j).astype(f32)
    return total[:n] + swap(held(total[n:].astype(bf16), hold.get(2, ())), 4).astype(f32)


def gather_direct(array, index, swap):
    pair = index & 4
    high = (index >> 2) & 1
    two = jnp.zeros((2,) + array.shape, array.dtype)
    two = lax.dynamic_update_index_in_dim(two, array, high, 0)
    two = lax.dynamic_update_index_in_dim(two, swap(array, 4), 1 - high, 0)
    ring = index & 3
    out = jnp.zeros((2, 4) + array.shape, array.dtype)
    out = lax.dynamic_update_index_in_dim(out, two, ring, 1)
    for step in (1, 3, 2):
        out = lax.dynamic_update_index_in_dim(out, swap(two, step), ring ^ step, 1)
    return out.reshape((8,) + array.shape)


def scatter_direct(pieces, index, swap):
    high = (index >> 2) & 1
    ring = index & 3
    quads = pieces.reshape((2, 4) + pieces.shape[1:])
    total = lax.dynamic_index_in_dim(quads, ring, 1, keepdims=False).astype(f32)
    for step in (1, 3, 2):
        piece = lax.dynamic_index_in_dim(quads, ring ^ step, 1, keepdims=False)
        total = total + swap(piece, step).astype(f32)
    mine = lax.dynamic_index_in_dim(total, high, 0, keepdims=False)
    theirs = lax.dynamic_index_in_dim(total, 1 - high, 0, keepdims=False)
    return mine + swap(theirs.astype(bf16), 4).astype(f32)


def place_kernel(sizes, index_ref, *refs):
    arrays, outs = refs[:9], refs[9:]
    for (k, h), (i, at) in where_parts(0, 9, sizes).items():
        outs[h][index_ref[0] ^ k] = arrays[i][at : at + sizes[h]]


def place(arrays, na, index):
    rows, columns = arrays[0].shape
    eights = [x.reshape(x.shape[0] // 8, 8, columns) for x in arrays]
    sizes = (na // 8, (rows - na) // 8)
    return pl.pallas_call(
        functools.partial(place_kernel, sizes),
        in_specs=[SMEM] + [VMEM] * 9,
        out_specs=[VMEM] * 2,
        out_shape=[jax.ShapeDtypeStruct((8, n, 8, columns), bf16) for n in sizes],
        compiler_params=pltpu.CompilerParams(vmem_limit_bytes=20 * 1024 * 1024),
        name="place",
    )(index.reshape(1), *eights)


def interleave_kernel(cuts, core_ref, *refs):
    mine, theirs, outs = refs[:2], refs[2:4], refs[4:]
    core = core_ref[0]
    for out, (which, first, n) in zip(outs, cuts):
        for i in range(8):
            out[i, core] = mine[which][i, first : first + n]
            out[i, 1 - core] = theirs[which][i, first : first + n]


def interleave(halves_of, cuts, core):
    theirs = [core_swap(x) for x in halves_of]
    columns = halves_of[0].shape[-1]
    outs = pl.pallas_call(
        functools.partial(interleave_kernel, cuts),
        in_specs=[SMEM] + [VMEM] * 4,
        out_specs=[VMEM] * len(cuts),
        out_shape=[jax.ShapeDtypeStruct((8, 2, n, 8, columns), bf16) for _, _, n in cuts],
        compiler_params=pltpu.CompilerParams(vmem_limit_bytes=40 * 1024 * 1024),
        name="interleave",
    )(core.reshape(1), *halves_of, *theirs)
    return [x.reshape(-1, columns) for x in outs]


def gelu_parts(gate):
    c0 = 0.7978845608028654
    c1 = 0.044715
    square = gate * gate
    tanh = jnp.tanh(c0 * gate * (1.0 + c1 * square))
    half = 0.5 * (1.0 + tanh)
    slope = half + 0.5 * gate * (1.0 - tanh * tanh) * c0 * (1.0 + 3.0 * c1 * square)
    return gate * half, slope


def feed_block(rows, seed, gate_weight, up_weight, down_weight, valid):
    into, out_of = (dot_t, dot) if valid is None else (dot, dot_t)
    gate = into(rows, gate_weight)
    up = into(rows, up_weight)
    active, slope = gelu_parts(gate)
    product_delta = dot_t(seed, down_weight)
    if valid is not None:
        active = active * valid
        product_delta = product_delta * valid
    product = (active * up).astype(bf16)
    gate_delta = (product_delta * up * slope).astype(bf16)
    up_delta = (product_delta * active).astype(bf16)
    rows_delta = out_of(gate_delta, gate_weight) + out_of(up_delta, up_weight)
    return product, gate_delta, up_delta, rows_delta.astype(bf16)


def feed_kernel(layout, *refs):
    arrays = 1 + max(i for parts in layout for i, _ in parts)
    rows_refs, seed_refs, refs = refs[:arrays], refs[arrays : 2 * arrays], refs[2 * arrays :]
    gate_ref, up_ref, down_ref = refs[:3]
    action_gate_ref, action_up_ref, action_down_ref, valid_ref = refs[3:7]
    count = len(layout)
    outs = refs[-(2 * count + 8) :]
    products, deltas, kept_rows, kept_seeds = outs[:4]
    action_products, action_deltas, action_rows, action_seeds = outs[4:8]
    width = action_gate_ref.shape[0]
    rest = PREF - HALF_A

    def prefix_of(blocks):
        parts = []
        for (ia, a), (ib, b) in layout:
            parts += [blocks[ia][a : a + HALF_A], blocks[ib][b : b + rest]]
        return join(*parts)

    def action_of(blocks):
        parts = []
        for _, (ib, b) in layout:
            parts.append(blocks[ib][b + rest : b + HALF_B, :width])
        return join(*parts) if count > 1 else parts[0]

    rows, seed = prefix_of(rows_refs), prefix_of(seed_refs)
    product, gate_delta, up_delta, rows_delta = feed_block(
        rows, seed, gate_ref[...], up_ref[...], down_ref[...], None
    )
    hidden = product.shape[1]
    spare = jnp.zeros((count * PREF, HIDDEN_PAD - hidden), bf16)
    products[:, :hidden] = product
    products[:, hidden:] = spare
    deltas[:, :hidden] = gate_delta
    deltas[:, hidden:HIDDEN_PAD] = spare
    deltas[:, HIDDEN_PAD : HIDDEN_PAD + hidden] = up_delta
    deltas[:, HIDDEN_PAD + hidden :] = spare
    kept_rows[...] = rows
    kept_seeds[...] = seed
    rows, seed = action_of(rows_refs), action_of(seed_refs)
    product, gate_delta, up_delta, action_rows_delta = feed_block(
        rows,
        seed,
        action_gate_ref[...],
        action_up_ref[...],
        action_down_ref[...],
        valid_ref[...],
    )
    slots = gate_delta.shape[1]
    action_products[...] = product
    action_deltas[:, :slots] = gate_delta
    action_deltas[:, slots:] = up_delta
    action_rows[...] = rows
    action_seeds[...] = seed
    blank = jnp.zeros((ACT_PAD, rows_delta.shape[1] - width), bf16)
    for i in range(count):
        a, b, c = i * PREF, i * PREF + HALF_A, (i + 1) * PREF
        extra = slice(i * ACT_PAD, (i + 1) * ACT_PAD)
        ref_a, ref_b = outs[8 + 2 * i : 10 + 2 * i]
        ref_a[...] = rows_delta[a:b]
        ref_b[:rest] = rows_delta[b:c]
        ref_b[rest:, :width] = action_rows_delta[extra]
        ref_b[rest:, width:] = blank


def feed(arrays, seeds, weights, layout, base, kept, after):
    count = len(layout)
    width = arrays[0].shape[1]
    hidden = weights[0].shape[0]
    action_width, slots = weights[3].shape
    once = pl.Buffered(1)
    at = base // count

    def whole(array):
        return pl.BlockSpec(array.shape, lambda i: (0, 0), pipeline_mode=once)

    def part(size, columns):
        return (
            jax.ShapeDtypeStruct((N_MP * size, columns), bf16),
            pl.BlockSpec((count * size, columns), lambda i: (at, 0), pipeline_mode=once),
        )

    def own(size):
        return (
            jax.ShapeDtypeStruct((size, width), bf16),
            pl.BlockSpec((size, width), lambda i: (0, 0), pipeline_mode=once),
        )

    outs = [
        part(PREF, HIDDEN_PAD),
        part(PREF, 2 * HIDDEN_PAD),
        part(PREF, width),
        part(PREF, width),
        part(ACT_PAD, slots),
        part(ACT_PAD, 2 * slots),
        part(ACT_PAD, action_width),
        part(ACT_PAD, action_width),
    ] + [own(HALF_A), own(HALF_B)] * count
    reused = [] if kept is None else list(kept)
    given = [*arrays, *seeds]
    placed = len(given) + len(weights)
    results = pl.pallas_call(
        functools.partial(feed_kernel, layout),
        grid=(1,),
        in_specs=[whole(x) for x in given]
        + [VMEM] * len(weights)
        + [ANY] * (len(reused) + len(after)),
        out_shape=[shape for shape, _ in outs],
        out_specs=[spec for _, spec in outs],
        input_output_aliases={placed + i: i for i in range(len(reused))},
        compiler_params=pltpu.CompilerParams(
            dimension_semantics=("arbitrary",), vmem_limit_bytes=VMEM_FEED * 1024 * 1024
        ),
        cost_estimate=pl.CostEstimate(
            flops=10 * count * (PREF * width * hidden + ACT_PAD * action_width * slots),
            bytes_accessed=6 * (width * hidden + action_width * slots),
            transcendentals=count * PREF * hidden,
        ),
        name="feed",
    )(*given, *weights, *reused, *after)
    blocks = [results[8 + 2 * i : 10 + 2 * i] for i in range(count)]
    return blocks, results[:8]


def see(own_ref, key_ref):
    own, key = own_ref[...], key_ref[...]
    return (own[:, 0:1] == key[0:1]) | (own[:, 1:2] == key[1:2])


def attend_kernel(*refs):
    (normed_d, normed_a, x_d, x_a, wq_d, wq_a, wo_m, wo_e, wo_a) = refs[:9]
    (gain_d, gain_a, cosine, sine, own_codes, key_codes) = refs[9:15]
    kv = refs[15:24]
    (queries, context, tops, totals, hidden_d, hidden_a, block) = refs[24:]
    raw = join(dot(normed_d[...], wq_d[...]), dot(normed_a[...], wq_a[...]))
    keys = join(*[ref[:, :HD] for ref in kv])
    values = join(*[ref[:, HD:] for ref in kv])
    visible = see(own_codes, key_codes)
    cos, sin = cosine[...], sine[...]
    heads = []
    for h in range(HEADS):
        rows = slice(h * BLOCK, (h + 1) * BLOCK)
        query = (rotate(raw[:, h * HD : (h + 1) * HD], cos, sin) * HD**-0.5).astype(bf16)
        queries[rows] = query
        scores = jnp.where(visible, dot_t(query, keys), -1e30)
        top = jnp.max(scores, axis=1, keepdims=True)
        shifted = jnp.exp(scores - top)
        total = jnp.sum(shifted, axis=1, keepdims=True)
        tops[rows] = top
        totals[rows] = total
        heads.append(dot((shifted / total).astype(bf16), values).astype(bf16))
    mixed = jnp.concatenate(heads, axis=1)
    context[...] = mixed
    main, width_d, width_a = wo_m.shape[1], x_d.shape[1], x_a.shape[1]
    low_d, low_a = mixed[:PREF], mixed[PREF:]
    state = x_d[...].astype(f32) + jnp.concatenate(
        [dot(low_d, wo_m[...]), dot(low_d, wo_e[...])], axis=1
    )
    hidden_d[...] = state
    second_d = (state * inverse_rms(state) * gain_d[...]).astype(bf16)
    real = lax.broadcasted_iota(jnp.int32, (ACT_PAD, width_a), 0) < ACT
    state = jnp.where(real, x_a[...].astype(f32) + dot(low_a, wo_a[...]), 0.0)
    hidden_a[...] = state
    second_a = (state * inverse_rms(state) * gain_a[...]).astype(bf16)
    block[:PREF] = second_d
    block[PREF:, :width_a] = second_a
    block[PREF:, width_a:] = jnp.zeros((ACT_PAD, width_d - width_a), bf16)


def attend(*given):
    x_d, x_a = given[2:4]
    width_d, width_a = x_d.shape[1], x_a.shape[1]
    shape = jax.ShapeDtypeStruct
    stacked = HEADS * BLOCK
    return pl.pallas_call(
        attend_kernel,
        out_shape=[
            shape((stacked, HD), bf16),
            shape((BLOCK, HEADS * HD), bf16),
            shape((stacked, 1), f32),
            shape((stacked, 1), f32),
            shape((PREF, width_d), f32),
            shape((ACT_PAD, width_a), f32),
            shape((BLOCK, width_d), bf16),
        ],
        compiler_params=pltpu.CompilerParams(vmem_limit_bytes=50 * 1024 * 1024),
        cost_estimate=pl.CostEstimate(
            flops=4 * BLOCK * HEADS * HD * (N_MP * BLOCK + width_d),
            bytes_accessed=4 * 1024 * 1024 * 5,
            transcendentals=stacked * N_MP * BLOCK,
        ),
        name="attend",
    )(*given)


def attend_back_kernel(*refs):
    pieces = refs[:5]
    (hidden_d, hidden_a, cotangent_d, cotangent_a, share, gain_d, gain_a) = refs[5:12]
    (wo_m, wo_e, wo_a, queries, tops, totals, cosine, sine, own_codes, key_codes) = refs[12:22]
    kv = refs[22:31]
    outs = refs[-(6 + len(PARTS)) :]
    (hidden_delta_d, hidden_delta_a, low, terms_d, terms_a, query_delta) = outs[:6]
    kv_deltas = outs[6:]
    delta = join(*total_of([piece[...] for piece in pieces]))
    width_d, width_a = hidden_d.shape[1], hidden_a.shape[1]
    lows = []
    for rows, state_ref, cotangent, gain, out, terms in (
        (slice(0, PREF), hidden_d, cotangent_d, gain_d, hidden_delta_d, terms_d),
        (slice(PREF, BLOCK), hidden_a, cotangent_a, gain_a, hidden_delta_a, terms_a),
    ):
        state = state_ref[...]
        change = delta[rows, : state.shape[1]]
        scale = inverse_rms(state)
        seed = cotangent[...].astype(f32) * share[rows]
        back = seed + normalize_back(state, scale, gain[...], change)
        out[...] = back
        terms[...] = (change * state * scale).astype(bf16)
        lows.append(back.astype(bf16))
    low_d, low_a = lows
    low[:PREF] = low_d
    low[PREF:, :width_a] = low_a
    low[PREF:, width_a:] = jnp.zeros((ACT_PAD, width_d - width_a), bf16)
    main = wo_m.shape[1]
    context_delta = join(
        dot_t(low_d[:, :main], wo_m[...]) + dot_t(low_d[:, main:], wo_e[...]),
        dot_t(low_a, wo_a[...]),
    ).astype(bf16)
    keys = join(*[ref[:, :HD] for ref in kv])
    values = join(*[ref[:, HD:] for ref in kv])
    visible = see(own_codes, key_codes)
    cos, sin = cosine[...], sine[...]
    keys_delta, values_delta = None, None
    for h in range(HEADS):
        rows = slice(h * BLOCK, (h + 1) * BLOCK)
        query = queries[rows]
        change = context_delta[:, h * HD : (h + 1) * HD]
        scores = jnp.where(visible, dot_t(query, keys), -1e30)
        probs = jnp.exp(scores - tops[rows]) / totals[rows]
        probs_delta = dot_t(change, values)
        row_dot = jnp.sum(probs * probs_delta, axis=1, keepdims=True)
        score_delta = (probs * (probs_delta - row_dot)).astype(bf16)
        turned = unrotate(dot(score_delta, keys), cos, sin) * HD**-0.5
        query_delta[:, h * HD : (h + 1) * HD] = turned.astype(bf16)
        key_part = t_dot(score_delta, query)
        value_part = t_dot(probs.astype(bf16), change)
        keys_delta = key_part if h == 0 else keys_delta + key_part
        values_delta = value_part if h == 0 else values_delta + value_part
    at = 0
    for (_, half), out in zip(PARTS, kv_deltas):
        n = (HALF_A, HALF_B)[half]
        out[:, :HD] = keys_delta[at : at + n].astype(bf16)
        out[:, HD:] = values_delta[at : at + n].astype(bf16)
        at += n


def attend_back(*given):
    hidden_d, hidden_a = given[5:7]
    width_d, width_a = hidden_d.shape[1], hidden_a.shape[1]
    shape = jax.ShapeDtypeStruct
    stacked = HEADS * BLOCK
    outs = pl.pallas_call(
        attend_back_kernel,
        out_shape=[
            shape((PREF, width_d), f32),
            shape((ACT_PAD, width_a), f32),
            shape((BLOCK, width_d), bf16),
            shape((PREF, width_d), bf16),
            shape((ACT_PAD, width_a), bf16),
            shape((BLOCK, HEADS * HD), bf16),
        ]
        + [shape(((HALF_A, HALF_B)[half], 2 * HD), bf16) for _, half in PARTS],
        compiler_params=pltpu.CompilerParams(vmem_limit_bytes=50 * 1024 * 1024),
        cost_estimate=pl.CostEstimate(
            flops=2 * BLOCK * HEADS * HD, bytes_accessed=4 * BLOCK, transcendentals=stacked
        ),
        name="attend_back",
    )(*given)
    kv_deltas = dict(zip(PARTS, outs[6:]))
    pa = {k: kv_deltas[k, 0] for k in range(8)}
    pb = {k: kv_deltas[k, 1] for k in range(8)}
    return outs[:6], pa, pb


def pad_action(rows):
    return jnp.pad(rows, ((0, ACT_PAD - ACT), (0, 0)))


def widen(rows, width):
    return jnp.pad(rows, ((0, 0), (0, width - rows.shape[1])))


def block_of(prefix_rows, action_rows):
    return join(prefix_rows, widen(action_rows, prefix_rows.shape[1]))


def order_matrix(size, rows):
    d = jnp.arange(size, dtype=jnp.int32)
    r = d % rows
    mp = (d // rows) % 8
    dp = d // (8 * rows)
    place = (dp % 2) * (size // 2) + mp * (8 * rows) + (dp // 2) * rows + r
    return (place[:, None] == jnp.arange(size, dtype=jnp.int32)[None, :]).astype(bf16)


def dot(a, b):
    return jnp.dot(a, b, preferred_element_type=f32)


def dot_t(a, b):
    return lax.dot_general(a, b, (((1,), (1,)), ((), ())), preferred_element_type=f32)


def t_dot(a, b):
    return lax.dot_general(a, b, (((0,), (0,)), ((), ())), preferred_element_type=f32)


def inverse_rms(rows):
    return lax.rsqrt(jnp.mean(rows * rows, axis=-1, keepdims=True) + EPSILON)


def normalize_back(rows, scale, gain, delta):
    a = delta * gain
    return scale * (a - rows * (scale * scale) * jnp.mean(a * rows, axis=-1, keepdims=True))


def rotate(rows, cosine, sine):
    half = HD // 2
    first, second = rows[:, :half], rows[:, half:]
    return jnp.concatenate(
        [first * cosine - second * sine, second * cosine + first * sine], axis=1
    )


def unrotate(rows, cosine, sine):
    return rotate(rows, cosine, -sine)


def angle_tables(place):
    half = HD // 2
    frequency = ROPE_BASE ** (-jnp.arange(half, dtype=f32) / half)
    angles = place.astype(f32)[:, None] * frequency[None, :]
    return jnp.cos(angles), jnp.sin(angles)


def on_device(
    prefix_input,
    action_input,
    prefix_cotangent,
    action_cotangent,
    prefix_lengths,
    mixture,
    cut_points,
    prefix_query,
    prefix_key,
    prefix_value,
    prefix_out,
    prefix_first_gain,
    prefix_second_gain,
    action_query,
    action_key,
    action_value,
    action_out,
    action_first_gain,
    action_second_gain,
    prefix_gate,
    prefix_up,
    prefix_down,
    action_gate,
    action_up,
    action_down,
):
    mp = lax.axis_index("mp")
    dp = lax.axis_index("dp")
    core = dp & 1
    yz = (dp >> 3) * 4 + ((dp >> 1) & 3)
    D = prefix_input.shape[2]
    DA = action_input.shape[2]

    def column_block(first, second):
        return jnp.pad(jnp.stack([first, second], axis=1), ((0, 0), (0, 126)))

    pack_d = jnp.concatenate(
        [
            prefix_key,
            prefix_value,
            column_block(prefix_first_gain, prefix_second_gain),
            prefix_query,
        ],
        axis=1,
    )
    wide = pack_d.shape[1]
    pack = jnp.concatenate(
        [
            pack_d[:8],
            action_key,
            action_value,
            column_block(action_first_gain, action_second_gain),
            action_query,
            action_out,
            prefix_out,
            jnp.pad(pack_d[8:].reshape(8, wide // 8), ((0, 0), (0, 48))),
        ],
        axis=1,
    )
    lengths = prefix_lengths[0]
    first_length = lengths[0]

    def tables(source, row):
        is_action = row >= PREF
        prefix_row = source * PREF + row
        prefix_item = (prefix_row >= first_length).astype(jnp.int32)
        prefix_place = prefix_row - jnp.where(prefix_item == 1, first_length, 0)
        action_row = source * ACT + row - PREF
        action_item = (action_row >= ACT_LEN).astype(jnp.int32)
        action_place = jnp.where(action_item == 1, lengths[1], first_length) + action_row % ACT_LEN
        action_item = jnp.where(row - PREF < ACT, action_item, 2)
        item = jnp.where(is_action, action_item, prefix_item)
        place = jnp.where(is_action, action_place, prefix_place)
        return item, place, is_action

    own_item, own_place, own_is_action = tables(mp, jnp.arange(BLOCK, dtype=jnp.int32))
    key_item, _, key_is_action = tables(jnp.asarray(ROW_BLOCK) ^ mp, jnp.asarray(ROW_ID))
    own_codes = jnp.stack([own_item, jnp.where(own_is_action, own_item, -2)], axis=1)
    key_codes = jnp.stack(
        [jnp.where(key_is_action, -1, key_item), jnp.where(key_is_action, key_item, -1)], axis=0
    )
    own_cos, own_sin = angle_tables(own_place)

    share = mixture[0].astype(f32) / 32.0
    row_share = jnp.where(own_item == 1, share[1], share[0])[:, None]
    cotangent_a = pad_action(action_cotangent[0])
    prefix_seed = prefix_cotangent[0].astype(f32) * row_share[:PREF]
    action_seed = cotangent_a.astype(f32) * row_share[PREF:]
    seed_block = block_of(prefix_seed.astype(bf16), action_seed.astype(bf16))

    near = gather_direct(pack, mp, mp_swap)
    last_row = near[:, :, pack.shape[1] - 256 : pack.shape[1] - 48].reshape(8, 1, wide)
    near_d = jnp.concatenate([near[:, :, :wide], last_row], axis=1).reshape(72, wide)
    near_a = near[:, :, wide : pack.shape[1] - 256].reshape(64, -1)
    kv_a = jnp.concatenate([near_a[:, :640], near_a[:, 2688 + 1024 :]], axis=1)
    kv_d = widen(near_d[:, :640], 768)
    qo_a = join(near_a[:, 640:1664], near_a[:, 1664:2688])
    qo_b = join(near_d[:, 640:], near_a[:, 2688 : 2688 + 1024])

    seed_block = fence(seed_block, near)
    seeds = relay_gather(seed_block[:HALF_A], seed_block[HALF_A:], mp_swap)
    arrived = {}

    def note(name):
        def during(stage, blocks, sends):
            arrived[name, stage] = blocks
            return ()

        return during

    kv_halves = place(relay_gather(kv_a, kv_d, yz_swap, note("kv"), {3: seeds[1:4]}), 64, yz)
    kv_a, kv_d = interleave(kv_halves, ((0, 0, 8), (1, 0, 9)), core)
    wkv_d, wkv_a, wo_e = kv_d[:, :512], kv_a[:, :512], kv_a[:, 640:]
    gains_d = kv_d[:, 512:640].T.astype(f32)
    gains_a = kv_a[:, 512:640].T.astype(f32)
    first_gain_d, second_gain_d = gains_d[0:1], gains_d[1:2]
    first_gain_a, second_gain_a = gains_a[0:1], gains_a[1:2]

    own_action = pad_action(action_input[0])
    x_d, x_a = prefix_input[0].astype(f32), own_action.astype(f32)
    rms_d, rms_a = inverse_rms(x_d), inverse_rms(x_a)
    normed_d = (x_d * rms_d * first_gain_d).astype(bf16)
    normed_a = (x_a * rms_a * first_gain_a).astype(bf16)
    kv_raw = join(dot(normed_d, wkv_d), dot(normed_a, wkv_a))
    kv_own = jnp.concatenate(
        [rotate(kv_raw[:, :HD], own_cos, own_sin).astype(bf16), kv_raw[:, HD:].astype(bf16)],
        axis=1,
    )
    kv_rows = relay_gather(kv_own[:HALF_A], kv_own[HALF_A:], mp_swap, note("rows"))
    qo_a = fence(qo_a, arrived["kv", 2][0])
    qo_hold = {2: (kv_own, *seeds[4:7]), 3: (*arrived["rows", 2], *seeds[7:9])}
    qo_halves = place(relay_gather(qo_a, qo_b, yz_swap, note("qo"), qo_hold), 128, yz)
    cuts = ((0, 0, 8), (0, 8, 8), (1, 0, 9), (1, 9, 8))
    wq_a, wo_a, wq_d, wo_m = interleave(qo_halves, cuts, core)
    queries, context, tops, totals, hidden_d, hidden_a, second_block = attend(
        normed_d,
        normed_a,
        prefix_input[0],
        own_action,
        wq_d,
        wq_a,
        wo_m,
        wo_e,
        wo_a,
        second_gain_d,
        second_gain_a,
        own_cos,
        own_sin,
        own_codes,
        key_codes,
        *kv_rows,
    )

    slots = action_gate.shape[2]
    cut_pair = lax.dynamic_slice_in_dim(cut_points, mp, 2)
    valid = (jnp.arange(slots, dtype=jnp.int32) < cut_pair[1] - cut_pair[0]).astype(f32)[None, :]
    weights = (prefix_gate.T, prefix_up.T, prefix_down)
    weights += (action_gate[0], action_up[0], action_down[0], valid)
    kept = None
    results = {}

    def run(arrays, first, blocks, base, after):
        nonlocal kept
        where = where_parts(first, len(arrays), (HALF_A, HALF_B))
        layout = tuple((where[k, 0], where[k, 1]) for k in blocks)
        some = seeds[first : first + len(arrays)]
        done, kept = feed(arrays, some, weights, layout, base, kept, after)
        results.update(zip(blocks, done))
        return (done[0][0],)

    def feed_during(stage, arrays, sends):
        first, blocks, base = {1: (0, (0,), 6), 2: (1, (1, 3, 4), 0), 3: (4, (2, 5, 7), 3)}[stage]
        return run(arrays, first, blocks, base, sends)

    second_block = fence(second_block, seeds[8])
    arrays = relay_gather(
        second_block[:HALF_A], second_block[HALF_A:], mp_swap, feed_during
    )
    run(arrays[7:], 7, (6,), 7, ())
    product_d, deltas_d, rows_d, seeds_d, product_a, deltas_a, rows_a, seeds_a = kept

    grads = (
        t_dot(deltas_d, rows_d),
        t_dot(product_d, seeds_d),
        t_dot(rows_a, deltas_a),
        t_dot(product_a, seeds_a),
    )
    hidden = prefix_down.shape[0]
    grads = tuple(g.astype(bf16) for g in grads)
    after_grads = tuple(grads)
    one = lax.psum(grads[0], "dp")
    grads = (one,) + tuple(lax.psum(fence(g, one), "dp") for g in grads[1:])
    finished = (
        grads[0][:hidden].astype(f32),
        grads[0][HIDDEN_PAD : HIDDEN_PAD + hidden].astype(f32),
        grads[1][:hidden].astype(f32),
        grads[2][:, :slots].astype(f32),
        grads[2][:, slots:].astype(f32),
        grads[3].astype(f32),
    )

    pa = {k: v[0] for k, v in results.items()}
    pb = {k: v[1] for k, v in results.items()}
    delta_pieces = relay_scatter(pa, pb, mp_swap, {3: lambda: after_grads})
    (hidden_delta_d, hidden_delta_a, low, terms_d, terms_a, query_delta), pa, pb = attend_back(
        *delta_pieces,
        hidden_d,
        hidden_a,
        prefix_cotangent[0],
        cotangent_a,
        row_share,
        second_gain_d,
        second_gain_a,
        wo_m,
        wo_e,
        wo_a,
        queries,
        tops,
        totals,
        own_cos,
        own_sin,
        own_codes,
        key_codes,
        *kv_rows,
    )
    low_d, low_a = low[:PREF], low[PREF:, :DA]

    order_d, order_a = order_matrix(D, 9), order_matrix(DA, 8)
    turned_d = dot(normed_d, order_d).astype(bf16)
    turned_a = dot(normed_a, order_a).astype(bf16)
    turned_context = dot(context, order_a).astype(bf16)
    second_term_d = t_dot(dot(terms_d, order_d).astype(bf16), jnp.ones((PREF, 128), bf16))
    second_term_a = t_dot(dot(terms_a, order_a).astype(bf16), jnp.ones((ACT_PAD, 128), bf16))
    out_grad_d = t_dot(turned_context[:PREF], low_d).astype(bf16)
    out_grad_a = t_dot(turned_context[PREF:], low_a).astype(bf16)
    q_grad_d = t_dot(turned_d, query_delta[:PREF]).astype(bf16)
    q_grad_a = t_dot(turned_a, query_delta[PREF:]).astype(bf16)

    def split(array):
        return array.reshape(2, 8, -1, array.shape[1])

    def sum_cores(pieces):
        mine = lax.dynamic_index_in_dim(pieces, core, 0, keepdims=False)
        theirs = lax.dynamic_index_in_dim(pieces, 1 - core, 0, keepdims=False)
        return add_low(mine, core_swap(theirs))

    def sum_mp(pack, sent=None):
        pack = sum_cores(pack)
        pieces = [lax.dynamic_index_in_dim(pack, mp ^ k, 0, keepdims=False) for k in range(8)]
        return ring_scatter(pieces, mp_swap, {}, sent).astype(bf16)

    qo = [q_grad_a, out_grad_a, q_grad_d, out_grad_d[:, :1024]]
    qo_sent, kv_sent = [], []
    qo = sum_mp(jnp.concatenate([split(g) for g in qo], axis=2), qo_sent)
    kv_sum = ring_scatter(
        [join(pa[k], pb[k]) for k in range(8)], mp_swap, {2: tuple(qo_sent)}
    )
    kv_raw_delta = jnp.concatenate(
        [unrotate(kv_sum[:, :HD], own_cos, own_sin), kv_sum[:, HD:]], axis=1
    ).astype(bf16)
    kv_grad_d = t_dot(turned_d, kv_raw_delta[:PREF])
    kv_grad_a = t_dot(turned_a, kv_raw_delta[PREF:])
    kv_grad_d = jnp.concatenate([kv_grad_d, second_term_d], axis=1).astype(bf16)
    kv_grad_a = jnp.concatenate(
        [kv_grad_a.astype(bf16), second_term_a.astype(bf16), out_grad_d[:, 1024:]], axis=1
    )
    kv = sum_mp(jnp.concatenate([split(kv_grad_a), split(widen(kv_grad_d, 768))], axis=2), kv_sent)
    kv_a, kv_d = kv[:64], kv[64:, :640]
    qo_a, qo_b = qo[:128], qo[128:]

    product_d = fence(product_d, qo_sent[0])
    partial_d = dot(product_d[:, :hidden], prefix_down).astype(bf16)
    partial_a = dot(product_a, action_down[0]).astype(bf16)
    out = []
    for k in range(8):
        i = (1, 3, 4, 2, 5, 7, 0, 6).index(k)
        mine = partial_a[i * ACT_PAD : (i + 1) * ACT_PAD]
        out.append(block_of(partial_d[i * PREF : (i + 1) * PREF], mine))
    out = ring_scatter(out, mp_swap, {1: tuple(qo_sent)})
    prefix_output = (hidden_d + out[:PREF]).astype(bf16)[None]
    action_output = (hidden_a + out[PREF:, :DA])[:ACT].astype(bf16)[None]

    last_d = jnp.concatenate([kv_d, qo_b[:72]], axis=1).reshape(8, 9, wide)
    last_a = jnp.concatenate(
        [kv_a[:, :640], qo_a[:64], qo_a[64:], qo_b[72:], kv_a[:, 640:]], axis=1
    ).reshape(8, 8, -1)
    last = jnp.concatenate(
        [
            last_d[:, :8],
            last_a,
            jnp.pad(last_d[:, 8:].reshape(8, 8, wide // 8), ((0, 0), (0, 0), (0, 48))),
        ],
        axis=2,
    )
    last = scatter_direct(last, yz, yz_swap)
    ninth = last[:, last.shape[1] - 256 : last.shape[1] - 48].reshape(1, wide)
    grads_d = join(last[:, :wide], ninth)
    grads_a = last[:, wide : last.shape[1] - 256]

    def split_grads(grads, query, key, value, gain):
        key_grad = grads[:, :256]
        value_grad = grads[:, 256:512]
        second = grads[:, 512]
        query_grad = grads[:, 640:1664]
        first = (
            jnp.sum(query_grad * query.astype(f32), axis=1)
            + jnp.sum(key_grad * key.astype(f32), axis=1)
            + jnp.sum(value_grad * value.astype(f32), axis=1)
        ) / gain.astype(f32)
        return query_grad, key_grad, value_grad, first, second

    gd = split_grads(grads_d, prefix_query, prefix_key, prefix_value, prefix_first_gain)
    ga = split_grads(grads_a, action_query, action_key, action_value, action_first_gain)
    action_out_grad = grads_a[:, 1664:2688]
    prefix_out_grad = grads_a[:, 2688:]

    first_delta_d = dot_t(query_delta[:PREF], wq_d) + dot_t(kv_raw_delta[:PREF], wkv_d)
    first_delta_a = dot_t(query_delta[PREF:], wq_a) + dot_t(kv_raw_delta[PREF:], wkv_a)
    input_d = hidden_delta_d + normalize_back(x_d, rms_d, first_gain_d, first_delta_d)
    input_a = hidden_delta_a + normalize_back(x_a, rms_a, first_gain_a, first_delta_a)

    return (
        prefix_output,
        action_output,
        input_d.astype(bf16)[None],
        input_a[:ACT].astype(bf16)[None],
        gd[0],
        gd[1],
        gd[2],
        prefix_out_grad,
        gd[3],
        gd[4],
        ga[0],
        ga[1],
        ga[2],
        action_out_grad,
        ga[3],
        ga[4],
        finished[0].T,
        finished[1].T,
        finished[2],
        finished[3][None],
        finished[4][None],
        finished[5][None],
    )


def solution(mesh):
    rows = P("dp", "mp", None)
    both = P(("dp", "mp"), None)
    vector = P(("dp", "mp"))
    slots = P("mp", None, None)
    return jax.shard_map(
        on_device,
        mesh=mesh,
        in_specs=(rows,) * 4
        + (P("dp", None), P("dp", None), P())
        + (both,) * 4
        + (vector,) * 2
        + (both,) * 4
        + (vector,) * 2
        + (P(None, "mp"), P(None, "mp"), P("mp", None))
        + (slots,) * 3,
        out_specs=(rows,) * 4
        + (both,) * 4
        + (vector,) * 2
        + (both,) * 4
        + (vector,) * 2
        + (P(None, "mp"), P(None, "mp"), P("mp", None))
        + (slots,) * 3,
        check_vma=False,
    )
```

time: 806 us -> 707 us (0.88)
  Pallas kernels: 0 us -> 84.8 us
  matrix products: 126 us -> 52.2 us
  starting transfers between devices: 158 us -> 99 us
  other arithmetic: 120 us -> 90.2 us
  waiting for transfers between devices: 304 us -> 275 us
    psum x1 -> x2, waiting for transfers between devices: 0.01 us -> 96.5 us  [the longest x1 96.5 us: on_device(): one = lax.psum(grads[0], 'dp')]
    ppermute x48 -> x26, waiting for transfers between devices: 131 us -> 41.6 us  [dp_swap(): return lax.ppermute(array, 'dp', [(i, i ^ step) for i in range(16)])]
    pallas_call x0 -> x36, Pallas kernels: none -> 84.8 us  [the longest x4 51.5 us: feed(): pl.pallas_call(functools.partial(feed_kernel, layout), grid=(1,), in_spec...]
    ppermute x48 -> x26, starting transfers between devices: 84 us -> 32.4 us  [dp_swap(): return lax.ppermute(array, 'dp', [(i, i ^ step) for i in range(16)])]
    dot_general x35 -> x7, matrix products: 51.7 us -> 15.6 us  [dot(): return jnp.dot(a, b, preferred_element_type=f32)]
    ppermute x42 -> x52, waiting for transfers between devices: 173 us -> 137 us  [mp_swap(): return lax.ppermute(array, 'mp', [(i, i ^ step) for i in range(N_MP)])]
    dot_general x35 -> x4, matrix products: 35.4 us -> 3.78 us  [dot_t(): lax.dot_general(a, b, (((1,), (1,)), ((), ())), preferred_element_type=f32)]
    another operation x22 -> x5, other arithmetic: 17.6 us -> 1.76 us
  transfers between devices with their start and end apart: 93 -> 80, of which waited for: 36 -> 33; matrix products, arithmetic and copies ran while one was open for 27% -> 23% of each run, Pallas kernels for 0% -> 10%
where the time goes in v2:
time: 707 us; the launch traced here: 696 us
  waiting for transfers between devices  275 us (39%)
  starting transfers between devices  99 us (14%)
  other arithmetic  90.2 us (13%)
  Pallas kernels  84.8 us (12%)
  local copies, waits for them, and re-layouts  76.7 us (11%)
  matrix products  52.2 us (7%)
  between operations  18.2 us (3%)
    ppermute x52, waiting for transfers between devices, mp_swap(): return lax.ppermute(array, 'mp', [(i, i ^ step) for i in range(N_MP)])  137 us
    psum x1, waiting for transfers between devices, on_device(): one = lax.psum(grads[0], 'dp')  96.5 us
    ppermute x52, starting transfers between devices, mp_swap(): return lax.ppermute(array, 'mp', [(i, i ^ step) for i in range(N_MP)])  66.3 us
    pallas_call x4, Pallas kernels, feed(): pl.pallas_call(functools.partial(feed_kernel, layout), grid=(1,), in_spec...  51.5 us
    unnamed x405, local copies, waits for them, and re-layouts  43.6 us
    ppermute x26, waiting for transfers between devices, dp_swap(): return lax.ppermute(array, 'dp', [(i, i ^ step) for i in range(16)])  41.6 us
    dot_general x12, matrix products, t_dot(): lax.dot_general(a, b, (((0,), (0,)), ((), ())), preferred_element_type=f32)  32.8 us
    ppermute x26, starting transfers between devices, dp_swap(): return lax.ppermute(array, 'dp', [(i, i ^ step) for i in range(16)])  32.4 us
  transfers between devices with their start and end apart: 80, of which 33 were waited for; matrix products, arithmetic and copies ran while one was open for 23% of the time, Pallas kernels for 10%

profile of v2, /device:TPU:0, one launch (start us, length us, event | category | flops | bytes accessed | tf_op | source)
XLA Modules:
  0.0 696.1 jit_solution(17566365136275623710)
XLA Ops:
  32.9 5.5 collective-permute-done.2
  44.1 3.7 collective-permute-start.6
  56.8 9.4 %collective-permute-done.7 = bf16[128,768]{1,0:T(8,128)(2,1)S(1)} collective-permute-done((bf16[128,768]{1,0:T(8,128)(2,1)S(1)}, bf16[128,768]{1,0:T(8,128)(2,1)S(1)}, u32[]{:S(2)}, u32[]{:S(2)}) %collective-permute-start.7) | collective-permute-done | bytes 196640 | tf_op jit(solution)/shard_map/ppermute | solution.py:53
  88.2 8.6 %collective-permute-done.19 = bf16[264,1024]{1,0:T(8,128)(2,1)S(1)} collective-permute-done((bf16[264,1024]{1,0:T(8,128)(2,1)}, bf16[264,1024]{1,0:T(8,128)(2,1)S(1)}, u32[]{:S(2)}, u32[]{:S(2)}) %collective-permute-start.19) | collective-permute-done | bytes 540704 | tf_op jit(solution)/shard_map/ppermute | solution.py:53
  113.7 3.8 collective-permute-start.23
  138.9 5.2 collective-permute-done.31
  148.3 3.7 place.3
  167.3 5.5 interleave.3
  176.9 10.8 %attend.1 = (bf16[832,256]{1,0:T(8,128)(2,1)S(1)}, bf16[208,1024]{1,0:T(8,128)(2,1)S(1)}, f32[832,1]{1,0:T(8,128)S(1)}, f32[832,1]{1,0:T(8,128)}, f32[192,1152]{...) custom-call(bf16[192,1152]{1,0:T(8,128)(2,1)} %copy-done.136, ...), custom_call_target="tpu_custom_call" | custom-call | flops 2399141888 | bytes 20971520 | tf_op jit(solution)/shard_map/attend/pallas_call | solution.py:435
  199.4 10.0 %feed.4 = (bf16[1536,896]{1,0:T(8,128)(2,1)}, bf16[1536,1792]{1,0:T(8,128)(2,1)}, bf16[1536,1152]{1,0:T(8,128)(2,1)}, bf16[1536,1152]{1,0:T(8,128)(2,1)}, bf16[1...) custom-call(bf16[208,1152]{1,0:T(8,128)(2,1)S(1)} %copy-done.17, ...), custom_call_target="tpu_custom_call" | custom-call | flops 2078801920 | bytes 12263424 | tf_op jit(solution)/shard_map/feed/pallas_call | solution.py:362
  218.8 15.7 %feed.5 = (bf16[1536,896]{1,0:T(8,128)(2,1)}, bf16[1536,1792]{1,0:T(8,128)(2,1)}, bf16[1536,1152]{1,0:T(8,128)(2,1)}, bf16[1536,1152]{1,0:T(8,128)(2,1)}, bf16[1...) custom-call(bf16[208,1152]{1,0:T(8,128)(2,1)S(1)} %collective-permut, ...), custom_call_target="tpu_custom_call", output_to_operand_aliasing={{0}: (13, {}), {1}: (14, {}), {2}: (15, {}), {3}: (16, {}),... | custom-call | flops 6236405760 | bytes 12263424 | tf_op jit(solution)/shard_map/feed/pallas_call | solution.py:362
  246.3 15.7 %feed.6 = (bf16[1536,896]{1,0:T(8,128)(2,1)}, bf16[1536,1792]{1,0:T(8,128)(2,1)}, bf16[1536,1152]{1,0:T(8,128)(2,1)}, bf16[1536,1152]{1,0:T(8,128)(2,1)}, bf16[1...) custom-call(bf16[192,1152]{1,0:T(8,128)(2,1)S(1)} %copy-done.44, ...), custom_call_target="tpu_custom_call", output_to_operand_aliasing={{0}: (13, {}), {1}: (14, {}), {2}: (15, {}), {3}: (16, {}),... | custom-call | flops 6236405760 | bytes 12263424 | tf_op jit(solution)/shard_map/feed/pallas_call | solution.py:362
  265.9 10.1 %feed.7 = (bf16[1536,896]{1,0:T(8,128)(2,1)}, bf16[1536,1792]{1,0:T(8,128)(2,1)}, bf16[1536,1152]{1,0:T(8,128)(2,1)}, bf16[1536,1152]{1,0:T(8,128)(2,1)}, bf16[1...) custom-call(bf16[96,1152]{1,0:T(8,128)(2,1)} %collective-permute-don, ...), custom_call_target="tpu_custom_call", output_to_operand_aliasing={{0}: (11, {}), {1}: (12, {}), {2}: (13, {}), {3}: (14, {}),... | custom-call | flops 2078801920 | bytes 12263424 | tf_op jit(solution)/shard_map/feed/pallas_call | solution.py:362
  281.0 7.3 %convolution_convert_fusion.5.refs_2_.refs_0_ = bf16[896,1152]{1,0:T(8,128)(2,1)} fusion(bf16[1536,896]{1,0:T(8,128)(2,1)S(1)} %copy-done.106, bf16[1536,1152]{1,0:T(8,128)(2,1)} %get-tuple-element.157), kind=kOutput, calls=%fused_computation.22 | convolution fusion | flops 3171926016 | bytes 8355840 | tf_op jit(solution)/shard_map/dot_general | solution.py:574
  288.3 8.9 %convolution_convert_fusion.1.refs_1_ = bf16[1792,1152]{1,0:T(8,128)(2,1)} fusion(bf16[1536,1792]{1,0:T(8,128)(2,1)S(1)} %bitcast.236, bf16[1536,1152]{1,0:T(8,128)(2,1)S(1)} %copy-done.109), kind=kOutput, calls=%fused_computation.4 | convolution fusion | flops 6343852032 | bytes 13172736 | tf_op jit(solution)/shard_map/dot_general | solution.py:574
  305.3 4.0 collective-permute-done.53
  327.5 12.9 %attend_back.1 = (f32[192,1152]{1,0:T(8,128)}, f32[16,1024]{1,0:T(8,128)S(1)}, bf16[208,1152]{1,0:T(8,128)(2,1)}, bf16[192,1152]{1,0:T(8,128)(2,1)}, bf16[16,102...) custom-call(bf16[96,1152]{1,0:T(8,128)(2,1)S(1)} %copy-done.24, ...), custom_call_target="tpu_custom_call" | custom-call | flops 425984 | bytes 832 | tf_op jit(solution)/shard_map/attend_back/pallas_call | solution.py:521
  366.8 11.3 %collective-permute-done.62 = bf16[416,512]{1,0:T(8,128)(2,1)S(1)} collective-permute-done((bf16[416,512]{1,0:T(8,128)(2,1)}, bf16[416,512]{1,0:T(8,128)(2,1)S(1)}, u32[]{:S(2)}, u32[]{:S(2)}) %collective-permute-start.62) | collective-permute-done | bytes 426016 | tf_op jit(solution)/shard_map/ppermute | solution.py:49
  379.9 96.5 %all-reduce.20.cloned.1.call-done.refs_1_ = bf16[1792,1152]{1,0:T(8,128)(2,1)} async-done(((bf16[1792,1152]{1,0:T(8,128)(2,1)}), bf16[1792,1152]{1,0:T(8,128)(2,1)}) %all-reduce.20.cloned.1.call-update) | async-done | bytes 4128784 | tf_op jit(solution)/shard_map/psum | solution.py:796
  476.4 5.9 convert_bitcast_fusion
  482.3 5.7 fusion
  495.7 6.6 convolution_convert_fusion
  522.6 3.6 copy.172
  535.2 45.5 %collective-permute-done.58 = bf16[416,1152]{1,0:T(8,128)(2,1)} collective-permute-done((bf16[416,1152]{1,0:T(8,128)(2,1)}, bf16[416,1152]{1,0:T(8,128)(2,1)}, u32[]{:S(2)}, u32[]{:S(2)}) %collective-permute-start.58) | collective-permute-done | bytes 958496 | tf_op jit(solution)/shard_map/ppermute | solution.py:49
  585.1 20.1 %collective-permute-done.70 = bf16[528,1024]{1,0:T(8,128)(2,1)S(1)} collective-permute-done((bf16[528,1024]{1,0:T(8,128)(2,1)S(1)}, bf16[528,1024]{1,0:T(8,128)(2,1)S(1)}, u32[]{:S(2)}, u32[]{:S(2)}) %collective-permute-start.70) | collective-permute-done | bytes 1081376 | tf_op jit(solution)/shard_map/ppermute | solution.py:49
  612.9 4.0 collective-permute-done.60
  617.0 4.1 collective-permute-done.66
  621.1 6.1 collective-permute-done.67
  630.8 14.8 %collective-permute-done.73 = bf16[264,1024]{1,0:T(8,128)(2,1)S(1)} collective-permute-done((bf16[264,1024]{1,0:T(8,128)(2,1)S(1)}, bf16[264,1024]{1,0:T(8,128)(2,1)S(1)}, u32[]{:S(2)}, u32[]{:S(2)}) %collective-permute-start.73) | collective-permute-done | bytes 540704 | tf_op jit(solution)/shard_map/ppermute | solution.py:49
  657.7 5.7 collective-permute-done.75
  666.3 5.2 collective-permute-done.77
  677.6 6.8 fusion.13
  (804 shorter events, 295.2 us)
Async XLA Ops:
  47.8 21.5 %collective-permute-start.10 = (bf16[208,1152]{1,0:T(8,128)(2,1)}, bf16[208,1152]{1,0:T(8,128)(2,1)S(1)}, u32[]{:S(2)}, u32[]{:S(2)}) collective-permute-start(bf16[208,1152]{1,0:T(8,128)(2,1)} %fence.26.refs_1_), channel_id=1, source_target_pairs={{0,1},{1,0},{2,3},{3,2},{4,5},{5,4},{6,7},{7,6},{8,9},{9,8},{10,11... | collective-permute-start | bytes 1437704 | tf_op jit(solution)/shard_map/ppermute | solution.py:49
  47.9 21.5 %collective-permute-start.11 = (bf16[208,1152]{1,0:T(8,128)(2,1)}, bf16[208,1152]{1,0:T(8,128)(2,1)S(1)}, u32[]{:S(2)}, u32[]{:S(2)}) collective-permute-start(bf16[208,1152]{1,0:T(8,128)(2,1)} %fence.26.refs_1_), channel_id=1, source_target_pairs={{0,3},{1,2},{2,1},{3,0},{4,7},{5,6},{6,5},{7,4},{8,11},{9,10},{10,... | collective-permute-start | bytes 1437704 | tf_op jit(solution)/shard_map/ppermute | solution.py:49
  50.1 19.3 %collective-permute-start.12 = (bf16[208,1152]{1,0:T(8,128)(2,1)}, bf16[208,1152]{1,0:T(8,128)(2,1)S(1)}, u32[]{:S(2)}, u32[]{:S(2)}) collective-permute-start(bf16[208,1152]{1,0:T(8,128)(2,1)} %fence.26.refs_1_), channel_id=1, source_target_pairs={{0,4},{1,5},{2,6},{3,7},{4,0},{5,1},{6,2},{7,3},{8,12},{9,13},{10,... | collective-permute-start | bytes 1437704 | tf_op jit(solution)/shard_map/ppermute | solution.py:49
  78.3 22.4 %collective-permute-start.16 = (bf16[8,9,8,768]{3,2,1,0:T(8,128)(2,1)S(1)}, bf16[8,9,8,768]{3,2,1,0:T(8,128)(2,1)S(1)}, u32[]{:S(2)}, u32[]{:S(2)}) collective-permute-start(bf16[8,9,8,768]{3,2,1,0:T(8,128)(2,1)S(1)} %get-tuple-element.110.refs_1_), channel_id=1, source_target_pairs={{0,8},{8,0},{16,24},{24,16},{32,40},{40,32},{48,56},{56,48},{64,72... | collective-permute-start | bytes 2654216 | tf_op jit(solution)/shard_map/ppermute | solution.py:53
  84.7 28.1 %collective-permute-start.17 = (bf16[264,1024]{1,0:T(8,128)(2,1)}, bf16[264,1024]{1,0:T(8,128)(2,1)S(1)}, u32[]{:S(2)}, u32[]{:S(2)}) collective-permute-start(bf16[264,1024]{1,0:T(8,128)(2,1)} %get-tuple-element.246), channel_id=1, source_target_pairs={{0,16},{8,24},{16,0},{24,8},{32,48},{40,56},{48,32},{56,40},{64,80... | collective-permute-start | bytes 1622024 | tf_op jit(solution)/shard_map/ppermute | solution.py:53
  113.7 23.1 %collective-permute-start.23 = (bf16[256,1024]{1,0:T(8,128)(2,1)}, bf16[256,1024]{1,0:T(8,128)(2,1)S(1)}, u32[]{:S(2)}, u32[]{:S(2)}) collective-permute-start(bf16[256,1024]{1,0:T(8,128)(2,1)} %fence.30), channel_id=1, source_target_pairs={{0,64},{8,72},{16,80},{24,88},{32,96},{40,104},{48,112},{56,120},{... | collective-permute-start | bytes 1572872 | tf_op jit(solution)/shard_map/ppermute | solution.py:53
  155.0 21.8 %collective-permute-start.37 = (bf16[224,512]{1,0:T(8,128)(2,1)S(1)}, bf16[224,512]{1,0:T(8,128)(2,1)S(1)}, u32[]{:S(2)}, u32[]{:S(2)}) collective-permute-start(bf16[224,512]{1,0:T(8,128)(2,1)S(1)} %pad_maximum_fusion.32), channel_id=1, source_target_pairs={{0,3},{1,2},{2,1},{3,0},{4,7},{5,6},{6,5},{7,4},{8,11},{9,10},{10,... | collective-permute-start | bytes 688136 | tf_op jit(solution)/shard_map/ppermute | solution.py:49
  189.9 21.0 %collective-permute-start.43 = (bf16[208,1152]{1,0:T(8,128)(2,1)}, bf16[208,1152]{1,0:T(8,128)(2,1)}, u32[]{:S(2)}, u32[]{:S(2)}) collective-permute-start(bf16[208,1152]{1,0:T(8,128)(2,1)} %fence.35.refs_0_.refs_9_), channel_id=1, source_target_pairs={{0,4},{1,5},{2,6},{3,7},{4,0},{5,1},{6,2},{7,3},{8,12},{9,13},{10,... | collective-permute-start | bytes 1437704 | tf_op jit(solution)/shard_map/ppermute | solution.py:49
  191.6 20.4 %collective-permute-start.40 = (bf16[208,1152]{1,0:T(8,128)(2,1)}, bf16[208,1152]{1,0:T(8,128)(2,1)S(1)}, u32[]{:S(2)}, u32[]{:S(2)}) collective-permute-start(bf16[208,1152]{1,0:T(8,128)(2,1)} %fence.35.refs_0_.refs_9_), channel_id=1, source_target_pairs={{0,1},{1,0},{2,3},{3,2},{4,5},{5,4},{6,7},{7,6},{8,9},{9,8},{10,11... | collective-permute-start | bytes 1437704 | tf_op jit(solution)/shard_map/ppermute | solution.py:49
  215.4 25.5 %collective-permute-start.45 = (bf16[208,1152]{1,0:T(8,128)(2,1)}, bf16[208,1152]{1,0:T(8,128)(2,1)}, u32[]{:S(2)}, u32[]{:S(2)}) collective-permute-start(bf16[208,1152]{1,0:T(8,128)(2,1)} %fence.37.refs_22_), channel_id=1, source_target_pairs={{0,1},{1,0},{2,3},{3,2},{4,5},{5,4},{6,7},{7,6},{8,9},{9,8},{10,11... | collective-permute-start | bytes 1437704 | tf_op jit(solution)/shard_map/ppermute | solution.py:49
  215.5 22.5 %collective-permute-start.42 = (bf16[192,1152]{1,0:T(8,128)(2,1)}, bf16[192,1152]{1,0:T(8,128)(2,1)S(1)}, u32[]{:S(2)}, u32[]{:S(2)}) collective-permute-start(bf16[192,1152]{1,0:T(8,128)(2,1)} %fence.36.refs_21_), channel_id=1, source_target_pairs={{0,4},{1,5},{2,6},{3,7},{4,0},{5,1},{6,2},{7,3},{8,12},{9,13},{10,... | collective-permute-start | bytes 1327112 | tf_op jit(solution)/shard_map/ppermute | solution.py:49
  215.9 28.5 %collective-permute-start.47 = (bf16[224,1152]{1,0:T(8,128)(2,1)}, bf16[224,1152]{1,0:T(8,128)(2,1)}, u32[]{:S(2)}, u32[]{:S(2)}) collective-permute-start(bf16[224,1152]{1,0:T(8,128)(2,1)} %fence.38.refs_23_), channel_id=1, source_target_pairs={{0,3},{1,2},{2,1},{3,0},{4,7},{5,6},{6,5},{7,4},{8,11},{9,10},{10,... | collective-permute-start | bytes 1548296 | tf_op jit(solution)/shard_map/ppermute | solution.py:49
  239.5 25.3 %collective-permute-start.44 = (bf16[96,1152]{1,0:T(8,128)(2,1)}, bf16[96,1152]{1,0:T(8,128)(2,1)}, u32[]{:S(2)}, u32[]{:S(2)}) collective-permute-start(bf16[96,1152]{1,0:T(8,128)(2,1)} %fence.39.refs_21_), channel_id=1, source_target_pairs={{0,1},{1,0},{2,3},{3,2},{4,5},{5,4},{6,7},{7,6},{8,9},{9,8},{10,11... | collective-permute-start | bytes 663560 | tf_op jit(solution)/shard_map/ppermute | solution.py:49
  242.6 22.2 %collective-permute-start.46 = (bf16[112,1152]{1,0:T(8,128)(2,1)}, bf16[112,1152]{1,0:T(8,128)(2,1)S(1)}, u32[]{:S(2)}, u32[]{:S(2)}) collective-permute-start(bf16[112,1152]{1,0:T(8,128)(2,1)} %fence.40.refs_22_), channel_id=1, source_target_pairs={{0,3},{1,2},{2,1},{3,0},{4,7},{5,6},{6,5},{7,4},{8,11},{9,10},{10,... | collective-permute-start | bytes 774152 | tf_op jit(solution)/shard_map/ppermute | solution.py:49
  262.9 42.4 %collective-permute-start.50 = (bf16[224,1152]{1,0:T(8,128)(2,1)}, bf16[224,1152]{1,0:T(8,128)(2,1)}, u32[]{:S(2)}, u32[]{:S(2)}) collective-permute-start(bf16[224,1152]{1,0:T(8,128)(2,1)} %pad_maximum_fusion.13), channel_id=1, source_target_pairs={{0,3},{1,2},{2,1},{3,0},{4,7},{5,6},{6,5},{7,4},{8,11},{9,10},{10,... | collective-permute-start | bytes 1548296 | tf_op jit(solution)/shard_map/ppermute | solution.py:49
  276.0 23.4 %collective-permute-start.52 = (bf16[112,1152]{1,0:T(8,128)(2,1)S(1)}, bf16[112,1152]{1,0:T(8,128)(2,1)}, u32[]{:S(2)}, u32[]{:S(2)}) collective-permute-start(bf16[112,1152]{1,0:T(8,128)(2,1)S(1)} %get-tuple-element.165), channel_id=1, source_target_pairs={{0,3},{1,2},{2,1},{3,0},{4,7},{5,6},{6,5},{7,4},{8,11},{9,10},{10,... | collective-permute-start | bytes 774152 | tf_op jit(solution)/shard_map/ppermute | solution.py:49
  277.4 25.1 %collective-permute-start.48 = (bf16[96,1152]{1,0:T(8,128)(2,1)}, bf16[96,1152]{1,0:T(8,128)(2,1)}, u32[]{:S(2)}, u32[]{:S(2)}) collective-permute-start(bf16[96,1152]{1,0:T(8,128)(2,1)} %get-tuple-element.151), channel_id=1, source_target_pairs={{0,1},{1,0},{2,3},{3,2},{4,5},{5,4},{6,7},{7,6},{8,9},{9,8},{10,11... | collective-permute-start | bytes 663560 | tf_op jit(solution)/shard_map/ppermute | solution.py:49
  313.9 162.5 %all-reduce.20.cloned.1.call-start = ((), (), s32[]{:S(2)}) async-start(), calls=%async_computation | async-start | bytes 8257536 | tf_op jit(solution)/shard_map/psum | solution.py:796
  324.0 353.6 %all-reduce.22.cloned.1.call-start = ((), (), s32[]{:S(2)}) async-start(), calls=%async_computation.1 | async-start | bytes 16711680 | tf_op jit(solution)/shard_map/psum | solution.py:797
  350.7 131.6 %collective-permute-start.56 = (bf16[8,264,1024]{2,1,0:T(8,128)(2,1)}, bf16[8,264,1024]{2,1,0:T(8,128)(2,1)}, u32[]{:S(2)}, u32[]{:S(2)}) collective-permute-start(bf16[8,264,1024]{2,1,0:T(8,128)(2,1)} %dynamic-slice_bitcast_fusion), channel_id=1, source_target_pairs={{0,8},{8,0},{16,24},{24,16},{32,40},{40,32},{48,56},{56,48},{64,72... | collective-permute-start | bytes 12976136 | tf_op jit(solution)/shard_map/ppermute | solution.py:53
  355.6 22.4 %collective-permute-start.62 = (bf16[416,512]{1,0:T(8,128)(2,1)}, bf16[416,512]{1,0:T(8,128)(2,1)S(1)}, u32[]{:S(2)}, u32[]{:S(2)}) collective-permute-start(bf16[416,512]{1,0:T(8,128)(2,1)} %pad_maximum_fusion.25), channel_id=1, source_target_pairs={{0,3},{1,2},{2,1},{3,0},{4,7},{5,6},{6,5},{7,4},{8,11},{9,10},{10,... | collective-permute-start | bytes 1277960 | tf_op jit(solution)/shard_map/ppermute | solution.py:49
  357.8 20.3 %collective-permute-start.63 = (bf16[416,512]{1,0:T(8,128)(2,1)}, bf16[416,512]{1,0:T(8,128)(2,1)S(1)}, u32[]{:S(2)}, u32[]{:S(2)}) collective-permute-start(bf16[416,512]{1,0:T(8,128)(2,1)} %pad_maximum_fusion.26), channel_id=1, source_target_pairs={{0,2},{1,3},{2,0},{3,1},{4,6},{5,7},{6,4},{7,5},{8,10},{9,11},{10,... | collective-permute-start | bytes 1277960 | tf_op jit(solution)/shard_map/ppermute | solution.py:49
  489.6 95.4 %collective-permute-start.71 = (bf16[528,1024]{1,0:T(8,128)(2,1)S(1)}, bf16[528,1024]{1,0:T(8,128)(2,1)}, u32[]{:S(2)}, u32[]{:S(2)}) collective-permute-start(bf16[528,1024]{1,0:T(8,128)(2,1)S(1)} %pad_maximum_fusion.5.refs_3_), channel_id=1, source_target_pairs={{0,3},{1,2},{2,1},{3,0},{4,7},{5,6},{6,5},{7,4},{8,11},{9,10},{10,... | collective-permute-start | bytes 3244040 | tf_op jit(solution)/shard_map/ppermute | solution.py:49
  504.5 29.6 %collective-permute-start.57 = (bf16[416,1152]{1,0:T(8,128)(2,1)}, bf16[416,1152]{1,0:T(8,128)(2,1)}, u32[]{:S(2)}, u32[]{:S(2)}) collective-permute-start(bf16[416,1152]{1,0:T(8,128)(2,1)} %fence.45), channel_id=1, source_target_pairs={{0,1},{1,0},{2,3},{3,2},{4,5},{5,4},{6,7},{7,6},{8,9},{9,8},{10,11... | collective-permute-start | bytes 2875400 | tf_op jit(solution)/shard_map/ppermute | solution.py:49
  506.8 73.8 %collective-permute-start.58 = (bf16[416,1152]{1,0:T(8,128)(2,1)}, bf16[416,1152]{1,0:T(8,128)(2,1)}, u32[]{:S(2)}, u32[]{:S(2)}) collective-permute-start(bf16[416,1152]{1,0:T(8,128)(2,1)} %fence.46), channel_id=1, source_target_pairs={{0,3},{1,2},{2,1},{3,0},{4,7},{5,6},{6,5},{7,4},{8,11},{9,10},{10,... | collective-permute-start | bytes 2875400 | tf_op jit(solution)/shard_map/ppermute | solution.py:49
  509.1 72.6 %collective-permute-start.59 = (bf16[416,1152]{1,0:T(8,128)(2,1)}, bf16[416,1152]{1,0:T(8,128)(2,1)}, u32[]{:S(2)}, u32[]{:S(2)}) collective-permute-start(bf16[416,1152]{1,0:T(8,128)(2,1)} %fence.47), channel_id=1, source_target_pairs={{0,2},{1,3},{2,0},{3,1},{4,6},{5,7},{6,4},{7,5},{8,10},{9,11},{10,... | collective-permute-start | bytes 2875400 | tf_op jit(solution)/shard_map/ppermute | solution.py:49
  528.3 79.4 %collective-permute-start.65 = (bf16[8,136,768]{2,1,0:T(8,128)(2,1)S(1)}, bf16[8,136,768]{2,1,0:T(8,128)(2,1)S(1)}, u32[]{:S(2)}, u32[]{:S(2)}) collective-permute-start(bf16[8,136,768]{2,1,0:T(8,128)(2,1)S(1)} %fusion.24), channel_id=1, source_target_pairs={{0,8},{8,0},{16,24},{24,16},{32,40},{40,32},{48,56},{56,48},{64,72... | collective-permute-start | bytes 5013512 | tf_op jit(solution)/shard_map/ppermute | solution.py:53
  534.1 51.0 %collective-permute-start.72 = (bf16[528,1024]{1,0:T(8,128)(2,1)S(1)}, bf16[528,1024]{1,0:T(8,128)(2,1)S(1)}, u32[]{:S(2)}, u32[]{:S(2)}) collective-permute-start(bf16[528,1024]{1,0:T(8,128)(2,1)S(1)} %copy-done.111), channel_id=1, source_target_pairs={{0,2},{1,3},{2,0},{3,1},{4,6},{5,7},{6,4},{7,5},{8,10},{9,11},{10,... | collective-permute-start | bytes 3244040 | tf_op jit(solution)/shard_map/ppermute | solution.py:49
  580.7 24.5 %collective-permute-start.70 = (bf16[528,1024]{1,0:T(8,128)(2,1)S(1)}, bf16[528,1024]{1,0:T(8,128)(2,1)S(1)}, u32[]{:S(2)}, u32[]{:S(2)}) collective-permute-start(bf16[528,1024]{1,0:T(8,128)(2,1)S(1)} %copy-done.107), channel_id=1, source_target_pairs={{0,1},{1,0},{2,3},{3,2},{4,5},{5,4},{6,7},{7,6},{8,9},{9,8},{10,11... | collective-permute-start | bytes 3244040 | tf_op jit(solution)/shard_map/ppermute | solution.py:49
  584.1 32.8 %collective-permute-start.60 = (bf16[208,1152]{1,0:T(8,128)(2,1)S(1)}, bf16[208,1152]{1,0:T(8,128)(2,1)S(1)}, u32[]{:S(2)}, u32[]{:S(2)}) collective-permute-start(bf16[208,1152]{1,0:T(8,128)(2,1)S(1)} %slice.891), channel_id=1, source_target_pairs={{0,4},{1,5},{2,6},{3,7},{4,0},{5,1},{6,2},{7,3},{8,12},{9,13},{10,... | collective-permute-start | bytes 1437704 | tf_op jit(solution)/shard_map/ppermute | solution.py:49
  607.4 38.2 %collective-permute-start.73 = (bf16[264,1024]{1,0:T(8,128)(2,1)S(1)}, bf16[264,1024]{1,0:T(8,128)(2,1)S(1)}, u32[]{:S(2)}, u32[]{:S(2)}) collective-permute-start(bf16[264,1024]{1,0:T(8,128)(2,1)S(1)} %slice.890), channel_id=1, source_target_pairs={{0,4},{1,5},{2,6},{3,7},{4,0},{5,1},{6,2},{7,3},{8,12},{9,13},{10,... | collective-permute-start | bytes 1622024 | tf_op jit(solution)/shard_map/ppermute | solution.py:49
  629.0 19.8 %collective-permute-start.69 = (bf16[136,768]{1,0:T(8,128)(2,1)S(1)}, bf16[136,768]{1,0:T(8,128)(2,1)S(1)}, u32[]{:S(2)}, u32[]{:S(2)}) collective-permute-start(bf16[136,768]{1,0:T(8,128)(2,1)S(1)} %slice.893), channel_id=1, source_target_pairs={{0,4},{1,5},{2,6},{3,7},{4,0},{5,1},{6,2},{7,3},{8,12},{9,13},{10,... | collective-permute-start | bytes 626696 | tf_op jit(solution)/shard_map/ppermute | solution.py:49
  (249 other events, 2368.1 us)
Sparse Core Ops, SparseCore 0:
  324.1 152.2 all-reduce.19
  479.7 165.9 all-reduce.21

commit v3 on v2

--- a/solution.py
+++ b/solution.py
@@ -39,10 +39,16 @@
     ((6, 1),),
 )
 PARTS = tuple(part for parts in ARRIVALS for part in parts)
-ROW_BLOCK = np.concatenate([np.full((HALF_A, HALF_B)[h], k) for k, h in PARTS]).astype(np.int32)
-ROW_ID = np.concatenate(
-    [np.arange(HALF_A) if h == 0 else np.arange(HALF_A, BLOCK) for _, h in PARTS]
+KEY_BLOCK = np.concatenate(
+    [np.full(HALF_A, k) for k, _ in PARTS] + [np.full(ACT_PAD, k) for k, h in PARTS if h]
 ).astype(np.int32)
+KEY_ROW = np.concatenate(
+    [np.arange(HALF_A) + h * HALF_A for _, h in PARTS]
+    + [np.arange(PREF, BLOCK) for _, h in PARTS if h]
+).astype(np.int32)
+
+
+ROW_PAIR, ACT_PAIR = 3 * PREF, 3 * ACT_PAD
 
 
 def mp_swap(array, step):
@@ -102,20 +108,46 @@
     return fence(array, *after) if after else array
 
 
-def relay_gather(a, b, swap, during=None, hold=None):
-    na, nb = a.shape[0], b.shape[0]
+def sends_kernel(count, layout, *refs):
+    for out, parts in zip(refs[len(refs) - len(layout) :], layout):
+        at = 0
+        for which, first, n in parts:
+            out[at : at + n] = refs[which][first : first + n]
+            at += n
+
+
+def make_sends(arrays, layout, after=()):
+    width = arrays[0].shape[1]
+    low = lambda parts: jax.ShapeDtypeStruct((sum(n for _, _, n in parts), width), arrays[0].dtype)
+    return pl.pallas_call(
+        functools.partial(sends_kernel, len(arrays), layout),
+        in_specs=[VMEM] * len(arrays) + [ANY] * len(after),
+        out_specs=[VMEM] * len(layout),
+        out_shape=[low(parts) for parts in layout],
+        compiler_params=pltpu.CompilerParams(vmem_limit_bytes=16 * 1024 * 1024),
+        cost_estimate=pl.CostEstimate(flops=0, bytes_accessed=0, transcendentals=0),
+        name="sends",
+    )(*arrays, *after)
+
+
+def relay_gather(own, na, swap, during=None, hold=None):
+    nb = own.shape[0] - na
     during = during or (lambda stage, arrived, sends: ())
     hold = hold or {}
-    own = held(join(a, b), hold.get(1, ()))
+    own = held(own, hold.get(1, ()))
     s1, s3, s4 = swap(own, 1), swap(own, 3), swap(own, 4)
     after = during(1, (own,), (own,)) + hold.get(2, ())
-    sends = (join(s1[:na], s3[:na]), join(s3[:na], s4[na:]), join(s1[na:], s4[na:]))
-    sends = tuple(held(x, after) for x in sends)
+    layout = (
+        ((0, 0, na), (1, 0, na)),
+        ((1, 0, na), (2, na, nb)),
+        ((0, na, nb), (2, na, nb)),
+    )
+    sends = make_sends((s1, s3, s4), layout, after)
     zz, v1, v3 = swap(sends[0], 4), swap(sends[1], 1), swap(sends[2], 3)
-    after = during(2, (s1, s3, s4), sends) + hold.get(3, ())
-    sends = (held(zz[na:], after), held(v1[na:], after))
+    after = during(2, (s1, s3, s4), tuple(sends)) + hold.get(3, ())
+    sends = make_sends((zz, v1), (((0, na, na),), ((1, na, nb),)), after)
     z2a, z2b = swap(sends[0], 1), swap(sends[1], 3)
-    during(3, (zz, v1, v3), sends)
+    during(3, (zz, v1, v3), tuple(sends))
     return own, s1, s3, s4, zz, v1, v3, z2a, z2b
 
 
@@ -190,47 +222,87 @@
     return mine + swap(theirs.astype(bf16), 4).astype(f32)
 
 
-def place_kernel(sizes, index_ref, *refs):
-    arrays, outs = refs[:9], refs[9:]
+def assemble_kernel(cuts, sizes, place_ref, *refs):
+    arrays, outs = refs[:18], refs[18:]
+    index, core = place_ref[0], place_ref[1]
     for (k, h), (i, at) in where_parts(0, 9, sizes).items():
-        outs[h][index_ref[0] ^ k] = arrays[i][at : at + sizes[h]]
-
-
-def place(arrays, na, index):
-    rows, columns = arrays[0].shape
-    eights = [x.reshape(x.shape[0] // 8, 8, columns) for x in arrays]
+        for out, (which, first, n, column, width) in zip(outs, cuts):
+            if which == h:
+                rows, columns = slice(at + first, at + first + n), slice(column, column + width)
+                out[index ^ k, core] = arrays[i][rows, :, columns]
+                out[index ^ k, 1 - core] = arrays[9 + i][rows, :, columns]
+
+
+def assemble(mine, theirs, na, cuts, index, core):
+    rows, columns = mine[0].shape
+    eights = [x.reshape(x.shape[0] // 8, 8, columns) for x in (*mine, *theirs)]
     sizes = (na // 8, (rows - na) // 8)
+    outs = pl.pallas_call(
+        functools.partial(assemble_kernel, cuts, sizes),
+        in_specs=[SMEM] + [VMEM] * 18,
+        out_specs=[VMEM] * len(cuts),
+        out_shape=[jax.ShapeDtypeStruct((8, 2, n, 8, width), bf16) for _, _, n, _, width in cuts],
+        compiler_params=pltpu.CompilerParams(vmem_limit_bytes=40 * 1024 * 1024),
+        name="assemble",
+    )(jnp.stack([index, core]), *eights)
+    return [x.reshape(-1, x.shape[-1]) for x in outs]
+
+
+def gain_rows(block):
+    pick = lax.broadcasted_iota(jnp.int32, (ACT_PAD, 128), 0)
+    pick = (pick == lax.broadcasted_iota(jnp.int32, (ACT_PAD, 128), 1)).astype(bf16)
+    turned = dot_t(pick, block)
+    return turned[0:1], turned[1:2]
+
+
+def keys_kernel(*refs):
+    rows, (gain_d, gain_a, weight_d, weight_a, cosine, sine) = refs[:9], refs[9:15]
+    normed_d, normed_a, keys, values = refs[-4:]
+    gain_d, gain_a = gain_rows(gain_d[...])[0], gain_rows(gain_a[...])[0]
+    width = weight_a.shape[0]
+    prefix, action = [], []
+    for i, parts in enumerate(ARRIVALS):
+        at = 0
+        for _, h in parts:
+            prefix.append(rows[i][at : at + HALF_A])
+            at += HALF_A
+            if h:
+                action.append(rows[i][at : at + ACT_PAD, :width])
+                at += ACT_PAD
+    x = join(*prefix).astype(f32)
+    low_d = (x * inverse_rms(x) * gain_d).astype(bf16)
+    x = join(*action).astype(f32)
+    low_a = (x * inverse_rms(x) * gain_a).astype(bf16)
+    normed_d[:PREF] = low_d[:PREF]
+    normed_a[:ACT_PAD] = low_a[:ACT_PAD]
+    normed_d[PREF:] = low_d[ROW_PAIR : ROW_PAIR + PREF]
+    normed_a[ACT_PAD:] = low_a[ACT_PAIR : ACT_PAIR + ACT_PAD]
+    raw = join(dot(low_d, weight_d[...]), dot(low_a, weight_a[...]))
+    keys[...] = rotate(raw[:, :HD], cosine[...], sine[...]).astype(bf16)
+    values[...] = raw[:, HD:].astype(bf16)
+
+
+def keys_of(rows, gain_d, gain_a, weight_d, weight_a, cosine, sine, after):
+    width_d, width_a = gain_d.shape[0], gain_a.shape[0]
+    count = cosine.shape[0]
+    shape = lambda *dims: jax.ShapeDtypeStruct(dims, bf16)
+    given = [*rows, gain_d, gain_a, weight_d, weight_a, cosine, sine]
     return pl.pallas_call(
-        functools.partial(place_kernel, sizes),
-        in_specs=[SMEM] + [VMEM] * 9,
-        out_specs=[VMEM] * 2,
-        out_shape=[jax.ShapeDtypeStruct((8, n, 8, columns), bf16) for n in sizes],
-        compiler_params=pltpu.CompilerParams(vmem_limit_bytes=20 * 1024 * 1024),
-        name="place",
-    )(index.reshape(1), *eights)
-
-
-def interleave_kernel(cuts, core_ref, *refs):
-    mine, theirs, outs = refs[:2], refs[2:4], refs[4:]
-    core = core_ref[0]
-    for out, (which, first, n) in zip(outs, cuts):
-        for i in range(8):
-            out[i, core] = mine[which][i, first : first + n]
-            out[i, 1 - core] = theirs[which][i, first : first + n]
-
-
-def interleave(halves_of, cuts, core):
-    theirs = [core_swap(x) for x in halves_of]
-    columns = halves_of[0].shape[-1]
-    outs = pl.pallas_call(
-        functools.partial(interleave_kernel, cuts),
-        in_specs=[SMEM] + [VMEM] * 4,
-        out_specs=[VMEM] * len(cuts),
-        out_shape=[jax.ShapeDtypeStruct((8, 2, n, 8, columns), bf16) for _, _, n in cuts],
-        compiler_params=pltpu.CompilerParams(vmem_limit_bytes=40 * 1024 * 1024),
-        name="interleave",
-    )(core.reshape(1), *halves_of, *theirs)
-    return [x.reshape(-1, columns) for x in outs]
+        keys_kernel,
+        in_specs=[VMEM] * len(given) + [ANY] * len(after),
+        out_specs=[VMEM] * 4,
+        out_shape=[
+            shape(2 * PREF, width_d),
+            shape(2 * ACT_PAD, width_a),
+            shape(count, HD),
+            shape(count, HD),
+        ],
+        compiler_params=pltpu.CompilerParams(vmem_limit_bytes=48 * 1024 * 1024),
+        cost_estimate=pl.CostEstimate(
+            flops=4 * count * width_d * HD, bytes_accessed=8 * 1024 * 1024, transcendentals=count
+        ),
+        name="keys_of",
+    )(*given, *after)
 
 
 def gelu_parts(gate):
@@ -390,11 +462,10 @@
 def attend_kernel(*refs):
     (normed_d, normed_a, x_d, x_a, wq_d, wq_a, wo_m, wo_e, wo_a) = refs[:9]
     (gain_d, gain_a, cosine, sine, own_codes, key_codes) = refs[9:15]
-    kv = refs[15:24]
-    (queries, context, tops, totals, hidden_d, hidden_a, block) = refs[24:]
-    raw = join(dot(normed_d[...], wq_d[...]), dot(normed_a[...], wq_a[...]))
-    keys = join(*[ref[:, :HD] for ref in kv])
-    values = join(*[ref[:, HD:] for ref in kv])
+    keys, values = refs[15][...], refs[16][...]
+    (queries, context, tops, totals, hidden_d, hidden_a, block) = refs[-7:]
+    gain_d, gain_a = gain_rows(gain_d[...])[1], gain_rows(gain_a[...])[1]
+    raw = join(dot(normed_d[:PREF], wq_d[...]), dot(normed_a[:ACT_PAD], wq_a[...]))
     visible = see(own_codes, key_codes)
     cos, sin = cosine[...], sine[...]
     heads = []
@@ -417,23 +488,25 @@
         [dot(low_d, wo_m[...]), dot(low_d, wo_e[...])], axis=1
     )
     hidden_d[...] = state
-    second_d = (state * inverse_rms(state) * gain_d[...]).astype(bf16)
+    second_d = (state * inverse_rms(state) * gain_d).astype(bf16)
     real = lax.broadcasted_iota(jnp.int32, (ACT_PAD, width_a), 0) < ACT
     state = jnp.where(real, x_a[...].astype(f32) + dot(low_a, wo_a[...]), 0.0)
     hidden_a[...] = state
-    second_a = (state * inverse_rms(state) * gain_a[...]).astype(bf16)
+    second_a = (state * inverse_rms(state) * gain_a).astype(bf16)
     block[:PREF] = second_d
     block[PREF:, :width_a] = second_a
     block[PREF:, width_a:] = jnp.zeros((ACT_PAD, width_d - width_a), bf16)
 
 
-def attend(*given):
+def attend(*given, after):
     x_d, x_a = given[2:4]
     width_d, width_a = x_d.shape[1], x_a.shape[1]
     shape = jax.ShapeDtypeStruct
     stacked = HEADS * BLOCK
     return pl.pallas_call(
         attend_kernel,
+        in_specs=[VMEM] * len(given) + [ANY] * len(after),
+        out_specs=[VMEM] * 7,
         out_shape=[
             shape((stacked, HD), bf16),
             shape((BLOCK, HEADS * HD), bf16),
@@ -450,17 +523,18 @@
             transcendentals=stacked * N_MP * BLOCK,
         ),
         name="attend",
-    )(*given)
+    )(*given, *after)
 
 
 def attend_back_kernel(*refs):
     pieces = refs[:5]
     (hidden_d, hidden_a, cotangent_d, cotangent_a, share, gain_d, gain_a) = refs[5:12]
     (wo_m, wo_e, wo_a, queries, tops, totals, cosine, sine, own_codes, key_codes) = refs[12:22]
-    kv = refs[22:31]
+    keys, values = refs[22][...], refs[23][...]
     outs = refs[-(6 + len(PARTS)) :]
     (hidden_delta_d, hidden_delta_a, low, terms_d, terms_a, query_delta) = outs[:6]
     kv_deltas = outs[6:]
+    gain_d, gain_a = gain_rows(gain_d[...])[1], gain_rows(gain_a[...])[1]
     delta = join(*total_of([piece[...] for piece in pieces]))
     width_d, width_a = hidden_d.shape[1], hidden_a.shape[1]
     lows = []
@@ -472,7 +546,7 @@
         change = delta[rows, : state.shape[1]]
         scale = inverse_rms(state)
         seed = cotangent[...].astype(f32) * share[rows]
-        back = seed + normalize_back(state, scale, gain[...], change)
+        back = seed + normalize_back(state, scale, gain, change)
         out[...] = back
         terms[...] = (change * state * scale).astype(bf16)
         lows.append(back.astype(bf16))
@@ -485,8 +559,6 @@
         dot_t(low_d[:, :main], wo_m[...]) + dot_t(low_d[:, main:], wo_e[...]),
         dot_t(low_a, wo_a[...]),
     ).astype(bf16)
-    keys = join(*[ref[:, :HD] for ref in kv])
-    values = join(*[ref[:, HD:] for ref in kv])
     visible = see(own_codes, key_codes)
     cos, sin = cosine[...], sine[...]
     keys_delta, values_delta = None, None
@@ -505,12 +577,14 @@
         value_part = t_dot(probs.astype(bf16), change)
         keys_delta = key_part if h == 0 else keys_delta + key_part
         values_delta = value_part if h == 0 else values_delta + value_part
-    at = 0
+    at, extra = 0, len(PARTS) * HALF_A
     for (_, half), out in zip(PARTS, kv_deltas):
-        n = (HALF_A, HALF_B)[half]
-        out[:, :HD] = keys_delta[at : at + n].astype(bf16)
-        out[:, HD:] = values_delta[at : at + n].astype(bf16)
-        at += n
+        for columns, change in ((slice(0, HD), keys_delta), (slice(HD, 2 * HD), values_delta)):
+            out[:HALF_A, columns] = change[at : at + HALF_A].astype(bf16)
+            if half:
+                out[HALF_A:, columns] = change[extra : extra + ACT_PAD].astype(bf16)
+        at += HALF_A
+        extra += half * ACT_PAD
 
 
 def attend_back(*given):
@@ -539,6 +613,64 @@
     pa = {k: kv_deltas[k, 0] for k in range(8)}
     pb = {k: kv_deltas[k, 1] for k in range(8)}
     return outs[:6], pa, pb
+
+
+def theirs_kernel(cuts, place_ref, *refs):
+    out = refs[-1]
+    core = place_ref[1]
+    for ref, (row, n, source, column, width) in zip(refs, cuts):
+        out[:, row : row + n, :, column : column + width] = ref[
+            1 - core, :, :, :, source : source + width
+        ]
+
+
+def near_kernel(cuts, place_ref, *refs):
+    got, outs = refs[len(cuts)], refs[-4:]
+    mp, core = place_ref[0], place_ref[1]
+    for step, out in zip((0, 1, 3, 2), outs):
+        for pair in range(2):
+            block = mp ^ step ^ (4 * pair)
+            base = pair * got.shape[1]
+            for ref, (row, n, source, column, width) in zip(refs, cuts):
+                columns = slice(column, column + width)
+                mine = ref[core, block, :, :, source : source + width].astype(f32)
+                total = mine + got[block, row : row + n, :, columns].astype(f32)
+                out[base + row : base + row + n, :, columns] = total.astype(bf16)
+
+
+def sum_weights(grads, cuts, columns, place, sent, got, after, before_last):
+    views = [g.reshape(2, 8, -1, 8, g.shape[1]) for g in grads]
+    eights = max(row + n for row, n, _, _, _ in cuts)
+    params = pltpu.CompilerParams(vmem_limit_bytes=44 * 1024 * 1024)
+    cost = pl.CostEstimate(flops=0, bytes_accessed=0, transcendentals=0)
+    low = lambda *dims: jax.ShapeDtypeStruct(dims, bf16)
+    theirs = pl.pallas_call(
+        functools.partial(theirs_kernel, cuts),
+        in_specs=[SMEM] + [VMEM] * len(views),
+        out_specs=VMEM,
+        out_shape=low(8, eights, 8, columns),
+        compiler_params=params,
+        cost_estimate=cost,
+        name="theirs",
+    )(place, *views)
+    near = pl.pallas_call(
+        functools.partial(near_kernel, cuts),
+        in_specs=[SMEM] + [VMEM] * (len(views) + 1) + [ANY] * len(after),
+        out_specs=[VMEM] * 4,
+        out_shape=[low(2 * eights, 8, columns)] * 4,
+        compiler_params=params,
+        cost_estimate=cost,
+        name="near",
+    )(place, *views, core_swap(theirs), *after)
+    near = [x.reshape(16 * eights, columns) for x in near]
+    sent += near[1:]
+    total = near[0].astype(f32)
+    for step, x in zip((1, 3, 2), near[1:]):
+        got.append(mp_swap(x, step))
+        total = total + got[-1].astype(f32)
+    half = 8 * eights
+    last = held(total[half:].astype(bf16), before_last)
+    return (total[:half] + mp_swap(last, 4).astype(f32)).astype(bf16)
 
 
 def pad_action(rows):
@@ -679,7 +811,8 @@
         return item, place, is_action
 
     own_item, own_place, own_is_action = tables(mp, jnp.arange(BLOCK, dtype=jnp.int32))
-    key_item, _, key_is_action = tables(jnp.asarray(ROW_BLOCK) ^ mp, jnp.asarray(ROW_ID))
+    key_item, key_place, key_is_action = tables(jnp.asarray(KEY_BLOCK) ^ mp, jnp.asarray(KEY_ROW))
+    key_cos, key_sin = angle_tables(key_place)
     own_codes = jnp.stack([own_item, jnp.where(own_is_action, own_item, -2)], axis=1)
     key_codes = jnp.stack(
         [jnp.where(key_is_action, -1, key_item), jnp.where(key_is_action, key_item, -1)], axis=0
@@ -697,46 +830,61 @@
     last_row = near[:, :, pack.shape[1] - 256 : pack.shape[1] - 48].reshape(8, 1, wide)
     near_d = jnp.concatenate([near[:, :, :wide], last_row], axis=1).reshape(72, wide)
     near_a = near[:, :, wide : pack.shape[1] - 256].reshape(64, -1)
-    kv_a = jnp.concatenate([near_a[:, :640], near_a[:, 2688 + 1024 :]], axis=1)
-    kv_d = widen(near_d[:, :640], 768)
-    qo_a = join(near_a[:, 640:1664], near_a[:, 1664:2688])
-    qo_b = join(near_d[:, 640:], near_a[:, 2688 : 2688 + 1024])
-
-    seed_block = fence(seed_block, near)
-    seeds = relay_gather(seed_block[:HALF_A], seed_block[HALF_A:], mp_swap)
+    edge = near_a[:, 2688 + 1024 :]
+    kv_a = widen(jnp.concatenate([near_a[:, :640], edge], axis=1), 1024)
+    pack_a = join(near_a[:, 640:1664], near_a[:, 1664:2688], kv_a)
+    pack_b = join(near_d[:, 640:], near_a[:, 2688 : 2688 + 1024], widen(near_d[:, :640], 1024))
     arrived = {}
 
     def note(name):
         def during(stage, blocks, sends):
             arrived[name, stage] = blocks
+            arrived[name, "sends", stage] = sends
             return ()
 
         return during
 
-    kv_halves = place(relay_gather(kv_a, kv_d, yz_swap, note("kv"), {3: seeds[1:4]}), 64, yz)
-    kv_a, kv_d = interleave(kv_halves, ((0, 0, 8), (1, 0, 9)), core)
-    wkv_d, wkv_a, wo_e = kv_d[:, :512], kv_a[:, :512], kv_a[:, 640:]
-    gains_d = kv_d[:, 512:640].T.astype(f32)
-    gains_a = kv_a[:, 512:640].T.astype(f32)
-    first_gain_d, second_gain_d = gains_d[0:1], gains_d[1:2]
-    first_gain_a, second_gain_a = gains_a[0:1], gains_a[1:2]
-
     own_action = pad_action(action_input[0])
+    own_block = block_of(prefix_input[0], own_action)
+    own_block = fence(own_block, near)
+    x_rows = relay_gather(own_block, HALF_A, mp_swap)
+    hold = {2: x_rows[1:4], 3: x_rows[4:7]}
+    mine = relay_gather(join(pack_a, pack_b), pack_a.shape[0], yz_swap, note("weights"), hold)
+    theirs = [core_swap(x) for x in mine]
+    cuts = (
+        (0, 0, 8, 0, 1024),
+        (0, 8, 8, 0, 1024),
+        (0, 16, 8, 0, 512),
+        (0, 16, 8, 512, 128),
+        (0, 16, 8, 640, 128),
+        (1, 0, 9, 0, 1024),
+        (1, 9, 8, 0, 1024),
+        (1, 17, 9, 0, 512),
+        (1, 17, 9, 512, 128),
+    )
+    wq_a, wo_a, wkv_a, gains_a, wo_e, wq_d, wo_m, wkv_d, gains_d = assemble(
+        mine, theirs, pack_a.shape[0], cuts, yz, core
+    )
+    seeds = relay_gather(
+        seed_block,
+        HALF_A,
+        mp_swap,
+        note("seeds"),
+        {1: arrived["weights", "sends", 3][:1]},
+    )
+
+    normed_d, normed_a, keys, values = keys_of(
+        x_rows,
+        gains_d,
+        gains_a,
+        wkv_d,
+        wkv_a,
+        key_cos,
+        key_sin,
+        arrived["seeds", "sends", 2],
+    )
     x_d, x_a = prefix_input[0].astype(f32), own_action.astype(f32)
     rms_d, rms_a = inverse_rms(x_d), inverse_rms(x_a)
-    normed_d = (x_d * rms_d * first_gain_d).astype(bf16)
-    normed_a = (x_a * rms_a * first_gain_a).astype(bf16)
-    kv_raw = join(dot(normed_d, wkv_d), dot(normed_a, wkv_a))
-    kv_own = jnp.concatenate(
-        [rotate(kv_raw[:, :HD], own_cos, own_sin).astype(bf16), kv_raw[:, HD:].astype(bf16)],
-        axis=1,
-    )
-    kv_rows = relay_gather(kv_own[:HALF_A], kv_own[HALF_A:], mp_swap, note("rows"))
-    qo_a = fence(qo_a, arrived["kv", 2][0])
-    qo_hold = {2: (kv_own, *seeds[4:7]), 3: (*arrived["rows", 2], *seeds[7:9])}
-    qo_halves = place(relay_gather(qo_a, qo_b, yz_swap, note("qo"), qo_hold), 128, yz)
-    cuts = ((0, 0, 8), (0, 8, 8), (1, 0, 9), (1, 9, 8))
-    wq_a, wo_a, wq_d, wo_m = interleave(qo_halves, cuts, core)
     queries, context, tops, totals, hidden_d, hidden_a, second_block = attend(
         normed_d,
         normed_a,
@@ -747,13 +895,15 @@
         wo_m,
         wo_e,
         wo_a,
-        second_gain_d,
-        second_gain_a,
+        gains_d,
+        gains_a,
         own_cos,
         own_sin,
         own_codes,
         key_codes,
-        *kv_rows,
+        keys,
+        values,
+        after=arrived["seeds", "sends", 3],
     )
 
     slots = action_gate.shape[2]
@@ -774,14 +924,14 @@
         return (done[0][0],)
 
     def feed_during(stage, arrays, sends):
-        first, blocks, base = {1: (0, (0,), 6), 2: (1, (1, 3, 4), 0), 3: (4, (2, 5, 7), 3)}[stage]
+        if stage == 3:
+            return ()
+        first, blocks, base = {1: (0, (0,), 3), 2: (1, (1, 3, 4), 0)}[stage]
         return run(arrays, first, blocks, base, sends)
 
     second_block = fence(second_block, seeds[8])
-    arrays = relay_gather(
-        second_block[:HALF_A], second_block[HALF_A:], mp_swap, feed_during
-    )
-    run(arrays[7:], 7, (6,), 7, ())
+    arrays = relay_gather(second_block, HALF_A, mp_swap, feed_during)
+    run(arrays[4:], 4, (2, 5, 7, 6), 4, ())
     product_d, deltas_d, rows_d, seeds_d, product_a, deltas_a, rows_a, seeds_a = kept
 
     grads = (
@@ -793,8 +943,7 @@
     hidden = prefix_down.shape[0]
     grads = tuple(g.astype(bf16) for g in grads)
     after_grads = tuple(grads)
-    one = lax.psum(grads[0], "dp")
-    grads = (one,) + tuple(lax.psum(fence(g, one), "dp") for g in grads[1:])
+    grads = tuple(lax.psum(g, "dp") for g in grads)
     finished = (
         grads[0][:hidden].astype(f32),
         grads[0][HIDDEN_PAD : HIDDEN_PAD + hidden].astype(f32),
@@ -806,7 +955,7 @@
 
     pa = {k: v[0] for k, v in results.items()}
     pb = {k: v[1] for k, v in results.items()}
-    delta_pieces = relay_scatter(pa, pb, mp_swap, {3: lambda: after_grads})
+    delta_pieces = relay_scatter(pa, pb, mp_swap)
     (hidden_delta_d, hidden_delta_a, low, terms_d, terms_a, query_delta), pa, pb = attend_back(
         *delta_pieces,
         hidden_d,
@@ -814,8 +963,8 @@
         prefix_cotangent[0],
         cotangent_a,
         row_share,
-        second_gain_d,
-        second_gain_a,
+        gains_d,
+        gains_a,
         wo_m,
         wo_e,
         wo_a,
@@ -826,62 +975,81 @@
         own_sin,
         own_codes,
         key_codes,
-        *kv_rows,
+        keys,
+        values,
     )
     low_d, low_a = low[:PREF], low[PREF:, :DA]
+
+    kv_near = [join(pa[k], pb[k], pa[k ^ 4], pb[k ^ 4]) for k in range(4)]
+    kv_part = kv_near[0].astype(f32)
+    for k in (1, 3, 2):
+        kv_part = kv_part + mp_swap(kv_near[k], k).astype(f32)
+    pair = lambda table: join(
+        own_cos if table is key_cos else own_sin,
+        table[ROW_PAIR : ROW_PAIR + PREF],
+        table[len(PARTS) * HALF_A + ACT_PAIR : len(PARTS) * HALF_A + ACT_PAIR + ACT_PAD],
+    )
+    kv_turned = jnp.concatenate(
+        [unrotate(kv_part[:, :HD], pair(key_cos), pair(key_sin)), kv_part[:, HD:]], axis=1
+    )
+    kv_turned_low = kv_turned.astype(bf16)
+    kv_rows_d = join(kv_turned_low[:PREF], kv_turned_low[BLOCK : BLOCK + PREF])
+    kv_rows_a = join(kv_turned_low[PREF:BLOCK], kv_turned_low[BLOCK + PREF :])
 
     order_d, order_a = order_matrix(D, 9), order_matrix(DA, 8)
     turned_d = dot(normed_d, order_d).astype(bf16)
     turned_a = dot(normed_a, order_a).astype(bf16)
     turned_context = dot(context, order_a).astype(bf16)
-    second_term_d = t_dot(dot(terms_d, order_d).astype(bf16), jnp.ones((PREF, 128), bf16))
+    second_term_d = t_dot(dot(terms_d, order_d).astype(bf16), jnp.ones((PREF, 256), bf16))
     second_term_a = t_dot(dot(terms_a, order_a).astype(bf16), jnp.ones((ACT_PAD, 128), bf16))
     out_grad_d = t_dot(turned_context[:PREF], low_d).astype(bf16)
     out_grad_a = t_dot(turned_context[PREF:], low_a).astype(bf16)
-    q_grad_d = t_dot(turned_d, query_delta[:PREF]).astype(bf16)
-    q_grad_a = t_dot(turned_a, query_delta[PREF:]).astype(bf16)
-
-    def split(array):
-        return array.reshape(2, 8, -1, array.shape[1])
-
-    def sum_cores(pieces):
-        mine = lax.dynamic_index_in_dim(pieces, core, 0, keepdims=False)
-        theirs = lax.dynamic_index_in_dim(pieces, 1 - core, 0, keepdims=False)
-        return add_low(mine, core_swap(theirs))
-
-    def sum_mp(pack, sent=None):
-        pack = sum_cores(pack)
-        pieces = [lax.dynamic_index_in_dim(pack, mp ^ k, 0, keepdims=False) for k in range(8)]
-        return ring_scatter(pieces, mp_swap, {}, sent).astype(bf16)
-
-    qo = [q_grad_a, out_grad_a, q_grad_d, out_grad_d[:, :1024]]
-    qo_sent, kv_sent = [], []
-    qo = sum_mp(jnp.concatenate([split(g) for g in qo], axis=2), qo_sent)
-    kv_sum = ring_scatter(
-        [join(pa[k], pb[k]) for k in range(8)], mp_swap, {2: tuple(qo_sent)}
-    )
+    q_grad_d = t_dot(turned_d[:PREF], query_delta[:PREF]).astype(bf16)
+    q_grad_a = t_dot(turned_a[:ACT_PAD], query_delta[PREF:]).astype(bf16)
+    place = jnp.stack([mp, core])
+    cuts = (
+        (0, 8, 0, 0, 1024),
+        (8, 8, 0, 0, 1024),
+        (16, 9, 0, 0, 1024),
+        (25, 8, 0, 0, 1024),
+    )
+    qo_sent, kv_sent, kv_got = [], [], []
+    qo_grads = (q_grad_a, out_grad_a, q_grad_d, out_grad_d)
+    qo = sum_weights(qo_grads, cuts, 1024, place, qo_sent, [], (), grads[:1])
+    kv_grad_d = t_dot(turned_d, kv_rows_d).astype(bf16)
+    kv_grad_a = t_dot(turned_a, kv_rows_a).astype(bf16)
+    cuts = (
+        (0, 8, 0, 0, 512),
+        (0, 8, 0, 512, 128),
+        (0, 8, 1024, 640, 128),
+        (8, 9, 0, 0, 512),
+        (8, 9, 0, 512, 256),
+    )
+    kv_grads = (
+        kv_grad_a,
+        second_term_a.astype(bf16),
+        out_grad_d,
+        kv_grad_d,
+        second_term_d.astype(bf16),
+    )
+    kv = sum_weights(kv_grads, cuts, 768, place, kv_sent, kv_got, qo_sent, grads[:1])
+    kv_a, kv_d = kv[:64], kv[64:, :640]
+    qo_a, qo_b = qo[:128], qo[128:]
+    kv_other = mp_swap(held(kv_part[BLOCK:].astype(bf16), tuple(kv_sent)), 4)
+    kv_sum = kv_part[:BLOCK] + kv_other.astype(f32)
     kv_raw_delta = jnp.concatenate(
         [unrotate(kv_sum[:, :HD], own_cos, own_sin), kv_sum[:, HD:]], axis=1
     ).astype(bf16)
-    kv_grad_d = t_dot(turned_d, kv_raw_delta[:PREF])
-    kv_grad_a = t_dot(turned_a, kv_raw_delta[PREF:])
-    kv_grad_d = jnp.concatenate([kv_grad_d, second_term_d], axis=1).astype(bf16)
-    kv_grad_a = jnp.concatenate(
-        [kv_grad_a.astype(bf16), second_term_a.astype(bf16), out_grad_d[:, 1024:]], axis=1
-    )
-    kv = sum_mp(jnp.concatenate([split(kv_grad_a), split(widen(kv_grad_d, 768))], axis=2), kv_sent)
-    kv_a, kv_d = kv[:64], kv[64:, :640]
-    qo_a, qo_b = qo[:128], qo[128:]
-
-    product_d = fence(product_d, qo_sent[0])
+
+    product_d = fence(product_d, kv_sent[0])
     partial_d = dot(product_d[:, :hidden], prefix_down).astype(bf16)
     partial_a = dot(product_a, action_down[0]).astype(bf16)
     out = []
     for k in range(8):
-        i = (1, 3, 4, 2, 5, 7, 0, 6).index(k)
+        i = (1, 3, 4, 0, 2, 5, 7, 6).index(k)
         mine = partial_a[i * ACT_PAD : (i + 1) * ACT_PAD]
         out.append(block_of(partial_d[i * PREF : (i + 1) * PREF], mine))
-    out = ring_scatter(out, mp_swap, {1: tuple(qo_sent)})
+    out = ring_scatter(out, mp_swap, {1: tuple(kv_got)})
     prefix_output = (hidden_d + out[:PREF]).astype(bf16)[None]
     action_output = (hidden_a + out[PREF:, :DA])[:ACT].astype(bf16)[None]
 
@@ -897,7 +1065,7 @@
         ],
         axis=2,
     )
-    last = scatter_direct(last, yz, yz_swap)
+    last = scatter_direct(fence(last, *finished), yz, yz_swap)
     ninth = last[:, last.shape[1] - 256 : last.shape[1] - 48].reshape(1, wide)
     grads_d = join(last[:, :wide], ninth)
     grads_a = last[:, wide : last.shape[1] - 256]
@@ -921,6 +1089,7 @@
 
     first_delta_d = dot_t(query_delta[:PREF], wq_d) + dot_t(kv_raw_delta[:PREF], wkv_d)
     first_delta_a = dot_t(query_delta[PREF:], wq_a) + dot_t(kv_raw_delta[PREF:], wkv_a)
+    first_gain_d, first_gain_a = gain_rows(gains_d)[0], gain_rows(gains_a)[0]
     input_d = hidden_delta_d + normalize_back(x_d, rms_d, first_gain_d, first_delta_d)
     input_a = hidden_delta_a + normalize_back(x_a, rms_a, first_gain_a, first_delta_a)
 

time: 707 us -> 563 us (0.80)
  waiting for transfers between devices: 275 us -> 151 us
  local copies, waits for them, and re-layouts: 76.7 us -> 48.7 us
  Pallas kernels: 84.8 us -> 105 us
  other arithmetic: 90.2 us -> 77.8 us
    psum x2 -> x1, waiting for transfers between devices: 96.5 us -> 0.02 us  [on_device(): grads = tuple((lax.psum(g, 'dp') for g in grads))]
    pallas_call x5 -> x15, Pallas kernels: 20.3 us -> 48.5 us  [the longest x1 11.3 us: attend(): pl.pallas_call(attend_kernel, in_specs=[VMEM] * len(given) + [ANY] * len(...]
    ppermute x26 -> x23, waiting for transfers between devices: 41.6 us -> 20.4 us  [dp_swap(): return lax.ppermute(array, 'dp', [(i, i ^ step) for i in range(16)])]
    concatenate x37 -> x15, other arithmetic: 24 us -> 11.4 us  [join(): return jnp.concatenate(parts, axis=0)]
    unnamed x405 -> x335, local copies, waits for them, and re-layouts: 43.6 us -> 33.2 us
    convert_element_type x6 -> x4, other arithmetic: 9.72 us -> 0.42 us  [add_low(): return total.astype(bf16)]
    slice x47 -> x10, local copies, waits for them, and re-layouts: 15.9 us -> 6.87 us  [the longest x2 3.08 us: on_device(): table[ROW_PAIR:ROW_PAIR + PREF]]
    pallas_call x4 -> x3, Pallas kernels: 51.5 us -> 44 us  [feed(): pl.pallas_call(functools.partial(feed_kernel, layout), grid=(1,), in_spec...]
  transfers between devices with their start and end apart: 80 -> 76, of which waited for: 33 -> 26; matrix products, arithmetic and copies ran while one was open for 23% -> 23% of each run, Pallas kernels for 10% -> 16%
where the time goes in v3:
time: 563 us; the launch traced here: 552 us
  waiting for transfers between devices  151 us (27%)
  Pallas kernels  105 us (19%)
  starting transfers between devices  96.8 us (17%)
  other arithmetic  77.8 us (14%)
  matrix products  55.4 us (10%)
  local copies, waits for them, and re-layouts  48.7 us (9%)
  between operations  17.4 us (3%)
    ppermute x52, waiting for transfers between devices, mp_swap(): return lax.ppermute(array, 'mp', [(i, i ^ step) for i in range(N_MP)])  130 us
    ppermute x52, starting transfers between devices, mp_swap(): return lax.ppermute(array, 'mp', [(i, i ^ step) for i in range(N_MP)])  70.9 us
    pallas_call x3, Pallas kernels, feed(): pl.pallas_call(functools.partial(feed_kernel, layout), grid=(1,), in_spec...  44 us
    unnamed x335, local copies, waits for them, and re-layouts  33.2 us
    dot_general x12, matrix products, t_dot(): lax.dot_general(a, b, (((0,), (0,)), ((), ())), preferred_element_type=f32)  32.4 us
    ppermute x23, starting transfers between devices, dp_swap(): return lax.ppermute(array, 'dp', [(i, i ^ step) for i in range(16)])  25.8 us
    ppermute x23, waiting for transfers between devices, dp_swap(): return lax.ppermute(array, 'dp', [(i, i ^ step) for i in range(16)])  20.4 us
    dot_general x5, matrix products, dot(): return jnp.dot(a, b, preferred_element_type=f32)  14.9 us
  transfers between devices with their start and end apart: 76, of which 26 were waited for; matrix products, arithmetic and copies ran while one was open for 23% of the time, Pallas kernels for 16%

profile of v3, /device:TPU:0, one launch (start us, length us, event | category | flops | bytes accessed | tf_op | source)
XLA Modules:
  0.0 551.6 jit_solution(9972230794042882624)
XLA Ops:
  23.0 7.4 %collective-permute-done.1 = bf16[2,8,5760]{2,1,0:T(8,128)(2,1)S(1)} collective-permute-done((bf16[2,8,5760]{2,1,0:T(8,128)(2,1)S(1)}, bf16[2,8,5760]{2,1,0:T(8,128)(2,1)S(1)}, u32[]{:S(2)}, u32[]{:S(2)}) %collective-permute-start.1) | collective-permute-done | bytes 184352 | tf_op jit(solution)/shard_map/ppermute | solution.py:55
  35.8 3.6 collective-permute-start.14
  49.3 5.8 %collective-permute-done.5.refs_1_.refs_4_.refs_2_ = bf16[208,1152]{1,0:T(8,128)(2,1)S(1)} collective-permute-done((bf16[208,1152]{1,0:T(8,128)(2,1)S(1)}, bf16[208,1152]{1,0:T(8,128)(2,1)S(1)}, u32[]{:S(2)}, u32[]{:S(2)}) %collective-permute-start.5) | collective-permute-done | bytes 479264 | tf_op jit(solution)/shard_map/ppermute | solution.py:55
  59.5 6.1 %collective-permute-done.14.refs_2_ = bf16[400,1024]{1,0:T(8,128)(2,1)S(1)} collective-permute-done((bf16[400,1024]{1,0:T(8,128)(2,1)}, bf16[400,1024]{1,0:T(8,128)(2,1)S(1)}, u32[]{:S(2)}, u32[]{:S(2)}) %collective-permute-start.14) | collective-permute-done | bytes 819232 | tf_op jit(solution)/shard_map/ppermute | solution.py:59
  68.7 4.2 multiply_sine_fusion
  78.6 6.7 %collective-permute-done.9.refs_4_.refs_6_ = bf16[224,1152]{1,0:T(8,128)(2,1)} collective-permute-done((bf16[224,1152]{1,0:T(8,128)(2,1)}, bf16[224,1152]{1,0:T(8,128)(2,1)}, u32[]{:S(2)}, u32[]{:S(2)}) %collective-permute-start.9) | collective-permute-done | bytes 516128 | tf_op jit(solution)/shard_map/ppermute | solution.py:55
  108.9 4.1 collective-permute-done.19
  118.9 3.6 collective-permute-done.29.refs_0_.refs_3_
  140.5 8.5 %assemble.1 = (bf16[8,2,8,8,1024]{4,3,2,1,0:T(8,128)(2,1)}, bf16[8,2,8,8,1024]{4,3,2,1,0:T(8,128)(2,1)}, bf16[8,2,8,8,512]{4,3,2,1,0:T(8,128)(2,1)}, bf16[8,2,8,...) custom-call(s32[2]{0:T(128)S(1)} %pad_add_fusion.2.place_ref, ...), custom_call_target="tpu_custom_call" | custom-call | tf_op jit(solution)/shard_map/assemble/pallas_call | solution.py:240
  153.2 6.4 %keys_of.1 = (bf16[384,1152]{1,0:T(8,128)(2,1)}, bf16[32,1024]{1,0:T(8,128)(2,1)S(1)}, bf16[1664,256]{1,0:T(8,128)(2,1)}, bf16[1664,256]{1,0:T(8,128)(2,1)}) custom-call(bf16[208,1152]{1,0:T(8,128)(2,1)S(1)} %copy-done.13, bf16[208,1152]{1,0:T(8,128)(2,1)S(1)} %collective-permute-done.4.refs_0_.refs_3_.refs_1_, ...), custom_call_target="tpu_custom_call" | custom-call | flops 1962934272 | bytes 8388608 | tf_op jit(solution)/shard_map/keys_of/pallas_call | solution.py:290
  159.6 11.3 %attend.1 = (bf16[832,256]{1,0:T(8,128)(2,1)S(1)}, bf16[208,1024]{1,0:T(8,128)(2,1)S(1)}, f32[832,1]{1,0:T(8,128)S(1)}, f32[832,1]{1,0:T(8,128)S(1)}, f32[192,11...) custom-call(bf16[384,1152]{1,0:T(8,128)(2,1)} %get-tuple-element.149.refs_0_, ...), custom_call_target="tpu_custom_call" | custom-call | flops 2399141888 | bytes 20971520 | tf_op jit(solution)/shard_map/attend/pallas_call | solution.py:506
  177.9 10.0 %feed.3 = (bf16[1536,896]{1,0:T(8,128)(2,1)}, bf16[1536,1792]{1,0:T(8,128)(2,1)}, bf16[1536,1152]{1,0:T(8,128)(2,1)}, bf16[1536,1152]{1,0:T(8,128)(2,1)}, bf16[1...) custom-call(bf16[208,1152]{1,0:T(8,128)(2,1)S(1)} %copy-done.14, ...), custom_call_target="tpu_custom_call" | custom-call | flops 2078801920 | bytes 12263424 | tf_op jit(solution)/shard_map/feed/pallas_call | solution.py:434
  194.9 15.6 %feed.4 = (bf16[1536,896]{1,0:T(8,128)(2,1)}, bf16[1536,1792]{1,0:T(8,128)(2,1)}, bf16[1536,1152]{1,0:T(8,128)(2,1)}, bf16[1536,1152]{1,0:T(8,128)(2,1)}, bf16[1...) custom-call(bf16[208,1152]{1,0:T(8,128)(2,1)S(1)} %collective-permut, ...), custom_call_target="tpu_custom_call", output_to_operand_aliasing={{0}: (13, {}), {1}: (14, {}), {2}: (15, {}), {3}: (16, {}),... | custom-call | flops 6236405760 | bytes 12263424 | tf_op jit(solution)/shard_map/feed/pallas_call | solution.py:434
  222.0 18.4 %feed.5 = (bf16[1536,896]{1,0:T(8,128)(2,1)}, bf16[1536,1792]{1,0:T(8,128)(2,1)}, bf16[1536,1152]{1,0:T(8,128)(2,1)}, bf16[1536,1152]{1,0:T(8,128)(2,1)}, bf16[1...) custom-call(bf16[192,1152]{1,0:T(8,128)(2,1)S(1)} %collective-permut, ...), custom_call_target="tpu_custom_call", output_to_operand_aliasing={{0}: (17, {}), {1}: (18, {}), {2}: (19, {}), {3}: (20, {}),... | custom-call | flops 8315207680 | bytes 12263424 | tf_op jit(solution)/shard_map/feed/pallas_call | solution.py:434
  244.6 11.9 %convolution_convert_fusion = bf16[1792,1152]{1,0:T(8,128)(2,1)} fusion(bf16[1536,1792]{1,0:T(8,128)(2,1)} %get-tuple-element.235, bf16[1536,1152]{1,0:T(8,128)(2,1)} %get-tuple-element.236), kind=kOutput, calls=%fused_computation | convolution fusion | flops 6343852032 | bytes 13172736 | tf_op jit(solution)/shard_map/dot_general | solution.py:706
  258.2 5.2 convolution_convert_fusion.5
  275.1 3.3 convolution_convert_fusion.4
  280.6 12.4 %attend_back.1 = (f32[192,1152]{1,0:T(8,128)}, f32[16,1024]{1,0:T(8,128)S(1)}, bf16[208,1152]{1,0:T(8,128)(2,1)}, bf16[192,1152]{1,0:T(8,128)(2,1)}, bf16[16,102...) custom-call(bf16[96,1152]{1,0:T(8,128)(2,1)S(1)} %get-tuple-element., ...), custom_call_target="tpu_custom_call" | custom-call | flops 425984 | bytes 832 | tf_op jit(solution)/shard_map/attend_back/pallas_call | solution.py:595
  314.4 3.5 convolution_convert_fusion.7
  320.8 8.8 %collective-permute-done.54 = bf16[416,512]{1,0:T(8,128)(2,1)} collective-permute-done((bf16[416,512]{1,0:T(8,128)(2,1)}, bf16[416,512]{1,0:T(8,128)(2,1)}, u32[]{:S(2)}, u32[]{:S(2)}) %collective-permute-start.54) | collective-permute-done | bytes 426016 | tf_op jit(solution)/shard_map/ppermute | solution.py:55
  345.3 4.9 near.2
  351.2 4.0 near.3
  364.7 6.6 %convolution_convert_fusion.1 = bf16[1536,1152]{1,0:T(8,128)(2,1)S(1)} fusion(bf16[864,1152]{1,0:T(8,128)(2,1)} %refs_12_.1, bf16[1536,896]{1,0:T(8,128)(2,1)} %fence.14), kind=kOutput, calls=%fused_computation.1 | convolution fusion | flops 3059417088 | bytes 8282112 | tf_op jit(solution)/shard_map/dot_general | solution.py:698
  381.2 23.0 %collective-permute-done.59.refs_2_ = bf16[272,768]{1,0:T(8,128)(2,1)} collective-permute-done((bf16[272,768]{1,0:T(8,128)(2,1)}, bf16[272,768]{1,0:T(8,128)(2,1)}, u32[]{:S(2)}, u32[]{:S(2)}) %collective-permute-start.59) | collective-permute-done | bytes 417824 | tf_op jit(solution)/shard_map/ppermute | solution.py:55
  411.8 17.6 %collective-permute-done.61 = bf16[416,1152]{1,0:T(8,128)(2,1)} collective-permute-done((bf16[416,1152]{1,0:T(8,128)(2,1)}, bf16[416,1152]{1,0:T(8,128)(2,1)}, u32[]{:S(2)}, u32[]{:S(2)}) %collective-permute-start.61) | collective-permute-done | bytes 958496 | tf_op jit(solution)/shard_map/ppermute | solution.py:55
  431.5 39.6 %collective-permute-done.62 = bf16[416,1152]{1,0:T(8,128)(2,1)} collective-permute-done((bf16[416,1152]{1,0:T(8,128)(2,1)}, bf16[416,1152]{1,0:T(8,128)(2,1)}, u32[]{:S(2)}, u32[]{:S(2)}) %collective-permute-start.62) | collective-permute-done | bytes 958496 | tf_op jit(solution)/shard_map/ppermute | solution.py:55
  482.1 3.9 slice_convert_fusion.2.refs_3_
  486.0 6.3 %fusion.56 = (f32[1152,864]{0,1:T(8,128)}, f32[1152,864]{0,1:T(8,128)}, f32[864,1152]{1,0:T(8,128)}, f32[864,1152]{1,0:T(8,128)}) fusion(bf16[1792,1152]{1,0:T(8,128)(2,1)S(1)} %copy-done.89), kind=kLoop, calls=%fused_computation.107 | loop fusion | flops 1990656 | bytes 19906560 | tf_op jit(solution)/shard_map/transpose | solution.py:1114
  494.5 9.4 %fusion.48 = (f32[1,1024,1024]{2,1,0:T(8,128)}, f32[1,1024,1024]{2,1,0:T(8,128)}, f32[1024,1024]{1,0:T(8,128)}, f32[1024,1024]{1,0:T(8,128)}) fusion(bf16[1024,2048]{1,0:T(8,128)(2,1)} %get-tuple-element.248), kind=kLoop, calls=%fused_computation.97 | loop fusion | flops 2097152 | bytes 20971520 | tf_op jit(solution)/shard_map/broadcast_in_dim | solution.py:1117
  503.9 4.5 convert_bitcast_fusion
  524.9 3.3 collective-permute-done.73
  531.2 4.8 collective-permute-start.74
  (639 shorter events, 249.6 us)
Async XLA Ops:
  7.2 474.9 %all-reduce.20.cloned.1.call-start = ((), (), s32[]{:S(2)}) async-start(), calls=%async_computation | async-start | bytes 24969216 | tf_op jit(solution)/shard_map/psum | solution.py:946
  35.8 29.9 %collective-permute-start.14 = (bf16[400,1024]{1,0:T(8,128)(2,1)}, bf16[400,1024]{1,0:T(8,128)(2,1)S(1)}, u32[]{:S(2)}, u32[]{:S(2)}) collective-permute-start(bf16[400,1024]{1,0:T(8,128)(2,1)} %fusion.93), channel_id=1, source_target_pairs={{0,64},{8,72},{16,80},{24,88},{32,96},{40,104},{48,112},{56,120},{... | collective-permute-start | bytes 2457608 | tf_op jit(solution)/shard_map/ppermute | solution.py:59
  39.4 26.3 %collective-permute-start.13 = (bf16[400,1024]{1,0:T(8,128)(2,1)}, bf16[400,1024]{1,0:T(8,128)(2,1)S(1)}, u32[]{:S(2)}, u32[]{:S(2)}) collective-permute-start(bf16[400,1024]{1,0:T(8,128)(2,1)} %fusion.93), channel_id=1, source_target_pairs={{0,48},{8,56},{16,32},{24,40},{32,16},{40,24},{48,0},{56,8},{64,11... | collective-permute-start | bytes 2457608 | tf_op jit(solution)/shard_map/ppermute | solution.py:59
  42.4 23.3 %collective-permute-start.12 = (bf16[400,1024]{1,0:T(8,128)(2,1)}, bf16[400,1024]{1,0:T(8,128)(2,1)S(1)}, u32[]{:S(2)}, u32[]{:S(2)}) collective-permute-start(bf16[400,1024]{1,0:T(8,128)(2,1)} %fusion.93), channel_id=1, source_target_pairs={{0,16},{8,24},{16,0},{24,8},{32,48},{40,56},{48,32},{56,40},{64,80... | collective-permute-start | bytes 2457608 | tf_op jit(solution)/shard_map/ppermute | solution.py:59
  67.1 23.4 %collective-permute-start.15 = (bf16[384,1024]{1,0:T(8,128)(2,1)}, bf16[384,1024]{1,0:T(8,128)(2,1)}, u32[]{:S(2)}, u32[]{:S(2)}) collective-permute-start(bf16[384,1024]{1,0:T(8,128)(2,1)} %get-tuple-element.137), channel_id=1, source_target_pairs={{0,64},{8,72},{16,80},{24,88},{32,96},{40,104},{48,112},{56,120},{... | collective-permute-start | bytes 2359304 | tf_op jit(solution)/shard_map/ppermute | solution.py:59
  67.1 23.4 %collective-permute-start.16 = (bf16[400,1024]{1,0:T(8,128)(2,1)}, bf16[400,1024]{1,0:T(8,128)(2,1)}, u32[]{:S(2)}, u32[]{:S(2)}) collective-permute-start(bf16[400,1024]{1,0:T(8,128)(2,1)} %get-tuple-element.138), channel_id=1, source_target_pairs={{0,16},{8,24},{16,0},{24,8},{32,48},{40,56},{48,32},{56,40},{64,80... | collective-permute-start | bytes 2457608 | tf_op jit(solution)/shard_map/ppermute | solution.py:59
  76.0 18.5 %collective-permute-start.20 = (bf16[400,1024]{1,0:T(8,128)(2,1)}, bf16[400,1024]{1,0:T(8,128)(2,1)S(1)}, u32[]{:S(2)}, u32[]{:S(2)}) collective-permute-start(bf16[400,1024]{1,0:T(8,128)(2,1)} %fusion.93), channel_id=1, source_target_pairs={{0,8},{8,0},{16,24},{24,16},{32,40},{40,32},{48,56},{56,48},{64,72... | collective-permute-start | bytes 2457608 | tf_op jit(solution)/shard_map/ppermute | solution.py:59
  76.0 21.0 %collective-permute-start.23 = (bf16[400,1024]{1,0:T(8,128)(2,1)}, bf16[400,1024]{1,0:T(8,128)(2,1)S(1)}, u32[]{:S(2)}, u32[]{:S(2)}) collective-permute-start(bf16[400,1024]{1,0:T(8,128)(2,1)} %copy-done.18), channel_id=1, source_target_pairs={{0,8},{8,0},{16,24},{24,16},{32,40},{40,32},{48,56},{56,48},{64,72... | collective-permute-start | bytes 2457608 | tf_op jit(solution)/shard_map/ppermute | solution.py:59
  85.3 23.0 %collective-permute-start.17 = (bf16[416,1024]{1,0:T(8,128)(2,1)}, bf16[416,1024]{1,0:T(8,128)(2,1)}, u32[]{:S(2)}, u32[]{:S(2)}) collective-permute-start(bf16[416,1024]{1,0:T(8,128)(2,1)} %copy-done.84), channel_id=1, source_target_pairs={{0,48},{8,56},{16,32},{24,40},{32,16},{40,24},{48,0},{56,8},{64,11... | collective-permute-start | bytes 2555912 | tf_op jit(solution)/shard_map/ppermute | solution.py:59
  108.2 18.9 %collective-permute-start.24 = (bf16[384,1024]{1,0:T(8,128)(2,1)}, bf16[384,1024]{1,0:T(8,128)(2,1)}, u32[]{:S(2)}, u32[]{:S(2)}) collective-permute-start(bf16[384,1024]{1,0:T(8,128)(2,1)} %collective-permute-done.15.refs_0_), channel_id=1, source_target_pairs={{0,8},{8,0},{16,24},{24,16},{32,40},{40,32},{48,56},{56,48},{64,72... | collective-permute-start | bytes 2359304 | tf_op jit(solution)/shard_map/ppermute | solution.py:59
  115.5 18.6 %collective-permute-start.26 = (bf16[416,1024]{1,0:T(8,128)(2,1)}, bf16[416,1024]{1,0:T(8,128)(2,1)}, u32[]{:S(2)}, u32[]{:S(2)}) collective-permute-start(bf16[416,1024]{1,0:T(8,128)(2,1)} %collective-permute-done.17), channel_id=1, source_target_pairs={{0,8},{8,0},{16,24},{24,16},{32,40},{40,32},{48,56},{56,48},{64,72... | collective-permute-start | bytes 2555912 | tf_op jit(solution)/shard_map/ppermute | solution.py:59
  127.2 21.8 %collective-permute-start.33 = (bf16[208,1152]{1,0:T(8,128)(2,1)}, bf16[208,1152]{1,0:T(8,128)(2,1)}, u32[]{:S(2)}, u32[]{:S(2)}) collective-permute-start(bf16[208,1152]{1,0:T(8,128)(2,1)} %get-tuple-element.147.refs_16_), channel_id=1, source_target_pairs={{0,1},{1,0},{2,3},{3,2},{4,5},{5,4},{6,7},{7,6},{8,9},{9,8},{10,11... | collective-permute-start | bytes 1437704 | tf_op jit(solution)/shard_map/ppermute | solution.py:55
  127.5 21.5 %collective-permute-start.32 = (bf16[192,1152]{1,0:T(8,128)(2,1)}, bf16[192,1152]{1,0:T(8,128)(2,1)S(1)}, u32[]{:S(2)}, u32[]{:S(2)}) collective-permute-start(bf16[192,1152]{1,0:T(8,128)(2,1)} %copy-done.56), channel_id=1, source_target_pairs={{0,4},{1,5},{2,6},{3,7},{4,0},{5,1},{6,2},{7,3},{8,12},{9,13},{10,... | collective-permute-start | bytes 1327112 | tf_op jit(solution)/shard_map/ppermute | solution.py:55
  128.6 24.6 %collective-permute-start.11 = (bf16[112,1152]{1,0:T(8,128)(2,1)S(1)}, bf16[112,1152]{1,0:T(8,128)(2,1)S(1)}, u32[]{:S(2)}, u32[]{:S(2)}) collective-permute-start(bf16[112,1152]{1,0:T(8,128)(2,1)S(1)} %get-tuple-element.136), channel_id=1, source_target_pairs={{0,3},{1,2},{2,1},{3,0},{4,7},{5,6},{6,5},{7,4},{8,11},{9,10},{10,... | collective-permute-start | bytes 774152 | tf_op jit(solution)/shard_map/ppermute | solution.py:55
  132.8 20.3 %collective-permute-start.10 = (bf16[96,1152]{1,0:T(8,128)(2,1)S(1)}, bf16[96,1152]{1,0:T(8,128)(2,1)S(1)}, u32[]{:S(2)}, u32[]{:S(2)}) collective-permute-start(bf16[96,1152]{1,0:T(8,128)(2,1)S(1)} %get-tuple-element.135), channel_id=1, source_target_pairs={{0,1},{1,0},{2,3},{3,2},{4,5},{5,4},{6,7},{7,6},{8,9},{9,8},{10,11... | collective-permute-start | bytes 663560 | tf_op jit(solution)/shard_map/ppermute | solution.py:55
  134.0 82.9 %collective-permute-start.43 = (bf16[224,1152]{1,0:T(8,128)(2,1)}, bf16[224,1152]{1,0:T(8,128)(2,1)}, u32[]{:S(2)}, u32[]{:S(2)}) collective-permute-start(bf16[224,1152]{1,0:T(8,128)(2,1)} %copy-done.52), channel_id=1, source_target_pairs={{0,3},{1,2},{2,1},{3,0},{4,7},{5,6},{6,5},{7,4},{8,11},{9,10},{10,... | collective-permute-start | bytes 1548296 | tf_op jit(solution)/shard_map/ppermute | solution.py:55
  150.4 22.8 %collective-permute-start.34 = (bf16[112,1152]{1,0:T(8,128)(2,1)S(1)}, bf16[112,1152]{1,0:T(8,128)(2,1)}, u32[]{:S(2)}, u32[]{:S(2)}) collective-permute-start(bf16[112,1152]{1,0:T(8,128)(2,1)S(1)} %get-tuple-element.159.refs_18_), channel_id=1, source_target_pairs={{0,3},{1,2},{2,1},{3,0},{4,7},{5,6},{6,5},{7,4},{8,11},{9,10},{10,... | collective-permute-start | bytes 774152 | tf_op jit(solution)/shard_map/ppermute | solution.py:55
  188.9 21.6 %collective-permute-start.38 = (bf16[192,1152]{1,0:T(8,128)(2,1)S(1)}, bf16[192,1152]{1,0:T(8,128)(2,1)S(1)}, u32[]{:S(2)}, u32[]{:S(2)}) collective-permute-start(bf16[192,1152]{1,0:T(8,128)(2,1)S(1)} %get-tuple-element.163.refs_21_), channel_id=1, source_target_pairs={{0,4},{1,5},{2,6},{3,7},{4,0},{5,1},{6,2},{7,3},{8,12},{9,13},{10,... | collective-permute-start | bytes 1327112 | tf_op jit(solution)/shard_map/ppermute | solution.py:55
  190.1 20.4 %collective-permute-start.39 = (bf16[208,1152]{1,0:T(8,128)(2,1)S(1)}, bf16[208,1152]{1,0:T(8,128)(2,1)S(1)}, u32[]{:S(2)}, u32[]{:S(2)}) collective-permute-start(bf16[208,1152]{1,0:T(8,128)(2,1)S(1)} %get-tuple-element.164.refs_22_), channel_id=1, source_target_pairs={{0,1},{1,0},{2,3},{3,2},{4,5},{5,4},{6,7},{7,6},{8,9},{9,8},{10,11... | collective-permute-start | bytes 1437704 | tf_op jit(solution)/shard_map/ppermute | solution.py:55
  192.1 27.5 %collective-permute-start.40 = (bf16[224,1152]{1,0:T(8,128)(2,1)S(1)}, bf16[224,1152]{1,0:T(8,128)(2,1)S(1)}, u32[]{:S(2)}, u32[]{:S(2)}) collective-permute-start(bf16[224,1152]{1,0:T(8,128)(2,1)S(1)} %get-tuple-element.165.refs_23_), channel_id=1, source_target_pairs={{0,3},{1,2},{2,1},{3,0},{4,7},{5,6},{6,5},{7,4},{8,11},{9,10},{10,... | collective-permute-start | bytes 1548296 | tf_op jit(solution)/shard_map/ppermute | solution.py:55
  243.2 26.1 %collective-permute-start.47 = (bf16[224,1152]{1,0:T(8,128)(2,1)S(1)}, bf16[224,1152]{1,0:T(8,128)(2,1)S(1)}, u32[]{:S(2)}, u32[]{:S(2)}) collective-permute-start(bf16[224,1152]{1,0:T(8,128)(2,1)S(1)} %pad_maximum_fusion), channel_id=1, source_target_pairs={{0,3},{1,2},{2,1},{3,0},{4,7},{5,6},{6,5},{7,4},{8,11},{9,10},{10,... | collective-permute-start | bytes 1548296 | tf_op jit(solution)/shard_map/ppermute | solution.py:55
  301.1 44.1 %collective-permute-start.57 = (bf16[8,33,8,1024]{3,2,1,0:T(8,128)(2,1)}, bf16[8,33,8,1024]{3,2,1,0:T(8,128)(2,1)}, u32[]{:S(2)}, u32[]{:S(2)}) collective-permute-start(bf16[8,33,8,1024]{3,2,1,0:T(8,128)(2,1)} %theirs.3), channel_id=1, source_target_pairs={{0,8},{8,0},{16,24},{24,16},{32,40},{40,32},{48,56},{56,48},{64,72... | collective-permute-start | bytes 12976136 | tf_op jit(solution)/shard_map/ppermute | solution.py:59
  309.5 20.1 %collective-permute-start.54 = (bf16[416,512]{1,0:T(8,128)(2,1)}, bf16[416,512]{1,0:T(8,128)(2,1)}, u32[]{:S(2)}, u32[]{:S(2)}) collective-permute-start(bf16[416,512]{1,0:T(8,128)(2,1)} %pad_maximum_fusion.8), channel_id=1, source_target_pairs={{0,3},{1,2},{2,1},{3,0},{4,7},{5,6},{6,5},{7,4},{8,11},{9,10},{10,... | collective-permute-start | bytes 1277960 | tf_op jit(solution)/shard_map/ppermute | solution.py:55
  357.8 46.4 %collective-permute-start.58 = (bf16[272,768]{1,0:T(8,128)(2,1)S(1)}, bf16[272,768]{1,0:T(8,128)(2,1)S(1)}, u32[]{:S(2)}, u32[]{:S(2)}) collective-permute-start(bf16[272,768]{1,0:T(8,128)(2,1)S(1)} %bitcast.189), channel_id=1, source_target_pairs={{0,1},{1,0},{2,3},{3,2},{4,5},{5,4},{6,7},{7,6},{8,9},{9,8},{10,11... | collective-permute-start | bytes 1253384 | tf_op jit(solution)/shard_map/ppermute | solution.py:55
  359.1 118.0 %collective-permute-start.68 = (bf16[528,1024]{1,0:T(8,128)(2,1)S(1)}, bf16[528,1024]{1,0:T(8,128)(2,1)}, u32[]{:S(2)}, u32[]{:S(2)}) collective-permute-start(bf16[528,1024]{1,0:T(8,128)(2,1)S(1)} %bitcast.195), channel_id=1, source_target_pairs={{0,3},{1,2},{2,1},{3,0},{4,7},{5,6},{6,5},{7,4},{8,11},{9,10},{10,... | collective-permute-start | bytes 3244040 | tf_op jit(solution)/shard_map/ppermute | solution.py:55
  360.9 43.3 %collective-permute-start.59 = (bf16[272,768]{1,0:T(8,128)(2,1)}, bf16[272,768]{1,0:T(8,128)(2,1)}, u32[]{:S(2)}, u32[]{:S(2)}) collective-permute-start(bf16[272,768]{1,0:T(8,128)(2,1)} %bitcast.71.refs_2_), channel_id=1, source_target_pairs={{0,3},{1,2},{2,1},{3,0},{4,7},{5,6},{6,5},{7,4},{8,11},{9,10},{10,... | collective-permute-start | bytes 1253384 | tf_op jit(solution)/shard_map/ppermute | solution.py:55
  362.3 41.9 %collective-permute-start.60 = (bf16[272,768]{1,0:T(8,128)(2,1)}, bf16[272,768]{1,0:T(8,128)(2,1)}, u32[]{:S(2)}, u32[]{:S(2)}) collective-permute-start(bf16[272,768]{1,0:T(8,128)(2,1)} %bitcast.72.refs_3_), channel_id=1, source_target_pairs={{0,2},{1,3},{2,0},{3,1},{4,6},{5,7},{6,4},{7,5},{8,10},{9,11},{10,... | collective-permute-start | bytes 1253384 | tf_op jit(solution)/shard_map/ppermute | solution.py:55
  376.4 100.6 %collective-permute-start.67 = (bf16[528,1024]{1,0:T(8,128)(2,1)S(1)}, bf16[528,1024]{1,0:T(8,128)(2,1)}, u32[]{:S(2)}, u32[]{:S(2)}) collective-permute-start(bf16[528,1024]{1,0:T(8,128)(2,1)S(1)} %bitcast.193), channel_id=1, source_target_pairs={{0,1},{1,0},{2,3},{3,2},{4,5},{5,4},{6,7},{7,6},{8,9},{9,8},{10,11... | collective-permute-start | bytes 3244040 | tf_op jit(solution)/shard_map/ppermute | solution.py:55
  405.0 24.5 %collective-permute-start.61 = (bf16[416,1152]{1,0:T(8,128)(2,1)}, bf16[416,1152]{1,0:T(8,128)(2,1)}, u32[]{:S(2)}, u32[]{:S(2)}) collective-permute-start(bf16[416,1152]{1,0:T(8,128)(2,1)} %fence.15), channel_id=1, source_target_pairs={{0,1},{1,0},{2,3},{3,2},{4,5},{5,4},{6,7},{7,6},{8,9},{9,8},{10,11... | collective-permute-start | bytes 2875400 | tf_op jit(solution)/shard_map/ppermute | solution.py:55
  405.0 66.1 %collective-permute-start.62 = (bf16[416,1152]{1,0:T(8,128)(2,1)}, bf16[416,1152]{1,0:T(8,128)(2,1)}, u32[]{:S(2)}, u32[]{:S(2)}) collective-permute-start(bf16[416,1152]{1,0:T(8,128)(2,1)} %fence.16), channel_id=1, source_target_pairs={{0,3},{1,2},{2,1},{3,0},{4,7},{5,6},{6,5},{7,4},{8,11},{9,10},{10,... | collective-permute-start | bytes 2875400 | tf_op jit(solution)/shard_map/ppermute | solution.py:55
  407.0 64.1 %collective-permute-start.63 = (bf16[416,1152]{1,0:T(8,128)(2,1)}, bf16[416,1152]{1,0:T(8,128)(2,1)S(1)}, u32[]{:S(2)}, u32[]{:S(2)}) collective-permute-start(bf16[416,1152]{1,0:T(8,128)(2,1)} %fence.17), channel_id=1, source_target_pairs={{0,2},{1,3},{2,0},{3,1},{4,6},{5,7},{6,4},{7,5},{8,10},{9,11},{10,... | collective-permute-start | bytes 2875400 | tf_op jit(solution)/shard_map/ppermute | solution.py:55
  429.5 47.6 %collective-permute-start.69 = (bf16[528,1024]{1,0:T(8,128)(2,1)S(1)}, bf16[528,1024]{1,0:T(8,128)(2,1)S(1)}, u32[]{:S(2)}, u32[]{:S(2)}) collective-permute-start(bf16[528,1024]{1,0:T(8,128)(2,1)S(1)} %bitcast.191), channel_id=1, source_target_pairs={{0,2},{1,3},{2,0},{3,1},{4,6},{5,7},{6,4},{7,5},{8,10},{9,11},{10,... | collective-permute-start | bytes 3244040 | tf_op jit(solution)/shard_map/ppermute | solution.py:55
  (203 other events, 2286.5 us)
Sparse Core Ops, SparseCore 0:
  278.6 181.4 all-reduce.19

commit v4 on v3

--- a/solution.py
+++ b/solution.py
@@ -182,17 +182,19 @@
     return total_a, total_b
 
 
-def ring_scatter(pieces, swap, hold=None, sent=None):
-    n = pieces[0].shape[0]
-    hold = hold or {}
+def ring_scatter(pieces, swap, after, sent):
     near = [join(pieces[j], pieces[j ^ 4]) for j in range(4)]
-    near[1:] = [held(x, hold.get(1, ())) for x in near[1:]]
-    if sent is not None:
-        sent += near[1:]
+    near[1:] = [held(x, after) for x in near[1:]]
+    sent += near[1:]
     total = near[0].astype(f32)
     for j in (1, 3, 2):
         total = total + swap(near[j], j).astype(f32)
-    return total[:n] + swap(held(total[n:].astype(bf16), hold.get(2, ())), 4).astype(f32)
+    return total
+
+
+def pair_sum(total, swap, after=()):
+    half = total.shape[0] // 2
+    return total[:half] + swap(held(total[half:].astype(bf16), after), 4).astype(f32)
 
 
 def gather_direct(array, index, swap):
@@ -222,29 +224,49 @@
     return mine + swap(theirs.astype(bf16), 4).astype(f32)
 
 
-def assemble_kernel(cuts, sizes, place_ref, *refs):
-    arrays, outs = refs[:18], refs[18:]
-    index, core = place_ref[0], place_ref[1]
+def place_kernel(cuts, sizes, index_ref, *refs):
+    arrays, outs = refs[:9], refs[len(refs) - len(cuts) :]
     for (k, h), (i, at) in where_parts(0, 9, sizes).items():
-        for out, (which, first, n, column, width) in zip(outs, cuts):
+        for out, (which, first, n, width) in zip(outs, cuts):
             if which == h:
-                rows, columns = slice(at + first, at + first + n), slice(column, column + width)
-                out[index ^ k, core] = arrays[i][rows, :, columns]
-                out[index ^ k, 1 - core] = arrays[9 + i][rows, :, columns]
-
-
-def assemble(mine, theirs, na, cuts, index, core):
-    rows, columns = mine[0].shape
-    eights = [x.reshape(x.shape[0] // 8, 8, columns) for x in (*mine, *theirs)]
+                rows = slice(at + first, at + first + n)
+                out[index_ref[0] ^ k] = arrays[i][rows, :, :width]
+
+
+def place(arrays, na, cuts, index, after):
+    rows, columns = arrays[0].shape
+    eights = [x.reshape(x.shape[0] // 8, 8, columns) for x in arrays]
     sizes = (na // 8, (rows - na) // 8)
+    return pl.pallas_call(
+        functools.partial(place_kernel, cuts, sizes),
+        in_specs=[SMEM] + [VMEM] * 9 + [ANY] * len(after),
+        out_specs=[VMEM] * len(cuts),
+        out_shape=[jax.ShapeDtypeStruct((8, n, 8, width), bf16) for _, _, n, width in cuts],
+        compiler_params=pltpu.CompilerParams(vmem_limit_bytes=24 * 1024 * 1024),
+        name="place",
+    )(index.reshape(1), *eights, *after)
+
+
+def interleave_kernel(cuts, core_ref, *refs):
+    count = (len(refs) - len(cuts)) // 2
+    mine, theirs, outs = refs[:count], refs[count : 2 * count], refs[2 * count :]
+    core = core_ref[0]
+    for out, (which, first, n, column, width) in zip(outs, cuts):
+        columns = slice(column, column + width)
+        for i in range(8):
+            out[i, core] = mine[which][i, first : first + n, :, columns]
+            out[i, 1 - core] = theirs[which][i, first : first + n, :, columns]
+
+
+def interleave(mine, theirs, cuts, core):
     outs = pl.pallas_call(
-        functools.partial(assemble_kernel, cuts, sizes),
-        in_specs=[SMEM] + [VMEM] * 18,
+        functools.partial(interleave_kernel, cuts),
+        in_specs=[SMEM] + [VMEM] * (2 * len(mine)),
         out_specs=[VMEM] * len(cuts),
         out_shape=[jax.ShapeDtypeStruct((8, 2, n, 8, width), bf16) for _, _, n, _, width in cuts],
         compiler_params=pltpu.CompilerParams(vmem_limit_bytes=40 * 1024 * 1024),
-        name="assemble",
-    )(jnp.stack([index, core]), *eights)
+        name="interleave",
+    )(core.reshape(1), *mine, *theirs)
     return [x.reshape(-1, x.shape[-1]) for x in outs]
 
 
@@ -587,13 +609,15 @@
         extra += half * ACT_PAD
 
 
-def attend_back(*given):
+def attend_back(*given, after):
     hidden_d, hidden_a = given[5:7]
     width_d, width_a = hidden_d.shape[1], hidden_a.shape[1]
     shape = jax.ShapeDtypeStruct
     stacked = HEADS * BLOCK
     outs = pl.pallas_call(
         attend_back_kernel,
+        in_specs=[VMEM] * len(given) + [ANY] * len(after),
+        out_specs=[VMEM] * (6 + len(PARTS)),
         out_shape=[
             shape((PREF, width_d), f32),
             shape((ACT_PAD, width_a), f32),
@@ -608,7 +632,7 @@
             flops=2 * BLOCK * HEADS * HD, bytes_accessed=4 * BLOCK, transcendentals=stacked
         ),
         name="attend_back",
-    )(*given)
+    )(*given, *after)
     kv_deltas = dict(zip(PARTS, outs[6:]))
     pa = {k: kv_deltas[k, 0] for k in range(8)}
     pb = {k: kv_deltas[k, 1] for k in range(8)}
@@ -638,7 +662,7 @@
                 out[base + row : base + row + n, :, columns] = total.astype(bf16)
 
 
-def sum_weights(grads, cuts, columns, place, sent, got, after, before_last):
+def sum_weights(grads, cuts, columns, place, sent, after):
     views = [g.reshape(2, 8, -1, 8, g.shape[1]) for g in grads]
     eights = max(row + n for row, n, _, _, _ in cuts)
     params = pltpu.CompilerParams(vmem_limit_bytes=44 * 1024 * 1024)
@@ -666,11 +690,9 @@
     sent += near[1:]
     total = near[0].astype(f32)
     for step, x in zip((1, 3, 2), near[1:]):
-        got.append(mp_swap(x, step))
-        total = total + got[-1].astype(f32)
+        total = total + mp_swap(x, step).astype(f32)
     half = 8 * eights
-    last = held(total[half:].astype(bf16), before_last)
-    return (total[:half] + mp_swap(last, 4).astype(f32)).astype(bf16)
+    return (total[:half] + mp_swap(total[half:].astype(bf16), 4).astype(f32)).astype(bf16)
 
 
 def pad_action(rows):
@@ -846,31 +868,25 @@
 
     own_action = pad_action(action_input[0])
     own_block = block_of(prefix_input[0], own_action)
-    own_block = fence(own_block, near)
-    x_rows = relay_gather(own_block, HALF_A, mp_swap)
-    hold = {2: x_rows[1:4], 3: x_rows[4:7]}
-    mine = relay_gather(join(pack_a, pack_b), pack_a.shape[0], yz_swap, note("weights"), hold)
+    pack = join(pack_a, pack_b)
+    x_hold = {2: (pack,)}
+    x_rows = relay_gather(own_block, HALF_A, mp_swap, note("rows"), x_hold)
+    hold = {1: x_rows[1:4], 3: x_rows[4:7]}
+    pieces = relay_gather(pack, pack_a.shape[0], yz_swap, note("weights"), hold)
+    cuts = ((0, 16, 8, 768), (1, 17, 9, 640), (0, 0, 16, 1024), (1, 0, 17, 1024))
+    mine = place(pieces, pack_a.shape[0], cuts, yz, arrived["rows", "sends", 3])
     theirs = [core_swap(x) for x in mine]
-    cuts = (
-        (0, 0, 8, 0, 1024),
-        (0, 8, 8, 0, 1024),
-        (0, 16, 8, 0, 512),
-        (0, 16, 8, 512, 128),
-        (0, 16, 8, 640, 128),
-        (1, 0, 9, 0, 1024),
-        (1, 9, 8, 0, 1024),
-        (1, 17, 9, 0, 512),
-        (1, 17, 9, 512, 128),
-    )
-    wq_a, wo_a, wkv_a, gains_a, wo_e, wq_d, wo_m, wkv_d, gains_d = assemble(
-        mine, theirs, pack_a.shape[0], cuts, yz, core
-    )
+    cuts = ((0, 0, 8, 0, 512), (0, 0, 8, 512, 128), (0, 0, 8, 640, 128))
+    cuts += ((1, 0, 9, 0, 512), (1, 0, 9, 512, 128))
+    wkv_a, gains_a, wo_e, wkv_d, gains_d = interleave(mine[:2], theirs[:2], cuts, core)
+    cuts = ((0, 0, 8, 0, 1024), (0, 8, 8, 0, 1024), (1, 0, 9, 0, 1024), (1, 9, 8, 0, 1024))
+    wq_a, wo_a, wq_d, wo_m = interleave(mine[2:], theirs[2:], cuts, core)
     seeds = relay_gather(
         seed_block,
         HALF_A,
         mp_swap,
         note("seeds"),
-        {1: arrived["weights", "sends", 3][:1]},
+        {1: pieces[7:9]},
     )
 
     normed_d, normed_a, keys, values = keys_of(
@@ -881,7 +897,7 @@
         wkv_a,
         key_cos,
         key_sin,
-        arrived["seeds", "sends", 2],
+        arrived["seeds", "sends", 1],
     )
     x_d, x_a = prefix_input[0].astype(f32), own_action.astype(f32)
     rms_d, rms_a = inverse_rms(x_d), inverse_rms(x_a)
@@ -903,7 +919,7 @@
         key_codes,
         keys,
         values,
-        after=arrived["seeds", "sends", 3],
+        after=arrived["seeds", "sends", 2],
     )
 
     slots = action_gate.shape[2]
@@ -929,7 +945,7 @@
         first, blocks, base = {1: (0, (0,), 3), 2: (1, (1, 3, 4), 0)}[stage]
         return run(arrays, first, blocks, base, sends)
 
-    second_block = fence(second_block, seeds[8])
+    second_block = fence(second_block, *arrived["seeds", "sends", 3])
     arrays = relay_gather(second_block, HALF_A, mp_swap, feed_during)
     run(arrays[4:], 4, (2, 5, 7, 6), 4, ())
     product_d, deltas_d, rows_d, seeds_d, product_a, deltas_a, rows_a, seeds_a = kept
@@ -955,7 +971,19 @@
 
     pa = {k: v[0] for k, v in results.items()}
     pb = {k: v[1] for k, v in results.items()}
-    delta_pieces = relay_scatter(pa, pb, mp_swap)
+    delta_sent = {}
+    delta_pieces = relay_scatter(pa, pb, mp_swap, sent=delta_sent)
+
+    partial_d = dot(product_d[:, :hidden], prefix_down).astype(bf16)
+    partial_a = dot(product_a, action_down[0]).astype(bf16)
+    out = []
+    for k in range(8):
+        i = (1, 3, 4, 0, 2, 5, 7, 6).index(k)
+        mine = partial_a[i * ACT_PAD : (i + 1) * ACT_PAD]
+        out.append(block_of(partial_d[i * PREF : (i + 1) * PREF], mine))
+    out_sent = []
+    out = ring_scatter(out, mp_swap, delta_sent[3], out_sent)
+
     (hidden_delta_d, hidden_delta_a, low, terms_d, terms_a, query_delta), pa, pb = attend_back(
         *delta_pieces,
         hidden_d,
@@ -977,6 +1005,7 @@
         key_codes,
         keys,
         values,
+        after=(),
     )
     low_d, low_a = low[:PREF], low[PREF:, :DA]
 
@@ -1006,16 +1035,16 @@
     out_grad_a = t_dot(turned_context[PREF:], low_a).astype(bf16)
     q_grad_d = t_dot(turned_d[:PREF], query_delta[:PREF]).astype(bf16)
     q_grad_a = t_dot(turned_a[:ACT_PAD], query_delta[PREF:]).astype(bf16)
-    place = jnp.stack([mp, core])
+    here = jnp.stack([mp, core])
     cuts = (
         (0, 8, 0, 0, 1024),
         (8, 8, 0, 0, 1024),
         (16, 9, 0, 0, 1024),
         (25, 8, 0, 0, 1024),
     )
-    qo_sent, kv_sent, kv_got = [], [], []
+    qo_sent, kv_sent = [], []
     qo_grads = (q_grad_a, out_grad_a, q_grad_d, out_grad_d)
-    qo = sum_weights(qo_grads, cuts, 1024, place, qo_sent, [], (), grads[:1])
+    qo = sum_weights(qo_grads, cuts, 1024, here, qo_sent, ())
     kv_grad_d = t_dot(turned_d, kv_rows_d).astype(bf16)
     kv_grad_a = t_dot(turned_a, kv_rows_a).astype(bf16)
     cuts = (
@@ -1032,7 +1061,7 @@
         kv_grad_d,
         second_term_d.astype(bf16),
     )
-    kv = sum_weights(kv_grads, cuts, 768, place, kv_sent, kv_got, qo_sent, grads[:1])
+    kv = sum_weights(kv_grads, cuts, 768, here, kv_sent, qo_sent)
     kv_a, kv_d = kv[:64], kv[64:, :640]
     qo_a, qo_b = qo[:128], qo[128:]
     kv_other = mp_swap(held(kv_part[BLOCK:].astype(bf16), tuple(kv_sent)), 4)
@@ -1041,15 +1070,7 @@
         [unrotate(kv_sum[:, :HD], own_cos, own_sin), kv_sum[:, HD:]], axis=1
     ).astype(bf16)
 
-    product_d = fence(product_d, kv_sent[0])
-    partial_d = dot(product_d[:, :hidden], prefix_down).astype(bf16)
-    partial_a = dot(product_a, action_down[0]).astype(bf16)
-    out = []
-    for k in range(8):
-        i = (1, 3, 4, 0, 2, 5, 7, 6).index(k)
-        mine = partial_a[i * ACT_PAD : (i + 1) * ACT_PAD]
-        out.append(block_of(partial_d[i * PREF : (i + 1) * PREF], mine))
-    out = ring_scatter(out, mp_swap, {1: tuple(kv_got)})
+    out = pair_sum(out, mp_swap, (*qo_sent, *kv_sent))
     prefix_output = (hidden_d + out[:PREF]).astype(bf16)[None]
     action_output = (hidden_a + out[PREF:, :DA])[:ACT].astype(bf16)[None]
 
@@ -1065,7 +1086,7 @@
         ],
         axis=2,
     )
-    last = scatter_direct(fence(last, *finished), yz, yz_swap)
+    last = scatter_direct(fence(last, grads[0]), yz, yz_swap)
     ninth = last[:, last.shape[1] - 256 : last.shape[1] - 48].reshape(1, wide)
     grads_d = join(last[:, :wide], ninth)
     grads_a = last[:, wide : last.shape[1] - 256]

time: 563 us -> 605 us (1.075); the launches traced: 552 us -> 601 us
  waiting for transfers between devices: 151 us -> 203 us
  other arithmetic: 77.8 us -> 67.4 us
  starting transfers between devices: 96.8 us -> 107 us
    ppermute x52, waiting for transfers between devices: 130 us -> 182 us  [mp_swap(): return lax.ppermute(array, 'mp', [(i, i ^ step) for i in range(N_MP)])]
    ppermute x23 -> x18, starting transfers between devices: 25.8 us -> 30.2 us  [dp_swap(): return lax.ppermute(array, 'dp', [(i, i ^ step) for i in range(16)])]
    pallas_call x2 -> x4, Pallas kernels: 20.9 us -> 23.9 us  [the longest x1 12.7 us: attend_back(): pl.pallas_call(attend_back_kernel, in_specs=[VMEM] * len(given) + [ANY] *...]
    unnamed x335 -> x415, local copies, waits for them, and re-layouts: 33.2 us -> 35.4 us
    ppermute x23 -> x18, waiting for transfers between devices: 20.4 us -> 21 us  [dp_swap(): return lax.ppermute(array, 'dp', [(i, i ^ step) for i in range(16)])]
  transfers between devices with their start and end apart: 76 -> 71, of which waited for: 26 -> 31; matrix products, arithmetic and copies ran while one was open for 23% -> 20% of each run, Pallas kernels for 16% -> 13%
where the time goes in v4:
time: 605 us; the launch traced here: 601 us
  waiting for transfers between devices  203 us (34%)
  starting transfers between devices  107 us (18%)
  Pallas kernels  106 us (18%)
  other arithmetic  67.4 us (11%)
  local copies, waits for them, and re-layouts  51.1 us (8%)
  matrix products  49.6 us (8%)
  between operations  17.8 us (3%)
    ppermute x52, waiting for transfers between devices, mp_swap(): return lax.ppermute(array, 'mp', [(i, i ^ step) for i in range(N_MP)])  182 us
    ppermute x52, starting transfers between devices, mp_swap(): return lax.ppermute(array, 'mp', [(i, i ^ step) for i in range(N_MP)])  76.5 us
    pallas_call x3, Pallas kernels, feed(): pl.pallas_call(functools.partial(feed_kernel, layout), grid=(1,), in_spec...  44.6 us
    unnamed x415, local copies, waits for them, and re-layouts  35.4 us
    dot_general x12, matrix products, t_dot(): lax.dot_general(a, b, (((0,), (0,)), ((), ())), preferred_element_type=f32)  33.1 us
    ppermute x18, starting transfers between devices, dp_swap(): return lax.ppermute(array, 'dp', [(i, i ^ step) for i in range(16)])  30.2 us
    ppermute x18, waiting for transfers between devices, dp_swap(): return lax.ppermute(array, 'dp', [(i, i ^ step) for i in range(16)])  21 us
    pallas_call x1, Pallas kernels, attend_back(): pl.pallas_call(attend_back_kernel, in_specs=[VMEM] * len(given) + [ANY] *...  12.7 us
  transfers between devices with their start and end apart: 71, of which 31 were waited for; matrix products, arithmetic and copies ran while one was open for 20% of the time, Pallas kernels for 13%

profile of v4, /device:TPU:0, one launch (start us, length us, event | category | flops | bytes accessed | tf_op | source)
XLA Modules:
  0.0 600.9 jit_solution(8877506267180535655)
XLA Ops:
  21.1 4.4 collective-permute-done.3
  28.5 7.5 %collective-permute-done.4 = bf16[2,8,5760]{2,1,0:T(8,128)(2,1)S(1)} collective-permute-done((bf16[2,8,5760]{2,1,0:T(8,128)(2,1)S(1)}, bf16[2,8,5760]{2,1,0:T(8,128)(2,1)S(1)}, u32[]{:S(2)}, u32[]{:S(2)}) %collective-permute-start.4) | collective-permute-done | bytes 184352 | tf_op jit(solution)/shard_map/ppermute | solution.py:55
  36.5 6.3 %collective-permute-done.5 = bf16[2,8,5760]{2,1,0:T(8,128)(2,1)S(1)} collective-permute-done((bf16[2,8,5760]{2,1,0:T(8,128)(2,1)S(1)}, bf16[2,8,5760]{2,1,0:T(8,128)(2,1)S(1)}, u32[]{:S(2)}, u32[]{:S(2)}) %collective-permute-start.5) | collective-permute-done | bytes 184352 | tf_op jit(solution)/shard_map/ppermute | solution.py:55
  60.1 14.0 %collective-permute-done.14.refs_2_ = bf16[400,1024]{1,0:T(8,128)(2,1)S(1)} collective-permute-done((bf16[400,1024]{1,0:T(8,128)(2,1)}, bf16[400,1024]{1,0:T(8,128)(2,1)S(1)}, u32[]{:S(2)}, u32[]{:S(2)}) %collective-permute-start.14) | collective-permute-done | bytes 819232 | tf_op jit(solution)/shard_map/ppermute | solution.py:59
  88.5 4.8 collective-permute-done.8.refs_1_.refs_3_.refs_5_
  125.3 8.5 %collective-permute-done.26.refs_2_.refs_5_ = bf16[208,1152]{1,0:T(8,128)(2,1)S(1)} collective-permute-done((bf16[208,1152]{1,0:T(8,128)(2,1)}, bf16[208,1152]{1,0:T(8,128)(2,1)S(1)}, u32[]{:S(2)}, u32[]{:S(2)}) %collective-permute-start.26) | collective-permute-done | bytes 479264 | tf_op jit(solution)/shard_map/ppermute | solution.py:55
  139.3 8.9 %collective-permute-done.24.refs_0_.refs_3_ = bf16[208,1152]{1,0:T(8,128)(2,1)S(1)} collective-permute-done((bf16[208,1152]{1,0:T(8,128)(2,1)}, bf16[208,1152]{1,0:T(8,128)(2,1)S(1)}, u32[]{:S(2)}, u32[]{:S(2)}) %collective-permute-start.24) | collective-permute-done | bytes 479264 | tf_op jit(solution)/shard_map/ppermute | solution.py:55
  149.4 4.6 collective-permute-done.10.refs_7_
  167.3 5.9 keys_of.1
  176.5 5.5 interleave.3
  186.0 11.3 %attend.1 = (bf16[832,256]{1,0:T(8,128)(2,1)S(1)}, bf16[208,1024]{1,0:T(8,128)(2,1)S(1)}, f32[832,1]{1,0:T(8,128)S(1)}, f32[832,1]{1,0:T(8,128)S(1)}, f32[192,11...) custom-call(bf16[384,1152]{1,0:T(8,128)(2,1)} %get-tuple-element.152.refs_0_, ...), custom_call_target="tpu_custom_call" | custom-call | flops 2399141888 | bytes 20971520 | tf_op jit(solution)/shard_map/attend/pallas_call | solution.py:528
  205.4 12.5 %collective-permute-start.39 = (bf16[112,1152]{1,0:T(8,128)(2,1)S(1)}, bf16[112,1152]{1,0:T(8,128)(2,1)S(1)}, u32[]{:S(2)}, u32[]{:S(2)}) collective-permute-start(bf16[112,1152]{1,0:T(8,128)(2,1)S(1)} %copy-done.92), channel_id=1, source_target_pairs={{0,3},{1,2},{2,1},{3,0},{4,7},{5,6},{6,5},{7,4},{8,11},{9,10},{10,... | collective-permute-start | bytes 774152 | tf_op jit(solution)/shard_map/ppermute | solution.py:55
  217.9 10.0 %feed.3 = (bf16[1536,896]{1,0:T(8,128)(2,1)}, bf16[1536,1792]{1,0:T(8,128)(2,1)}, bf16[1536,1152]{1,0:T(8,128)(2,1)}, bf16[1536,1152]{1,0:T(8,128)(2,1)}, bf16[1...) custom-call(bf16[208,1152]{1,0:T(8,128)(2,1)S(1)} %copy-done.29, ...), custom_call_target="tpu_custom_call" | custom-call | flops 2078801920 | bytes 12263424 | tf_op jit(solution)/shard_map/feed/pallas_call | solution.py:456
  232.7 15.5 %feed.4 = (bf16[1536,896]{1,0:T(8,128)(2,1)}, bf16[1536,1792]{1,0:T(8,128)(2,1)}, bf16[1536,1152]{1,0:T(8,128)(2,1)}, bf16[1536,1152]{1,0:T(8,128)(2,1)}, bf16[1...) custom-call(bf16[208,1152]{1,0:T(8,128)(2,1)S(1)} %collective-permut, ...), custom_call_target="tpu_custom_call", output_to_operand_aliasing={{0}: (13, {}), {1}: (14, {}), {2}: (15, {}), {3}: (16, {}),... | custom-call | flops 6236405760 | bytes 12263424 | tf_op jit(solution)/shard_map/feed/pallas_call | solution.py:456
  259.9 19.0 %feed.5 = (bf16[1536,896]{1,0:T(8,128)(2,1)}, bf16[1536,1792]{1,0:T(8,128)(2,1)}, bf16[1536,1152]{1,0:T(8,128)(2,1)}, bf16[1536,1152]{1,0:T(8,128)(2,1)}, bf16[1...) custom-call(bf16[192,1152]{1,0:T(8,128)(2,1)S(1)} %collective-permut, ...), custom_call_target="tpu_custom_call", output_to_operand_aliasing={{0}: (17, {}), {1}: (18, {}), {2}: (19, {}), {3}: (20, {}),... | custom-call | flops 8315207680 | bytes 12263424 | tf_op jit(solution)/shard_map/feed/pallas_call | solution.py:456
  283.4 8.1 %convolution_convert_fusion.5 = bf16[896,1152]{1,0:T(8,128)(2,1)} fusion(bf16[1536,896]{1,0:T(8,128)(2,1)} %get-tuple-element.193, bf16[1536,1152]{1,0:T(8,128)(2,1)} %get-tuple-element.246), kind=kOutput, calls=%fused_computation.14 | convolution fusion | flops 3171926016 | bytes 8355840 | tf_op jit(solution)/shard_map/dot_general | solution.py:728
  291.5 9.0 %convolution_convert_fusion = bf16[1792,1152]{1,0:T(8,128)(2,1)} fusion(bf16[1536,1792]{1,0:T(8,128)(2,1)S(1)} %bitcast.216, bf16[1536,1152]{1,0:T(8,128)(2,1)S(1)} %copy-done.123), kind=kOutput, calls=%fused_computation | convolution fusion | flops 6343852032 | bytes 13172736 | tf_op jit(solution)/shard_map/dot_general | solution.py:728
  311.0 5.9 convolution_convert_fusion.1
  334.4 30.1 %collective-permute-done.50.refs_4_ = bf16[208,1152]{1,0:T(8,128)(2,1)S(1)} collective-permute-done((bf16[208,1152]{1,0:T(8,128)(2,1)S(1)}, bf16[208,1152]{1,0:T(8,128)(2,1)S(1)}, u32[]{:S(2)}, u32[]{:S(2)}) %collective-permute-start.50) | collective-permute-done | bytes 479264 | tf_op jit(solution)/shard_map/ppermute | solution.py:55
  365.2 12.7 %attend_back.1 = (f32[192,1152]{1,0:T(8,128)}, f32[16,1024]{1,0:T(8,128)S(1)}, bf16[208,1152]{1,0:T(8,128)(2,1)}, bf16[192,1152]{1,0:T(8,128)(2,1)}, bf16[16,102...) custom-call(bf16[96,1152]{1,0:T(8,128)(2,1)S(1)} %get-tuple-element., ...), custom_call_target="tpu_custom_call" | custom-call | flops 425984 | bytes 832 | tf_op jit(solution)/shard_map/attend_back/pallas_call | solution.py:617
  390.2 4.4 collective-permute-start.53
  403.8 8.8 %collective-permute-done.53 = bf16[416,512]{1,0:T(8,128)(2,1)} collective-permute-done((bf16[416,512]{1,0:T(8,128)(2,1)}, bf16[416,512]{1,0:T(8,128)(2,1)}, u32[]{:S(2)}, u32[]{:S(2)}) %collective-permute-start.53) | collective-permute-done | bytes 426016 | tf_op jit(solution)/shard_map/ppermute | solution.py:55
  430.9 5.0 near.2
  446.5 22.1 %collective-permute-done.46 = bf16[416,1152]{1,0:T(8,128)(2,1)} collective-permute-done((bf16[416,1152]{1,0:T(8,128)(2,1)}, bf16[416,1152]{1,0:T(8,128)(2,1)}, u32[]{:S(2)}, u32[]{:S(2)}) %collective-permute-start.46) | collective-permute-done | bytes 958496 | tf_op jit(solution)/shard_map/ppermute | solution.py:55
  478.6 5.3 collective-permute-done.57
  503.3 14.0 %collective-permute-done.63 = bf16[528,1024]{1,0:T(8,128)(2,1)} collective-permute-done((bf16[528,1024]{1,0:T(8,128)(2,1)S(1)}, bf16[528,1024]{1,0:T(8,128)(2,1)}, u32[]{:S(2)}, u32[]{:S(2)}) %collective-permute-start.63) | collective-permute-done | bytes 1081376 | tf_op jit(solution)/shard_map/ppermute | solution.py:55
  517.3 4.3 collective-permute-done.62
  521.7 20.7 %collective-permute-done.64 = bf16[528,1024]{1,0:T(8,128)(2,1)S(1)} collective-permute-done((bf16[528,1024]{1,0:T(8,128)(2,1)S(1)}, bf16[528,1024]{1,0:T(8,128)(2,1)S(1)}, u32[]{:S(2)}, u32[]{:S(2)}) %collective-permute-start.64) | collective-permute-done | bytes 1081376 | tf_op jit(solution)/shard_map/ppermute | solution.py:55
  546.9 8.3 %collective-permute-done.65 = bf16[264,1024]{1,0:T(8,128)(2,1)S(1)} collective-permute-done((bf16[264,1024]{1,0:T(8,128)(2,1)S(1)}, bf16[264,1024]{1,0:T(8,128)(2,1)S(1)}, u32[]{:S(2)}, u32[]{:S(2)}) %collective-permute-start.65) | collective-permute-done | bytes 540704 | tf_op jit(solution)/shard_map/ppermute | solution.py:55
  556.8 5.9 convert_bitcast_fusion
  574.8 6.1 %collective-permute-start.69 = (bf16[8,5760]{1,0:T(8,128)(2,1)S(1)}, bf16[8,5760]{1,0:T(8,128)(2,1)S(1)}, u32[]{:S(2)}, u32[]{:S(2)}) collective-permute-start(bf16[8,5760]{1,0:T(8,128)(2,1)S(1)} %fusion.97), channel_id=1, source_target_pairs={{0,64},{8,72},{16,80},{24,88},{32,96},{40,104},{48,112},{56,120},{... | collective-permute-start | bytes 276488 | tf_op jit(solution)/shard_map/ppermute | solution.py:59
  580.8 4.4 fusion.13
  (709 shorter events, 269.3 us)
Async XLA Ops:
  7.2 549.6 %all-reduce.20.cloned.1.call-start = ((), (), s32[]{:S(2)}) async-start(), calls=%async_computation | async-start | bytes 24969216 | tf_op jit(solution)/shard_map/psum | solution.py:962
  9.7 39.6 %collective-permute-start.2 = (bf16[208,1152]{1,0:T(8,128)(2,1)S(1)}, bf16[208,1152]{1,0:T(8,128)(2,1)S(1)}, u32[]{:S(2)}, u32[]{:S(2)}) collective-permute-start(bf16[208,1152]{1,0:T(8,128)(2,1)S(1)} %fusion.56.refs_0_), channel_id=1, source_target_pairs={{0,4},{1,5},{2,6},{3,7},{4,0},{5,1},{6,2},{7,3},{8,12},{9,13},{10,... | collective-permute-start | bytes 1437704 | tf_op jit(solution)/shard_map/ppermute | solution.py:55
  11.8 37.5 %collective-permute-start.1 = (bf16[208,1152]{1,0:T(8,128)(2,1)S(1)}, bf16[208,1152]{1,0:T(8,128)(2,1)S(1)}, u32[]{:S(2)}, u32[]{:S(2)}) collective-permute-start(bf16[208,1152]{1,0:T(8,128)(2,1)S(1)} %fusion.56.refs_0_), channel_id=1, source_target_pairs={{0,3},{1,2},{2,1},{3,0},{4,7},{5,6},{6,5},{7,4},{8,11},{9,10},{10,... | collective-permute-start | bytes 1437704 | tf_op jit(solution)/shard_map/ppermute | solution.py:55
  14.5 34.8 %collective-permute-start = (bf16[208,1152]{1,0:T(8,128)(2,1)S(1)}, bf16[208,1152]{1,0:T(8,128)(2,1)S(1)}, u32[]{:S(2)}, u32[]{:S(2)}) collective-permute-start(bf16[208,1152]{1,0:T(8,128)(2,1)S(1)} %fusion.56.refs_0_), channel_id=1, source_target_pairs={{0,1},{1,0},{2,3},{3,2},{4,5},{5,4},{6,7},{7,6},{8,9},{9,8},{10,11... | collective-permute-start | bytes 1437704 | tf_op jit(solution)/shard_map/ppermute | solution.py:55
  51.2 23.0 %collective-permute-start.14 = (bf16[400,1024]{1,0:T(8,128)(2,1)}, bf16[400,1024]{1,0:T(8,128)(2,1)S(1)}, u32[]{:S(2)}, u32[]{:S(2)}) collective-permute-start(bf16[400,1024]{1,0:T(8,128)(2,1)} %fence.9), channel_id=1, source_target_pairs={{0,64},{8,72},{16,80},{24,88},{32,96},{40,104},{48,112},{56,120},{... | collective-permute-start | bytes 2457608 | tf_op jit(solution)/shard_map/ppermute | solution.py:59
  58.5 26.3 %collective-permute-start.7 = (bf16[192,1152]{1,0:T(8,128)(2,1)}, bf16[192,1152]{1,0:T(8,128)(2,1)S(1)}, u32[]{:S(2)}, u32[]{:S(2)}) collective-permute-start(bf16[192,1152]{1,0:T(8,128)(2,1)} %get-tuple-element.136), channel_id=1, source_target_pairs={{0,4},{1,5},{2,6},{3,7},{4,0},{5,1},{6,2},{7,3},{8,12},{9,13},{10,... | collective-permute-start | bytes 1327112 | tf_op jit(solution)/shard_map/ppermute | solution.py:55
  84.8 23.6 %collective-permute-start.17 = (bf16[416,1024]{1,0:T(8,128)(2,1)}, bf16[416,1024]{1,0:T(8,128)(2,1)}, u32[]{:S(2)}, u32[]{:S(2)}) collective-permute-start(bf16[416,1024]{1,0:T(8,128)(2,1)} %get-tuple-element.143), channel_id=1, source_target_pairs={{0,48},{8,56},{16,32},{24,40},{32,16},{40,24},{48,0},{56,8},{64,11... | collective-permute-start | bytes 2555912 | tf_op jit(solution)/shard_map/ppermute | solution.py:59
  116.8 59.6 %collective-permute-start.23 = (bf16[8,17,8,1024]{3,2,1,0:T(8,128)(2,1)}, bf16[8,17,8,1024]{3,2,1,0:T(8,128)(2,1)}, u32[]{:S(2)}, u32[]{:S(2)}) collective-permute-start(bf16[8,17,8,1024]{3,2,1,0:T(8,128)(2,1)} %get-tuple-element.155.refs_1_), channel_id=1, source_target_pairs={{0,8},{8,0},{16,24},{24,16},{32,40},{40,32},{48,56},{56,48},{64,72... | collective-permute-start | bytes 6684680 | tf_op jit(solution)/shard_map/ppermute | solution.py:59
  117.5 59.0 %collective-permute-start.22 = (bf16[8,16,8,1024]{3,2,1,0:T(8,128)(2,1)}, bf16[8,16,8,1024]{3,2,1,0:T(8,128)(2,1)}, u32[]{:S(2)}, u32[]{:S(2)}) collective-permute-start(bf16[8,16,8,1024]{3,2,1,0:T(8,128)(2,1)} %get-tuple-element.154.refs_0_), channel_id=1, source_target_pairs={{0,8},{8,0},{16,24},{24,16},{32,40},{40,32},{48,56},{56,48},{64,72... | collective-permute-start | bytes 6291464 | tf_op jit(solution)/shard_map/ppermute | solution.py:59
  125.2 29.8 %collective-permute-start.21 = (bf16[8,9,8,640]{3,2,1,0:T(8,128)(2,1)}, bf16[8,9,8,640]{3,2,1,0:T(8,128)(2,1)}, u32[]{:S(2)}, u32[]{:S(2)}) collective-permute-start(bf16[8,9,8,640]{3,2,1,0:T(8,128)(2,1)} %copy-done.74), channel_id=1, source_target_pairs={{0,8},{8,0},{16,24},{24,16},{32,40},{40,32},{48,56},{56,48},{64,72... | collective-permute-start | bytes 2211848 | tf_op jit(solution)/shard_map/ppermute | solution.py:59
  166.2 85.6 %collective-permute-start.37 = (bf16[224,1152]{1,0:T(8,128)(2,1)}, bf16[224,1152]{1,0:T(8,128)(2,1)}, u32[]{:S(2)}, u32[]{:S(2)}) collective-permute-start(bf16[224,1152]{1,0:T(8,128)(2,1)} %get-tuple-element.165.refs_19_), channel_id=1, source_target_pairs={{0,3},{1,2},{2,1},{3,0},{4,7},{5,6},{6,5},{7,4},{8,11},{9,10},{10,... | collective-permute-start | bytes 1548296 | tf_op jit(solution)/shard_map/ppermute | solution.py:55
  199.6 29.2 %collective-permute-start.31 = (bf16[208,1152]{1,0:T(8,128)(2,1)}, bf16[208,1152]{1,0:T(8,128)(2,1)S(1)}, u32[]{:S(2)}, u32[]{:S(2)}) collective-permute-start(bf16[208,1152]{1,0:T(8,128)(2,1)} %fence.11.refs_0_.refs_9_), channel_id=1, source_target_pairs={{0,4},{1,5},{2,6},{3,7},{4,0},{5,1},{6,2},{7,3},{8,12},{9,13},{10,... | collective-permute-start | bytes 1437704 | tf_op jit(solution)/shard_map/ppermute | solution.py:55
  200.8 28.0 %collective-permute-start.30 = (bf16[208,1152]{1,0:T(8,128)(2,1)}, bf16[208,1152]{1,0:T(8,128)(2,1)S(1)}, u32[]{:S(2)}, u32[]{:S(2)}) collective-permute-start(bf16[208,1152]{1,0:T(8,128)(2,1)} %fence.11.refs_0_.refs_9_), channel_id=1, source_target_pairs={{0,3},{1,2},{2,1},{3,0},{4,7},{5,6},{6,5},{7,4},{8,11},{9,10},{10,... | collective-permute-start | bytes 1437704 | tf_op jit(solution)/shard_map/ppermute | solution.py:55
  202.8 25.9 %collective-permute-start.29 = (bf16[208,1152]{1,0:T(8,128)(2,1)}, bf16[208,1152]{1,0:T(8,128)(2,1)S(1)}, u32[]{:S(2)}, u32[]{:S(2)}) collective-permute-start(bf16[208,1152]{1,0:T(8,128)(2,1)} %fence.11.refs_0_.refs_9_), channel_id=1, source_target_pairs={{0,1},{1,0},{2,3},{3,2},{4,5},{5,4},{6,7},{7,6},{8,9},{9,8},{10,11... | collective-permute-start | bytes 1437704 | tf_op jit(solution)/shard_map/ppermute | solution.py:55
  205.4 52.1 %collective-permute-start.39 = (bf16[112,1152]{1,0:T(8,128)(2,1)S(1)}, bf16[112,1152]{1,0:T(8,128)(2,1)S(1)}, u32[]{:S(2)}, u32[]{:S(2)}) collective-permute-start(bf16[112,1152]{1,0:T(8,128)(2,1)S(1)} %copy-done.92), channel_id=1, source_target_pairs={{0,3},{1,2},{2,1},{3,0},{4,7},{5,6},{6,5},{7,4},{8,11},{9,10},{10,... | collective-permute-start | bytes 774152 | tf_op jit(solution)/shard_map/ppermute | solution.py:55
  230.5 27.0 %collective-permute-start.34 = (bf16[224,1152]{1,0:T(8,128)(2,1)S(1)}, bf16[224,1152]{1,0:T(8,128)(2,1)S(1)}, u32[]{:S(2)}, u32[]{:S(2)}) collective-permute-start(bf16[224,1152]{1,0:T(8,128)(2,1)S(1)} %get-tuple-element.173.refs_23_), channel_id=1, source_target_pairs={{0,3},{1,2},{2,1},{3,0},{4,7},{5,6},{6,5},{7,4},{8,11},{9,10},{10,... | collective-permute-start | bytes 1548296 | tf_op jit(solution)/shard_map/ppermute | solution.py:55
  278.9 27.1 %collective-permute-start.40 = (bf16[96,1152]{1,0:T(8,128)(2,1)}, bf16[96,1152]{1,0:T(8,128)(2,1)}, u32[]{:S(2)}, u32[]{:S(2)}) collective-permute-start(bf16[96,1152]{1,0:T(8,128)(2,1)} %get-tuple-element.197), channel_id=1, source_target_pairs={{0,1},{1,0},{2,3},{3,2},{4,5},{5,4},{6,7},{7,6},{8,9},{9,8},{10,11... | collective-permute-start | bytes 663560 | tf_op jit(solution)/shard_map/ppermute | solution.py:55
  279.2 30.0 %collective-permute-start.43 = (bf16[112,1152]{1,0:T(8,128)(2,1)}, bf16[112,1152]{1,0:T(8,128)(2,1)}, u32[]{:S(2)}, u32[]{:S(2)}) collective-permute-start(bf16[112,1152]{1,0:T(8,128)(2,1)} %get-tuple-element.204), channel_id=1, source_target_pairs={{0,3},{1,2},{2,1},{3,0},{4,7},{5,6},{6,5},{7,4},{8,11},{9,10},{10,... | collective-permute-start | bytes 774152 | tf_op jit(solution)/shard_map/ppermute | solution.py:55
  282.1 42.1 %collective-permute-start.42 = (bf16[224,1152]{1,0:T(8,128)(2,1)}, bf16[224,1152]{1,0:T(8,128)(2,1)}, u32[]{:S(2)}, u32[]{:S(2)}) collective-permute-start(bf16[224,1152]{1,0:T(8,128)(2,1)} %pad_maximum_fusion), channel_id=1, source_target_pairs={{0,3},{1,2},{2,1},{3,0},{4,7},{5,6},{6,5},{7,4},{8,11},{9,10},{10,... | collective-permute-start | bytes 1548296 | tf_op jit(solution)/shard_map/ppermute | solution.py:55
  326.1 38.3 %collective-permute-start.50 = (bf16[208,1152]{1,0:T(8,128)(2,1)S(1)}, bf16[208,1152]{1,0:T(8,128)(2,1)S(1)}, u32[]{:S(2)}, u32[]{:S(2)}) collective-permute-start(bf16[208,1152]{1,0:T(8,128)(2,1)S(1)} %pad_maximum_fusion.4.refs_3_), channel_id=1, source_target_pairs={{0,4},{1,5},{2,6},{3,7},{4,0},{5,1},{6,2},{7,3},{8,12},{9,13},{10,... | collective-permute-start | bytes 1437704 | tf_op jit(solution)/shard_map/ppermute | solution.py:55
  386.5 42.7 %collective-permute-start.51 = (bf16[8,33,8,1024]{3,2,1,0:T(8,128)(2,1)}, bf16[8,33,8,1024]{3,2,1,0:T(8,128)(2,1)}, u32[]{:S(2)}, u32[]{:S(2)}) collective-permute-start(bf16[8,33,8,1024]{3,2,1,0:T(8,128)(2,1)} %theirs.2), channel_id=1, source_target_pairs={{0,8},{8,0},{16,24},{24,16},{32,40},{40,32},{48,56},{56,48},{64,72... | collective-permute-start | bytes 12976136 | tf_op jit(solution)/shard_map/ppermute | solution.py:59
  390.2 22.4 %collective-permute-start.53 = (bf16[416,512]{1,0:T(8,128)(2,1)}, bf16[416,512]{1,0:T(8,128)(2,1)}, u32[]{:S(2)}, u32[]{:S(2)}) collective-permute-start(bf16[416,512]{1,0:T(8,128)(2,1)} %pad_maximum_fusion.8), channel_id=1, source_target_pairs={{0,3},{1,2},{2,1},{3,0},{4,7},{5,6},{6,5},{7,4},{8,11},{9,10},{10,... | collective-permute-start | bytes 1277960 | tf_op jit(solution)/shard_map/ppermute | solution.py:55
  422.2 24.3 %collective-permute-start.45 = (bf16[416,1152]{1,0:T(8,128)(2,1)}, bf16[416,1152]{1,0:T(8,128)(2,1)}, u32[]{:S(2)}, u32[]{:S(2)}) collective-permute-start(bf16[416,1152]{1,0:T(8,128)(2,1)} %fence.12), channel_id=1, source_target_pairs={{0,1},{1,0},{2,3},{3,2},{4,5},{5,4},{6,7},{7,6},{8,9},{9,8},{10,11... | collective-permute-start | bytes 2875400 | tf_op jit(solution)/shard_map/ppermute | solution.py:55
  423.2 45.4 %collective-permute-start.46 = (bf16[416,1152]{1,0:T(8,128)(2,1)}, bf16[416,1152]{1,0:T(8,128)(2,1)}, u32[]{:S(2)}, u32[]{:S(2)}) collective-permute-start(bf16[416,1152]{1,0:T(8,128)(2,1)} %fence.13), channel_id=1, source_target_pairs={{0,3},{1,2},{2,1},{3,0},{4,7},{5,6},{6,5},{7,4},{8,11},{9,10},{10,... | collective-permute-start | bytes 2875400 | tf_op jit(solution)/shard_map/ppermute | solution.py:55
  425.1 43.5 %collective-permute-start.47 = (bf16[416,1152]{1,0:T(8,128)(2,1)}, bf16[416,1152]{1,0:T(8,128)(2,1)}, u32[]{:S(2)}, u32[]{:S(2)}) collective-permute-start(bf16[416,1152]{1,0:T(8,128)(2,1)} %fence.14), channel_id=1, source_target_pairs={{0,2},{1,3},{2,0},{3,1},{4,6},{5,7},{6,4},{7,5},{8,10},{9,11},{10,... | collective-permute-start | bytes 2875400 | tf_op jit(solution)/shard_map/ppermute | solution.py:55
  443.9 40.0 %collective-permute-start.57 = (bf16[208,512]{1,0:T(8,128)(2,1)}, bf16[208,512]{1,0:T(8,128)(2,1)}, u32[]{:S(2)}, u32[]{:S(2)}) collective-permute-start(bf16[208,512]{1,0:T(8,128)(2,1)} %fence.16), channel_id=1, source_target_pairs={{0,4},{1,5},{2,6},{3,7},{4,0},{5,1},{6,2},{7,3},{8,12},{9,13},{10,... | collective-permute-start | bytes 638984 | tf_op jit(solution)/shard_map/ppermute | solution.py:55
  472.0 22.8 %collective-permute-start.59 = (bf16[272,768]{1,0:T(8,128)(2,1)S(1)}, bf16[272,768]{1,0:T(8,128)(2,1)}, u32[]{:S(2)}, u32[]{:S(2)}) collective-permute-start(bf16[272,768]{1,0:T(8,128)(2,1)S(1)} %bitcast.207), channel_id=1, source_target_pairs={{0,3},{1,2},{2,1},{3,0},{4,7},{5,6},{6,5},{7,4},{8,11},{9,10},{10,... | collective-permute-start | bytes 1253384 | tf_op jit(solution)/shard_map/ppermute | solution.py:55
  473.9 24.3 %collective-permute-start.60 = (bf16[272,768]{1,0:T(8,128)(2,1)S(1)}, bf16[272,768]{1,0:T(8,128)(2,1)}, u32[]{:S(2)}, u32[]{:S(2)}) collective-permute-start(bf16[272,768]{1,0:T(8,128)(2,1)S(1)} %bitcast.201), channel_id=1, source_target_pairs={{0,2},{1,3},{2,0},{3,1},{4,6},{5,7},{6,4},{7,5},{8,10},{9,11},{10,... | collective-permute-start | bytes 1253384 | tf_op jit(solution)/shard_map/ppermute | solution.py:55
  476.7 40.6 %collective-permute-start.63 = (bf16[528,1024]{1,0:T(8,128)(2,1)S(1)}, bf16[528,1024]{1,0:T(8,128)(2,1)}, u32[]{:S(2)}, u32[]{:S(2)}) collective-permute-start(bf16[528,1024]{1,0:T(8,128)(2,1)S(1)} %bitcast.186), channel_id=1, source_target_pairs={{0,3},{1,2},{2,1},{3,0},{4,7},{5,6},{6,5},{7,4},{8,11},{9,10},{10,... | collective-permute-start | bytes 3244040 | tf_op jit(solution)/shard_map/ppermute | solution.py:55
  494.9 26.8 %collective-permute-start.62 = (bf16[528,1024]{1,0:T(8,128)(2,1)S(1)}, bf16[528,1024]{1,0:T(8,128)(2,1)S(1)}, u32[]{:S(2)}, u32[]{:S(2)}) collective-permute-start(bf16[528,1024]{1,0:T(8,128)(2,1)S(1)} %bitcast.183), channel_id=1, source_target_pairs={{0,1},{1,0},{2,3},{3,2},{4,5},{5,4},{6,7},{7,6},{8,9},{9,8},{10,11... | collective-permute-start | bytes 3244040 | tf_op jit(solution)/shard_map/ppermute | solution.py:55
  494.9 47.5 %collective-permute-start.64 = (bf16[528,1024]{1,0:T(8,128)(2,1)S(1)}, bf16[528,1024]{1,0:T(8,128)(2,1)S(1)}, u32[]{:S(2)}, u32[]{:S(2)}) collective-permute-start(bf16[528,1024]{1,0:T(8,128)(2,1)S(1)} %bitcast.180), channel_id=1, source_target_pairs={{0,2},{1,3},{2,0},{3,1},{4,6},{5,7},{6,4},{7,5},{8,10},{9,11},{10,... | collective-permute-start | bytes 3244040 | tf_op jit(solution)/shard_map/ppermute | solution.py:55
  499.7 47.2 %collective-permute-start.61 = (bf16[136,768]{1,0:T(8,128)(2,1)S(1)}, bf16[136,768]{1,0:T(8,128)(2,1)S(1)}, u32[]{:S(2)}, u32[]{:S(2)}) collective-permute-start(bf16[136,768]{1,0:T(8,128)(2,1)S(1)} %slice.695), channel_id=1, source_target_pairs={{0,4},{1,5},{2,6},{3,7},{4,0},{5,1},{6,2},{7,3},{8,12},{9,13},{10,... | collective-permute-start | bytes 626696 | tf_op jit(solution)/shard_map/ppermute | solution.py:55
  (238 other events, 3058.1 us)
Sparse Core Ops, SparseCore 0:
  306.1 179.4 all-reduce.19

commit v5 on v4

--- a/solution.py
+++ b/solution.py
@@ -130,6 +130,40 @@
     )(*arrays, *after)
 
 
+class relay_stages:
+    def __init__(self, own, na, swap):
+        self.own, self.na, self.nb, self.swap = own, na, own.shape[0] - na, swap
+        self.got, self.stage = (), 0
+
+    def send(self, after=()):
+        self.stage += 1
+        na, nb = self.na, self.nb
+        if self.stage == 1:
+            self.own = held(self.own, after)
+            sends = [self.own] * 3
+            steps = (1, 3, 4)
+        elif self.stage == 2:
+            layout = (
+                ((0, 0, na), (1, 0, na)),
+                ((1, 0, na), (2, na, nb)),
+                ((0, na, nb), (2, na, nb)),
+            )
+            sends = make_sends(self.got, layout, after)
+            steps = (4, 1, 3)
+        else:
+            sends = make_sends(self.got[3:5], (((0, na, na),), ((1, na, nb),)), after)
+            steps = (1, 3)
+        self.flying = tuple(self.swap(x, step) for x, step in zip(sends, steps))
+        return tuple(sends)
+
+    def arrive(self):
+        self.got += self.flying
+
+    def finish(self):
+        self.arrive()
+        return (self.own, *self.got)
+
+
 def relay_gather(own, na, swap, during=None, hold=None):
     nb = own.shape[0] - na
     during = during or (lambda stage, arrived, sends: ())
@@ -208,7 +242,7 @@
     out = lax.dynamic_update_index_in_dim(out, two, ring, 1)
     for step in (1, 3, 2):
         out = lax.dynamic_update_index_in_dim(out, swap(two, step), ring ^ step, 1)
-    return out.reshape((8,) + array.shape)
+    return out.reshape((8,) + array.shape), two
 
 
 def scatter_direct(pieces, index, swap):
@@ -248,8 +282,8 @@
 
 
 def interleave_kernel(cuts, core_ref, *refs):
-    count = (len(refs) - len(cuts)) // 2
-    mine, theirs, outs = refs[:count], refs[count : 2 * count], refs[2 * count :]
+    count = 1 + max(which for which, _, _, _, _ in cuts)
+    mine, theirs, outs = refs[:count], refs[count : 2 * count], refs[len(refs) - len(cuts) :]
     core = core_ref[0]
     for out, (which, first, n, column, width) in zip(outs, cuts):
         columns = slice(column, column + width)
@@ -258,15 +292,15 @@
             out[i, 1 - core] = theirs[which][i, first : first + n, :, columns]
 
 
-def interleave(mine, theirs, cuts, core):
+def interleave(mine, theirs, cuts, core, after=()):
     outs = pl.pallas_call(
         functools.partial(interleave_kernel, cuts),
-        in_specs=[SMEM] + [VMEM] * (2 * len(mine)),
+        in_specs=[SMEM] + [VMEM] * (2 * len(mine)) + [ANY] * len(after),
         out_specs=[VMEM] * len(cuts),
         out_shape=[jax.ShapeDtypeStruct((8, 2, n, 8, width), bf16) for _, _, n, _, width in cuts],
         compiler_params=pltpu.CompilerParams(vmem_limit_bytes=40 * 1024 * 1024),
         name="interleave",
-    )(core.reshape(1), *mine, *theirs)
+    )(core.reshape(1), *mine, *theirs, *after)
     return [x.reshape(-1, x.shape[-1]) for x in outs]
 
 
@@ -287,10 +321,9 @@
         at = 0
         for _, h in parts:
             prefix.append(rows[i][at : at + HALF_A])
-            at += HALF_A
             if h:
-                action.append(rows[i][at : at + ACT_PAD, :width])
-                at += ACT_PAD
+                action.append(rows[i][at + HALF_A : at + HALF_B, :width])
+            at += 2 * (HALF_A, HALF_B)[h]
     x = join(*prefix).astype(f32)
     low_d = (x * inverse_rms(x) * gain_d).astype(bf16)
     x = join(*action).astype(f32)
@@ -353,7 +386,7 @@
     return product, gate_delta, up_delta, rows_delta.astype(bf16)
 
 
-def feed_kernel(layout, *refs):
+def feed_kernel(layout, seed_layout, *refs):
     arrays = 1 + max(i for parts in layout for i, _ in parts)
     rows_refs, seed_refs, refs = refs[:arrays], refs[arrays : 2 * arrays], refs[2 * arrays :]
     gate_ref, up_ref, down_ref = refs[:3]
@@ -365,19 +398,19 @@
     width = action_gate_ref.shape[0]
     rest = PREF - HALF_A
 
-    def prefix_of(blocks):
+    def prefix_of(blocks, layout):
         parts = []
         for (ia, a), (ib, b) in layout:
             parts += [blocks[ia][a : a + HALF_A], blocks[ib][b : b + rest]]
         return join(*parts)
 
-    def action_of(blocks):
+    def action_of(blocks, layout):
         parts = []
         for _, (ib, b) in layout:
             parts.append(blocks[ib][b + rest : b + HALF_B, :width])
         return join(*parts) if count > 1 else parts[0]
 
-    rows, seed = prefix_of(rows_refs), prefix_of(seed_refs)
+    rows, seed = prefix_of(rows_refs, layout), prefix_of(seed_refs, seed_layout)
     product, gate_delta, up_delta, rows_delta = feed_block(
         rows, seed, gate_ref[...], up_ref[...], down_ref[...], None
     )
@@ -391,7 +424,7 @@
     deltas[:, HIDDEN_PAD + hidden :] = spare
     kept_rows[...] = rows
     kept_seeds[...] = seed
-    rows, seed = action_of(rows_refs), action_of(seed_refs)
+    rows, seed = action_of(rows_refs, layout), action_of(seed_refs, seed_layout)
     product, gate_delta, up_delta, action_rows_delta = feed_block(
         rows,
         seed,
@@ -417,7 +450,7 @@
         ref_b[rest:, width:] = blank
 
 
-def feed(arrays, seeds, weights, layout, base, kept, after):
+def feed(arrays, seeds, weights, layout, seed_layout, base, kept, after):
     count = len(layout)
     width = arrays[0].shape[1]
     hidden = weights[0].shape[0]
@@ -454,7 +487,7 @@
     given = [*arrays, *seeds]
     placed = len(given) + len(weights)
     results = pl.pallas_call(
-        functools.partial(feed_kernel, layout),
+        functools.partial(feed_kernel, layout, seed_layout),
         grid=(1,),
         in_specs=[whole(x) for x in given]
         + [VMEM] * len(weights)
@@ -662,7 +695,7 @@
                 out[base + row : base + row + n, :, columns] = total.astype(bf16)
 
 
-def sum_weights(grads, cuts, columns, place, sent, after):
+def sum_weights(grads, cuts, columns, place, sent, got, after, before_last):
     views = [g.reshape(2, 8, -1, 8, g.shape[1]) for g in grads]
     eights = max(row + n for row, n, _, _, _ in cuts)
     params = pltpu.CompilerParams(vmem_limit_bytes=44 * 1024 * 1024)
@@ -690,9 +723,11 @@
     sent += near[1:]
     total = near[0].astype(f32)
     for step, x in zip((1, 3, 2), near[1:]):
-        total = total + mp_swap(x, step).astype(f32)
+        got.append(mp_swap(x, step))
+        total = total + got[-1].astype(f32)
     half = 8 * eights
-    return (total[:half] + mp_swap(total[half:].astype(bf16), 4).astype(f32)).astype(bf16)
+    last = held(total[half:].astype(bf16), before_last)
+    return (total[:half] + mp_swap(last, 4).astype(f32)).astype(bf16)
 
 
 def pad_action(rows):
@@ -848,7 +883,7 @@
     action_seed = cotangent_a.astype(f32) * row_share[PREF:]
     seed_block = block_of(prefix_seed.astype(bf16), action_seed.astype(bf16))
 
-    near = gather_direct(pack, mp, mp_swap)
+    near, two = gather_direct(pack, mp, mp_swap)
     last_row = near[:, :, pack.shape[1] - 256 : pack.shape[1] - 48].reshape(8, 1, wide)
     near_d = jnp.concatenate([near[:, :, :wide], last_row], axis=1).reshape(72, wide)
     near_a = near[:, :, wide : pack.shape[1] - 256].reshape(64, -1)
@@ -856,39 +891,34 @@
     kv_a = widen(jnp.concatenate([near_a[:, :640], edge], axis=1), 1024)
     pack_a = join(near_a[:, 640:1664], near_a[:, 1664:2688], kv_a)
     pack_b = join(near_d[:, 640:], near_a[:, 2688 : 2688 + 1024], widen(near_d[:, :640], 1024))
-    arrived = {}
-
-    def note(name):
-        def during(stage, blocks, sends):
-            arrived[name, stage] = blocks
-            arrived[name, "sends", stage] = sends
-            return ()
-
-        return during
-
     own_action = pad_action(action_input[0])
     own_block = block_of(prefix_input[0], own_action)
     pack = join(pack_a, pack_b)
-    x_hold = {2: (pack,)}
-    x_rows = relay_gather(own_block, HALF_A, mp_swap, note("rows"), x_hold)
-    hold = {1: x_rows[1:4], 3: x_rows[4:7]}
-    pieces = relay_gather(pack, pack_a.shape[0], yz_swap, note("weights"), hold)
+    both = join(
+        own_block[:HALF_A], seed_block[:HALF_A], own_block[HALF_A:], seed_block[HALF_A:]
+    )
+    gather = relay_stages(pack, pack_a.shape[0], yz_swap)
+    other = relay_stages(both, 2 * HALF_A, mp_swap)
+    other.send((two,))
+    gather.send()
+    gather.arrive()
+    sends = gather.send()
+    other.arrive()
+    other.send(sends)
+    gather.arrive()
+    sends = gather.send()
+    other.arrive()
+    row_sends = other.send(sends)
+    pieces = gather.finish()
+    x_rows = seeds = other.finish()
     cuts = ((0, 16, 8, 768), (1, 17, 9, 640), (0, 0, 16, 1024), (1, 0, 17, 1024))
-    mine = place(pieces, pack_a.shape[0], cuts, yz, arrived["rows", "sends", 3])
+    mine = place(pieces, pack_a.shape[0], cuts, yz, (*row_sends, x_rows[6]))
     theirs = [core_swap(x) for x in mine]
     cuts = ((0, 0, 8, 0, 512), (0, 0, 8, 512, 128), (0, 0, 8, 640, 128))
     cuts += ((1, 0, 9, 0, 512), (1, 0, 9, 512, 128))
-    wkv_a, gains_a, wo_e, wkv_d, gains_d = interleave(mine[:2], theirs[:2], cuts, core)
+    wkv_a, gains_a, wo_e, wkv_d, gains_d = interleave(mine[:2], theirs[:2], cuts, core, x_rows[7:])
     cuts = ((0, 0, 8, 0, 1024), (0, 8, 8, 0, 1024), (1, 0, 9, 0, 1024), (1, 9, 8, 0, 1024))
     wq_a, wo_a, wq_d, wo_m = interleave(mine[2:], theirs[2:], cuts, core)
-    seeds = relay_gather(
-        seed_block,
-        HALF_A,
-        mp_swap,
-        note("seeds"),
-        {1: pieces[7:9]},
-    )
-
     normed_d, normed_a, keys, values = keys_of(
         x_rows,
         gains_d,
@@ -897,7 +927,7 @@
         wkv_a,
         key_cos,
         key_sin,
-        arrived["seeds", "sends", 1],
+        (),
     )
     x_d, x_a = prefix_input[0].astype(f32), own_action.astype(f32)
     rms_d, rms_a = inverse_rms(x_d), inverse_rms(x_a)
@@ -919,7 +949,7 @@
         key_codes,
         keys,
         values,
-        after=arrived["seeds", "sends", 2],
+        after=(),
     )
 
     slots = action_gate.shape[2]
@@ -935,7 +965,10 @@
         where = where_parts(first, len(arrays), (HALF_A, HALF_B))
         layout = tuple((where[k, 0], where[k, 1]) for k in blocks)
         some = seeds[first : first + len(arrays)]
-        done, kept = feed(arrays, some, weights, layout, base, kept, after)
+        where = where_parts(first, len(arrays), (2 * HALF_A, 2 * HALF_B))
+        skip = lambda k, h: (where[k, h][0], where[k, h][1] + (HALF_A, HALF_B)[h])
+        seed_layout = tuple((skip(k, 0), skip(k, 1)) for k in blocks)
+        done, kept = feed(arrays, some, weights, layout, seed_layout, base, kept, after)
         results.update(zip(blocks, done))
         return (done[0][0],)
 
@@ -945,7 +978,6 @@
         first, blocks, base = {1: (0, (0,), 3), 2: (1, (1, 3, 4), 0)}[stage]
         return run(arrays, first, blocks, base, sends)
 
-    second_block = fence(second_block, *arrived["seeds", "sends", 3])
     arrays = relay_gather(second_block, HALF_A, mp_swap, feed_during)
     run(arrays[4:], 4, (2, 5, 7, 6), 4, ())
     product_d, deltas_d, rows_d, seeds_d, product_a, deltas_a, rows_a, seeds_a = kept
@@ -958,7 +990,11 @@
     )
     hidden = prefix_down.shape[0]
     grads = tuple(g.astype(bf16) for g in grads)
-    after_grads = tuple(grads)
+    pa = {k: v[0] for k, v in results.items()}
+    pb = {k: v[1] for k, v in results.items()}
+    delta_sent = {}
+    delta_pieces = relay_scatter(pa, pb, mp_swap, sent=delta_sent)
+    grads = grads[:3] + (fence(grads[3], *delta_sent[3]),)
     grads = tuple(lax.psum(g, "dp") for g in grads)
     finished = (
         grads[0][:hidden].astype(f32),
@@ -968,21 +1004,6 @@
         grads[2][:, slots:].astype(f32),
         grads[3].astype(f32),
     )
-
-    pa = {k: v[0] for k, v in results.items()}
-    pb = {k: v[1] for k, v in results.items()}
-    delta_sent = {}
-    delta_pieces = relay_scatter(pa, pb, mp_swap, sent=delta_sent)
-
-    partial_d = dot(product_d[:, :hidden], prefix_down).astype(bf16)
-    partial_a = dot(product_a, action_down[0]).astype(bf16)
-    out = []
-    for k in range(8):
-        i = (1, 3, 4, 0, 2, 5, 7, 6).index(k)
-        mine = partial_a[i * ACT_PAD : (i + 1) * ACT_PAD]
-        out.append(block_of(partial_d[i * PREF : (i + 1) * PREF], mine))
-    out_sent = []
-    out = ring_scatter(out, mp_swap, delta_sent[3], out_sent)
 
     (hidden_delta_d, hidden_delta_a, low, terms_d, terms_a, query_delta), pa, pb = attend_back(
         *delta_pieces,
@@ -1042,9 +1063,9 @@
         (16, 9, 0, 0, 1024),
         (25, 8, 0, 0, 1024),
     )
-    qo_sent, kv_sent = [], []
+    qo_sent, kv_sent, got = [], [], []
     qo_grads = (q_grad_a, out_grad_a, q_grad_d, out_grad_d)
-    qo = sum_weights(qo_grads, cuts, 1024, here, qo_sent, ())
+    qo = sum_weights(qo_grads, cuts, 1024, here, qo_sent, got, (), grads[:1])
     kv_grad_d = t_dot(turned_d, kv_rows_d).astype(bf16)
     kv_grad_a = t_dot(turned_a, kv_rows_a).astype(bf16)
     cuts = (
@@ -1061,7 +1082,7 @@
         kv_grad_d,
         second_term_d.astype(bf16),
     )
-    kv = sum_weights(kv_grads, cuts, 768, here, kv_sent, qo_sent)
+    kv = sum_weights(kv_grads, cuts, 768, here, kv_sent, got, qo_sent, grads[:1])
     kv_a, kv_d = kv[:64], kv[64:, :640]
     qo_a, qo_b = qo[:128], qo[128:]
     kv_other = mp_swap(held(kv_part[BLOCK:].astype(bf16), tuple(kv_sent)), 4)
@@ -1070,7 +1091,16 @@
         [unrotate(kv_sum[:, :HD], own_cos, own_sin), kv_sum[:, HD:]], axis=1
     ).astype(bf16)
 
-    out = pair_sum(out, mp_swap, (*qo_sent, *kv_sent))
+    partial_d = dot(product_d[:, :hidden], prefix_down).astype(bf16)
+    partial_a = dot(product_a, action_down[0]).astype(bf16)
+    out = []
+    for k in range(8):
+        i = (1, 3, 4, 0, 2, 5, 7, 6).index(k)
+        mine = partial_a[i * ACT_PAD : (i + 1) * ACT_PAD]
+        out.append(block_of(partial_d[i * PREF : (i + 1) * PREF], mine))
+    out_sent = []
+    out = ring_scatter(out, mp_swap, tuple(got), out_sent)
+    out = pair_sum(out, mp_swap)
     prefix_output = (hidden_d + out[:PREF]).astype(bf16)[None]
     action_output = (hidden_a + out[PREF:, :DA])[:ACT].astype(bf16)[None]
 
@@ -1086,7 +1116,7 @@
         ],
         axis=2,
     )
-    last = scatter_direct(fence(last, grads[0]), yz, yz_swap)
+    last = scatter_direct(last, yz, yz_swap)
     ninth = last[:, last.shape[1] - 256 : last.shape[1] - 48].reshape(1, wide)
     grads_d = join(last[:, :wide], ninth)
     grads_a = last[:, wide : last.shape[1] - 256]

time: 605 us -> 584 us (0.965); the launches traced: 601 us -> 574 us
  starting transfers between devices: 107 us -> 86 us
    ppermute x52 -> x44, starting transfers between devices: 76.5 us -> 60.3 us  [mp_swap(): return lax.ppermute(array, 'mp', [(i, i ^ step) for i in range(N_MP)])]
    ppermute x18, waiting for transfers between devices: 21 us -> 35.7 us  [dp_swap(): return lax.ppermute(array, 'dp', [(i, i ^ step) for i in range(16)])]
    ppermute x52 -> x44, waiting for transfers between devices: 182 us -> 173 us  [mp_swap(): return lax.ppermute(array, 'mp', [(i, i ^ step) for i in range(N_MP)])]
    unnamed x415 -> x287, local copies, waits for them, and re-layouts: 35.4 us -> 37.7 us
  transfers between devices with their start and end apart: 71 -> 63, of which waited for: 31 -> 29; matrix products, arithmetic and copies ran while one was open for 20% -> 19% of each run, Pallas kernels for 13% -> 11%
where the time goes in v5:
time: 584 us; the launch traced here: 574 us
  waiting for transfers between devices  208 us (36%)
  Pallas kernels  101 us (17%)
  starting transfers between devices  86 us (15%)
  other arithmetic  63.5 us (11%)
  local copies, waits for them, and re-layouts  50.7 us (9%)
  matrix products  46.9 us (8%)
  between operations  17.6 us (3%)
    ppermute x44, waiting for transfers between devices, mp_swap(): return lax.ppermute(array, 'mp', [(i, i ^ step) for i in range(N_MP)])  173 us
    ppermute x44, starting transfers between devices, mp_swap(): return lax.ppermute(array, 'mp', [(i, i ^ step) for i in range(N_MP)])  60.3 us
    pallas_call x3, Pallas kernels, feed(): pl.pallas_call(functools.partial(feed_kernel, layout, seed_layout), grid=...  44.9 us
    unnamed x287, local copies, waits for them, and re-layouts  37.7 us
    ppermute x18, waiting for transfers between devices, dp_swap(): return lax.ppermute(array, 'dp', [(i, i ^ step) for i in range(16)])  35.7 us
    dot_general x12, matrix products, t_dot(): lax.dot_general(a, b, (((0,), (0,)), ((), ())), preferred_element_type=f32)  32.3 us
    ppermute x18, starting transfers between devices, dp_swap(): return lax.ppermute(array, 'dp', [(i, i ^ step) for i in range(16)])  25.7 us
    pallas_call x1, Pallas kernels, attend_back(): pl.pallas_call(attend_back_kernel, in_specs=[VMEM] * len(given) + [ANY] *...  12.4 us
  transfers between devices with their start and end apart: 63, of which 29 were waited for; matrix products, arithmetic and copies ran while one was open for 19% of the time, Pallas kernels for 11%

profile of v5, /device:TPU:0, one launch (start us, length us, event | category | flops | bytes accessed | tf_op | source)
XLA Modules:
  0.0 573.7 jit_solution(10871109947321132022)
XLA Ops:
  28.0 7.4 %collective-permute-done.4 = bf16[2,8,5760]{2,1,0:T(8,128)(2,1)S(1)} collective-permute-done((bf16[2,8,5760]{2,1,0:T(8,128)(2,1)S(1)}, bf16[2,8,5760]{2,1,0:T(8,128)(2,1)S(1)}, u32[]{:S(2)}, u32[]{:S(2)}) %collective-permute-start.4) | collective-permute-done | bytes 184352 | tf_op jit(solution)/shard_map/ppermute | solution.py:55
  50.5 12.3 %collective-permute-done.9.refs_2_ = bf16[400,1024]{1,0:T(8,128)(2,1)S(1)} collective-permute-done((bf16[400,1024]{1,0:T(8,128)(2,1)}, bf16[400,1024]{1,0:T(8,128)(2,1)S(1)}, u32[]{:S(2)}, u32[]{:S(2)}) %collective-permute-start.9) | collective-permute-done | bytes 819232 | tf_op jit(solution)/shard_map/ppermute | solution.py:59
  70.3 12.9 %collective-permute-done.3.refs_2_.refs_3_.refs_5_ = bf16[416,1152]{1,0:T(8,128)(2,1)S(1)} collective-permute-done((bf16[416,1152]{1,0:T(8,128)(2,1)}, bf16[416,1152]{1,0:T(8,128)(2,1)S(1)}, u32[]{:S(2)}, u32[]{:S(2)}) %collective-permute-start.3) | collective-permute-done | bytes 958496 | tf_op jit(solution)/shard_map/ppermute | solution.py:55
  91.9 8.4 %collective-permute-done.13.refs_0_ = bf16[384,1024]{1,0:T(8,128)(2,1)S(1)} collective-permute-done((bf16[384,1024]{1,0:T(8,128)(2,1)S(1)}, bf16[384,1024]{1,0:T(8,128)(2,1)S(1)}, u32[]{:S(2)}, u32[]{:S(2)}) %collective-permute-start.13) | collective-permute-done | bytes 786464 | tf_op jit(solution)/shard_map/ppermute | solution.py:59
  109.3 8.5 %collective-permute-done.10.refs_0_.refs_4_.refs_5_ = bf16[384,1152]{1,0:T(8,128)(2,1)S(1)} collective-permute-done((bf16[384,1152]{1,0:T(8,128)(2,1)S(1)}, bf16[384,1152]{1,0:T(8,128)(2,1)S(1)}, u32[]{:S(2)}, u32[]{:S(2)}) %collective-permute-start.10) | collective-permute-done | bytes 884768 | tf_op jit(solution)/shard_map/ppermute | solution.py:55
  123.6 5.4 collective-permute-done.18
  132.4 4.0 place.1
  153.4 7.7 %collective-permute-done.15.refs_4_.refs_7_.refs_8_ = bf16[192,1152]{1,0:T(8,128)(2,1)S(1)} collective-permute-done((bf16[192,1152]{1,0:T(8,128)(2,1)S(1)}, bf16[192,1152]{1,0:T(8,128)(2,1)S(1)}, u32[]{:S(2)}, u32[]{:S(2)}) %collective-permute-start.15) | collective-permute-done | bytes 442400 | tf_op jit(solution)/shard_map/ppermute | solution.py:55
  164.7 10.5 %collective-permute-done.16.refs_5_.refs_8_.refs_9_ = bf16[224,1152]{1,0:T(8,128)(2,1)S(1)} collective-permute-done((bf16[224,1152]{1,0:T(8,128)(2,1)S(1)}, bf16[224,1152]{1,0:T(8,128)(2,1)S(1)}, u32[]{:S(2)}, u32[]{:S(2)}) %collective-permute-start.16) | collective-permute-done | bytes 516128 | tf_op jit(solution)/shard_map/ppermute | solution.py:55
  180.0 6.3 %keys_of.1 = (bf16[384,1152]{1,0:T(8,128)(2,1)S(1)}, bf16[32,1024]{1,0:T(8,128)(2,1)S(1)}, bf16[1664,256]{1,0:T(8,128)(2,1)S(1)}, bf16[1664,256]{1,0:T(8,128)(2,1)S(1)}) custom-call(bf16[416,1152]{1,0:T(8,128)(2,1)} %fence.8.refs_0_.refs_1_, bf16[416,1152]{1,0:T(8,128)(2,1)} %copy-done.12, bf16[416,1152]{1,0:T(8,128)(2,1)} %copy-done.11, ...), custom_call_target="tpu_custom_call" | custom-call | flops 1962934272 | bytes 8388608 | tf_op jit(solution)/shard_map/keys_of/pallas_call | solution.py:345
  189.2 5.5 interleave.3
  198.7 11.0 %attend.1 = (bf16[832,256]{1,0:T(8,128)(2,1)S(1)}, bf16[208,1024]{1,0:T(8,128)(2,1)S(1)}, f32[832,1]{1,0:T(8,128)S(1)}, f32[832,1]{1,0:T(8,128)S(1)}, f32[192,11...) custom-call(bf16[384,1152]{1,0:T(8,128)(2,1)} %copy-done.46, ...), custom_call_target="tpu_custom_call" | custom-call | flops 2399141888 | bytes 20971520 | tf_op jit(solution)/shard_map/attend/pallas_call | solution.py:561
  218.3 10.0 %feed.3 = (bf16[1536,896]{1,0:T(8,128)(2,1)}, bf16[1536,1792]{1,0:T(8,128)(2,1)}, bf16[1536,1152]{1,0:T(8,128)(2,1)}, bf16[1536,1152]{1,0:T(8,128)(2,1)}, bf16[1...) custom-call(bf16[208,1152]{1,0:T(8,128)(2,1)S(1)} %get-tuple-element, ...), custom_call_target="tpu_custom_call" | custom-call | flops 2078801920 | bytes 12263424 | tf_op jit(solution)/shard_map/feed/pallas_call | solution.py:489
  232.8 15.9 %feed.4 = (bf16[1536,896]{1,0:T(8,128)(2,1)}, bf16[1536,1792]{1,0:T(8,128)(2,1)}, bf16[1536,1152]{1,0:T(8,128)(2,1)}, bf16[1536,1152]{1,0:T(8,128)(2,1)}, bf16[1...) custom-call(bf16[208,1152]{1,0:T(8,128)(2,1)S(1)} %collective-permut, ...), custom_call_target="tpu_custom_call", output_to_operand_aliasing={{0}: (13, {}), {1}: (14, {}), {2}: (15, {}), {3}: (16, {}),... | custom-call | flops 6236405760 | bytes 12263424 | tf_op jit(solution)/shard_map/feed/pallas_call | solution.py:489
  253.1 5.0 collective-permute-done.30.refs_3_
  258.1 18.9 %feed.5 = (bf16[1536,896]{1,0:T(8,128)(2,1)}, bf16[1536,1792]{1,0:T(8,128)(2,1)}, bf16[1536,1152]{1,0:T(8,128)(2,1)}, bf16[1536,1152]{1,0:T(8,128)(2,1)}, bf16[1...) custom-call(bf16[192,1152]{1,0:T(8,128)(2,1)S(1)} %collective-permut, ...), custom_call_target="tpu_custom_call", output_to_operand_aliasing={{0}: (17, {}), {1}: (18, {}), {2}: (19, {}), {3}: (20, {}),... | custom-call | flops 8315207680 | bytes 12263424 | tf_op jit(solution)/shard_map/feed/pallas_call | solution.py:489
  281.0 11.9 %convolution_convert_fusion = bf16[1792,1152]{1,0:T(8,128)(2,1)} fusion(bf16[1536,1792]{1,0:T(8,128)(2,1)} %get-tuple-element.233, bf16[1536,1152]{1,0:T(8,128)(2,1)} %get-tuple-element.234), kind=kOutput, calls=%fused_computation | convolution fusion | flops 6343852032 | bytes 13172736 | tf_op jit(solution)/shard_map/dot_general | solution.py:763
  295.1 5.1 convolution_convert_fusion.5
  317.3 12.4 %attend_back.1 = (f32[192,1152]{1,0:T(8,128)}, f32[16,1024]{1,0:T(8,128)S(1)}, bf16[208,1152]{1,0:T(8,128)(2,1)}, bf16[192,1152]{1,0:T(8,128)(2,1)}, bf16[16,102...) custom-call(bf16[96,1152]{1,0:T(8,128)(2,1)S(1)} %get-tuple-element., ...), custom_call_target="tpu_custom_call" | custom-call | flops 425984 | bytes 832 | tf_op jit(solution)/shard_map/attend_back/pallas_call | solution.py:650
  339.6 5.6 convolution_convert_fusion.1
  356.8 3.8 collective-permute-done.46
  360.6 7.1 %collective-permute-done.45 = bf16[416,512]{1,0:T(8,128)(2,1)} collective-permute-done((bf16[416,512]{1,0:T(8,128)(2,1)}, bf16[416,512]{1,0:T(8,128)(2,1)}, u32[]{:S(2)}, u32[]{:S(2)}) %collective-permute-start.45) | collective-permute-done | bytes 426016 | tf_op jit(solution)/shard_map/ppermute | solution.py:55
  379.1 4.8 near.2
  397.0 9.6 %collective-permute-done.55 = bf16[208,512]{1,0:T(8,128)(2,1)S(1)} collective-permute-done((bf16[208,512]{1,0:T(8,128)(2,1)}, bf16[208,512]{1,0:T(8,128)(2,1)S(1)}, u32[]{:S(2)}, u32[]{:S(2)}) %collective-permute-start.55) | collective-permute-done | bytes 213024 | tf_op jit(solution)/shard_map/ppermute | solution.py:55
  415.8 45.5 %collective-permute-done.50.refs_6_ = bf16[272,768]{1,0:T(8,128)(2,1)S(1)} collective-permute-done((bf16[272,768]{1,0:T(8,128)(2,1)S(1)}, bf16[272,768]{1,0:T(8,128)(2,1)S(1)}, u32[]{:S(2)}, u32[]{:S(2)}) %collective-permute-start.50) | collective-permute-done | bytes 417824 | tf_op jit(solution)/shard_map/ppermute | solution.py:55
  469.2 17.4 %collective-permute-done.51 = bf16[416,1152]{1,0:T(8,128)(2,1)} collective-permute-done((bf16[416,1152]{1,0:T(8,128)(2,1)}, bf16[416,1152]{1,0:T(8,128)(2,1)}, u32[]{:S(2)}, u32[]{:S(2)}) %collective-permute-start.51) | collective-permute-done | bytes 958496 | tf_op jit(solution)/shard_map/ppermute | solution.py:55
  486.6 17.8 %collective-permute-done.52 = bf16[416,1152]{1,0:T(8,128)(2,1)} collective-permute-done((bf16[416,1152]{1,0:T(8,128)(2,1)}, bf16[416,1152]{1,0:T(8,128)(2,1)}, u32[]{:S(2)}, u32[]{:S(2)}) %collective-permute-start.52) | collective-permute-done | bytes 958496 | tf_op jit(solution)/shard_map/ppermute | solution.py:55
  514.2 4.6 collective-permute-done.54
  522.5 5.9 %convert_bitcast_fusion = (f32[1152,864]{0,1:T(8,128)}, f32[1152,864]{0,1:T(8,128)}) fusion(bf16[1792,1152]{1,0:T(8,128)(2,1)} %get-tuple-element.244.refs_1_), kind=kLoop, calls=%fused_computation.9 | loop fusion | flops 1990656 | bytes 11943936 | tf_op jit(solution)/shard_map/transpose | solution.py:1165
  529.5 6.6 %collective-permute-done.57 = bf16[264,1024]{1,0:T(8,128)(2,1)S(1)} collective-permute-done((bf16[264,1024]{1,0:T(8,128)(2,1)}, bf16[264,1024]{1,0:T(8,128)(2,1)S(1)}, u32[]{:S(2)}, u32[]{:S(2)}) %collective-permute-start.57) | collective-permute-done | bytes 540704 | tf_op jit(solution)/shard_map/ppermute | solution.py:55
  547.3 3.8 collective-permute-done.59
  553.4 4.4 fusion.13
  (568 shorter events, 239.8 us)
Async XLA Ops:
  7.2 513.3 %all-reduce.20.cloned.1.call-start = ((), (), s32[]{:S(2)}) async-start(), calls=%async_computation | async-start | bytes 24969216 | tf_op jit(solution)/shard_map/psum | solution.py:998
  40.0 22.9 %collective-permute-start.9 = (bf16[400,1024]{1,0:T(8,128)(2,1)}, bf16[400,1024]{1,0:T(8,128)(2,1)S(1)}, u32[]{:S(2)}, u32[]{:S(2)}) collective-permute-start(bf16[400,1024]{1,0:T(8,128)(2,1)} %fusion.89), channel_id=1, source_target_pairs={{0,64},{8,72},{16,80},{24,88},{32,96},{40,104},{48,112},{56,120},{... | collective-permute-start | bytes 2457608 | tf_op jit(solution)/shard_map/ppermute | solution.py:59
  43.7 21.2 %collective-permute-start.8 = (bf16[400,1024]{1,0:T(8,128)(2,1)}, bf16[400,1024]{1,0:T(8,128)(2,1)S(1)}, u32[]{:S(2)}, u32[]{:S(2)}) collective-permute-start(bf16[400,1024]{1,0:T(8,128)(2,1)} %fusion.89), channel_id=1, source_target_pairs={{0,48},{8,56},{16,32},{24,40},{32,16},{40,24},{48,0},{56,8},{64,11... | collective-permute-start | bytes 2457608 | tf_op jit(solution)/shard_map/ppermute | solution.py:59
  46.8 19.7 %collective-permute-start.7 = (bf16[400,1024]{1,0:T(8,128)(2,1)}, bf16[400,1024]{1,0:T(8,128)(2,1)}, u32[]{:S(2)}, u32[]{:S(2)}) collective-permute-start(bf16[400,1024]{1,0:T(8,128)(2,1)} %fusion.89), channel_id=1, source_target_pairs={{0,16},{8,24},{16,0},{24,8},{32,48},{40,56},{48,32},{56,40},{64,80... | collective-permute-start | bytes 2457608 | tf_op jit(solution)/shard_map/ppermute | solution.py:59
  47.9 35.3 %collective-permute-start.3 = (bf16[416,1152]{1,0:T(8,128)(2,1)}, bf16[416,1152]{1,0:T(8,128)(2,1)S(1)}, u32[]{:S(2)}, u32[]{:S(2)}) collective-permute-start(bf16[416,1152]{1,0:T(8,128)(2,1)} %fence.8.refs_0_.refs_1_), channel_id=1, source_target_pairs={{0,4},{1,5},{2,6},{3,7},{4,0},{5,1},{6,2},{7,3},{8,12},{9,13},{10,... | collective-permute-start | bytes 2875400 | tf_op jit(solution)/shard_map/ppermute | solution.py:55
  47.9 35.3 %collective-permute-start.2 = (bf16[416,1152]{1,0:T(8,128)(2,1)}, bf16[416,1152]{1,0:T(8,128)(2,1)S(1)}, u32[]{:S(2)}, u32[]{:S(2)}) collective-permute-start(bf16[416,1152]{1,0:T(8,128)(2,1)} %fence.8.refs_0_.refs_1_), channel_id=1, source_target_pairs={{0,3},{1,2},{2,1},{3,0},{4,7},{5,6},{6,5},{7,4},{8,11},{9,10},{10,... | collective-permute-start | bytes 2875400 | tf_op jit(solution)/shard_map/ppermute | solution.py:55
  62.9 21.6 %collective-permute-start.1 = (bf16[416,1152]{1,0:T(8,128)(2,1)}, bf16[416,1152]{1,0:T(8,128)(2,1)S(1)}, u32[]{:S(2)}, u32[]{:S(2)}) collective-permute-start(bf16[416,1152]{1,0:T(8,128)(2,1)} %fence.8.refs_0_.refs_1_), channel_id=1, source_target_pairs={{0,1},{1,0},{2,3},{3,2},{4,5},{5,4},{6,7},{7,6},{8,9},{9,8},{10,11... | collective-permute-start | bytes 2875400 | tf_op jit(solution)/shard_map/ppermute | solution.py:55
  68.5 31.7 %collective-permute-start.13 = (bf16[384,1024]{1,0:T(8,128)(2,1)S(1)}, bf16[384,1024]{1,0:T(8,128)(2,1)S(1)}, u32[]{:S(2)}, u32[]{:S(2)}) collective-permute-start(bf16[384,1024]{1,0:T(8,128)(2,1)S(1)} %get-tuple-element.131.refs_3_), channel_id=1, source_target_pairs={{0,64},{8,72},{16,80},{24,88},{32,96},{40,104},{48,112},{56,120},{... | collective-permute-start | bytes 2359304 | tf_op jit(solution)/shard_map/ppermute | solution.py:59
  86.2 31.7 %collective-permute-start.10 = (bf16[384,1152]{1,0:T(8,128)(2,1)S(1)}, bf16[384,1152]{1,0:T(8,128)(2,1)S(1)}, u32[]{:S(2)}, u32[]{:S(2)}) collective-permute-start(bf16[384,1152]{1,0:T(8,128)(2,1)S(1)} %get-tuple-element.134), channel_id=1, source_target_pairs={{0,4},{1,5},{2,6},{3,7},{4,0},{5,1},{6,2},{7,3},{8,12},{9,13},{10,... | collective-permute-start | bytes 2654216 | tf_op jit(solution)/shard_map/ppermute | solution.py:55
  89.3 34.3 %collective-permute-start.12 = (bf16[448,1152]{1,0:T(8,128)(2,1)}, bf16[448,1152]{1,0:T(8,128)(2,1)S(1)}, u32[]{:S(2)}, u32[]{:S(2)}) collective-permute-start(bf16[448,1152]{1,0:T(8,128)(2,1)} %get-tuple-element.136), channel_id=1, source_target_pairs={{0,3},{1,2},{2,1},{3,0},{4,7},{5,6},{6,5},{7,4},{8,11},{9,10},{10,... | collective-permute-start | bytes 3096584 | tf_op jit(solution)/shard_map/ppermute | solution.py:55
  91.9 29.8 %collective-permute-start.11 = (bf16[416,1152]{1,0:T(8,128)(2,1)}, bf16[416,1152]{1,0:T(8,128)(2,1)S(1)}, u32[]{:S(2)}, u32[]{:S(2)}) collective-permute-start(bf16[416,1152]{1,0:T(8,128)(2,1)} %get-tuple-element.135), channel_id=1, source_target_pairs={{0,1},{1,0},{2,3},{3,2},{4,5},{5,4},{6,7},{7,6},{8,9},{9,8},{10,11... | collective-permute-start | bytes 2875400 | tf_op jit(solution)/shard_map/ppermute | solution.py:55
  100.3 23.3 %collective-permute-start.17 = (bf16[416,1024]{1,0:T(8,128)(2,1)}, bf16[416,1024]{1,0:T(8,128)(2,1)S(1)}, u32[]{:S(2)}, u32[]{:S(2)}) collective-permute-start(bf16[416,1024]{1,0:T(8,128)(2,1)} %get-tuple-element.133.refs_5_), channel_id=1, source_target_pairs={{0,48},{8,56},{16,32},{24,40},{32,16},{40,24},{48,0},{56,8},{64,11... | collective-permute-start | bytes 2555912 | tf_op jit(solution)/shard_map/ppermute | solution.py:59
  106.3 23.8 %collective-permute-start.19 = (bf16[208,1024]{1,0:T(8,128)(2,1)}, bf16[208,1024]{1,0:T(8,128)(2,1)}, u32[]{:S(2)}, u32[]{:S(2)}) collective-permute-start(bf16[208,1024]{1,0:T(8,128)(2,1)} %get-tuple-element.138.refs_3_), channel_id=1, source_target_pairs={{0,48},{8,56},{16,32},{24,40},{32,16},{40,24},{48,0},{56,8},{64,11... | collective-permute-start | bytes 1277960 | tf_op jit(solution)/shard_map/ppermute | solution.py:59
  136.5 52.7 %collective-permute-start.23 = (bf16[8,17,8,1024]{3,2,1,0:T(8,128)(2,1)}, bf16[8,17,8,1024]{3,2,1,0:T(8,128)(2,1)}, u32[]{:S(2)}, u32[]{:S(2)}) collective-permute-start(bf16[8,17,8,1024]{3,2,1,0:T(8,128)(2,1)} %get-tuple-element.150.refs_1_), channel_id=1, source_target_pairs={{0,8},{8,0},{16,24},{24,16},{32,40},{40,32},{48,56},{56,48},{64,72... | collective-permute-start | bytes 6684680 | tf_op jit(solution)/shard_map/ppermute | solution.py:59
  136.6 52.5 %collective-permute-start.22 = (bf16[8,16,8,1024]{3,2,1,0:T(8,128)(2,1)}, bf16[8,16,8,1024]{3,2,1,0:T(8,128)(2,1)}, u32[]{:S(2)}, u32[]{:S(2)}) collective-permute-start(bf16[8,16,8,1024]{3,2,1,0:T(8,128)(2,1)} %get-tuple-element.149.refs_0_), channel_id=1, source_target_pairs={{0,8},{8,0},{16,24},{24,16},{32,40},{40,32},{48,56},{56,48},{64,72... | collective-permute-start | bytes 6291464 | tf_op jit(solution)/shard_map/ppermute | solution.py:59
  151.3 23.9 %collective-permute-start.21 = (bf16[8,9,8,640]{3,2,1,0:T(8,128)(2,1)}, bf16[8,9,8,640]{3,2,1,0:T(8,128)(2,1)S(1)}, u32[]{:S(2)}, u32[]{:S(2)}) collective-permute-start(bf16[8,9,8,640]{3,2,1,0:T(8,128)(2,1)} %copy-done.50), channel_id=1, source_target_pairs={{0,8},{8,0},{16,24},{24,16},{32,40},{40,32},{48,56},{56,48},{64,72... | collective-permute-start | bytes 2211848 | tf_op jit(solution)/shard_map/ppermute | solution.py:59
  151.4 23.8 %collective-permute-start.20 = (bf16[8,8,8,768]{3,2,1,0:T(8,128)(2,1)}, bf16[8,8,8,768]{3,2,1,0:T(8,128)(2,1)S(1)}, u32[]{:S(2)}, u32[]{:S(2)}) collective-permute-start(bf16[8,8,8,768]{3,2,1,0:T(8,128)(2,1)} %copy-done.48), channel_id=1, source_target_pairs={{0,8},{8,0},{16,24},{24,16},{32,40},{40,32},{48,56},{56,48},{64,72... | collective-permute-start | bytes 2359304 | tf_op jit(solution)/shard_map/ppermute | solution.py:59
  229.3 19.4 %collective-permute-start.27 = (bf16[192,1152]{1,0:T(8,128)(2,1)S(1)}, bf16[192,1152]{1,0:T(8,128)(2,1)S(1)}, u32[]{:S(2)}, u32[]{:S(2)}) collective-permute-start(bf16[192,1152]{1,0:T(8,128)(2,1)S(1)} %get-tuple-element.161.refs_21_), channel_id=1, source_target_pairs={{0,4},{1,5},{2,6},{3,7},{4,0},{5,1},{6,2},{7,3},{8,12},{9,13},{10,... | collective-permute-start | bytes 1327112 | tf_op jit(solution)/shard_map/ppermute | solution.py:55
  230.3 18.4 %collective-permute-start.28 = (bf16[208,1152]{1,0:T(8,128)(2,1)S(1)}, bf16[208,1152]{1,0:T(8,128)(2,1)S(1)}, u32[]{:S(2)}, u32[]{:S(2)}) collective-permute-start(bf16[208,1152]{1,0:T(8,128)(2,1)S(1)} %get-tuple-element.162.refs_22_), channel_id=1, source_target_pairs={{0,1},{1,0},{2,3},{3,2},{4,5},{5,4},{6,7},{7,6},{8,9},{9,8},{10,11... | collective-permute-start | bytes 1437704 | tf_op jit(solution)/shard_map/ppermute | solution.py:55
  232.3 20.7 %collective-permute-start.29 = (bf16[224,1152]{1,0:T(8,128)(2,1)S(1)}, bf16[224,1152]{1,0:T(8,128)(2,1)S(1)}, u32[]{:S(2)}, u32[]{:S(2)}) collective-permute-start(bf16[224,1152]{1,0:T(8,128)(2,1)S(1)} %get-tuple-element.163.refs_23_), channel_id=1, source_target_pairs={{0,3},{1,2},{2,1},{3,0},{4,7},{5,6},{6,5},{7,4},{8,11},{9,10},{10,... | collective-permute-start | bytes 1548296 | tf_op jit(solution)/shard_map/ppermute | solution.py:55
  278.4 27.2 %collective-permute-start.34 = (bf16[224,1152]{1,0:T(8,128)(2,1)S(1)}, bf16[224,1152]{1,0:T(8,128)(2,1)S(1)}, u32[]{:S(2)}, u32[]{:S(2)}) collective-permute-start(bf16[224,1152]{1,0:T(8,128)(2,1)S(1)} %pad_maximum_fusion.2), channel_id=1, source_target_pairs={{0,3},{1,2},{2,1},{3,0},{4,7},{5,6},{6,5},{7,4},{8,11},{9,10},{10,... | collective-permute-start | bytes 1548296 | tf_op jit(solution)/shard_map/ppermute | solution.py:55
  338.1 40.7 %collective-permute-start.40 = (bf16[8,33,8,1024]{3,2,1,0:T(8,128)(2,1)}, bf16[8,33,8,1024]{3,2,1,0:T(8,128)(2,1)}, u32[]{:S(2)}, u32[]{:S(2)}) collective-permute-start(bf16[8,33,8,1024]{3,2,1,0:T(8,128)(2,1)} %theirs.2), channel_id=1, source_target_pairs={{0,8},{8,0},{16,24},{24,16},{32,40},{40,32},{48,56},{56,48},{64,72... | collective-permute-start | bytes 12976136 | tf_op jit(solution)/shard_map/ppermute | solution.py:59
  349.5 18.2 %collective-permute-start.45 = (bf16[416,512]{1,0:T(8,128)(2,1)}, bf16[416,512]{1,0:T(8,128)(2,1)}, u32[]{:S(2)}, u32[]{:S(2)}) collective-permute-start(bf16[416,512]{1,0:T(8,128)(2,1)} %pad_maximum_fusion.10), channel_id=1, source_target_pairs={{0,3},{1,2},{2,1},{3,0},{4,7},{5,6},{6,5},{7,4},{8,11},{9,10},{10,... | collective-permute-start | bytes 1277960 | tf_op jit(solution)/shard_map/ppermute | solution.py:55
  392.3 23.2 %collective-permute-start.49 = (bf16[272,768]{1,0:T(8,128)(2,1)}, bf16[272,768]{1,0:T(8,128)(2,1)S(1)}, u32[]{:S(2)}, u32[]{:S(2)}) collective-permute-start(bf16[272,768]{1,0:T(8,128)(2,1)} %bitcast.215), channel_id=1, source_target_pairs={{0,3},{1,2},{2,1},{3,0},{4,7},{5,6},{6,5},{7,4},{8,11},{9,10},{10,... | collective-permute-start | bytes 1253384 | tf_op jit(solution)/shard_map/ppermute | solution.py:55
  394.4 21.4 %collective-permute-start.48 = (bf16[272,768]{1,0:T(8,128)(2,1)S(1)}, bf16[272,768]{1,0:T(8,128)(2,1)S(1)}, u32[]{:S(2)}, u32[]{:S(2)}) collective-permute-start(bf16[272,768]{1,0:T(8,128)(2,1)S(1)} %bitcast.213), channel_id=1, source_target_pairs={{0,1},{1,0},{2,3},{3,2},{4,5},{5,4},{6,7},{7,6},{8,9},{9,8},{10,11... | collective-permute-start | bytes 1253384 | tf_op jit(solution)/shard_map/ppermute | solution.py:55
  394.8 66.5 %collective-permute-start.42 = (bf16[528,1024]{1,0:T(8,128)(2,1)}, bf16[528,1024]{1,0:T(8,128)(2,1)}, u32[]{:S(2)}, u32[]{:S(2)}) collective-permute-start(bf16[528,1024]{1,0:T(8,128)(2,1)} %bitcast.204), channel_id=1, source_target_pairs={{0,3},{1,2},{2,1},{3,0},{4,7},{5,6},{6,5},{7,4},{8,11},{9,10},{10,... | collective-permute-start | bytes 3244040 | tf_op jit(solution)/shard_map/ppermute | solution.py:55
  396.4 65.0 %collective-permute-start.41 = (bf16[528,1024]{1,0:T(8,128)(2,1)}, bf16[528,1024]{1,0:T(8,128)(2,1)}, u32[]{:S(2)}, u32[]{:S(2)}) collective-permute-start(bf16[528,1024]{1,0:T(8,128)(2,1)} %bitcast.202), channel_id=1, source_target_pairs={{0,1},{1,0},{2,3},{3,2},{4,5},{5,4},{6,7},{7,6},{8,9},{9,8},{10,11... | collective-permute-start | bytes 3244040 | tf_op jit(solution)/shard_map/ppermute | solution.py:55
  406.6 55.5 %collective-permute-start.43 = (bf16[528,1024]{1,0:T(8,128)(2,1)S(1)}, bf16[528,1024]{1,0:T(8,128)(2,1)}, u32[]{:S(2)}, u32[]{:S(2)}) collective-permute-start(bf16[528,1024]{1,0:T(8,128)(2,1)S(1)} %bitcast.200), channel_id=1, source_target_pairs={{0,2},{1,3},{2,0},{3,1},{4,6},{5,7},{6,4},{7,5},{8,10},{9,11},{10,... | collective-permute-start | bytes 3244040 | tf_op jit(solution)/shard_map/ppermute | solution.py:55
  415.6 45.8 %collective-permute-start.50 = (bf16[272,768]{1,0:T(8,128)(2,1)S(1)}, bf16[272,768]{1,0:T(8,128)(2,1)S(1)}, u32[]{:S(2)}, u32[]{:S(2)}) collective-permute-start(bf16[272,768]{1,0:T(8,128)(2,1)S(1)} %bitcast.211), channel_id=1, source_target_pairs={{0,2},{1,3},{2,0},{3,1},{4,6},{5,7},{6,4},{7,5},{8,10},{9,11},{10,... | collective-permute-start | bytes 1253384 | tf_op jit(solution)/shard_map/ppermute | solution.py:55
  462.1 24.5 %collective-permute-start.51 = (bf16[416,1152]{1,0:T(8,128)(2,1)}, bf16[416,1152]{1,0:T(8,128)(2,1)}, u32[]{:S(2)}, u32[]{:S(2)}) collective-permute-start(bf16[416,1152]{1,0:T(8,128)(2,1)} %fence.9), channel_id=1, source_target_pairs={{0,1},{1,0},{2,3},{3,2},{4,5},{5,4},{6,7},{7,6},{8,9},{9,8},{10,11... | collective-permute-start | bytes 2875400 | tf_op jit(solution)/shard_map/ppermute | solution.py:55
  462.3 42.1 %collective-permute-start.52 = (bf16[416,1152]{1,0:T(8,128)(2,1)}, bf16[416,1152]{1,0:T(8,128)(2,1)}, u32[]{:S(2)}, u32[]{:S(2)}) collective-permute-start(bf16[416,1152]{1,0:T(8,128)(2,1)} %fence.10), channel_id=1, source_target_pairs={{0,3},{1,2},{2,1},{3,0},{4,7},{5,6},{6,5},{7,4},{8,11},{9,10},{10,... | collective-permute-start | bytes 2875400 | tf_op jit(solution)/shard_map/ppermute | solution.py:55
  464.3 41.8 %collective-permute-start.53 = (bf16[416,1152]{1,0:T(8,128)(2,1)}, bf16[416,1152]{1,0:T(8,128)(2,1)S(1)}, u32[]{:S(2)}, u32[]{:S(2)}) collective-permute-start(bf16[416,1152]{1,0:T(8,128)(2,1)} %fence.11), channel_id=1, source_target_pairs={{0,2},{1,3},{2,0},{3,1},{4,6},{5,7},{6,4},{7,5},{8,10},{9,11},{10,... | collective-permute-start | bytes 2875400 | tf_op jit(solution)/shard_map/ppermute | solution.py:55
  (167 other events, 2032.9 us)
Sparse Core Ops, SparseCore 0:
  311.5 182.1 all-reduce.19

commit v6 on v5

--- a/solution.py
+++ b/solution.py
@@ -242,7 +242,7 @@
     out = lax.dynamic_update_index_in_dim(out, two, ring, 1)
     for step in (1, 3, 2):
         out = lax.dynamic_update_index_in_dim(out, swap(two, step), ring ^ step, 1)
-    return out.reshape((8,) + array.shape), two
+    return out.reshape((8,) + array.shape)
 
 
 def scatter_direct(pieces, index, swap):
@@ -321,9 +321,10 @@
         at = 0
         for _, h in parts:
             prefix.append(rows[i][at : at + HALF_A])
+            at += HALF_A
             if h:
-                action.append(rows[i][at + HALF_A : at + HALF_B, :width])
-            at += 2 * (HALF_A, HALF_B)[h]
+                action.append(rows[i][at : at + ACT_PAD, :width])
+                at += ACT_PAD
     x = join(*prefix).astype(f32)
     low_d = (x * inverse_rms(x) * gain_d).astype(bf16)
     x = join(*action).astype(f32)
@@ -386,7 +387,7 @@
     return product, gate_delta, up_delta, rows_delta.astype(bf16)
 
 
-def feed_kernel(layout, seed_layout, *refs):
+def feed_kernel(layout, *refs):
     arrays = 1 + max(i for parts in layout for i, _ in parts)
     rows_refs, seed_refs, refs = refs[:arrays], refs[arrays : 2 * arrays], refs[2 * arrays :]
     gate_ref, up_ref, down_ref = refs[:3]
@@ -398,19 +399,19 @@
     width = action_gate_ref.shape[0]
     rest = PREF - HALF_A
 
-    def prefix_of(blocks, layout):
+    def prefix_of(blocks):
         parts = []
         for (ia, a), (ib, b) in layout:
             parts += [blocks[ia][a : a + HALF_A], blocks[ib][b : b + rest]]
         return join(*parts)
 
-    def action_of(blocks, layout):
+    def action_of(blocks):
         parts = []
         for _, (ib, b) in layout:
             parts.append(blocks[ib][b + rest : b + HALF_B, :width])
         return join(*parts) if count > 1 else parts[0]
 
-    rows, seed = prefix_of(rows_refs, layout), prefix_of(seed_refs, seed_layout)
+    rows, seed = prefix_of(rows_refs), prefix_of(seed_refs)
     product, gate_delta, up_delta, rows_delta = feed_block(
         rows, seed, gate_ref[...], up_ref[...], down_ref[...], None
     )
@@ -424,7 +425,7 @@
     deltas[:, HIDDEN_PAD + hidden :] = spare
     kept_rows[...] = rows
     kept_seeds[...] = seed
-    rows, seed = action_of(rows_refs, layout), action_of(seed_refs, seed_layout)
+    rows, seed = action_of(rows_refs), action_of(seed_refs)
     product, gate_delta, up_delta, action_rows_delta = feed_block(
         rows,
         seed,
@@ -450,7 +451,7 @@
         ref_b[rest:, width:] = blank
 
 
-def feed(arrays, seeds, weights, layout, seed_layout, base, kept, after):
+def feed(arrays, seeds, weights, layout, base, kept, after):
     count = len(layout)
     width = arrays[0].shape[1]
     hidden = weights[0].shape[0]
@@ -487,7 +488,7 @@
     given = [*arrays, *seeds]
     placed = len(given) + len(weights)
     results = pl.pallas_call(
-        functools.partial(feed_kernel, layout, seed_layout),
+        functools.partial(feed_kernel, layout),
         grid=(1,),
         in_specs=[whole(x) for x in given]
         + [VMEM] * len(weights)
@@ -695,7 +696,7 @@
                 out[base + row : base + row + n, :, columns] = total.astype(bf16)
 
 
-def sum_weights(grads, cuts, columns, place, sent, got, after, before_last):
+def sum_weights(grads, cuts, columns, place, sent, got, after, before_last, last_sent):
     views = [g.reshape(2, 8, -1, 8, g.shape[1]) for g in grads]
     eights = max(row + n for row, n, _, _, _ in cuts)
     params = pltpu.CompilerParams(vmem_limit_bytes=44 * 1024 * 1024)
@@ -726,8 +727,8 @@
         got.append(mp_swap(x, step))
         total = total + got[-1].astype(f32)
     half = 8 * eights
-    last = held(total[half:].astype(bf16), before_last)
-    return (total[:half] + mp_swap(last, 4).astype(f32)).astype(bf16)
+    last_sent.append(held(total[half:].astype(bf16), before_last))
+    return (total[:half] + mp_swap(last_sent[-1], 4).astype(f32)).astype(bf16)
 
 
 def pad_action(rows):
@@ -883,7 +884,7 @@
     action_seed = cotangent_a.astype(f32) * row_share[PREF:]
     seed_block = block_of(prefix_seed.astype(bf16), action_seed.astype(bf16))
 
-    near, two = gather_direct(pack, mp, mp_swap)
+    near = gather_direct(pack, mp, mp_swap)
     last_row = near[:, :, pack.shape[1] - 256 : pack.shape[1] - 48].reshape(8, 1, wide)
     near_d = jnp.concatenate([near[:, :, :wide], last_row], axis=1).reshape(72, wide)
     near_a = near[:, :, wide : pack.shape[1] - 256].reshape(64, -1)
@@ -891,34 +892,40 @@
     kv_a = widen(jnp.concatenate([near_a[:, :640], edge], axis=1), 1024)
     pack_a = join(near_a[:, 640:1664], near_a[:, 1664:2688], kv_a)
     pack_b = join(near_d[:, 640:], near_a[:, 2688 : 2688 + 1024], widen(near_d[:, :640], 1024))
+    arrived = {}
+
+    def note(name):
+        def during(stage, blocks, sends):
+            arrived[name, stage] = blocks
+            arrived[name, "sends", stage] = sends
+            return ()
+
+        return during
+
     own_action = pad_action(action_input[0])
     own_block = block_of(prefix_input[0], own_action)
+    own_block = fence(own_block, near)
     pack = join(pack_a, pack_b)
-    both = join(
-        own_block[:HALF_A], seed_block[:HALF_A], own_block[HALF_A:], seed_block[HALF_A:]
-    )
     gather = relay_stages(pack, pack_a.shape[0], yz_swap)
-    other = relay_stages(both, 2 * HALF_A, mp_swap)
-    other.send((two,))
+    other = relay_stages(own_block, HALF_A, mp_swap)
     gather.send()
+    other.send()
     gather.arrive()
-    sends = gather.send()
     other.arrive()
+    sends = gather.send(other.got)
     other.send(sends)
     gather.arrive()
+    other.arrive()
     sends = gather.send()
-    other.arrive()
     row_sends = other.send(sends)
     pieces = gather.finish()
-    x_rows = seeds = other.finish()
+    x_rows = other.finish()
     cuts = ((0, 16, 8, 768), (1, 17, 9, 640), (0, 0, 16, 1024), (1, 0, 17, 1024))
-    mine = place(pieces, pack_a.shape[0], cuts, yz, (*row_sends, x_rows[6]))
+    mine = place(pieces, pack_a.shape[0], cuts, yz, x_rows[6:])
     theirs = [core_swap(x) for x in mine]
     cuts = ((0, 0, 8, 0, 512), (0, 0, 8, 512, 128), (0, 0, 8, 640, 128))
     cuts += ((1, 0, 9, 0, 512), (1, 0, 9, 512, 128))
-    wkv_a, gains_a, wo_e, wkv_d, gains_d = interleave(mine[:2], theirs[:2], cuts, core, x_rows[7:])
-    cuts = ((0, 0, 8, 0, 1024), (0, 8, 8, 0, 1024), (1, 0, 9, 0, 1024), (1, 9, 8, 0, 1024))
-    wq_a, wo_a, wq_d, wo_m = interleave(mine[2:], theirs[2:], cuts, core)
+    wkv_a, gains_a, wo_e, wkv_d, gains_d = interleave(mine[:2], theirs[:2], cuts, core)
     normed_d, normed_a, keys, values = keys_of(
         x_rows,
         gains_d,
@@ -929,6 +936,10 @@
         key_sin,
         (),
     )
+    seeds = relay_stages(seed_block, HALF_A, mp_swap)
+    seed_sends = seeds.send((keys,))
+    cuts = ((0, 0, 8, 0, 1024), (0, 8, 8, 0, 1024), (1, 0, 9, 0, 1024), (1, 9, 8, 0, 1024))
+    wq_a, wo_a, wq_d, wo_m = interleave(mine[2:], theirs[2:], cuts, core, seed_sends[:1])
     x_d, x_a = prefix_input[0].astype(f32), own_action.astype(f32)
     rms_d, rms_a = inverse_rms(x_d), inverse_rms(x_a)
     queries, context, tops, totals, hidden_d, hidden_a, second_block = attend(
@@ -964,21 +975,22 @@
         nonlocal kept
         where = where_parts(first, len(arrays), (HALF_A, HALF_B))
         layout = tuple((where[k, 0], where[k, 1]) for k in blocks)
-        some = seeds[first : first + len(arrays)]
-        where = where_parts(first, len(arrays), (2 * HALF_A, 2 * HALF_B))
-        skip = lambda k, h: (where[k, h][0], where[k, h][1] + (HALF_A, HALF_B)[h])
-        seed_layout = tuple((skip(k, 0), skip(k, 1)) for k in blocks)
-        done, kept = feed(arrays, some, weights, layout, seed_layout, base, kept, after)
+        some = (seeds.own, *seeds.got)[first : first + len(arrays)]
+        done, kept = feed(arrays, some, weights, layout, base, kept, after)
         results.update(zip(blocks, done))
         return (done[0][0],)
 
     def feed_during(stage, arrays, sends):
+        if stage < 3:
+            seeds.arrive()
+            seeds.send(sends)
         if stage == 3:
             return ()
         first, blocks, base = {1: (0, (0,), 3), 2: (1, (1, 3, 4), 0)}[stage]
         return run(arrays, first, blocks, base, sends)
 
     arrays = relay_gather(second_block, HALF_A, mp_swap, feed_during)
+    seeds.arrive()
     run(arrays[4:], 4, (2, 5, 7, 6), 4, ())
     product_d, deltas_d, rows_d, seeds_d, product_a, deltas_a, rows_a, seeds_a = kept
 
@@ -1063,9 +1075,9 @@
         (16, 9, 0, 0, 1024),
         (25, 8, 0, 0, 1024),
     )
-    qo_sent, kv_sent, got = [], [], []
+    qo_sent, kv_sent, got, last_sent = [], [], [], []
     qo_grads = (q_grad_a, out_grad_a, q_grad_d, out_grad_d)
-    qo = sum_weights(qo_grads, cuts, 1024, here, qo_sent, got, (), grads[:1])
+    qo = sum_weights(qo_grads, cuts, 1024, here, qo_sent, got, (), grads[:1], last_sent)
     kv_grad_d = t_dot(turned_d, kv_rows_d).astype(bf16)
     kv_grad_a = t_dot(turned_a, kv_rows_a).astype(bf16)
     cuts = (
@@ -1082,7 +1094,7 @@
         kv_grad_d,
         second_term_d.astype(bf16),
     )
-    kv = sum_weights(kv_grads, cuts, 768, here, kv_sent, got, qo_sent, grads[:1])
+    kv = sum_weights(kv_grads, cuts, 768, here, kv_sent, got, qo_sent, grads[:1], last_sent)
     kv_a, kv_d = kv[:64], kv[64:, :640]
     qo_a, qo_b = qo[:128], qo[128:]
     kv_other = mp_swap(held(kv_part[BLOCK:].astype(bf16), tuple(kv_sent)), 4)
@@ -1100,7 +1112,7 @@
         out.append(block_of(partial_d[i * PREF : (i + 1) * PREF], mine))
     out_sent = []
     out = ring_scatter(out, mp_swap, tuple(got), out_sent)
-    out = pair_sum(out, mp_swap)
+    out = pair_sum(out, mp_swap, tuple(last_sent))
     prefix_output = (hidden_d + out[:PREF]).astype(bf16)[None]
     action_output = (hidden_a + out[PREF:, :DA])[:ACT].astype(bf16)[None]
 

time: 584 us -> 629 us (1.077)
  local copies, waits for them, and re-layouts: 50.7 us -> 68.2 us
  waiting for transfers between devices: 208 us -> 223 us
    ppermute x44 -> x52, waiting for transfers between devices: 173 us -> 192 us  [mp_swap(): return lax.ppermute(array, 'mp', [(i, i ^ step) for i in range(N_MP)])]
    unnamed x287 -> x371, local copies, waits for them, and re-layouts: 37.7 us -> 52.4 us
    ppermute x44 -> x52, starting transfers between devices: 60.3 us -> 71.9 us  [mp_swap(): return lax.ppermute(array, 'mp', [(i, i ^ step) for i in range(N_MP)])]
    concatenate x16 -> x15, other arithmetic: 11.9 us -> 13.7 us  [join(): return jnp.concatenate(parts, axis=0)]
  transfers between devices with their start and end apart: 63 -> 71, of which waited for: 29 -> 24; matrix products, arithmetic and copies ran while one was open for 19% -> 18% of each run, Pallas kernels for 11% -> 13%
where the time goes in v6:
time: 629 us; the launch traced here: 621 us
  waiting for transfers between devices  223 us (35%)
  Pallas kernels  105 us (17%)
  starting transfers between devices  92.2 us (15%)
  other arithmetic  68.2 us (11%)
  local copies, waits for them, and re-layouts  68.2 us (11%)
  matrix products  46.1 us (7%)
  between operations  17.7 us (3%)
    ppermute x52, waiting for transfers between devices, mp_swap(): return lax.ppermute(array, 'mp', [(i, i ^ step) for i in range(N_MP)])  192 us
    ppermute x52, starting transfers between devices, mp_swap(): return lax.ppermute(array, 'mp', [(i, i ^ step) for i in range(N_MP)])  71.9 us
    unnamed x371, local copies, waits for them, and re-layouts  52.4 us
    pallas_call x3, Pallas kernels, feed(): pl.pallas_call(functools.partial(feed_kernel, layout), grid=(1,), in_spec...  44.3 us
    dot_general x12, matrix products, t_dot(): lax.dot_general(a, b, (((0,), (0,)), ((), ())), preferred_element_type=f32)  32.1 us
    ppermute x18, waiting for transfers between devices, dp_swap(): return lax.ppermute(array, 'dp', [(i, i ^ step) for i in range(16)])  31.3 us
    ppermute x18, starting transfers between devices, dp_swap(): return lax.ppermute(array, 'dp', [(i, i ^ step) for i in range(16)])  20.2 us
    concatenate x15, other arithmetic, join(): return jnp.concatenate(parts, axis=0)  13.7 us
  transfers between devices with their start and end apart: 71, of which 24 were waited for; matrix products, arithmetic and copies ran while one was open for 18% of the time, Pallas kernels for 13%

profile of v6, /device:TPU:0, one launch (start us, length us, event | category | flops | bytes accessed | tf_op | source)
XLA Modules:
  0.0 620.7 jit_solution(8868861988513008152)
XLA Ops:
  23.0 7.4 %collective-permute-done.1 = bf16[2,8,5760]{2,1,0:T(8,128)(2,1)S(1)} collective-permute-done((bf16[2,8,5760]{2,1,0:T(8,128)(2,1)S(1)}, bf16[2,8,5760]{2,1,0:T(8,128)(2,1)S(1)}, u32[]{:S(2)}, u32[]{:S(2)}) %collective-permute-start.1) | collective-permute-done | bytes 184352 | tf_op jit(solution)/shard_map/ppermute | solution.py:55
  47.3 7.7 %collective-permute-done.5.refs_4_.refs_1_.refs_2_ = bf16[208,1152]{1,0:T(8,128)(2,1)S(1)} collective-permute-done((bf16[208,1152]{1,0:T(8,128)(2,1)S(1)}, bf16[208,1152]{1,0:T(8,128)(2,1)S(1)}, u32[]{:S(2)}, u32[]{:S(2)}) %collective-permute-start.5) | collective-permute-done | bytes 479264 | tf_op jit(solution)/shard_map/ppermute | solution.py:55
  56.4 7.6 %collective-permute-done.9.refs_2_ = bf16[400,1024]{1,0:T(8,128)(2,1)S(1)} collective-permute-done((bf16[400,1024]{1,0:T(8,128)(2,1)}, bf16[400,1024]{1,0:T(8,128)(2,1)S(1)}, u32[]{:S(2)}, u32[]{:S(2)}) %collective-permute-start.9) | collective-permute-done | bytes 819232 | tf_op jit(solution)/shard_map/ppermute | solution.py:59
  74.3 13.8 %collective-permute-done.13.refs_0_ = bf16[384,1024]{1,0:T(8,128)(2,1)S(1)} collective-permute-done((bf16[384,1024]{1,0:T(8,128)(2,1)S(1)}, bf16[384,1024]{1,0:T(8,128)(2,1)S(1)}, u32[]{:S(2)}, u32[]{:S(2)}) %collective-permute-start.13) | collective-permute-done | bytes 786464 | tf_op jit(solution)/shard_map/ppermute | solution.py:59
  108.7 4.7 collective-permute-done.15.refs_10_.refs_7_
  118.1 4.3 place.1
  127.7 4.2 multiply_sine_fusion
  137.4 5.8 keys_of.1
  151.5 5.5 interleave.3
  161.1 11.0 %attend.1 = (bf16[832,256]{1,0:T(8,128)(2,1)S(1)}, bf16[208,1024]{1,0:T(8,128)(2,1)S(1)}, f32[832,1]{1,0:T(8,128)S(1)}, f32[832,1]{1,0:T(8,128)S(1)}, f32[192,11...) custom-call(bf16[384,1152]{1,0:T(8,128)(2,1)} %get-tuple-element.152.refs_0_, ...), custom_call_target="tpu_custom_call" | custom-call | flops 2399141888 | bytes 20971520 | tf_op jit(solution)/shard_map/attend/pallas_call | solution.py:562
  183.2 10.1 %feed.3 = (bf16[1536,896]{1,0:T(8,128)(2,1)}, bf16[1536,1792]{1,0:T(8,128)(2,1)}, bf16[1536,1152]{1,0:T(8,128)(2,1)}, bf16[1536,1152]{1,0:T(8,128)(2,1)}, bf16[1...) custom-call(bf16[208,1152]{1,0:T(8,128)(2,1)S(1)} %get-tuple-element, ...), custom_call_target="tpu_custom_call" | custom-call | flops 2078801920 | bytes 12263424 | tf_op jit(solution)/shard_map/feed/pallas_call | solution.py:490
  207.9 15.8 %feed.4 = (bf16[1536,896]{1,0:T(8,128)(2,1)}, bf16[1536,1792]{1,0:T(8,128)(2,1)}, bf16[1536,1152]{1,0:T(8,128)(2,1)}, bf16[1536,1152]{1,0:T(8,128)(2,1)}, bf16[1...) custom-call(bf16[208,1152]{1,0:T(8,128)(2,1)} %collective-permute-do, ...), custom_call_target="tpu_custom_call", output_to_operand_aliasing={{0}: (13, {}), {1}: (14, {}), {2}: (15, {}), {3}: (16, {}),... | custom-call | flops 6236405760 | bytes 12263424 | tf_op jit(solution)/shard_map/feed/pallas_call | solution.py:490
  226.8 3.9 collective-permute-done.38.refs_8_
  233.1 18.4 %feed.5 = (bf16[1536,896]{1,0:T(8,128)(2,1)}, bf16[1536,1792]{1,0:T(8,128)(2,1)}, bf16[1536,1152]{1,0:T(8,128)(2,1)}, bf16[1536,1152]{1,0:T(8,128)(2,1)}, bf16[1...) custom-call(bf16[192,1152]{1,0:T(8,128)(2,1)S(1)} %collective-permut, ...), custom_call_target="tpu_custom_call", output_to_operand_aliasing={{0}: (17, {}), {1}: (18, {}), {2}: (19, {}), {3}: (20, {}),... | custom-call | flops 8315207680 | bytes 12263424 | tf_op jit(solution)/shard_map/feed/pallas_call | solution.py:490
  255.7 11.9 %convolution_convert_fusion = bf16[1792,1152]{1,0:T(8,128)(2,1)} fusion(bf16[1536,1792]{1,0:T(8,128)(2,1)} %get-tuple-element.241, bf16[1536,1152]{1,0:T(8,128)(2,1)} %get-tuple-element.242), kind=kOutput, calls=%fused_computation | convolution fusion | flops 6343852032 | bytes 13172736 | tf_op jit(solution)/shard_map/dot_general | solution.py:764
  267.6 5.2 convolution_convert_fusion.5
  303.1 3.9 collective-permute-done.46.refs_3_
  308.0 36.5 %collective-permute-done.47.refs_4_ = bf16[208,1152]{1,0:T(8,128)(2,1)S(1)} collective-permute-done((bf16[208,1152]{1,0:T(8,128)(2,1)S(1)}, bf16[208,1152]{1,0:T(8,128)(2,1)S(1)}, u32[]{:S(2)}, u32[]{:S(2)}) %collective-permute-start.47) | collective-permute-done | bytes 479264 | tf_op jit(solution)/shard_map/ppermute | solution.py:55
  345.3 12.6 %attend_back.1 = (f32[192,1152]{1,0:T(8,128)}, f32[16,1024]{1,0:T(8,128)S(1)}, bf16[208,1152]{1,0:T(8,128)(2,1)}, bf16[192,1152]{1,0:T(8,128)(2,1)}, bf16[16,102...) custom-call(bf16[96,1152]{1,0:T(8,128)(2,1)S(1)} %copy-done.56, ...), custom_call_target="tpu_custom_call" | custom-call | flops 425984 | bytes 832 | tf_op jit(solution)/shard_map/attend_back/pallas_call | solution.py:651
  366.5 5.6 convolution_convert_fusion.1
  387.5 7.1 %collective-permute-done.53 = bf16[416,512]{1,0:T(8,128)(2,1)} collective-permute-done((bf16[416,512]{1,0:T(8,128)(2,1)}, bf16[416,512]{1,0:T(8,128)(2,1)}, u32[]{:S(2)}, u32[]{:S(2)}) %collective-permute-start.53) | collective-permute-done | bytes 426016 | tf_op jit(solution)/shard_map/ppermute | solution.py:55
  406.0 4.8 near.2
  424.0 32.8 %collective-permute-done.63 = bf16[208,512]{1,0:T(8,128)(2,1)S(1)} collective-permute-done((bf16[208,512]{1,0:T(8,128)(2,1)}, bf16[208,512]{1,0:T(8,128)(2,1)S(1)}, u32[]{:S(2)}, u32[]{:S(2)}) %collective-permute-start.63) | collective-permute-done | bytes 213024 | tf_op jit(solution)/shard_map/ppermute | solution.py:55
  465.8 27.6 %collective-permute-done.58.refs_6_ = bf16[272,768]{1,0:T(8,128)(2,1)S(1)} collective-permute-done((bf16[272,768]{1,0:T(8,128)(2,1)S(1)}, bf16[272,768]{1,0:T(8,128)(2,1)S(1)}, u32[]{:S(2)}, u32[]{:S(2)}) %collective-permute-start.58) | collective-permute-done | bytes 417824 | tf_op jit(solution)/shard_map/ppermute | solution.py:55
  504.2 14.4 %collective-permute-done.59 = bf16[416,1152]{1,0:T(8,128)(2,1)} collective-permute-done((bf16[416,1152]{1,0:T(8,128)(2,1)}, bf16[416,1152]{1,0:T(8,128)(2,1)}, u32[]{:S(2)}, u32[]{:S(2)}) %collective-permute-start.59) | collective-permute-done | bytes 958496 | tf_op jit(solution)/shard_map/ppermute | solution.py:55
  518.6 21.3 %collective-permute-done.60 = bf16[416,1152]{1,0:T(8,128)(2,1)} collective-permute-done((bf16[416,1152]{1,0:T(8,128)(2,1)}, bf16[416,1152]{1,0:T(8,128)(2,1)}, u32[]{:S(2)}, u32[]{:S(2)}) %collective-permute-start.60) | collective-permute-done | bytes 958496 | tf_op jit(solution)/shard_map/ppermute | solution.py:55
  544.0 3.9 slice_convert_fusion
  551.6 4.8 collective-permute-start.64
  558.4 6.8 %fusion.13 = (f32[1,1024,1024]{2,1,0:T(8,128)}, f32[1,1024,1024]{2,1,0:T(8,128)}) fusion(bf16[1024,2048]{1,0:T(8,128)(2,1)} %get-tuple-element.256), kind=kLoop, calls=%fused_computation.30 | loop fusion | flops 2097152 | bytes 12582912 | tf_op jit(solution)/shard_map/broadcast_in_dim | solution.py:1180
  568.5 13.8 %collective-permute-done.62 = bf16[208,1152]{1,0:T(8,128)(2,1)S(1)} collective-permute-done((bf16[208,1152]{1,0:T(8,128)(2,1)}, bf16[208,1152]{1,0:T(8,128)(2,1)S(1)}, u32[]{:S(2)}, u32[]{:S(2)}) %collective-permute-start.62) | collective-permute-done | bytes 479264 | tf_op jit(solution)/shard_map/ppermute | solution.py:55
  591.7 4.0 collective-permute-start.68
  602.0 5.4 collective-permute-done.69
  (666 shorter events, 260.5 us)
Async XLA Ops:
  7.2 536.8 %all-reduce.20.cloned.1.call-start = ((), (), s32[]{:S(2)}) async-start(), calls=%async_computation | async-start | bytes 24969216 | tf_op jit(solution)/shard_map/psum | solution.py:1010
  35.7 28.3 %collective-permute-start.9 = (bf16[400,1024]{1,0:T(8,128)(2,1)}, bf16[400,1024]{1,0:T(8,128)(2,1)S(1)}, u32[]{:S(2)}, u32[]{:S(2)}) collective-permute-start(bf16[400,1024]{1,0:T(8,128)(2,1)} %fusion.89), channel_id=1, source_target_pairs={{0,64},{8,72},{16,80},{24,88},{32,96},{40,104},{48,112},{56,120},{... | collective-permute-start | bytes 2457608 | tf_op jit(solution)/shard_map/ppermute | solution.py:59
  39.3 24.7 %collective-permute-start.8 = (bf16[400,1024]{1,0:T(8,128)(2,1)}, bf16[400,1024]{1,0:T(8,128)(2,1)S(1)}, u32[]{:S(2)}, u32[]{:S(2)}) collective-permute-start(bf16[400,1024]{1,0:T(8,128)(2,1)} %fusion.89), channel_id=1, source_target_pairs={{0,48},{8,56},{16,32},{24,40},{32,16},{40,24},{48,0},{56,8},{64,11... | collective-permute-start | bytes 2457608 | tf_op jit(solution)/shard_map/ppermute | solution.py:59
  66.2 27.4 %collective-permute-start.14 = (bf16[400,1024]{1,0:T(8,128)(2,1)S(1)}, bf16[400,1024]{1,0:T(8,128)(2,1)S(1)}, u32[]{:S(2)}, u32[]{:S(2)}) collective-permute-start(bf16[400,1024]{1,0:T(8,128)(2,1)S(1)} %get-tuple-element.137.refs_4_), channel_id=1, source_target_pairs={{0,16},{8,24},{16,0},{24,8},{32,48},{40,56},{48,32},{56,40},{64,80... | collective-permute-start | bytes 2457608 | tf_op jit(solution)/shard_map/ppermute | solution.py:59
  67.8 40.8 %collective-permute-start.17 = (bf16[416,1024]{1,0:T(8,128)(2,1)}, bf16[416,1024]{1,0:T(8,128)(2,1)}, u32[]{:S(2)}, u32[]{:S(2)}) collective-permute-start(bf16[416,1024]{1,0:T(8,128)(2,1)} %get-tuple-element.138.refs_5_), channel_id=1, source_target_pairs={{0,48},{8,56},{16,32},{24,40},{32,16},{40,24},{48,0},{56,8},{64,11... | collective-permute-start | bytes 2555912 | tf_op jit(solution)/shard_map/ppermute | solution.py:59
  71.1 25.9 %collective-permute-start.10 = (bf16[192,1152]{1,0:T(8,128)(2,1)S(1)}, bf16[192,1152]{1,0:T(8,128)(2,1)S(1)}, u32[]{:S(2)}, u32[]{:S(2)}) collective-permute-start(bf16[192,1152]{1,0:T(8,128)(2,1)S(1)} %get-tuple-element.139), channel_id=1, source_target_pairs={{0,4},{1,5},{2,6},{3,7},{4,0},{5,1},{6,2},{7,3},{8,12},{9,13},{10,... | collective-permute-start | bytes 1327112 | tf_op jit(solution)/shard_map/ppermute | solution.py:55
  72.7 27.8 %collective-permute-start.11 = (bf16[208,1152]{1,0:T(8,128)(2,1)}, bf16[208,1152]{1,0:T(8,128)(2,1)}, u32[]{:S(2)}, u32[]{:S(2)}) collective-permute-start(bf16[208,1152]{1,0:T(8,128)(2,1)} %get-tuple-element.140), channel_id=1, source_target_pairs={{0,1},{1,0},{2,3},{3,2},{4,5},{5,4},{6,7},{7,6},{8,9},{9,8},{10,11... | collective-permute-start | bytes 1437704 | tf_op jit(solution)/shard_map/ppermute | solution.py:55
  122.5 28.0 %collective-permute-start.23 = (bf16[8,17,8,1024]{3,2,1,0:T(8,128)(2,1)}, bf16[8,17,8,1024]{3,2,1,0:T(8,128)(2,1)}, u32[]{:S(2)}, u32[]{:S(2)}) collective-permute-start(bf16[8,17,8,1024]{3,2,1,0:T(8,128)(2,1)} %get-tuple-element.155.refs_1_), channel_id=1, source_target_pairs={{0,8},{8,0},{16,24},{24,16},{32,40},{40,32},{48,56},{56,48},{64,72... | collective-permute-start | bytes 6684680 | tf_op jit(solution)/shard_map/ppermute | solution.py:59
  123.5 27.0 %collective-permute-start.22 = (bf16[8,16,8,1024]{3,2,1,0:T(8,128)(2,1)}, bf16[8,16,8,1024]{3,2,1,0:T(8,128)(2,1)}, u32[]{:S(2)}, u32[]{:S(2)}) collective-permute-start(bf16[8,16,8,1024]{3,2,1,0:T(8,128)(2,1)} %get-tuple-element.154.refs_0_), channel_id=1, source_target_pairs={{0,8},{8,0},{16,24},{24,16},{32,40},{40,32},{48,56},{56,48},{64,72... | collective-permute-start | bytes 6291464 | tf_op jit(solution)/shard_map/ppermute | solution.py:59
  145.0 30.3 %collective-permute-start.32 = (bf16[208,1152]{1,0:T(8,128)(2,1)}, bf16[208,1152]{1,0:T(8,128)(2,1)S(1)}, u32[]{:S(2)}, u32[]{:S(2)}) collective-permute-start(bf16[208,1152]{1,0:T(8,128)(2,1)} %fence.11.refs_4_.refs_1_), channel_id=1, source_target_pairs={{0,4},{1,5},{2,6},{3,7},{4,0},{5,1},{6,2},{7,3},{8,12},{9,13},{10,... | collective-permute-start | bytes 1437704 | tf_op jit(solution)/shard_map/ppermute | solution.py:55
  145.8 31.3 %collective-permute-start.31 = (bf16[208,1152]{1,0:T(8,128)(2,1)}, bf16[208,1152]{1,0:T(8,128)(2,1)S(1)}, u32[]{:S(2)}, u32[]{:S(2)}) collective-permute-start(bf16[208,1152]{1,0:T(8,128)(2,1)} %fence.11.refs_4_.refs_1_), channel_id=1, source_target_pairs={{0,3},{1,2},{2,1},{3,0},{4,7},{5,6},{6,5},{7,4},{8,11},{9,10},{10,... | collective-permute-start | bytes 1437704 | tf_op jit(solution)/shard_map/ppermute | solution.py:55
  148.7 28.4 %collective-permute-start.30 = (bf16[208,1152]{1,0:T(8,128)(2,1)}, bf16[208,1152]{1,0:T(8,128)(2,1)S(1)}, u32[]{:S(2)}, u32[]{:S(2)}) collective-permute-start(bf16[208,1152]{1,0:T(8,128)(2,1)} %fence.11.refs_4_.refs_1_), channel_id=1, source_target_pairs={{0,1},{1,0},{2,3},{3,2},{4,5},{5,4},{6,7},{7,6},{8,9},{9,8},{10,11... | collective-permute-start | bytes 1437704 | tf_op jit(solution)/shard_map/ppermute | solution.py:55
  174.6 23.9 %collective-permute-start.25 = (bf16[208,1152]{1,0:T(8,128)(2,1)S(1)}, bf16[208,1152]{1,0:T(8,128)(2,1)}, u32[]{:S(2)}, u32[]{:S(2)}) collective-permute-start(bf16[208,1152]{1,0:T(8,128)(2,1)S(1)} %get-tuple-element.164.refs_0_.refs_9_.refs_3_), channel_id=1, source_target_pairs={{0,3},{1,2},{2,1},{3,0},{4,7},{5,6},{6,5},{7,4},{8,11},{9,10},{10,... | collective-permute-start | bytes 1437704 | tf_op jit(solution)/shard_map/ppermute | solution.py:55
  179.8 24.1 %collective-permute-start.36 = (bf16[208,1152]{1,0:T(8,128)(2,1)}, bf16[208,1152]{1,0:T(8,128)(2,1)}, u32[]{:S(2)}, u32[]{:S(2)}) collective-permute-start(bf16[208,1152]{1,0:T(8,128)(2,1)} %get-tuple-element.181), channel_id=1, source_target_pairs={{0,1},{1,0},{2,3},{3,2},{4,5},{5,4},{6,7},{7,6},{8,9},{9,8},{10,11... | collective-permute-start | bytes 1437704 | tf_op jit(solution)/shard_map/ppermute | solution.py:55
  195.6 29.0 %collective-permute-start.37 = (bf16[224,1152]{1,0:T(8,128)(2,1)S(1)}, bf16[224,1152]{1,0:T(8,128)(2,1)S(1)}, u32[]{:S(2)}, u32[]{:S(2)}) collective-permute-start(bf16[224,1152]{1,0:T(8,128)(2,1)S(1)} %copy-done.92), channel_id=1, source_target_pairs={{0,3},{1,2},{2,1},{3,0},{4,7},{5,6},{6,5},{7,4},{8,11},{9,10},{10,... | collective-permute-start | bytes 1548296 | tf_op jit(solution)/shard_map/ppermute | solution.py:55
  203.2 27.5 %collective-permute-start.29 = (bf16[224,1152]{1,0:T(8,128)(2,1)S(1)}, bf16[224,1152]{1,0:T(8,128)(2,1)S(1)}, u32[]{:S(2)}, u32[]{:S(2)}) collective-permute-start(bf16[224,1152]{1,0:T(8,128)(2,1)S(1)} %get-tuple-element.168.refs_23_.refs_4_), channel_id=1, source_target_pairs={{0,3},{1,2},{2,1},{3,0},{4,7},{5,6},{6,5},{7,4},{8,11},{9,10},{10,... | collective-permute-start | bytes 1548296 | tf_op jit(solution)/shard_map/ppermute | solution.py:55
  205.1 25.6 %collective-permute-start.39 = (bf16[112,1152]{1,0:T(8,128)(2,1)S(1)}, bf16[112,1152]{1,0:T(8,128)(2,1)S(1)}, u32[]{:S(2)}, u32[]{:S(2)}) collective-permute-start(bf16[112,1152]{1,0:T(8,128)(2,1)S(1)} %get-tuple-element.184), channel_id=1, source_target_pairs={{0,3},{1,2},{2,1},{3,0},{4,7},{5,6},{6,5},{7,4},{8,11},{9,10},{10,... | collective-permute-start | bytes 774152 | tf_op jit(solution)/shard_map/ppermute | solution.py:55
  254.1 29.8 %collective-permute-start.42 = (bf16[224,1152]{1,0:T(8,128)(2,1)S(1)}, bf16[224,1152]{1,0:T(8,128)(2,1)S(1)}, u32[]{:S(2)}, u32[]{:S(2)}) collective-permute-start(bf16[224,1152]{1,0:T(8,128)(2,1)S(1)} %pad_maximum_fusion.1), channel_id=1, source_target_pairs={{0,3},{1,2},{2,1},{3,0},{4,7},{5,6},{6,5},{7,4},{8,11},{9,10},{10,... | collective-permute-start | bytes 1548296 | tf_op jit(solution)/shard_map/ppermute | solution.py:55
  299.3 45.1 %collective-permute-start.47 = (bf16[208,1152]{1,0:T(8,128)(2,1)S(1)}, bf16[208,1152]{1,0:T(8,128)(2,1)S(1)}, u32[]{:S(2)}, u32[]{:S(2)}) collective-permute-start(bf16[208,1152]{1,0:T(8,128)(2,1)S(1)} %copy-done.122), channel_id=1, source_target_pairs={{0,4},{1,5},{2,6},{3,7},{4,0},{5,1},{6,2},{7,3},{8,12},{9,13},{10,... | collective-permute-start | bytes 1437704 | tf_op jit(solution)/shard_map/ppermute | solution.py:55
  365.1 40.7 %collective-permute-start.48 = (bf16[8,33,8,1024]{3,2,1,0:T(8,128)(2,1)}, bf16[8,33,8,1024]{3,2,1,0:T(8,128)(2,1)}, u32[]{:S(2)}, u32[]{:S(2)}) collective-permute-start(bf16[8,33,8,1024]{3,2,1,0:T(8,128)(2,1)} %theirs.2), channel_id=1, source_target_pairs={{0,8},{8,0},{16,24},{24,16},{32,40},{40,32},{48,56},{56,48},{64,72... | collective-permute-start | bytes 12976136 | tf_op jit(solution)/shard_map/ppermute | solution.py:59
  416.9 39.9 %collective-permute-start.63 = (bf16[208,512]{1,0:T(8,128)(2,1)}, bf16[208,512]{1,0:T(8,128)(2,1)S(1)}, u32[]{:S(2)}, u32[]{:S(2)}) collective-permute-start(bf16[208,512]{1,0:T(8,128)(2,1)} %fence.18), channel_id=1, source_target_pairs={{0,4},{1,5},{2,6},{3,7},{4,0},{5,1},{6,2},{7,3},{8,12},{9,13},{10,... | collective-permute-start | bytes 638984 | tf_op jit(solution)/shard_map/ppermute | solution.py:55
  419.3 44.7 %collective-permute-start.57 = (bf16[272,768]{1,0:T(8,128)(2,1)}, bf16[272,768]{1,0:T(8,128)(2,1)S(1)}, u32[]{:S(2)}, u32[]{:S(2)}) collective-permute-start(bf16[272,768]{1,0:T(8,128)(2,1)} %bitcast.217), channel_id=1, source_target_pairs={{0,3},{1,2},{2,1},{3,0},{4,7},{5,6},{6,5},{7,4},{8,11},{9,10},{10,... | collective-permute-start | bytes 1253384 | tf_op jit(solution)/shard_map/ppermute | solution.py:55
  421.4 44.4 %collective-permute-start.56 = (bf16[272,768]{1,0:T(8,128)(2,1)S(1)}, bf16[272,768]{1,0:T(8,128)(2,1)S(1)}, u32[]{:S(2)}, u32[]{:S(2)}) collective-permute-start(bf16[272,768]{1,0:T(8,128)(2,1)S(1)} %bitcast.215), channel_id=1, source_target_pairs={{0,1},{1,0},{2,3},{3,2},{4,5},{5,4},{6,7},{7,6},{8,9},{9,8},{10,11... | collective-permute-start | bytes 1253384 | tf_op jit(solution)/shard_map/ppermute | solution.py:55
  422.6 70.8 %collective-permute-start.50 = (bf16[528,1024]{1,0:T(8,128)(2,1)}, bf16[528,1024]{1,0:T(8,128)(2,1)}, u32[]{:S(2)}, u32[]{:S(2)}) collective-permute-start(bf16[528,1024]{1,0:T(8,128)(2,1)} %bitcast.207), channel_id=1, source_target_pairs={{0,3},{1,2},{2,1},{3,0},{4,7},{5,6},{6,5},{7,4},{8,11},{9,10},{10,... | collective-permute-start | bytes 3244040 | tf_op jit(solution)/shard_map/ppermute | solution.py:55
  423.9 69.4 %collective-permute-start.49 = (bf16[528,1024]{1,0:T(8,128)(2,1)}, bf16[528,1024]{1,0:T(8,128)(2,1)}, u32[]{:S(2)}, u32[]{:S(2)}) collective-permute-start(bf16[528,1024]{1,0:T(8,128)(2,1)} %bitcast.205), channel_id=1, source_target_pairs={{0,1},{1,0},{2,3},{3,2},{4,5},{5,4},{6,7},{7,6},{8,9},{9,8},{10,11... | collective-permute-start | bytes 3244040 | tf_op jit(solution)/shard_map/ppermute | solution.py:55
  456.8 37.4 %collective-permute-start.51 = (bf16[528,1024]{1,0:T(8,128)(2,1)S(1)}, bf16[528,1024]{1,0:T(8,128)(2,1)}, u32[]{:S(2)}, u32[]{:S(2)}) collective-permute-start(bf16[528,1024]{1,0:T(8,128)(2,1)S(1)} %bitcast.203), channel_id=1, source_target_pairs={{0,2},{1,3},{2,0},{3,1},{4,6},{5,7},{6,4},{7,5},{8,10},{9,11},{10,... | collective-permute-start | bytes 3244040 | tf_op jit(solution)/shard_map/ppermute | solution.py:55
  464.1 29.3 %collective-permute-start.58 = (bf16[272,768]{1,0:T(8,128)(2,1)S(1)}, bf16[272,768]{1,0:T(8,128)(2,1)S(1)}, u32[]{:S(2)}, u32[]{:S(2)}) collective-permute-start(bf16[272,768]{1,0:T(8,128)(2,1)S(1)} %bitcast.213), channel_id=1, source_target_pairs={{0,2},{1,3},{2,0},{3,1},{4,6},{5,7},{6,4},{7,5},{8,10},{9,11},{10,... | collective-permute-start | bytes 1253384 | tf_op jit(solution)/shard_map/ppermute | solution.py:55
  494.1 24.5 %collective-permute-start.59 = (bf16[416,1152]{1,0:T(8,128)(2,1)}, bf16[416,1152]{1,0:T(8,128)(2,1)}, u32[]{:S(2)}, u32[]{:S(2)}) collective-permute-start(bf16[416,1152]{1,0:T(8,128)(2,1)} %fence.12), channel_id=1, source_target_pairs={{0,1},{1,0},{2,3},{3,2},{4,5},{5,4},{6,7},{7,6},{8,9},{9,8},{10,11... | collective-permute-start | bytes 2875400 | tf_op jit(solution)/shard_map/ppermute | solution.py:55
  495.6 44.3 %collective-permute-start.60 = (bf16[416,1152]{1,0:T(8,128)(2,1)}, bf16[416,1152]{1,0:T(8,128)(2,1)}, u32[]{:S(2)}, u32[]{:S(2)}) collective-permute-start(bf16[416,1152]{1,0:T(8,128)(2,1)} %fence.13), channel_id=1, source_target_pairs={{0,3},{1,2},{2,1},{3,0},{4,7},{5,6},{6,5},{7,4},{8,11},{9,10},{10,... | collective-permute-start | bytes 2875400 | tf_op jit(solution)/shard_map/ppermute | solution.py:55
  497.7 42.2 %collective-permute-start.61 = (bf16[416,1152]{1,0:T(8,128)(2,1)}, bf16[416,1152]{1,0:T(8,128)(2,1)S(1)}, u32[]{:S(2)}, u32[]{:S(2)}) collective-permute-start(bf16[416,1152]{1,0:T(8,128)(2,1)} %fence.14), channel_id=1, source_target_pairs={{0,2},{1,3},{2,0},{3,1},{4,6},{5,7},{6,4},{7,5},{8,10},{9,11},{10,... | collective-permute-start | bytes 2875400 | tf_op jit(solution)/shard_map/ppermute | solution.py:55
  556.4 25.9 %collective-permute-start.65 = (bf16[264,1024]{1,0:T(8,128)(2,1)}, bf16[264,1024]{1,0:T(8,128)(2,1)}, u32[]{:S(2)}, u32[]{:S(2)}) collective-permute-start(bf16[264,1024]{1,0:T(8,128)(2,1)} %fence.15.refs_1_), channel_id=1, source_target_pairs={{0,4},{1,5},{2,6},{3,7},{4,0},{5,1},{6,2},{7,3},{8,12},{9,13},{10,... | collective-permute-start | bytes 1622024 | tf_op jit(solution)/shard_map/ppermute | solution.py:55
  556.5 25.8 %collective-permute-start.62 = (bf16[208,1152]{1,0:T(8,128)(2,1)}, bf16[208,1152]{1,0:T(8,128)(2,1)S(1)}, u32[]{:S(2)}, u32[]{:S(2)}) collective-permute-start(bf16[208,1152]{1,0:T(8,128)(2,1)} %fence.17), channel_id=1, source_target_pairs={{0,4},{1,5},{2,6},{3,7},{4,0},{5,1},{6,2},{7,3},{8,12},{9,13},{10,... | collective-permute-start | bytes 1437704 | tf_op jit(solution)/shard_map/ppermute | solution.py:55
  (216 other events, 2441.6 us)
Sparse Core Ops, SparseCore 0:
  285.9 178.9 all-reduce.19

commit v7 on v3

--- a/solution.py
+++ b/solution.py
@@ -182,17 +182,19 @@
     return total_a, total_b
 
 
-def ring_scatter(pieces, swap, hold=None, sent=None):
-    n = pieces[0].shape[0]
-    hold = hold or {}
+def ring_scatter(pieces, swap, after, sent):
     near = [join(pieces[j], pieces[j ^ 4]) for j in range(4)]
-    near[1:] = [held(x, hold.get(1, ())) for x in near[1:]]
-    if sent is not None:
-        sent += near[1:]
+    near[1:] = [held(x, after) for x in near[1:]]
+    sent += near[1:]
     total = near[0].astype(f32)
     for j in (1, 3, 2):
         total = total + swap(near[j], j).astype(f32)
-    return total[:n] + swap(held(total[n:].astype(bf16), hold.get(2, ())), 4).astype(f32)
+    return total
+
+
+def pair_sum(total, swap, after=()):
+    half = total.shape[0] // 2
+    return total[:half] + swap(held(total[half:].astype(bf16), after), 4).astype(f32)
 
 
 def gather_direct(array, index, swap):
@@ -587,13 +589,15 @@
         extra += half * ACT_PAD
 
 
-def attend_back(*given):
+def attend_back(*given, after):
     hidden_d, hidden_a = given[5:7]
     width_d, width_a = hidden_d.shape[1], hidden_a.shape[1]
     shape = jax.ShapeDtypeStruct
     stacked = HEADS * BLOCK
     outs = pl.pallas_call(
         attend_back_kernel,
+        in_specs=[VMEM] * len(given) + [ANY] * len(after),
+        out_specs=[VMEM] * (6 + len(PARTS)),
         out_shape=[
             shape((PREF, width_d), f32),
             shape((ACT_PAD, width_a), f32),
@@ -608,7 +612,7 @@
             flops=2 * BLOCK * HEADS * HD, bytes_accessed=4 * BLOCK, transcendentals=stacked
         ),
         name="attend_back",
-    )(*given)
+    )(*given, *after)
     kv_deltas = dict(zip(PARTS, outs[6:]))
     pa = {k: kv_deltas[k, 0] for k in range(8)}
     pb = {k: kv_deltas[k, 1] for k in range(8)}
@@ -638,7 +642,7 @@
                 out[base + row : base + row + n, :, columns] = total.astype(bf16)
 
 
-def sum_weights(grads, cuts, columns, place, sent, got, after, before_last):
+def sum_weights(grads, cuts, columns, place, sent, got, after, before_last, last_sent):
     views = [g.reshape(2, 8, -1, 8, g.shape[1]) for g in grads]
     eights = max(row + n for row, n, _, _, _ in cuts)
     params = pltpu.CompilerParams(vmem_limit_bytes=44 * 1024 * 1024)
@@ -669,8 +673,8 @@
         got.append(mp_swap(x, step))
         total = total + got[-1].astype(f32)
     half = 8 * eights
-    last = held(total[half:].astype(bf16), before_last)
-    return (total[:half] + mp_swap(last, 4).astype(f32)).astype(bf16)
+    last_sent.append(held(total[half:].astype(bf16), before_last))
+    return (total[:half] + mp_swap(last_sent[-1], 4).astype(f32)).astype(bf16)
 
 
 def pad_action(rows):
@@ -942,7 +946,10 @@
     )
     hidden = prefix_down.shape[0]
     grads = tuple(g.astype(bf16) for g in grads)
-    after_grads = tuple(grads)
+    pa = {k: v[0] for k, v in results.items()}
+    pb = {k: v[1] for k, v in results.items()}
+    delta_pieces = relay_scatter(pa, pb, mp_swap)
+    grads = grads[:3] + (fence(grads[3], *delta_pieces[2:]),)
     grads = tuple(lax.psum(g, "dp") for g in grads)
     finished = (
         grads[0][:hidden].astype(f32),
@@ -953,9 +960,6 @@
         grads[3].astype(f32),
     )
 
-    pa = {k: v[0] for k, v in results.items()}
-    pb = {k: v[1] for k, v in results.items()}
-    delta_pieces = relay_scatter(pa, pb, mp_swap)
     (hidden_delta_d, hidden_delta_a, low, terms_d, terms_a, query_delta), pa, pb = attend_back(
         *delta_pieces,
         hidden_d,
@@ -977,6 +981,7 @@
         key_codes,
         keys,
         values,
+        after=(),
     )
     low_d, low_a = low[:PREF], low[PREF:, :DA]
 
@@ -1013,9 +1018,9 @@
         (16, 9, 0, 0, 1024),
         (25, 8, 0, 0, 1024),
     )
-    qo_sent, kv_sent, kv_got = [], [], []
+    qo_sent, kv_sent, got, last_sent = [], [], [], []
     qo_grads = (q_grad_a, out_grad_a, q_grad_d, out_grad_d)
-    qo = sum_weights(qo_grads, cuts, 1024, place, qo_sent, [], (), grads[:1])
+    qo = sum_weights(qo_grads, cuts, 1024, place, qo_sent, got, (), (), last_sent)
     kv_grad_d = t_dot(turned_d, kv_rows_d).astype(bf16)
     kv_grad_a = t_dot(turned_a, kv_rows_a).astype(bf16)
     cuts = (
@@ -1032,16 +1037,15 @@
         kv_grad_d,
         second_term_d.astype(bf16),
     )
-    kv = sum_weights(kv_grads, cuts, 768, place, kv_sent, kv_got, qo_sent, grads[:1])
+    kv = sum_weights(kv_grads, cuts, 768, place, kv_sent, got, qo_sent, grads[:1], last_sent)
     kv_a, kv_d = kv[:64], kv[64:, :640]
     qo_a, qo_b = qo[:128], qo[128:]
-    kv_other = mp_swap(held(kv_part[BLOCK:].astype(bf16), tuple(kv_sent)), 4)
+    kv_other = mp_swap(held(kv_part[BLOCK:].astype(bf16), (*kv_sent, grads[0])), 4)
     kv_sum = kv_part[:BLOCK] + kv_other.astype(f32)
     kv_raw_delta = jnp.concatenate(
         [unrotate(kv_sum[:, :HD], own_cos, own_sin), kv_sum[:, HD:]], axis=1
     ).astype(bf16)
 
-    product_d = fence(product_d, kv_sent[0])
     partial_d = dot(product_d[:, :hidden], prefix_down).astype(bf16)
     partial_a = dot(product_a, action_down[0]).astype(bf16)
     out = []
@@ -1049,7 +1053,9 @@
         i = (1, 3, 4, 0, 2, 5, 7, 6).index(k)
         mine = partial_a[i * ACT_PAD : (i + 1) * ACT_PAD]
         out.append(block_of(partial_d[i * PREF : (i + 1) * PREF], mine))
-    out = ring_scatter(out, mp_swap, {1: tuple(kv_got)})
+    out_sent = []
+    out = ring_scatter(out, mp_swap, tuple(got), out_sent)
+    out = pair_sum(out, mp_swap, tuple(last_sent))
     prefix_output = (hidden_d + out[:PREF]).astype(bf16)[None]
     action_output = (hidden_a + out[PREF:, :DA])[:ACT].astype(bf16)[None]
 
@@ -1065,7 +1071,7 @@
         ],
         axis=2,
     )
-    last = scatter_direct(fence(last, *finished), yz, yz_swap)
+    last = scatter_direct(last, yz, yz_swap)
     ninth = last[:, last.shape[1] - 256 : last.shape[1] - 48].reshape(1, wide)
     grads_d = join(last[:, :wide], ninth)
     grads_a = last[:, wide : last.shape[1] - 256]

time: 563 us -> 569 us (1.011)
  waiting for transfers between devices: 151 us -> 181 us
  other arithmetic: 77.8 us -> 65.7 us
  matrix products: 55.4 us -> 45.4 us
  local copies, waits for them, and re-layouts: 48.7 us -> 56.7 us
  starting transfers between devices: 96.8 us -> 90.4 us
    ppermute x52, waiting for transfers between devices: 130 us -> 157 us  [mp_swap(): return lax.ppermute(array, 'mp', [(i, i ^ step) for i in range(N_MP)])]
    dot_general x5, matrix products: 14.9 us -> 8.31 us  [dot(): return jnp.dot(a, b, preferred_element_type=f32)]
    unnamed x335 -> x349, local copies, waits for them, and re-layouts: 33.2 us -> 39.7 us
  transfers between devices with their start and end apart: 76 -> 76, of which waited for: 26 -> 20; matrix products, arithmetic and copies ran while one was open for 23% -> 21% of each run, Pallas kernels for 16% -> 15%
where the time goes in v7:
time: 569 us; the launch traced here: 558 us
  waiting for transfers between devices  181 us (32%)
  Pallas kernels  102 us (18%)
  starting transfers between devices  90.4 us (16%)
  other arithmetic  65.7 us (12%)
  local copies, waits for them, and re-layouts  56.7 us (10%)
  matrix products  45.4 us (8%)
  between operations  17.7 us (3%)
    ppermute x52, waiting for transfers between devices, mp_swap(): return lax.ppermute(array, 'mp', [(i, i ^ step) for i in range(N_MP)])  157 us
    ppermute x52, starting transfers between devices, mp_swap(): return lax.ppermute(array, 'mp', [(i, i ^ step) for i in range(N_MP)])  67.9 us
    pallas_call x3, Pallas kernels, feed(): pl.pallas_call(functools.partial(feed_kernel, layout), grid=(1,), in_spec...  44.2 us
    unnamed x349, local copies, waits for them, and re-layouts  39.7 us
    dot_general x12, matrix products, t_dot(): lax.dot_general(a, b, (((0,), (0,)), ((), ())), preferred_element_type=f32)  31.4 us
    ppermute x23, waiting for transfers between devices, dp_swap(): return lax.ppermute(array, 'dp', [(i, i ^ step) for i in range(16)])  24 us
    ppermute x23, starting transfers between devices, dp_swap(): return lax.ppermute(array, 'dp', [(i, i ^ step) for i in range(16)])  22.4 us
    pallas_call x1, Pallas kernels, attend_back(): pl.pallas_call(attend_back_kernel, in_specs=[VMEM] * len(given) + [ANY] *...  13.1 us
  transfers between devices with their start and end apart: 76, of which 20 were waited for; matrix products, arithmetic and copies ran while one was open for 21% of the time, Pallas kernels for 15%

profile of v7, /device:TPU:0, one launch (start us, length us, event | category | flops | bytes accessed | tf_op | source)
XLA Modules:
  0.0 558.2 jit_solution(17330088145835487270)
XLA Ops:
  23.0 7.4 %collective-permute-done.1 = bf16[2,8,5760]{2,1,0:T(8,128)(2,1)S(1)} collective-permute-done((bf16[2,8,5760]{2,1,0:T(8,128)(2,1)S(1)}, bf16[2,8,5760]{2,1,0:T(8,128)(2,1)S(1)}, u32[]{:S(2)}, u32[]{:S(2)}) %collective-permute-start.1) | collective-permute-done | bytes 184352 | tf_op jit(solution)/shard_map/ppermute | solution.py:55
  32.5 3.7 collective-permute-start.14
  41.7 4.1 collective-permute-done.6.refs_2_.refs_5_.refs_3_
  47.2 4.8 collective-permute-done.5.refs_1_.refs_4_.refs_2_
  52.0 4.3 collective-permute-done.4.refs_0_.refs_3_.refs_1_
  56.3 7.6 %collective-permute-done.14.refs_2_ = bf16[400,1024]{1,0:T(8,128)(2,1)S(1)} collective-permute-done((bf16[400,1024]{1,0:T(8,128)(2,1)S(1)}, bf16[400,1024]{1,0:T(8,128)(2,1)S(1)}, u32[]{:S(2)}, u32[]{:S(2)}) %collective-permute-start.14) | collective-permute-done | bytes 819232 | tf_op jit(solution)/shard_map/ppermute | solution.py:59
  75.6 19.8 %collective-permute-done.7.refs_0_.refs_2_.refs_4_ = bf16[192,1152]{1,0:T(8,128)(2,1)S(1)} collective-permute-done((bf16[192,1152]{1,0:T(8,128)(2,1)S(1)}, bf16[192,1152]{1,0:T(8,128)(2,1)S(1)}, u32[]{:S(2)}, u32[]{:S(2)}) %collective-permute-start.7) | collective-permute-done | bytes 442400 | tf_op jit(solution)/shard_map/ppermute | solution.py:55
  109.9 11.4 %collective-permute-done.17 = bf16[416,1024]{1,0:T(8,128)(2,1)} collective-permute-done((bf16[416,1024]{1,0:T(8,128)(2,1)}, bf16[416,1024]{1,0:T(8,128)(2,1)}, u32[]{:S(2)}, u32[]{:S(2)}) %collective-permute-start.17) | collective-permute-done | bytes 852000 | tf_op jit(solution)/shard_map/ppermute | solution.py:59
  124.5 5.0 collective-permute-done.19
  129.5 4.2 multiply_sine_fusion
  154.9 8.0 %assemble.1 = (bf16[8,2,8,8,1024]{4,3,2,1,0:T(8,128)(2,1)}, bf16[8,2,8,8,1024]{4,3,2,1,0:T(8,128)(2,1)}, bf16[8,2,8,8,512]{4,3,2,1,0:T(8,128)(2,1)}, bf16[8,2,8,...) custom-call(s32[2]{0:T(128)S(1)} %pad_add_fusion.2.place_ref, ...), custom_call_target="tpu_custom_call" | custom-call | tf_op jit(solution)/shard_map/assemble/pallas_call | solution.py:242
  165.1 6.3 %keys_of.1 = (bf16[384,1152]{1,0:T(8,128)(2,1)}, bf16[32,1024]{1,0:T(8,128)(2,1)S(1)}, bf16[1664,256]{1,0:T(8,128)(2,1)}, bf16[1664,256]{1,0:T(8,128)(2,1)}) custom-call(bf16[208,1152]{1,0:T(8,128)(2,1)S(1)} %copy-done.10, bf16[208,1152]{1,0:T(8,128)(2,1)S(1)} %collective-permute-done.4.refs_0_.refs_3_.refs_1_, ...), custom_call_target="tpu_custom_call" | custom-call | flops 1962934272 | bytes 8388608 | tf_op jit(solution)/shard_map/keys_of/pallas_call | solution.py:292
  171.5 11.3 %attend.1 = (bf16[832,256]{1,0:T(8,128)(2,1)S(1)}, bf16[208,1024]{1,0:T(8,128)(2,1)S(1)}, f32[832,1]{1,0:T(8,128)S(1)}, f32[832,1]{1,0:T(8,128)S(1)}, f32[192,11...) custom-call(bf16[384,1152]{1,0:T(8,128)(2,1)} %get-tuple-element.149.refs_0_, ...), custom_call_target="tpu_custom_call" | custom-call | flops 2399141888 | bytes 20971520 | tf_op jit(solution)/shard_map/attend/pallas_call | solution.py:508
  194.4 10.0 %feed.3 = (bf16[1536,896]{1,0:T(8,128)(2,1)}, bf16[1536,1792]{1,0:T(8,128)(2,1)}, bf16[1536,1152]{1,0:T(8,128)(2,1)}, bf16[1536,1152]{1,0:T(8,128)(2,1)}, bf16[1...) custom-call(bf16[208,1152]{1,0:T(8,128)(2,1)S(1)} %copy-done.11, ...), custom_call_target="tpu_custom_call" | custom-call | flops 2078801920 | bytes 12263424 | tf_op jit(solution)/shard_map/feed/pallas_call | solution.py:436
  211.2 15.7 %feed.4 = (bf16[1536,896]{1,0:T(8,128)(2,1)}, bf16[1536,1792]{1,0:T(8,128)(2,1)}, bf16[1536,1152]{1,0:T(8,128)(2,1)}, bf16[1536,1152]{1,0:T(8,128)(2,1)}, bf16[1...) custom-call(bf16[208,1152]{1,0:T(8,128)(2,1)} %collective-permute-do, ...), custom_call_target="tpu_custom_call", output_to_operand_aliasing={{0}: (13, {}), {1}: (14, {}), {2}: (15, {}), {3}: (16, {}),... | custom-call | flops 6236405760 | bytes 12263424 | tf_op jit(solution)/shard_map/feed/pallas_call | solution.py:436
  230.0 4.2 collective-permute-done.44.refs_8_
  236.6 18.5 %feed.5 = (bf16[1536,896]{1,0:T(8,128)(2,1)}, bf16[1536,1792]{1,0:T(8,128)(2,1)}, bf16[1536,1152]{1,0:T(8,128)(2,1)}, bf16[1536,1152]{1,0:T(8,128)(2,1)}, bf16[1...) custom-call(bf16[192,1152]{1,0:T(8,128)(2,1)S(1)} %collective-permut, ...), custom_call_target="tpu_custom_call", output_to_operand_aliasing={{0}: (17, {}), {1}: (18, {}), {2}: (19, {}), {3}: (20, {}),... | custom-call | flops 8315207680 | bytes 12263424 | tf_op jit(solution)/shard_map/feed/pallas_call | solution.py:436
  259.2 11.9 %convolution_convert_fusion = bf16[1792,1152]{1,0:T(8,128)(2,1)} fusion(bf16[1536,1792]{1,0:T(8,128)(2,1)} %get-tuple-element.234, bf16[1536,1152]{1,0:T(8,128)(2,1)} %get-tuple-element.235), kind=kOutput, calls=%fused_computation | convolution fusion | flops 6343852032 | bytes 13172736 | tf_op jit(solution)/shard_map/dot_general | solution.py:710
  273.6 5.2 convolution_convert_fusion.5
  282.7 3.6 collective-permute-start.51
  303.8 13.1 %attend_back.1 = (f32[192,1152]{1,0:T(8,128)}, f32[16,1024]{1,0:T(8,128)S(1)}, bf16[208,1152]{1,0:T(8,128)(2,1)}, bf16[192,1152]{1,0:T(8,128)(2,1)}, bf16[16,102...) custom-call(bf16[96,1152]{1,0:T(8,128)(2,1)S(1)} %copy-done.40, ...), custom_call_target="tpu_custom_call" | custom-call | flops 425984 | bytes 832 | tf_op jit(solution)/shard_map/attend_back/pallas_call | solution.py:597
  346.8 8.7 %collective-permute-done.58 = bf16[416,512]{1,0:T(8,128)(2,1)} collective-permute-done((bf16[416,512]{1,0:T(8,128)(2,1)}, bf16[416,512]{1,0:T(8,128)(2,1)}, u32[]{:S(2)}, u32[]{:S(2)}) %collective-permute-start.58) | collective-permute-done | bytes 426016 | tf_op jit(solution)/shard_map/ppermute | solution.py:55
  363.3 4.3 convolution_convert_fusion.1
  371.0 4.8 near.2
  385.9 49.2 %collective-permute-done.62.refs_5_ = bf16[272,768]{1,0:T(8,128)(2,1)S(1)} collective-permute-done((bf16[272,768]{1,0:T(8,128)(2,1)S(1)}, bf16[272,768]{1,0:T(8,128)(2,1)S(1)}, u32[]{:S(2)}, u32[]{:S(2)}) %collective-permute-start.62) | collective-permute-done | bytes 417824 | tf_op jit(solution)/shard_map/ppermute | solution.py:55
  438.6 8.8 %collective-permute-done.63.refs_6_ = bf16[272,768]{1,0:T(8,128)(2,1)S(1)} collective-permute-done((bf16[272,768]{1,0:T(8,128)(2,1)S(1)}, bf16[272,768]{1,0:T(8,128)(2,1)S(1)}, u32[]{:S(2)}, u32[]{:S(2)}) %collective-permute-start.63) | collective-permute-done | bytes 417824 | tf_op jit(solution)/shard_map/ppermute | solution.py:55
  459.6 25.1 %collective-permute-done.70 = bf16[264,1024]{1,0:T(8,128)(2,1)S(1)} collective-permute-done((bf16[264,1024]{1,0:T(8,128)(2,1)S(1)}, bf16[264,1024]{1,0:T(8,128)(2,1)S(1)}, u32[]{:S(2)}, u32[]{:S(2)}) %collective-permute-start.70) | collective-permute-done | bytes 540704 | tf_op jit(solution)/shard_map/ppermute | solution.py:55
  484.9 8.4 %collective-permute-done.65 = bf16[416,1152]{1,0:T(8,128)(2,1)} collective-permute-done((bf16[416,1152]{1,0:T(8,128)(2,1)}, bf16[416,1152]{1,0:T(8,128)(2,1)}, u32[]{:S(2)}, u32[]{:S(2)}) %collective-permute-start.65) | collective-permute-done | bytes 958496 | tf_op jit(solution)/shard_map/ppermute | solution.py:55
  496.2 3.9 slice_convert_fusion
  500.1 3.8 convert_bitcast_fusion
  504.8 6.8 %fusion.13 = (f32[1,1024,1024]{2,1,0:T(8,128)}, f32[1,1024,1024]{2,1,0:T(8,128)}) fusion(bf16[1024,2048]{1,0:T(8,128)(2,1)} %get-tuple-element.248), kind=kLoop, calls=%fused_computation.30 | loop fusion | flops 2097152 | bytes 12582912 | tf_op jit(solution)/shard_map/broadcast_in_dim | solution.py:1123
  538.9 3.5 collective-permute-start.74
  (653 shorter events, 233.2 us)
Async XLA Ops:
  7.2 489.0 %all-reduce.20.cloned.1.call-start = ((), (), s32[]{:S(2)}) async-start(), calls=%async_computation | async-start | bytes 24969216 | tf_op jit(solution)/shard_map/psum | solution.py:953
  32.5 31.5 %collective-permute-start.14 = (bf16[400,1024]{1,0:T(8,128)(2,1)S(1)}, bf16[400,1024]{1,0:T(8,128)(2,1)S(1)}, u32[]{:S(2)}, u32[]{:S(2)}) collective-permute-start(bf16[400,1024]{1,0:T(8,128)(2,1)S(1)} %fusion.89), channel_id=1, source_target_pairs={{0,64},{8,72},{16,80},{24,88},{32,96},{40,104},{48,112},{56,120},{... | collective-permute-start | bytes 2457608 | tf_op jit(solution)/shard_map/ppermute | solution.py:59
  36.1 27.8 %collective-permute-start.13 = (bf16[400,1024]{1,0:T(8,128)(2,1)S(1)}, bf16[400,1024]{1,0:T(8,128)(2,1)S(1)}, u32[]{:S(2)}, u32[]{:S(2)}) collective-permute-start(bf16[400,1024]{1,0:T(8,128)(2,1)S(1)} %fusion.89), channel_id=1, source_target_pairs={{0,48},{8,56},{16,32},{24,40},{32,16},{40,24},{48,0},{56,8},{64,11... | collective-permute-start | bytes 2457608 | tf_op jit(solution)/shard_map/ppermute | solution.py:59
  39.1 24.8 %collective-permute-start.12 = (bf16[400,1024]{1,0:T(8,128)(2,1)S(1)}, bf16[400,1024]{1,0:T(8,128)(2,1)S(1)}, u32[]{:S(2)}, u32[]{:S(2)}) collective-permute-start(bf16[400,1024]{1,0:T(8,128)(2,1)S(1)} %fusion.89), channel_id=1, source_target_pairs={{0,16},{8,24},{16,0},{24,8},{32,48},{40,56},{48,32},{56,40},{64,80... | collective-permute-start | bytes 2457608 | tf_op jit(solution)/shard_map/ppermute | solution.py:59
  66.4 33.8 %collective-permute-start.16 = (bf16[400,1024]{1,0:T(8,128)(2,1)}, bf16[400,1024]{1,0:T(8,128)(2,1)}, u32[]{:S(2)}, u32[]{:S(2)}) collective-permute-start(bf16[400,1024]{1,0:T(8,128)(2,1)} %get-tuple-element.138), channel_id=1, source_target_pairs={{0,16},{8,24},{16,0},{24,8},{32,48},{40,56},{48,32},{56,40},{64,80... | collective-permute-start | bytes 2457608 | tf_op jit(solution)/shard_map/ppermute | solution.py:59
  68.0 32.1 %collective-permute-start.15 = (bf16[384,1024]{1,0:T(8,128)(2,1)}, bf16[384,1024]{1,0:T(8,128)(2,1)}, u32[]{:S(2)}, u32[]{:S(2)}) collective-permute-start(bf16[384,1024]{1,0:T(8,128)(2,1)} %get-tuple-element.137), channel_id=1, source_target_pairs={{0,64},{8,72},{16,80},{24,88},{32,96},{40,104},{48,112},{56,120},{... | collective-permute-start | bytes 2359304 | tf_op jit(solution)/shard_map/ppermute | solution.py:59
  69.7 25.7 %collective-permute-start.8 = (bf16[208,1152]{1,0:T(8,128)(2,1)}, bf16[208,1152]{1,0:T(8,128)(2,1)S(1)}, u32[]{:S(2)}, u32[]{:S(2)}) collective-permute-start(bf16[208,1152]{1,0:T(8,128)(2,1)} %get-tuple-element.133), channel_id=1, source_target_pairs={{0,1},{1,0},{2,3},{3,2},{4,5},{5,4},{6,7},{7,6},{8,9},{9,8},{10,11... | collective-permute-start | bytes 1437704 | tf_op jit(solution)/shard_map/ppermute | solution.py:55
  71.4 24.0 %collective-permute-start.7 = (bf16[192,1152]{1,0:T(8,128)(2,1)S(1)}, bf16[192,1152]{1,0:T(8,128)(2,1)S(1)}, u32[]{:S(2)}, u32[]{:S(2)}) collective-permute-start(bf16[192,1152]{1,0:T(8,128)(2,1)S(1)} %get-tuple-element.132), channel_id=1, source_target_pairs={{0,4},{1,5},{2,6},{3,7},{4,0},{5,1},{6,2},{7,3},{8,12},{9,13},{10,... | collective-permute-start | bytes 1327112 | tf_op jit(solution)/shard_map/ppermute | solution.py:55
  73.0 24.8 %collective-permute-start.9 = (bf16[224,1152]{1,0:T(8,128)(2,1)}, bf16[224,1152]{1,0:T(8,128)(2,1)S(1)}, u32[]{:S(2)}, u32[]{:S(2)}) collective-permute-start(bf16[224,1152]{1,0:T(8,128)(2,1)} %copy-done.89), channel_id=1, source_target_pairs={{0,3},{1,2},{2,1},{3,0},{4,7},{5,6},{6,5},{7,4},{8,11},{9,10},{10,... | collective-permute-start | bytes 1548296 | tf_op jit(solution)/shard_map/ppermute | solution.py:55
  97.9 23.4 %collective-permute-start.17 = (bf16[416,1024]{1,0:T(8,128)(2,1)}, bf16[416,1024]{1,0:T(8,128)(2,1)}, u32[]{:S(2)}, u32[]{:S(2)}) collective-permute-start(bf16[416,1024]{1,0:T(8,128)(2,1)} %copy-done.88), channel_id=1, source_target_pairs={{0,48},{8,56},{16,32},{24,40},{32,16},{40,24},{48,0},{56,8},{64,11... | collective-permute-start | bytes 2555912 | tf_op jit(solution)/shard_map/ppermute | solution.py:59
  107.9 21.6 %collective-permute-start.19 = (bf16[208,1024]{1,0:T(8,128)(2,1)}, bf16[208,1024]{1,0:T(8,128)(2,1)}, u32[]{:S(2)}, u32[]{:S(2)}) collective-permute-start(bf16[208,1024]{1,0:T(8,128)(2,1)} %get-tuple-element.141), channel_id=1, source_target_pairs={{0,48},{8,56},{16,32},{24,40},{32,16},{40,24},{48,0},{56,8},{64,11... | collective-permute-start | bytes 1277960 | tf_op jit(solution)/shard_map/ppermute | solution.py:59
  109.6 29.7 %collective-permute-start.24 = (bf16[384,1024]{1,0:T(8,128)(2,1)}, bf16[384,1024]{1,0:T(8,128)(2,1)S(1)}, u32[]{:S(2)}, u32[]{:S(2)}) collective-permute-start(bf16[384,1024]{1,0:T(8,128)(2,1)} %collective-permute-done.15.refs_0_), channel_id=1, source_target_pairs={{0,8},{8,0},{16,24},{24,16},{32,40},{40,32},{48,56},{56,48},{64,72... | collective-permute-start | bytes 2359304 | tf_op jit(solution)/shard_map/ppermute | solution.py:59
  109.6 24.1 %collective-permute-start.31 = (bf16[208,1152]{1,0:T(8,128)(2,1)}, bf16[208,1152]{1,0:T(8,128)(2,1)S(1)}, u32[]{:S(2)}, u32[]{:S(2)}) collective-permute-start(bf16[208,1152]{1,0:T(8,128)(2,1)} %fence.11.refs_1_), channel_id=1, source_target_pairs={{0,4},{1,5},{2,6},{3,7},{4,0},{5,1},{6,2},{7,3},{8,12},{9,13},{10,... | collective-permute-start | bytes 1437704 | tf_op jit(solution)/shard_map/ppermute | solution.py:55
  140.1 22.8 %collective-permute-start.33 = (bf16[208,1152]{1,0:T(8,128)(2,1)}, bf16[208,1152]{1,0:T(8,128)(2,1)}, u32[]{:S(2)}, u32[]{:S(2)}) collective-permute-start(bf16[208,1152]{1,0:T(8,128)(2,1)} %get-tuple-element.147.refs_16_), channel_id=1, source_target_pairs={{0,1},{1,0},{2,3},{3,2},{4,5},{5,4},{6,7},{7,6},{8,9},{9,8},{10,11... | collective-permute-start | bytes 1437704 | tf_op jit(solution)/shard_map/ppermute | solution.py:55
  143.8 21.3 %collective-permute-start.11 = (bf16[112,1152]{1,0:T(8,128)(2,1)S(1)}, bf16[112,1152]{1,0:T(8,128)(2,1)S(1)}, u32[]{:S(2)}, u32[]{:S(2)}) collective-permute-start(bf16[112,1152]{1,0:T(8,128)(2,1)S(1)} %get-tuple-element.136), channel_id=1, source_target_pairs={{0,3},{1,2},{2,1},{3,0},{4,7},{5,6},{6,5},{7,4},{8,11},{9,10},{10,... | collective-permute-start | bytes 774152 | tf_op jit(solution)/shard_map/ppermute | solution.py:55
  164.4 20.7 %collective-permute-start.34 = (bf16[112,1152]{1,0:T(8,128)(2,1)S(1)}, bf16[112,1152]{1,0:T(8,128)(2,1)}, u32[]{:S(2)}, u32[]{:S(2)}) collective-permute-start(bf16[112,1152]{1,0:T(8,128)(2,1)S(1)} %get-tuple-element.159.refs_18_), channel_id=1, source_target_pairs={{0,3},{1,2},{2,1},{3,0},{4,7},{5,6},{6,5},{7,4},{8,11},{9,10},{10,... | collective-permute-start | bytes 774152 | tf_op jit(solution)/shard_map/ppermute | solution.py:55
  185.8 20.2 %collective-permute-start.37 = (bf16[208,1152]{1,0:T(8,128)(2,1)}, bf16[208,1152]{1,0:T(8,128)(2,1)S(1)}, u32[]{:S(2)}, u32[]{:S(2)}) collective-permute-start(bf16[208,1152]{1,0:T(8,128)(2,1)} %fence.12.refs_0_.refs_9_), channel_id=1, source_target_pairs={{0,4},{1,5},{2,6},{3,7},{4,0},{5,1},{6,2},{7,3},{8,12},{9,13},{10,... | collective-permute-start | bytes 1437704 | tf_op jit(solution)/shard_map/ppermute | solution.py:55
  191.9 38.0 %collective-permute-start.43 = (bf16[224,1152]{1,0:T(8,128)(2,1)}, bf16[224,1152]{1,0:T(8,128)(2,1)S(1)}, u32[]{:S(2)}, u32[]{:S(2)}) collective-permute-start(bf16[224,1152]{1,0:T(8,128)(2,1)} %get-tuple-element.148.refs_17_), channel_id=1, source_target_pairs={{0,3},{1,2},{2,1},{3,0},{4,7},{5,6},{6,5},{7,4},{8,11},{9,10},{10,... | collective-permute-start | bytes 1548296 | tf_op jit(solution)/shard_map/ppermute | solution.py:55
  208.6 25.6 %collective-permute-start.40 = (bf16[224,1152]{1,0:T(8,128)(2,1)S(1)}, bf16[224,1152]{1,0:T(8,128)(2,1)S(1)}, u32[]{:S(2)}, u32[]{:S(2)}) collective-permute-start(bf16[224,1152]{1,0:T(8,128)(2,1)S(1)} %get-tuple-element.165.refs_23_), channel_id=1, source_target_pairs={{0,3},{1,2},{2,1},{3,0},{4,7},{5,6},{6,5},{7,4},{8,11},{9,10},{10,... | collective-permute-start | bytes 1548296 | tf_op jit(solution)/shard_map/ppermute | solution.py:55
  257.8 28.5 %collective-permute-start.47 = (bf16[224,1152]{1,0:T(8,128)(2,1)S(1)}, bf16[224,1152]{1,0:T(8,128)(2,1)S(1)}, u32[]{:S(2)}, u32[]{:S(2)}) collective-permute-start(bf16[224,1152]{1,0:T(8,128)(2,1)S(1)} %pad_maximum_fusion.1), channel_id=1, source_target_pairs={{0,3},{1,2},{2,1},{3,0},{4,7},{5,6},{6,5},{7,4},{8,11},{9,10},{10,... | collective-permute-start | bytes 1548296 | tf_op jit(solution)/shard_map/ppermute | solution.py:55
  324.0 45.3 %collective-permute-start.53 = (bf16[8,33,8,1024]{3,2,1,0:T(8,128)(2,1)}, bf16[8,33,8,1024]{3,2,1,0:T(8,128)(2,1)}, u32[]{:S(2)}, u32[]{:S(2)}) collective-permute-start(bf16[8,33,8,1024]{3,2,1,0:T(8,128)(2,1)} %theirs.2), channel_id=1, source_target_pairs={{0,8},{8,0},{16,24},{24,16},{32,40},{40,32},{48,56},{56,48},{64,72... | collective-permute-start | bytes 12976136 | tf_op jit(solution)/shard_map/ppermute | solution.py:59
  334.9 20.6 %collective-permute-start.58 = (bf16[416,512]{1,0:T(8,128)(2,1)}, bf16[416,512]{1,0:T(8,128)(2,1)}, u32[]{:S(2)}, u32[]{:S(2)}) collective-permute-start(bf16[416,512]{1,0:T(8,128)(2,1)} %pad_maximum_fusion.9), channel_id=1, source_target_pairs={{0,3},{1,2},{2,1},{3,0},{4,7},{5,6},{6,5},{7,4},{8,11},{9,10},{10,... | collective-permute-start | bytes 1277960 | tf_op jit(solution)/shard_map/ppermute | solution.py:55
  375.8 71.6 %collective-permute-start.55 = (bf16[528,1024]{1,0:T(8,128)(2,1)S(1)}, bf16[528,1024]{1,0:T(8,128)(2,1)S(1)}, u32[]{:S(2)}, u32[]{:S(2)}) collective-permute-start(bf16[528,1024]{1,0:T(8,128)(2,1)S(1)} %bitcast.204), channel_id=1, source_target_pairs={{0,3},{1,2},{2,1},{3,0},{4,7},{5,6},{6,5},{7,4},{8,11},{9,10},{10,... | collective-permute-start | bytes 3244040 | tf_op jit(solution)/shard_map/ppermute | solution.py:55
  376.8 70.6 %collective-permute-start.54 = (bf16[528,1024]{1,0:T(8,128)(2,1)S(1)}, bf16[528,1024]{1,0:T(8,128)(2,1)S(1)}, u32[]{:S(2)}, u32[]{:S(2)}) collective-permute-start(bf16[528,1024]{1,0:T(8,128)(2,1)S(1)} %bitcast.202), channel_id=1, source_target_pairs={{0,1},{1,0},{2,3},{3,2},{4,5},{5,4},{6,7},{7,6},{8,9},{9,8},{10,11... | collective-permute-start | bytes 3244040 | tf_op jit(solution)/shard_map/ppermute | solution.py:55
  377.9 71.6 %collective-permute-start.56 = (bf16[528,1024]{1,0:T(8,128)(2,1)S(1)}, bf16[528,1024]{1,0:T(8,128)(2,1)}, u32[]{:S(2)}, u32[]{:S(2)}) collective-permute-start(bf16[528,1024]{1,0:T(8,128)(2,1)S(1)} %bitcast.200), channel_id=1, source_target_pairs={{0,2},{1,3},{2,0},{3,1},{4,6},{5,7},{6,4},{7,5},{8,10},{9,11},{10,... | collective-permute-start | bytes 3244040 | tf_op jit(solution)/shard_map/ppermute | solution.py:55
  382.8 52.2 %collective-permute-start.62 = (bf16[272,768]{1,0:T(8,128)(2,1)S(1)}, bf16[272,768]{1,0:T(8,128)(2,1)S(1)}, u32[]{:S(2)}, u32[]{:S(2)}) collective-permute-start(bf16[272,768]{1,0:T(8,128)(2,1)S(1)} %bitcast.215), channel_id=1, source_target_pairs={{0,3},{1,2},{2,1},{3,0},{4,7},{5,6},{6,5},{7,4},{8,11},{9,10},{10,... | collective-permute-start | bytes 1253384 | tf_op jit(solution)/shard_map/ppermute | solution.py:55
  385.9 52.7 %collective-permute-start.61 = (bf16[272,768]{1,0:T(8,128)(2,1)S(1)}, bf16[272,768]{1,0:T(8,128)(2,1)S(1)}, u32[]{:S(2)}, u32[]{:S(2)}) collective-permute-start(bf16[272,768]{1,0:T(8,128)(2,1)S(1)} %bitcast.213), channel_id=1, source_target_pairs={{0,1},{1,0},{2,3},{3,2},{4,5},{5,4},{6,7},{7,6},{8,9},{9,8},{10,11... | collective-permute-start | bytes 1253384 | tf_op jit(solution)/shard_map/ppermute | solution.py:55
  449.5 35.4 %collective-permute-start.64 = (bf16[416,1152]{1,0:T(8,128)(2,1)}, bf16[416,1152]{1,0:T(8,128)(2,1)}, u32[]{:S(2)}, u32[]{:S(2)}) collective-permute-start(bf16[416,1152]{1,0:T(8,128)(2,1)} %fence.13), channel_id=1, source_target_pairs={{0,1},{1,0},{2,3},{3,2},{4,5},{5,4},{6,7},{7,6},{8,9},{9,8},{10,11... | collective-permute-start | bytes 2875400 | tf_op jit(solution)/shard_map/ppermute | solution.py:55
  449.7 43.6 %collective-permute-start.65 = (bf16[416,1152]{1,0:T(8,128)(2,1)}, bf16[416,1152]{1,0:T(8,128)(2,1)}, u32[]{:S(2)}, u32[]{:S(2)}) collective-permute-start(bf16[416,1152]{1,0:T(8,128)(2,1)} %fence.14), channel_id=1, source_target_pairs={{0,3},{1,2},{2,1},{3,0},{4,7},{5,6},{6,5},{7,4},{8,11},{9,10},{10,... | collective-permute-start | bytes 2875400 | tf_op jit(solution)/shard_map/ppermute | solution.py:55
  450.7 42.6 %collective-permute-start.66 = (bf16[416,1152]{1,0:T(8,128)(2,1)}, bf16[416,1152]{1,0:T(8,128)(2,1)S(1)}, u32[]{:S(2)}, u32[]{:S(2)}) collective-permute-start(bf16[416,1152]{1,0:T(8,128)(2,1)} %fence.15), channel_id=1, source_target_pairs={{0,2},{1,3},{2,0},{3,1},{4,6},{5,7},{6,4},{7,5},{8,10},{9,11},{10,... | collective-permute-start | bytes 2875400 | tf_op jit(solution)/shard_map/ppermute | solution.py:55
  456.4 28.3 %collective-permute-start.70 = (bf16[264,1024]{1,0:T(8,128)(2,1)S(1)}, bf16[264,1024]{1,0:T(8,128)(2,1)S(1)}, u32[]{:S(2)}, u32[]{:S(2)}) collective-permute-start(bf16[264,1024]{1,0:T(8,128)(2,1)S(1)} %slice.693.refs_1_), channel_id=1, source_target_pairs={{0,4},{1,5},{2,6},{3,7},{4,0},{5,1},{6,2},{7,3},{8,12},{9,13},{10,... | collective-permute-start | bytes 1622024 | tf_op jit(solution)/shard_map/ppermute | solution.py:55
  515.3 27.2 %collective-permute-start.67 = (bf16[208,1152]{1,0:T(8,128)(2,1)}, bf16[208,1152]{1,0:T(8,128)(2,1)}, u32[]{:S(2)}, u32[]{:S(2)}) collective-permute-start(bf16[208,1152]{1,0:T(8,128)(2,1)} %fence.17), channel_id=1, source_target_pairs={{0,4},{1,5},{2,6},{3,7},{4,0},{5,1},{6,2},{7,3},{8,12},{9,13},{10,... | collective-permute-start | bytes 1437704 | tf_op jit(solution)/shard_map/ppermute | solution.py:55
  (210 other events, 2343.7 us)
Sparse Core Ops, SparseCore 0:
  297.0 180.6 all-reduce.19

commit v8 on v7

--- a/solution.py
+++ b/solution.py
@@ -960,6 +960,15 @@
         grads[3].astype(f32),
     )
 
+    partial_d = dot(product_d[:, :hidden], prefix_down).astype(bf16)
+    partial_a = dot(product_a, action_down[0]).astype(bf16)
+    out = []
+    for k in range(8):
+        i = (1, 3, 4, 0, 2, 5, 7, 6).index(k)
+        mine = partial_a[i * ACT_PAD : (i + 1) * ACT_PAD]
+        out.append(block_of(partial_d[i * PREF : (i + 1) * PREF], mine))
+    out_sent = []
+    out = ring_scatter(out, mp_swap, delta_pieces[2:], out_sent)
     (hidden_delta_d, hidden_delta_a, low, terms_d, terms_a, query_delta), pa, pb = attend_back(
         *delta_pieces,
         hidden_d,
@@ -981,7 +990,7 @@
         key_codes,
         keys,
         values,
-        after=(),
+        after=tuple(out_sent),
     )
     low_d, low_a = low[:PREF], low[PREF:, :DA]
 
@@ -1037,7 +1046,7 @@
         kv_grad_d,
         second_term_d.astype(bf16),
     )
-    kv = sum_weights(kv_grads, cuts, 768, place, kv_sent, got, qo_sent, grads[:1], last_sent)
+    kv = sum_weights(kv_grads, cuts, 768, place, kv_sent, got, qo_sent, (), last_sent)
     kv_a, kv_d = kv[:64], kv[64:, :640]
     qo_a, qo_b = qo[:128], qo[128:]
     kv_other = mp_swap(held(kv_part[BLOCK:].astype(bf16), (*kv_sent, grads[0])), 4)
@@ -1046,15 +1055,6 @@
         [unrotate(kv_sum[:, :HD], own_cos, own_sin), kv_sum[:, HD:]], axis=1
     ).astype(bf16)
 
-    partial_d = dot(product_d[:, :hidden], prefix_down).astype(bf16)
-    partial_a = dot(product_a, action_down[0]).astype(bf16)
-    out = []
-    for k in range(8):
-        i = (1, 3, 4, 0, 2, 5, 7, 6).index(k)
-        mine = partial_a[i * ACT_PAD : (i + 1) * ACT_PAD]
-        out.append(block_of(partial_d[i * PREF : (i + 1) * PREF], mine))
-    out_sent = []
-    out = ring_scatter(out, mp_swap, tuple(got), out_sent)
     out = pair_sum(out, mp_swap, tuple(last_sent))
     prefix_output = (hidden_d + out[:PREF]).astype(bf16)[None]
     action_output = (hidden_a + out[PREF:, :DA])[:ACT].astype(bf16)[None]
@@ -1071,7 +1071,7 @@
         ],
         axis=2,
     )
-    last = scatter_direct(last, yz, yz_swap)
+    last = scatter_direct(fence(last, grads[0]), yz, yz_swap)
     ninth = last[:, last.shape[1] - 256 : last.shape[1] - 48].reshape(1, wide)
     grads_d = join(last[:, :wide], ninth)
     grads_a = last[:, wide : last.shape[1] - 256]

time: 569 us -> 557 us (0.979)
  local copies, waits for them, and re-layouts: 56.7 us -> 47.5 us
  waiting for transfers between devices: 181 us -> 175 us
    unnamed x349 -> x315, local copies, waits for them, and re-layouts: 39.7 us -> 30.4 us
  transfers between devices with their start and end apart: 76 -> 76, of which waited for: 20 -> 29; matrix products, arithmetic and copies ran while one was open for 21% -> 21% of each run, Pallas kernels for 15% -> 15%
where the time goes in v8:
time: 557 us; the launch traced here: 546 us
  waiting for transfers between devices  175 us (31%)
  Pallas kernels  103 us (18%)
  starting transfers between devices  90 us (16%)
  other arithmetic  67.5 us (12%)
  local copies, waits for them, and re-layouts  47.5 us (9%)
  matrix products  46.5 us (8%)
  between operations  17.5 us (3%)
    ppermute x52, waiting for transfers between devices, mp_swap(): return lax.ppermute(array, 'mp', [(i, i ^ step) for i in range(N_MP)])  156 us
    ppermute x52, starting transfers between devices, mp_swap(): return lax.ppermute(array, 'mp', [(i, i ^ step) for i in range(N_MP)])  68.6 us
    pallas_call x3, Pallas kernels, feed(): pl.pallas_call(functools.partial(feed_kernel, layout), grid=(1,), in_spec...  44 us
    unnamed x315, local copies, waits for them, and re-layouts  30.4 us
    dot_general x12, matrix products, t_dot(): lax.dot_general(a, b, (((0,), (0,)), ((), ())), preferred_element_type=f32)  29.4 us
    ppermute x23, starting transfers between devices, dp_swap(): return lax.ppermute(array, 'dp', [(i, i ^ step) for i in range(16)])  21.4 us
    ppermute x23, waiting for transfers between devices, dp_swap(): return lax.ppermute(array, 'dp', [(i, i ^ step) for i in range(16)])  18.5 us
    dot_general x5, matrix products, dot(): return jnp.dot(a, b, preferred_element_type=f32)  13 us
  transfers between devices with their start and end apart: 76, of which 29 were waited for; matrix products, arithmetic and copies ran while one was open for 21% of the time, Pallas kernels for 15%

profile of v8, /device:TPU:0, one launch (start us, length us, event | category | flops | bytes accessed | tf_op | source)
XLA Modules:
  0.0 546.4 jit_solution(4566068205534633339)
XLA Ops:
  23.0 7.4 %collective-permute-done.1 = bf16[2,8,5760]{2,1,0:T(8,128)(2,1)S(1)} collective-permute-done((bf16[2,8,5760]{2,1,0:T(8,128)(2,1)S(1)}, bf16[2,8,5760]{2,1,0:T(8,128)(2,1)S(1)}, u32[]{:S(2)}, u32[]{:S(2)}) %collective-permute-start.1) | collective-permute-done | bytes 184352 | tf_op jit(solution)/shard_map/ppermute | solution.py:55
  35.8 3.6 collective-permute-start.14
  49.3 5.8 %collective-permute-done.5.refs_1_.refs_4_.refs_2_ = bf16[208,1152]{1,0:T(8,128)(2,1)S(1)} collective-permute-done((bf16[208,1152]{1,0:T(8,128)(2,1)S(1)}, bf16[208,1152]{1,0:T(8,128)(2,1)S(1)}, u32[]{:S(2)}, u32[]{:S(2)}) %collective-permute-start.5) | collective-permute-done | bytes 479264 | tf_op jit(solution)/shard_map/ppermute | solution.py:55
  59.5 6.1 %collective-permute-done.14.refs_2_ = bf16[400,1024]{1,0:T(8,128)(2,1)S(1)} collective-permute-done((bf16[400,1024]{1,0:T(8,128)(2,1)}, bf16[400,1024]{1,0:T(8,128)(2,1)S(1)}, u32[]{:S(2)}, u32[]{:S(2)}) %collective-permute-start.14) | collective-permute-done | bytes 819232 | tf_op jit(solution)/shard_map/ppermute | solution.py:59
  68.8 4.2 multiply_sine_fusion
  78.6 6.6 %collective-permute-done.9.refs_4_.refs_6_ = bf16[224,1152]{1,0:T(8,128)(2,1)S(1)} collective-permute-done((bf16[224,1152]{1,0:T(8,128)(2,1)}, bf16[224,1152]{1,0:T(8,128)(2,1)S(1)}, u32[]{:S(2)}, u32[]{:S(2)}) %collective-permute-start.9) | collective-permute-done | bytes 516128 | tf_op jit(solution)/shard_map/ppermute | solution.py:55
  109.5 3.5 collective-permute-done.19
  140.5 8.5 %assemble.1 = (bf16[8,2,8,8,1024]{4,3,2,1,0:T(8,128)(2,1)}, bf16[8,2,8,8,1024]{4,3,2,1,0:T(8,128)(2,1)}, bf16[8,2,8,8,512]{4,3,2,1,0:T(8,128)(2,1)}, bf16[8,2,8,...) custom-call(s32[2]{0:T(128)S(1)} %pad_add_fusion.2.place_ref, ...), custom_call_target="tpu_custom_call" | custom-call | tf_op jit(solution)/shard_map/assemble/pallas_call | solution.py:242
  152.7 6.2 %keys_of.1 = (bf16[384,1152]{1,0:T(8,128)(2,1)}, bf16[32,1024]{1,0:T(8,128)(2,1)S(1)}, bf16[1664,256]{1,0:T(8,128)(2,1)}, bf16[1664,256]{1,0:T(8,128)(2,1)}) custom-call(bf16[208,1152]{1,0:T(8,128)(2,1)S(1)} %copy-done.14, bf16[208,1152]{1,0:T(8,128)(2,1)S(1)} %collective-permute-done.4.refs_0_.refs_3_.refs_1_, ...), custom_call_target="tpu_custom_call" | custom-call | flops 1962934272 | bytes 8388608 | tf_op jit(solution)/shard_map/keys_of/pallas_call | solution.py:292
  159.0 11.3 %attend.1 = (bf16[832,256]{1,0:T(8,128)(2,1)S(1)}, bf16[208,1024]{1,0:T(8,128)(2,1)S(1)}, f32[832,1]{1,0:T(8,128)S(1)}, f32[832,1]{1,0:T(8,128)S(1)}, f32[192,11...) custom-call(bf16[384,1152]{1,0:T(8,128)(2,1)} %get-tuple-element.149.refs_0_, ...), custom_call_target="tpu_custom_call" | custom-call | flops 2399141888 | bytes 20971520 | tf_op jit(solution)/shard_map/attend/pallas_call | solution.py:508
  177.9 10.0 %feed.3 = (bf16[1536,896]{1,0:T(8,128)(2,1)}, bf16[1536,1792]{1,0:T(8,128)(2,1)}, bf16[1536,1152]{1,0:T(8,128)(2,1)}, bf16[1536,1152]{1,0:T(8,128)(2,1)}, bf16[1...) custom-call(bf16[208,1152]{1,0:T(8,128)(2,1)S(1)} %copy-done.15, ...), custom_call_target="tpu_custom_call" | custom-call | flops 2078801920 | bytes 12263424 | tf_op jit(solution)/shard_map/feed/pallas_call | solution.py:436
  194.1 15.5 %feed.4 = (bf16[1536,896]{1,0:T(8,128)(2,1)}, bf16[1536,1792]{1,0:T(8,128)(2,1)}, bf16[1536,1152]{1,0:T(8,128)(2,1)}, bf16[1536,1152]{1,0:T(8,128)(2,1)}, bf16[1...) custom-call(bf16[208,1152]{1,0:T(8,128)(2,1)S(1)} %collective-permut, ...), custom_call_target="tpu_custom_call", output_to_operand_aliasing={{0}: (13, {}), {1}: (14, {}), {2}: (15, {}), {3}: (16, {}),... | custom-call | flops 6236405760 | bytes 12263424 | tf_op jit(solution)/shard_map/feed/pallas_call | solution.py:436
  221.4 18.4 %feed.5 = (bf16[1536,896]{1,0:T(8,128)(2,1)}, bf16[1536,1792]{1,0:T(8,128)(2,1)}, bf16[1536,1152]{1,0:T(8,128)(2,1)}, bf16[1536,1152]{1,0:T(8,128)(2,1)}, bf16[1...) custom-call(bf16[192,1152]{1,0:T(8,128)(2,1)S(1)} %collective-permut, ...), custom_call_target="tpu_custom_call", output_to_operand_aliasing={{0}: (17, {}), {1}: (18, {}), {2}: (19, {}), {3}: (20, {}),... | custom-call | flops 8315207680 | bytes 12263424 | tf_op jit(solution)/shard_map/feed/pallas_call | solution.py:436
  243.7 6.7 %convolution_convert_fusion.1 = bf16[1536,1152]{1,0:T(8,128)(2,1)S(1)} fusion(bf16[864,1152]{1,0:T(8,128)(2,1)} %refs_12_.1, bf16[1536,896]{1,0:T(8,128)(2,1)} %get-tuple-element.185), kind=kOutput, calls=%fused_computation.1 | convolution fusion | flops 3059417088 | bytes 8282112 | tf_op jit(solution)/shard_map/dot_general | solution.py:702
  250.5 5.1 convolution_convert_fusion.5
  255.6 9.0 %convolution_convert_fusion = bf16[1792,1152]{1,0:T(8,128)(2,1)} fusion(bf16[1536,1792]{1,0:T(8,128)(2,1)S(1)} %bitcast.214, bf16[1536,1152]{1,0:T(8,128)(2,1)S(1)} %copy-done.81), kind=kOutput, calls=%fused_computation | convolution fusion | flops 6343852032 | bytes 13172736 | tf_op jit(solution)/shard_map/dot_general | solution.py:710
  270.9 3.9 collective-permute-done.46
  283.1 3.3 convolution_convert_fusion.4
  295.5 12.4 %attend_back.1 = (f32[192,1152]{1,0:T(8,128)}, f32[16,1024]{1,0:T(8,128)S(1)}, bf16[208,1152]{1,0:T(8,128)(2,1)}, bf16[192,1152]{1,0:T(8,128)(2,1)}, bf16[16,102...) custom-call(bf16[96,1152]{1,0:T(8,128)(2,1)S(1)} %get-tuple-element., ...), custom_call_target="tpu_custom_call" | custom-call | flops 425984 | bytes 832 | tf_op jit(solution)/shard_map/attend_back/pallas_call | solution.py:597
  329.2 3.5 convolution_convert_fusion.7
  335.6 8.8 %collective-permute-done.61 = bf16[416,512]{1,0:T(8,128)(2,1)} collective-permute-done((bf16[416,512]{1,0:T(8,128)(2,1)}, bf16[416,512]{1,0:T(8,128)(2,1)}, u32[]{:S(2)}, u32[]{:S(2)}) %collective-permute-start.61) | collective-permute-done | bytes 426016 | tf_op jit(solution)/shard_map/ppermute | solution.py:55
  359.2 4.9 near.2
  369.0 6.1 %collective-permute-done.53 = bf16[416,1152]{1,0:T(8,128)(2,1)} collective-permute-done((bf16[416,1152]{1,0:T(8,128)(2,1)}, bf16[416,1152]{1,0:T(8,128)(2,1)}, u32[]{:S(2)}, u32[]{:S(2)}) %collective-permute-start.53) | collective-permute-done | bytes 958496 | tf_op jit(solution)/shard_map/ppermute | solution.py:55
  377.0 21.6 %collective-permute-done.54 = bf16[416,1152]{1,0:T(8,128)(2,1)} collective-permute-done((bf16[416,1152]{1,0:T(8,128)(2,1)}, bf16[416,1152]{1,0:T(8,128)(2,1)}, u32[]{:S(2)}, u32[]{:S(2)}) %collective-permute-start.54) | collective-permute-done | bytes 958496 | tf_op jit(solution)/shard_map/ppermute | solution.py:55
  401.0 3.5 collective-permute-done.64
  410.2 51.8 %collective-permute-done.65 = bf16[272,768]{1,0:T(8,128)(2,1)S(1)} collective-permute-done((bf16[272,768]{1,0:T(8,128)(2,1)S(1)}, bf16[272,768]{1,0:T(8,128)(2,1)S(1)}, u32[]{:S(2)}, u32[]{:S(2)}) %collective-permute-start.65) | collective-permute-done | bytes 417824 | tf_op jit(solution)/shard_map/ppermute | solution.py:55
  475.7 8.5 %collective-permute-done.67 = bf16[208,1152]{1,0:T(8,128)(2,1)S(1)} collective-permute-done((bf16[208,1152]{1,0:T(8,128)(2,1)}, bf16[208,1152]{1,0:T(8,128)(2,1)S(1)}, u32[]{:S(2)}, u32[]{:S(2)}) %collective-permute-start.67) | collective-permute-done | bytes 479264 | tf_op jit(solution)/shard_map/ppermute | solution.py:55
  485.8 9.8 %collective-permute-done.70 = bf16[264,1024]{1,0:T(8,128)(2,1)S(1)} collective-permute-done((bf16[264,1024]{1,0:T(8,128)(2,1)S(1)}, bf16[264,1024]{1,0:T(8,128)(2,1)S(1)}, u32[]{:S(2)}, u32[]{:S(2)}) %collective-permute-start.70) | collective-permute-done | bytes 540704 | tf_op jit(solution)/shard_map/ppermute | solution.py:55
  497.3 3.9 slice_convert_fusion
  504.9 3.8 convert_bitcast_fusion
  510.3 4.9 collective-permute-start.73
  515.2 6.7 %fusion.13 = (f32[1,1024,1024]{2,1,0:T(8,128)}, f32[1,1024,1024]{2,1,0:T(8,128)}) fusion(bf16[1024,2048]{1,0:T(8,128)(2,1)} %get-tuple-element.248), kind=kLoop, calls=%fused_computation.30 | loop fusion | flops 2097152 | bytes 12582912 | tf_op jit(solution)/shard_map/broadcast_in_dim | solution.py:1123
  (619 shorter events, 243.7 us)
Async XLA Ops:
  7.2 490.1 %all-reduce.20.cloned.1.call-start = ((), (), s32[]{:S(2)}) async-start(), calls=%async_computation | async-start | bytes 24969216 | tf_op jit(solution)/shard_map/psum | solution.py:953
  35.8 29.9 %collective-permute-start.14 = (bf16[400,1024]{1,0:T(8,128)(2,1)}, bf16[400,1024]{1,0:T(8,128)(2,1)S(1)}, u32[]{:S(2)}, u32[]{:S(2)}) collective-permute-start(bf16[400,1024]{1,0:T(8,128)(2,1)} %fusion.91), channel_id=1, source_target_pairs={{0,64},{8,72},{16,80},{24,88},{32,96},{40,104},{48,112},{56,120},{... | collective-permute-start | bytes 2457608 | tf_op jit(solution)/shard_map/ppermute | solution.py:59
  39.4 26.3 %collective-permute-start.13 = (bf16[400,1024]{1,0:T(8,128)(2,1)}, bf16[400,1024]{1,0:T(8,128)(2,1)S(1)}, u32[]{:S(2)}, u32[]{:S(2)}) collective-permute-start(bf16[400,1024]{1,0:T(8,128)(2,1)} %fusion.91), channel_id=1, source_target_pairs={{0,48},{8,56},{16,32},{24,40},{32,16},{40,24},{48,0},{56,8},{64,11... | collective-permute-start | bytes 2457608 | tf_op jit(solution)/shard_map/ppermute | solution.py:59
  42.4 23.3 %collective-permute-start.12 = (bf16[400,1024]{1,0:T(8,128)(2,1)}, bf16[400,1024]{1,0:T(8,128)(2,1)S(1)}, u32[]{:S(2)}, u32[]{:S(2)}) collective-permute-start(bf16[400,1024]{1,0:T(8,128)(2,1)} %fusion.91), channel_id=1, source_target_pairs={{0,16},{8,24},{16,0},{24,8},{32,48},{40,56},{48,32},{56,40},{64,80... | collective-permute-start | bytes 2457608 | tf_op jit(solution)/shard_map/ppermute | solution.py:59
  67.2 23.3 %collective-permute-start.15 = (bf16[384,1024]{1,0:T(8,128)(2,1)}, bf16[384,1024]{1,0:T(8,128)(2,1)}, u32[]{:S(2)}, u32[]{:S(2)}) collective-permute-start(bf16[384,1024]{1,0:T(8,128)(2,1)} %get-tuple-element.137), channel_id=1, source_target_pairs={{0,64},{8,72},{16,80},{24,88},{32,96},{40,104},{48,112},{56,120},{... | collective-permute-start | bytes 2359304 | tf_op jit(solution)/shard_map/ppermute | solution.py:59
  67.2 23.3 %collective-permute-start.16 = (bf16[400,1024]{1,0:T(8,128)(2,1)}, bf16[400,1024]{1,0:T(8,128)(2,1)}, u32[]{:S(2)}, u32[]{:S(2)}) collective-permute-start(bf16[400,1024]{1,0:T(8,128)(2,1)} %get-tuple-element.138), channel_id=1, source_target_pairs={{0,16},{8,24},{16,0},{24,8},{32,48},{40,56},{48,32},{56,40},{64,80... | collective-permute-start | bytes 2457608 | tf_op jit(solution)/shard_map/ppermute | solution.py:59
  76.0 20.9 %collective-permute-start.23 = (bf16[400,1024]{1,0:T(8,128)(2,1)}, bf16[400,1024]{1,0:T(8,128)(2,1)S(1)}, u32[]{:S(2)}, u32[]{:S(2)}) collective-permute-start(bf16[400,1024]{1,0:T(8,128)(2,1)} %copy-done.18), channel_id=1, source_target_pairs={{0,8},{8,0},{16,24},{24,16},{32,40},{40,32},{48,56},{56,48},{64,72... | collective-permute-start | bytes 2457608 | tf_op jit(solution)/shard_map/ppermute | solution.py:59
  85.2 23.7 %collective-permute-start.17 = (bf16[416,1024]{1,0:T(8,128)(2,1)}, bf16[416,1024]{1,0:T(8,128)(2,1)}, u32[]{:S(2)}, u32[]{:S(2)}) collective-permute-start(bf16[416,1024]{1,0:T(8,128)(2,1)} %copy-done.76), channel_id=1, source_target_pairs={{0,48},{8,56},{16,32},{24,40},{32,16},{40,24},{48,0},{56,8},{64,11... | collective-permute-start | bytes 2555912 | tf_op jit(solution)/shard_map/ppermute | solution.py:59
  127.5 21.5 %collective-permute-start.33 = (bf16[208,1152]{1,0:T(8,128)(2,1)}, bf16[208,1152]{1,0:T(8,128)(2,1)}, u32[]{:S(2)}, u32[]{:S(2)}) collective-permute-start(bf16[208,1152]{1,0:T(8,128)(2,1)} %get-tuple-element.147.refs_16_), channel_id=1, source_target_pairs={{0,1},{1,0},{2,3},{3,2},{4,5},{5,4},{6,7},{7,6},{8,9},{9,8},{10,11... | collective-permute-start | bytes 1437704 | tf_op jit(solution)/shard_map/ppermute | solution.py:55
  127.8 21.2 %collective-permute-start.32 = (bf16[192,1152]{1,0:T(8,128)(2,1)}, bf16[192,1152]{1,0:T(8,128)(2,1)S(1)}, u32[]{:S(2)}, u32[]{:S(2)}) collective-permute-start(bf16[192,1152]{1,0:T(8,128)(2,1)} %copy-done.49), channel_id=1, source_target_pairs={{0,4},{1,5},{2,6},{3,7},{4,0},{5,1},{6,2},{7,3},{8,12},{9,13},{10,... | collective-permute-start | bytes 1327112 | tf_op jit(solution)/shard_map/ppermute | solution.py:55
  128.9 23.8 %collective-permute-start.11 = (bf16[112,1152]{1,0:T(8,128)(2,1)S(1)}, bf16[112,1152]{1,0:T(8,128)(2,1)S(1)}, u32[]{:S(2)}, u32[]{:S(2)}) collective-permute-start(bf16[112,1152]{1,0:T(8,128)(2,1)S(1)} %get-tuple-element.136), channel_id=1, source_target_pairs={{0,3},{1,2},{2,1},{3,0},{4,7},{5,6},{6,5},{7,4},{8,11},{9,10},{10,... | collective-permute-start | bytes 774152 | tf_op jit(solution)/shard_map/ppermute | solution.py:55
  132.3 20.4 %collective-permute-start.10 = (bf16[96,1152]{1,0:T(8,128)(2,1)S(1)}, bf16[96,1152]{1,0:T(8,128)(2,1)S(1)}, u32[]{:S(2)}, u32[]{:S(2)}) collective-permute-start(bf16[96,1152]{1,0:T(8,128)(2,1)S(1)} %get-tuple-element.135), channel_id=1, source_target_pairs={{0,1},{1,0},{2,3},{3,2},{4,5},{5,4},{6,7},{7,6},{8,9},{9,8},{10,11... | collective-permute-start | bytes 663560 | tf_op jit(solution)/shard_map/ppermute | solution.py:55
  133.6 83.1 %collective-permute-start.43 = (bf16[224,1152]{1,0:T(8,128)(2,1)}, bf16[224,1152]{1,0:T(8,128)(2,1)}, u32[]{:S(2)}, u32[]{:S(2)}) collective-permute-start(bf16[224,1152]{1,0:T(8,128)(2,1)} %copy-done.45), channel_id=1, source_target_pairs={{0,3},{1,2},{2,1},{3,0},{4,7},{5,6},{6,5},{7,4},{8,11},{9,10},{10,... | collective-permute-start | bytes 1548296 | tf_op jit(solution)/shard_map/ppermute | solution.py:55
  150.5 22.0 %collective-permute-start.34 = (bf16[112,1152]{1,0:T(8,128)(2,1)S(1)}, bf16[112,1152]{1,0:T(8,128)(2,1)}, u32[]{:S(2)}, u32[]{:S(2)}) collective-permute-start(bf16[112,1152]{1,0:T(8,128)(2,1)S(1)} %get-tuple-element.159.refs_18_), channel_id=1, source_target_pairs={{0,3},{1,2},{2,1},{3,0},{4,7},{5,6},{6,5},{7,4},{8,11},{9,10},{10,... | collective-permute-start | bytes 774152 | tf_op jit(solution)/shard_map/ppermute | solution.py:55
  188.9 20.8 %collective-permute-start.38 = (bf16[192,1152]{1,0:T(8,128)(2,1)S(1)}, bf16[192,1152]{1,0:T(8,128)(2,1)S(1)}, u32[]{:S(2)}, u32[]{:S(2)}) collective-permute-start(bf16[192,1152]{1,0:T(8,128)(2,1)S(1)} %get-tuple-element.163.refs_21_), channel_id=1, source_target_pairs={{0,4},{1,5},{2,6},{3,7},{4,0},{5,1},{6,2},{7,3},{8,12},{9,13},{10,... | collective-permute-start | bytes 1327112 | tf_op jit(solution)/shard_map/ppermute | solution.py:55
  189.8 19.8 %collective-permute-start.39 = (bf16[208,1152]{1,0:T(8,128)(2,1)S(1)}, bf16[208,1152]{1,0:T(8,128)(2,1)S(1)}, u32[]{:S(2)}, u32[]{:S(2)}) collective-permute-start(bf16[208,1152]{1,0:T(8,128)(2,1)S(1)} %get-tuple-element.164.refs_22_), channel_id=1, source_target_pairs={{0,1},{1,0},{2,3},{3,2},{4,5},{5,4},{6,7},{7,6},{8,9},{9,8},{10,11... | collective-permute-start | bytes 1437704 | tf_op jit(solution)/shard_map/ppermute | solution.py:55
  191.8 27.2 %collective-permute-start.40 = (bf16[224,1152]{1,0:T(8,128)(2,1)S(1)}, bf16[224,1152]{1,0:T(8,128)(2,1)S(1)}, u32[]{:S(2)}, u32[]{:S(2)}) collective-permute-start(bf16[224,1152]{1,0:T(8,128)(2,1)S(1)} %get-tuple-element.165.refs_23_), channel_id=1, source_target_pairs={{0,3},{1,2},{2,1},{3,0},{4,7},{5,6},{6,5},{7,4},{8,11},{9,10},{10,... | collective-permute-start | bytes 1548296 | tf_op jit(solution)/shard_map/ppermute | solution.py:55
  239.8 26.5 %collective-permute-start.45 = (bf16[96,1152]{1,0:T(8,128)(2,1)S(1)}, bf16[96,1152]{1,0:T(8,128)(2,1)S(1)}, u32[]{:S(2)}, u32[]{:S(2)}) collective-permute-start(bf16[96,1152]{1,0:T(8,128)(2,1)S(1)} %get-tuple-element.189), channel_id=1, source_target_pairs={{0,1},{1,0},{2,3},{3,2},{4,5},{5,4},{6,7},{7,6},{8,9},{9,8},{10,11... | collective-permute-start | bytes 663560 | tf_op jit(solution)/shard_map/ppermute | solution.py:55
  240.2 27.4 %collective-permute-start.49 = (bf16[112,1152]{1,0:T(8,128)(2,1)S(1)}, bf16[112,1152]{1,0:T(8,128)(2,1)S(1)}, u32[]{:S(2)}, u32[]{:S(2)}) collective-permute-start(bf16[112,1152]{1,0:T(8,128)(2,1)S(1)} %get-tuple-element.196), channel_id=1, source_target_pairs={{0,3},{1,2},{2,1},{3,0},{4,7},{5,6},{6,5},{7,4},{8,11},{9,10},{10,... | collective-permute-start | bytes 774152 | tf_op jit(solution)/shard_map/ppermute | solution.py:55
  242.3 36.7 %collective-permute-start.47 = (bf16[224,1152]{1,0:T(8,128)(2,1)S(1)}, bf16[224,1152]{1,0:T(8,128)(2,1)S(1)}, u32[]{:S(2)}, u32[]{:S(2)}) collective-permute-start(bf16[224,1152]{1,0:T(8,128)(2,1)S(1)} %pad_maximum_fusion), channel_id=1, source_target_pairs={{0,3},{1,2},{2,1},{3,0},{4,7},{5,6},{6,5},{7,4},{8,11},{9,10},{10,... | collective-permute-start | bytes 1548296 | tf_op jit(solution)/shard_map/ppermute | solution.py:55
  316.0 40.0 %collective-permute-start.56 = (bf16[8,33,8,1024]{3,2,1,0:T(8,128)(2,1)}, bf16[8,33,8,1024]{3,2,1,0:T(8,128)(2,1)}, u32[]{:S(2)}, u32[]{:S(2)}) collective-permute-start(bf16[8,33,8,1024]{3,2,1,0:T(8,128)(2,1)} %theirs.2), channel_id=1, source_target_pairs={{0,8},{8,0},{16,24},{24,16},{32,40},{40,32},{48,56},{56,48},{64,72... | collective-permute-start | bytes 12976136 | tf_op jit(solution)/shard_map/ppermute | solution.py:59
  325.2 19.2 %collective-permute-start.61 = (bf16[416,512]{1,0:T(8,128)(2,1)}, bf16[416,512]{1,0:T(8,128)(2,1)}, u32[]{:S(2)}, u32[]{:S(2)}) collective-permute-start(bf16[416,512]{1,0:T(8,128)(2,1)} %pad_maximum_fusion.8), channel_id=1, source_target_pairs={{0,3},{1,2},{2,1},{3,0},{4,7},{5,6},{6,5},{7,4},{8,11},{9,10},{10,... | collective-permute-start | bytes 1277960 | tf_op jit(solution)/shard_map/ppermute | solution.py:55
  350.7 24.3 %collective-permute-start.53 = (bf16[416,1152]{1,0:T(8,128)(2,1)}, bf16[416,1152]{1,0:T(8,128)(2,1)}, u32[]{:S(2)}, u32[]{:S(2)}) collective-permute-start(bf16[416,1152]{1,0:T(8,128)(2,1)} %fence.13.refs_24_), channel_id=1, source_target_pairs={{0,1},{1,0},{2,3},{3,2},{4,5},{5,4},{6,7},{7,6},{8,9},{9,8},{10,11... | collective-permute-start | bytes 2875400 | tf_op jit(solution)/shard_map/ppermute | solution.py:55
  352.5 46.1 %collective-permute-start.54 = (bf16[416,1152]{1,0:T(8,128)(2,1)}, bf16[416,1152]{1,0:T(8,128)(2,1)}, u32[]{:S(2)}, u32[]{:S(2)}) collective-permute-start(bf16[416,1152]{1,0:T(8,128)(2,1)} %fence.14.refs_26_), channel_id=1, source_target_pairs={{0,3},{1,2},{2,1},{3,0},{4,7},{5,6},{6,5},{7,4},{8,11},{9,10},{10,... | collective-permute-start | bytes 2875400 | tf_op jit(solution)/shard_map/ppermute | solution.py:55
  353.8 45.8 %collective-permute-start.55 = (bf16[416,1152]{1,0:T(8,128)(2,1)}, bf16[416,1152]{1,0:T(8,128)(2,1)}, u32[]{:S(2)}, u32[]{:S(2)}) collective-permute-start(bf16[416,1152]{1,0:T(8,128)(2,1)} %fence.15.refs_25_), channel_id=1, source_target_pairs={{0,2},{1,3},{2,0},{3,1},{4,6},{5,7},{6,4},{7,5},{8,10},{9,11},{10,... | collective-permute-start | bytes 2875400 | tf_op jit(solution)/shard_map/ppermute | solution.py:55
  366.6 37.9 %collective-permute-start.64 = (bf16[272,768]{1,0:T(8,128)(2,1)S(1)}, bf16[272,768]{1,0:T(8,128)(2,1)S(1)}, u32[]{:S(2)}, u32[]{:S(2)}) collective-permute-start(bf16[272,768]{1,0:T(8,128)(2,1)S(1)} %bitcast.204), channel_id=1, source_target_pairs={{0,1},{1,0},{2,3},{3,2},{4,5},{5,4},{6,7},{7,6},{8,9},{9,8},{10,11... | collective-permute-start | bytes 1253384 | tf_op jit(solution)/shard_map/ppermute | solution.py:55
  368.7 96.0 %collective-permute-start.57 = (bf16[528,1024]{1,0:T(8,128)(2,1)S(1)}, bf16[528,1024]{1,0:T(8,128)(2,1)S(1)}, u32[]{:S(2)}, u32[]{:S(2)}) collective-permute-start(bf16[528,1024]{1,0:T(8,128)(2,1)S(1)} %bitcast.197), channel_id=1, source_target_pairs={{0,1},{1,0},{2,3},{3,2},{4,5},{5,4},{6,7},{7,6},{8,9},{9,8},{10,11... | collective-permute-start | bytes 3244040 | tf_op jit(solution)/shard_map/ppermute | solution.py:55
  375.1 89.6 %collective-permute-start.58 = (bf16[528,1024]{1,0:T(8,128)(2,1)S(1)}, bf16[528,1024]{1,0:T(8,128)(2,1)S(1)}, u32[]{:S(2)}, u32[]{:S(2)}) collective-permute-start(bf16[528,1024]{1,0:T(8,128)(2,1)S(1)} %bitcast.195), channel_id=1, source_target_pairs={{0,3},{1,2},{2,1},{3,0},{4,7},{5,6},{6,5},{7,4},{8,11},{9,10},{10,... | collective-permute-start | bytes 3244040 | tf_op jit(solution)/shard_map/ppermute | solution.py:55
  398.6 66.1 %collective-permute-start.59 = (bf16[528,1024]{1,0:T(8,128)(2,1)S(1)}, bf16[528,1024]{1,0:T(8,128)(2,1)S(1)}, u32[]{:S(2)}, u32[]{:S(2)}) collective-permute-start(bf16[528,1024]{1,0:T(8,128)(2,1)S(1)} %bitcast.193), channel_id=1, source_target_pairs={{0,2},{1,3},{2,0},{3,1},{4,6},{5,7},{6,4},{7,5},{8,10},{9,11},{10,... | collective-permute-start | bytes 3244040 | tf_op jit(solution)/shard_map/ppermute | solution.py:55
  399.6 62.5 %collective-permute-start.65 = (bf16[272,768]{1,0:T(8,128)(2,1)S(1)}, bf16[272,768]{1,0:T(8,128)(2,1)S(1)}, u32[]{:S(2)}, u32[]{:S(2)}) collective-permute-start(bf16[272,768]{1,0:T(8,128)(2,1)S(1)} %bitcast.206), channel_id=1, source_target_pairs={{0,3},{1,2},{2,1},{3,0},{4,7},{5,6},{6,5},{7,4},{8,11},{9,10},{10,... | collective-permute-start | bytes 1253384 | tf_op jit(solution)/shard_map/ppermute | solution.py:55
  404.5 57.5 %collective-permute-start.66 = (bf16[272,768]{1,0:T(8,128)(2,1)S(1)}, bf16[272,768]{1,0:T(8,128)(2,1)S(1)}, u32[]{:S(2)}, u32[]{:S(2)}) collective-permute-start(bf16[272,768]{1,0:T(8,128)(2,1)S(1)} %bitcast.208), channel_id=1, source_target_pairs={{0,2},{1,3},{2,0},{3,1},{4,6},{5,7},{6,4},{7,5},{8,10},{9,11},{10,... | collective-permute-start | bytes 1253384 | tf_op jit(solution)/shard_map/ppermute | solution.py:55
  475.1 20.5 %collective-permute-start.70 = (bf16[264,1024]{1,0:T(8,128)(2,1)S(1)}, bf16[264,1024]{1,0:T(8,128)(2,1)S(1)}, u32[]{:S(2)}, u32[]{:S(2)}) collective-permute-start(bf16[264,1024]{1,0:T(8,128)(2,1)S(1)} %copy-done.100), channel_id=1, source_target_pairs={{0,4},{1,5},{2,6},{3,7},{4,0},{5,1},{6,2},{7,3},{8,12},{9,13},{10,... | collective-permute-start | bytes 1622024 | tf_op jit(solution)/shard_map/ppermute | solution.py:55
  (193 other events, 2375.4 us)
Sparse Core Ops, SparseCore 0:
  290.1 181.5 all-reduce.19

commit v9 on v8

--- a/solution.py
+++ b/solution.py
@@ -1029,7 +1029,7 @@
     )
     qo_sent, kv_sent, got, last_sent = [], [], [], []
     qo_grads = (q_grad_a, out_grad_a, q_grad_d, out_grad_d)
-    qo = sum_weights(qo_grads, cuts, 1024, place, qo_sent, got, (), (), last_sent)
+    qo = sum_weights(qo_grads, cuts, 1024, place, qo_sent, got, (), grads[:1], last_sent)
     kv_grad_d = t_dot(turned_d, kv_rows_d).astype(bf16)
     kv_grad_a = t_dot(turned_a, kv_rows_a).astype(bf16)
     cuts = (
@@ -1046,16 +1046,16 @@
         kv_grad_d,
         second_term_d.astype(bf16),
     )
-    kv = sum_weights(kv_grads, cuts, 768, place, kv_sent, got, qo_sent, (), last_sent)
+    kv = sum_weights(kv_grads, cuts, 768, place, kv_sent, got, qo_sent, grads[:1], last_sent)
     kv_a, kv_d = kv[:64], kv[64:, :640]
     qo_a, qo_b = qo[:128], qo[128:]
-    kv_other = mp_swap(held(kv_part[BLOCK:].astype(bf16), (*kv_sent, grads[0])), 4)
+    kv_other = mp_swap(held(kv_part[BLOCK:].astype(bf16), tuple(last_sent)), 4)
     kv_sum = kv_part[:BLOCK] + kv_other.astype(f32)
     kv_raw_delta = jnp.concatenate(
         [unrotate(kv_sum[:, :HD], own_cos, own_sin), kv_sum[:, HD:]], axis=1
     ).astype(bf16)
 
-    out = pair_sum(out, mp_swap, tuple(last_sent))
+    out = pair_sum(out, mp_swap)
     prefix_output = (hidden_d + out[:PREF]).astype(bf16)[None]
     action_output = (hidden_a + out[PREF:, :DA])[:ACT].astype(bf16)[None]
 
@@ -1071,7 +1071,7 @@
         ],
         axis=2,
     )
-    last = scatter_direct(fence(last, grads[0]), yz, yz_swap)
+    last = scatter_direct(last, yz, yz_swap)
     ninth = last[:, last.shape[1] - 256 : last.shape[1] - 48].reshape(1, wide)
     grads_d = join(last[:, :wide], ninth)
     grads_a = last[:, wide : last.shape[1] - 256]

time: 557 us -> 597 us (1.072)
  waiting for transfers between devices: 175 us -> 207 us
  starting transfers between devices: 90 us -> 103 us
    ppermute x52, waiting for transfers between devices: 156 us -> 173 us  [mp_swap(): return lax.ppermute(array, 'mp', [(i, i ^ step) for i in range(N_MP)])]
    ppermute x23, waiting for transfers between devices: 18.5 us -> 34.1 us  [dp_swap(): return lax.ppermute(array, 'dp', [(i, i ^ step) for i in range(16)])]
    ppermute x52, starting transfers between devices: 68.6 us -> 80.2 us  [mp_swap(): return lax.ppermute(array, 'mp', [(i, i ^ step) for i in range(N_MP)])]
    unnamed x315 -> x309, local copies, waits for them, and re-layouts: 30.4 us -> 35.2 us
  transfers between devices with their start and end apart: 76 -> 76, of which waited for: 29 -> 24; matrix products, arithmetic and copies ran while one was open for 21% -> 18% of each run, Pallas kernels for 15% -> 13%
where the time goes in v9:
time: 597 us; the launch traced here: 591 us
  waiting for transfers between devices  207 us (35%)
  starting transfers between devices  103 us (17%)
  Pallas kernels  99.6 us (17%)
  other arithmetic  64.5 us (11%)
  local copies, waits for them, and re-layouts  50.5 us (8%)
  matrix products  48.5 us (8%)
  between operations  17.5 us (3%)
    ppermute x52, waiting for transfers between devices, mp_swap(): return lax.ppermute(array, 'mp', [(i, i ^ step) for i in range(N_MP)])  173 us
    ppermute x52, starting transfers between devices, mp_swap(): return lax.ppermute(array, 'mp', [(i, i ^ step) for i in range(N_MP)])  80.2 us
    pallas_call x3, Pallas kernels, feed(): pl.pallas_call(functools.partial(feed_kernel, layout), grid=(1,), in_spec...  44.1 us
    unnamed x309, local copies, waits for them, and re-layouts  35.2 us
    ppermute x23, waiting for transfers between devices, dp_swap(): return lax.ppermute(array, 'dp', [(i, i ^ step) for i in range(16)])  34.1 us
    dot_general x12, matrix products, t_dot(): lax.dot_general(a, b, (((0,), (0,)), ((), ())), preferred_element_type=f32)  32.2 us
    ppermute x23, starting transfers between devices, dp_swap(): return lax.ppermute(array, 'dp', [(i, i ^ step) for i in range(16)])  22.9 us
    pallas_call x1, Pallas kernels, attend_back(): pl.pallas_call(attend_back_kernel, in_specs=[VMEM] * len(given) + [ANY] *...  12.6 us
  transfers between devices with their start and end apart: 76, of which 24 were waited for; matrix products, arithmetic and copies ran while one was open for 18% of the time, Pallas kernels for 13%

profile of v9, /device:TPU:0, one launch (start us, length us, event | category | flops | bytes accessed | tf_op | source)
XLA Modules:
  0.0 591.0 jit_solution(11446861299750275786)
XLA Ops:
  23.0 7.4 %collective-permute-done.1 = bf16[2,8,5760]{2,1,0:T(8,128)(2,1)S(1)} collective-permute-done((bf16[2,8,5760]{2,1,0:T(8,128)(2,1)S(1)}, bf16[2,8,5760]{2,1,0:T(8,128)(2,1)S(1)}, u32[]{:S(2)}, u32[]{:S(2)}) %collective-permute-start.1) | collective-permute-done | bytes 184352 | tf_op jit(solution)/shard_map/ppermute | solution.py:55
  41.8 4.1 collective-permute-done.6.refs_2_.refs_5_.refs_3_
  47.3 4.8 collective-permute-done.5.refs_1_.refs_4_.refs_2_
  52.1 4.3 collective-permute-done.4.refs_0_.refs_3_.refs_1_
  56.4 7.6 %collective-permute-done.14.refs_2_ = bf16[400,1024]{1,0:T(8,128)(2,1)S(1)} collective-permute-done((bf16[400,1024]{1,0:T(8,128)(2,1)S(1)}, bf16[400,1024]{1,0:T(8,128)(2,1)S(1)}, u32[]{:S(2)}, u32[]{:S(2)}) %collective-permute-start.14) | collective-permute-done | bytes 819232 | tf_op jit(solution)/shard_map/ppermute | solution.py:59
  74.9 20.5 %collective-permute-done.7.refs_0_.refs_2_.refs_4_ = bf16[192,1152]{1,0:T(8,128)(2,1)S(1)} collective-permute-done((bf16[192,1152]{1,0:T(8,128)(2,1)S(1)}, bf16[192,1152]{1,0:T(8,128)(2,1)S(1)}, u32[]{:S(2)}, u32[]{:S(2)}) %collective-permute-start.7) | collective-permute-done | bytes 442400 | tf_op jit(solution)/shard_map/ppermute | solution.py:55
  110.0 11.3 %collective-permute-done.17 = bf16[416,1024]{1,0:T(8,128)(2,1)} collective-permute-done((bf16[416,1024]{1,0:T(8,128)(2,1)}, bf16[416,1024]{1,0:T(8,128)(2,1)}, u32[]{:S(2)}, u32[]{:S(2)}) %collective-permute-start.17) | collective-permute-done | bytes 852000 | tf_op jit(solution)/shard_map/ppermute | solution.py:59
  124.5 4.9 collective-permute-done.19
  129.4 4.2 multiply_sine_fusion
  156.3 7.9 %assemble.1 = (bf16[8,2,8,8,1024]{4,3,2,1,0:T(8,128)(2,1)}, bf16[8,2,8,8,1024]{4,3,2,1,0:T(8,128)(2,1)}, bf16[8,2,8,8,512]{4,3,2,1,0:T(8,128)(2,1)}, bf16[8,2,8,...) custom-call(s32[2]{0:T(128)S(1)} %pad_add_fusion.2.place_ref, ...), custom_call_target="tpu_custom_call" | custom-call | tf_op jit(solution)/shard_map/assemble/pallas_call | solution.py:242
  166.3 6.3 %keys_of.1 = (bf16[384,1152]{1,0:T(8,128)(2,1)}, bf16[32,1024]{1,0:T(8,128)(2,1)S(1)}, bf16[1664,256]{1,0:T(8,128)(2,1)}, bf16[1664,256]{1,0:T(8,128)(2,1)}) custom-call(bf16[208,1152]{1,0:T(8,128)(2,1)S(1)} %copy-done.10, bf16[208,1152]{1,0:T(8,128)(2,1)S(1)} %collective-permute-done.4.refs_0_.refs_3_.refs_1_, ...), custom_call_target="tpu_custom_call" | custom-call | flops 1962934272 | bytes 8388608 | tf_op jit(solution)/shard_map/keys_of/pallas_call | solution.py:292
  172.7 11.2 %attend.1 = (bf16[832,256]{1,0:T(8,128)(2,1)S(1)}, bf16[208,1024]{1,0:T(8,128)(2,1)S(1)}, f32[832,1]{1,0:T(8,128)S(1)}, f32[832,1]{1,0:T(8,128)S(1)}, f32[192,11...) custom-call(bf16[384,1152]{1,0:T(8,128)(2,1)} %get-tuple-element.149.refs_0_, ...), custom_call_target="tpu_custom_call" | custom-call | flops 2399141888 | bytes 20971520 | tf_op jit(solution)/shard_map/attend/pallas_call | solution.py:508
  193.1 11.6 %collective-permute-start.43 = (bf16[224,1152]{1,0:T(8,128)(2,1)}, bf16[224,1152]{1,0:T(8,128)(2,1)S(1)}, u32[]{:S(2)}, u32[]{:S(2)}) collective-permute-start(bf16[224,1152]{1,0:T(8,128)(2,1)} %copy-done.47), channel_id=1, source_target_pairs={{0,3},{1,2},{2,1},{3,0},{4,7},{5,6},{6,5},{7,4},{8,11},{9,10},{10,... | collective-permute-start | bytes 1548296 | tf_op jit(solution)/shard_map/ppermute | solution.py:55
  205.7 10.0 %feed.3 = (bf16[1536,896]{1,0:T(8,128)(2,1)}, bf16[1536,1792]{1,0:T(8,128)(2,1)}, bf16[1536,1152]{1,0:T(8,128)(2,1)}, bf16[1536,1152]{1,0:T(8,128)(2,1)}, bf16[1...) custom-call(bf16[208,1152]{1,0:T(8,128)(2,1)S(1)} %copy-done.11, ...), custom_call_target="tpu_custom_call" | custom-call | flops 2078801920 | bytes 12263424 | tf_op jit(solution)/shard_map/feed/pallas_call | solution.py:436
  221.3 15.6 %feed.4 = (bf16[1536,896]{1,0:T(8,128)(2,1)}, bf16[1536,1792]{1,0:T(8,128)(2,1)}, bf16[1536,1152]{1,0:T(8,128)(2,1)}, bf16[1536,1152]{1,0:T(8,128)(2,1)}, bf16[1...) custom-call(bf16[208,1152]{1,0:T(8,128)(2,1)S(1)} %collective-permut, ...), custom_call_target="tpu_custom_call", output_to_operand_aliasing={{0}: (13, {}), {1}: (14, {}), {2}: (15, {}), {3}: (16, {}),... | custom-call | flops 6236405760 | bytes 12263424 | tf_op jit(solution)/shard_map/feed/pallas_call | solution.py:436
  240.1 4.1 collective-permute-done.44.refs_8_
  246.6 18.5 %feed.5 = (bf16[1536,896]{1,0:T(8,128)(2,1)}, bf16[1536,1792]{1,0:T(8,128)(2,1)}, bf16[1536,1152]{1,0:T(8,128)(2,1)}, bf16[1536,1152]{1,0:T(8,128)(2,1)}, bf16[1...) custom-call(bf16[192,1152]{1,0:T(8,128)(2,1)S(1)} %collective-permut, ...), custom_call_target="tpu_custom_call", output_to_operand_aliasing={{0}: (17, {}), {1}: (18, {}), {2}: (19, {}), {3}: (20, {}),... | custom-call | flops 8315207680 | bytes 12263424 | tf_op jit(solution)/shard_map/feed/pallas_call | solution.py:436
  269.0 11.9 %convolution_convert_fusion = bf16[1792,1152]{1,0:T(8,128)(2,1)} fusion(bf16[1536,1792]{1,0:T(8,128)(2,1)} %get-tuple-element.229, bf16[1536,1152]{1,0:T(8,128)(2,1)} %get-tuple-element.230), kind=kOutput, calls=%fused_computation | convolution fusion | flops 6343852032 | bytes 13172736 | tf_op jit(solution)/shard_map/dot_general | solution.py:710
  283.3 5.2 convolution_convert_fusion.5
  316.5 4.8 convolution_convert_fusion.1
  326.8 12.6 %attend_back.1 = (f32[192,1152]{1,0:T(8,128)}, f32[16,1024]{1,0:T(8,128)S(1)}, bf16[208,1152]{1,0:T(8,128)(2,1)}, bf16[192,1152]{1,0:T(8,128)(2,1)}, bf16[16,102...) custom-call(bf16[96,1152]{1,0:T(8,128)(2,1)S(1)} %copy-done.40, ...), custom_call_target="tpu_custom_call" | custom-call | flops 425984 | bytes 832 | tf_op jit(solution)/shard_map/attend_back/pallas_call | solution.py:597
  368.3 18.0 %collective-permute-done.59 = bf16[416,512]{1,0:T(8,128)(2,1)} collective-permute-done((bf16[416,512]{1,0:T(8,128)(2,1)}, bf16[416,512]{1,0:T(8,128)(2,1)}, u32[]{:S(2)}, u32[]{:S(2)}) %collective-permute-start.59) | collective-permute-done | bytes 426016 | tf_op jit(solution)/shard_map/ppermute | solution.py:55
  388.9 6.2 %collective-permute-done.57 = bf16[416,512]{1,0:T(8,128)(2,1)} collective-permute-done((bf16[416,512]{1,0:T(8,128)(2,1)}, bf16[416,512]{1,0:T(8,128)(2,1)}, u32[]{:S(2)}, u32[]{:S(2)}) %collective-permute-start.57) | collective-permute-done | bytes 426016 | tf_op jit(solution)/shard_map/ppermute | solution.py:55
  401.8 28.8 %collective-permute-done.54 = bf16[416,1152]{1,0:T(8,128)(2,1)S(1)} collective-permute-done((bf16[416,1152]{1,0:T(8,128)(2,1)}, bf16[416,1152]{1,0:T(8,128)(2,1)S(1)}, u32[]{:S(2)}, u32[]{:S(2)}) %collective-permute-start.54) | collective-permute-done | bytes 958496 | tf_op jit(solution)/shard_map/ppermute | solution.py:55
  437.3 4.7 near.2
  448.6 40.9 %collective-permute-done.56 = bf16[208,1152]{1,0:T(8,128)(2,1)S(1)} collective-permute-done((bf16[208,1152]{1,0:T(8,128)(2,1)}, bf16[208,1152]{1,0:T(8,128)(2,1)S(1)}, u32[]{:S(2)}, u32[]{:S(2)}) %collective-permute-start.56) | collective-permute-done | bytes 479264 | tf_op jit(solution)/shard_map/ppermute | solution.py:55
  492.9 5.4 collective-permute-done.65
  501.7 9.7 %collective-permute-done.66 = bf16[272,768]{1,0:T(8,128)(2,1)S(1)} collective-permute-done((bf16[272,768]{1,0:T(8,128)(2,1)S(1)}, bf16[272,768]{1,0:T(8,128)(2,1)S(1)}, u32[]{:S(2)}, u32[]{:S(2)}) %collective-permute-start.66) | collective-permute-done | bytes 417824 | tf_op jit(solution)/shard_map/ppermute | solution.py:55
  527.6 6.7 %fusion.13 = (f32[1,1024,1024]{2,1,0:T(8,128)}, f32[1,1024,1024]{2,1,0:T(8,128)}) fusion(bf16[1024,2048]{1,0:T(8,128)(2,1)} %get-tuple-element.248), kind=kLoop, calls=%fused_computation.30 | loop fusion | flops 2097152 | bytes 12582912 | tf_op jit(solution)/shard_map/broadcast_in_dim | solution.py:1123
  537.4 10.2 %collective-permute-done.68 = bf16[208,512]{1,0:T(8,128)(2,1)S(1)} collective-permute-done((bf16[208,512]{1,0:T(8,128)(2,1)}, bf16[208,512]{1,0:T(8,128)(2,1)S(1)}, u32[]{:S(2)}, u32[]{:S(2)}) %collective-permute-start.68) | collective-permute-done | bytes 213024 | tf_op jit(solution)/shard_map/ppermute | solution.py:55
  558.4 5.1 collective-permute-start.72
  564.9 4.9 collective-permute-done.72
  (613 shorter events, 244.0 us)
Async XLA Ops:
  7.2 507.0 %all-reduce.20.cloned.1.call-start = ((), (), s32[]{:S(2)}) async-start(), calls=%async_computation | async-start | bytes 24969216 | tf_op jit(solution)/shard_map/psum | solution.py:953
  32.5 31.5 %collective-permute-start.14 = (bf16[400,1024]{1,0:T(8,128)(2,1)S(1)}, bf16[400,1024]{1,0:T(8,128)(2,1)S(1)}, u32[]{:S(2)}, u32[]{:S(2)}) collective-permute-start(bf16[400,1024]{1,0:T(8,128)(2,1)S(1)} %fusion.89), channel_id=1, source_target_pairs={{0,64},{8,72},{16,80},{24,88},{32,96},{40,104},{48,112},{56,120},{... | collective-permute-start | bytes 2457608 | tf_op jit(solution)/shard_map/ppermute | solution.py:59
  36.1 27.9 %collective-permute-start.13 = (bf16[400,1024]{1,0:T(8,128)(2,1)S(1)}, bf16[400,1024]{1,0:T(8,128)(2,1)S(1)}, u32[]{:S(2)}, u32[]{:S(2)}) collective-permute-start(bf16[400,1024]{1,0:T(8,128)(2,1)S(1)} %fusion.89), channel_id=1, source_target_pairs={{0,48},{8,56},{16,32},{24,40},{32,16},{40,24},{48,0},{56,8},{64,11... | collective-permute-start | bytes 2457608 | tf_op jit(solution)/shard_map/ppermute | solution.py:59
  39.1 24.9 %collective-permute-start.12 = (bf16[400,1024]{1,0:T(8,128)(2,1)S(1)}, bf16[400,1024]{1,0:T(8,128)(2,1)S(1)}, u32[]{:S(2)}, u32[]{:S(2)}) collective-permute-start(bf16[400,1024]{1,0:T(8,128)(2,1)S(1)} %fusion.89), channel_id=1, source_target_pairs={{0,16},{8,24},{16,0},{24,8},{32,48},{40,56},{48,32},{56,40},{64,80... | collective-permute-start | bytes 2457608 | tf_op jit(solution)/shard_map/ppermute | solution.py:59
  66.4 33.8 %collective-permute-start.16 = (bf16[400,1024]{1,0:T(8,128)(2,1)}, bf16[400,1024]{1,0:T(8,128)(2,1)}, u32[]{:S(2)}, u32[]{:S(2)}) collective-permute-start(bf16[400,1024]{1,0:T(8,128)(2,1)} %get-tuple-element.138), channel_id=1, source_target_pairs={{0,16},{8,24},{16,0},{24,8},{32,48},{40,56},{48,32},{56,40},{64,80... | collective-permute-start | bytes 2457608 | tf_op jit(solution)/shard_map/ppermute | solution.py:59
  68.1 32.1 %collective-permute-start.15 = (bf16[384,1024]{1,0:T(8,128)(2,1)}, bf16[384,1024]{1,0:T(8,128)(2,1)}, u32[]{:S(2)}, u32[]{:S(2)}) collective-permute-start(bf16[384,1024]{1,0:T(8,128)(2,1)} %get-tuple-element.137), channel_id=1, source_target_pairs={{0,64},{8,72},{16,80},{24,88},{32,96},{40,104},{48,112},{56,120},{... | collective-permute-start | bytes 2359304 | tf_op jit(solution)/shard_map/ppermute | solution.py:59
  69.0 26.5 %collective-permute-start.8 = (bf16[208,1152]{1,0:T(8,128)(2,1)}, bf16[208,1152]{1,0:T(8,128)(2,1)S(1)}, u32[]{:S(2)}, u32[]{:S(2)}) collective-permute-start(bf16[208,1152]{1,0:T(8,128)(2,1)} %get-tuple-element.133), channel_id=1, source_target_pairs={{0,1},{1,0},{2,3},{3,2},{4,5},{5,4},{6,7},{7,6},{8,9},{9,8},{10,11... | collective-permute-start | bytes 1437704 | tf_op jit(solution)/shard_map/ppermute | solution.py:55
  70.7 24.8 %collective-permute-start.7 = (bf16[192,1152]{1,0:T(8,128)(2,1)S(1)}, bf16[192,1152]{1,0:T(8,128)(2,1)S(1)}, u32[]{:S(2)}, u32[]{:S(2)}) collective-permute-start(bf16[192,1152]{1,0:T(8,128)(2,1)S(1)} %get-tuple-element.132), channel_id=1, source_target_pairs={{0,4},{1,5},{2,6},{3,7},{4,0},{5,1},{6,2},{7,3},{8,12},{9,13},{10,... | collective-permute-start | bytes 1327112 | tf_op jit(solution)/shard_map/ppermute | solution.py:55
  72.4 25.6 %collective-permute-start.9 = (bf16[224,1152]{1,0:T(8,128)(2,1)S(1)}, bf16[224,1152]{1,0:T(8,128)(2,1)S(1)}, u32[]{:S(2)}, u32[]{:S(2)}) collective-permute-start(bf16[224,1152]{1,0:T(8,128)(2,1)S(1)} %get-tuple-element.134), channel_id=1, source_target_pairs={{0,3},{1,2},{2,1},{3,0},{4,7},{5,6},{6,5},{7,4},{8,11},{9,10},{10,... | collective-permute-start | bytes 1548296 | tf_op jit(solution)/shard_map/ppermute | solution.py:55
  109.6 30.2 %collective-permute-start.24 = (bf16[384,1024]{1,0:T(8,128)(2,1)}, bf16[384,1024]{1,0:T(8,128)(2,1)S(1)}, u32[]{:S(2)}, u32[]{:S(2)}) collective-permute-start(bf16[384,1024]{1,0:T(8,128)(2,1)} %collective-permute-done.15.refs_0_), channel_id=1, source_target_pairs={{0,8},{8,0},{16,24},{24,16},{32,40},{40,32},{48,56},{56,48},{64,72... | collective-permute-start | bytes 2359304 | tf_op jit(solution)/shard_map/ppermute | solution.py:59
  109.6 24.0 %collective-permute-start.31 = (bf16[208,1152]{1,0:T(8,128)(2,1)}, bf16[208,1152]{1,0:T(8,128)(2,1)S(1)}, u32[]{:S(2)}, u32[]{:S(2)}) collective-permute-start(bf16[208,1152]{1,0:T(8,128)(2,1)} %fence.11.refs_1_), channel_id=1, source_target_pairs={{0,4},{1,5},{2,6},{3,7},{4,0},{5,1},{6,2},{7,3},{8,12},{9,13},{10,... | collective-permute-start | bytes 1437704 | tf_op jit(solution)/shard_map/ppermute | solution.py:55
  140.7 23.6 %collective-permute-start.33 = (bf16[208,1152]{1,0:T(8,128)(2,1)}, bf16[208,1152]{1,0:T(8,128)(2,1)}, u32[]{:S(2)}, u32[]{:S(2)}) collective-permute-start(bf16[208,1152]{1,0:T(8,128)(2,1)} %get-tuple-element.147.refs_16_), channel_id=1, source_target_pairs={{0,1},{1,0},{2,3},{3,2},{4,5},{5,4},{6,7},{7,6},{8,9},{9,8},{10,11... | collective-permute-start | bytes 1437704 | tf_op jit(solution)/shard_map/ppermute | solution.py:55
  186.9 30.3 %collective-permute-start.37 = (bf16[208,1152]{1,0:T(8,128)(2,1)}, bf16[208,1152]{1,0:T(8,128)(2,1)S(1)}, u32[]{:S(2)}, u32[]{:S(2)}) collective-permute-start(bf16[208,1152]{1,0:T(8,128)(2,1)} %fence.12.refs_0_.refs_9_), channel_id=1, source_target_pairs={{0,4},{1,5},{2,6},{3,7},{4,0},{5,1},{6,2},{7,3},{8,12},{9,13},{10,... | collective-permute-start | bytes 1437704 | tf_op jit(solution)/shard_map/ppermute | solution.py:55
  188.5 28.7 %collective-permute-start.36 = (bf16[208,1152]{1,0:T(8,128)(2,1)}, bf16[208,1152]{1,0:T(8,128)(2,1)S(1)}, u32[]{:S(2)}, u32[]{:S(2)}) collective-permute-start(bf16[208,1152]{1,0:T(8,128)(2,1)} %fence.12.refs_0_.refs_9_), channel_id=1, source_target_pairs={{0,3},{1,2},{2,1},{3,0},{4,7},{5,6},{6,5},{7,4},{8,11},{9,10},{10,... | collective-permute-start | bytes 1437704 | tf_op jit(solution)/shard_map/ppermute | solution.py:55
  191.1 26.1 %collective-permute-start.35 = (bf16[208,1152]{1,0:T(8,128)(2,1)}, bf16[208,1152]{1,0:T(8,128)(2,1)S(1)}, u32[]{:S(2)}, u32[]{:S(2)}) collective-permute-start(bf16[208,1152]{1,0:T(8,128)(2,1)} %fence.12.refs_0_.refs_9_), channel_id=1, source_target_pairs={{0,1},{1,0},{2,3},{3,2},{4,5},{5,4},{6,7},{7,6},{8,9},{9,8},{10,11... | collective-permute-start | bytes 1437704 | tf_op jit(solution)/shard_map/ppermute | solution.py:55
  193.1 47.1 %collective-permute-start.43 = (bf16[224,1152]{1,0:T(8,128)(2,1)}, bf16[224,1152]{1,0:T(8,128)(2,1)S(1)}, u32[]{:S(2)}, u32[]{:S(2)}) collective-permute-start(bf16[224,1152]{1,0:T(8,128)(2,1)} %copy-done.47), channel_id=1, source_target_pairs={{0,3},{1,2},{2,1},{3,0},{4,7},{5,6},{6,5},{7,4},{8,11},{9,10},{10,... | collective-permute-start | bytes 1548296 | tf_op jit(solution)/shard_map/ppermute | solution.py:55
  218.7 25.5 %collective-permute-start.40 = (bf16[224,1152]{1,0:T(8,128)(2,1)S(1)}, bf16[224,1152]{1,0:T(8,128)(2,1)S(1)}, u32[]{:S(2)}, u32[]{:S(2)}) collective-permute-start(bf16[224,1152]{1,0:T(8,128)(2,1)S(1)} %get-tuple-element.165.refs_23_), channel_id=1, source_target_pairs={{0,3},{1,2},{2,1},{3,0},{4,7},{5,6},{6,5},{7,4},{8,11},{9,10},{10,... | collective-permute-start | bytes 1548296 | tf_op jit(solution)/shard_map/ppermute | solution.py:55
  267.8 28.2 %collective-permute-start.47 = (bf16[224,1152]{1,0:T(8,128)(2,1)S(1)}, bf16[224,1152]{1,0:T(8,128)(2,1)S(1)}, u32[]{:S(2)}, u32[]{:S(2)}) collective-permute-start(bf16[224,1152]{1,0:T(8,128)(2,1)S(1)} %pad_maximum_fusion.1), channel_id=1, source_target_pairs={{0,3},{1,2},{2,1},{3,0},{4,7},{5,6},{6,5},{7,4},{8,11},{9,10},{10,... | collective-permute-start | bytes 1548296 | tf_op jit(solution)/shard_map/ppermute | solution.py:55
  347.9 89.4 %collective-permute-start.60 = (bf16[8,33,8,1024]{3,2,1,0:T(8,128)(2,1)}, bf16[8,33,8,1024]{3,2,1,0:T(8,128)(2,1)}, u32[]{:S(2)}, u32[]{:S(2)}) collective-permute-start(bf16[8,33,8,1024]{3,2,1,0:T(8,128)(2,1)} %theirs.2), channel_id=1, source_target_pairs={{0,8},{8,0},{16,24},{24,16},{32,40},{40,32},{48,56},{56,48},{64,72... | collective-permute-start | bytes 12976136 | tf_op jit(solution)/shard_map/ppermute | solution.py:59
  352.5 49.3 %collective-permute-start.53 = (bf16[416,1152]{1,0:T(8,128)(2,1)}, bf16[416,1152]{1,0:T(8,128)(2,1)}, u32[]{:S(2)}, u32[]{:S(2)}) collective-permute-start(bf16[416,1152]{1,0:T(8,128)(2,1)} %fence.13.refs_24_), channel_id=1, source_target_pairs={{0,1},{1,0},{2,3},{3,2},{4,5},{5,4},{6,7},{7,6},{8,9},{9,8},{10,11... | collective-permute-start | bytes 2875400 | tf_op jit(solution)/shard_map/ppermute | solution.py:55
  355.8 30.5 %collective-permute-start.59 = (bf16[416,512]{1,0:T(8,128)(2,1)}, bf16[416,512]{1,0:T(8,128)(2,1)}, u32[]{:S(2)}, u32[]{:S(2)}) collective-permute-start(bf16[416,512]{1,0:T(8,128)(2,1)} %pad_maximum_fusion.10), channel_id=1, source_target_pairs={{0,2},{1,3},{2,0},{3,1},{4,6},{5,7},{6,4},{7,5},{8,10},{9,11},{10,... | collective-permute-start | bytes 1277960 | tf_op jit(solution)/shard_map/ppermute | solution.py:55
  358.6 30.1 %collective-permute-start.58 = (bf16[416,512]{1,0:T(8,128)(2,1)}, bf16[416,512]{1,0:T(8,128)(2,1)}, u32[]{:S(2)}, u32[]{:S(2)}) collective-permute-start(bf16[416,512]{1,0:T(8,128)(2,1)} %pad_maximum_fusion.9), channel_id=1, source_target_pairs={{0,3},{1,2},{2,1},{3,0},{4,7},{5,6},{6,5},{7,4},{8,11},{9,10},{10,... | collective-permute-start | bytes 1277960 | tf_op jit(solution)/shard_map/ppermute | solution.py:55
  362.8 32.4 %collective-permute-start.57 = (bf16[416,512]{1,0:T(8,128)(2,1)}, bf16[416,512]{1,0:T(8,128)(2,1)}, u32[]{:S(2)}, u32[]{:S(2)}) collective-permute-start(bf16[416,512]{1,0:T(8,128)(2,1)} %pad_maximum_fusion.8), channel_id=1, source_target_pairs={{0,1},{1,0},{2,3},{3,2},{4,5},{5,4},{6,7},{7,6},{8,9},{9,8},{10,11... | collective-permute-start | bytes 1277960 | tf_op jit(solution)/shard_map/ppermute | solution.py:55
  386.3 44.3 %collective-permute-start.54 = (bf16[416,1152]{1,0:T(8,128)(2,1)}, bf16[416,1152]{1,0:T(8,128)(2,1)S(1)}, u32[]{:S(2)}, u32[]{:S(2)}) collective-permute-start(bf16[416,1152]{1,0:T(8,128)(2,1)} %fence.14.refs_26_), channel_id=1, source_target_pairs={{0,3},{1,2},{2,1},{3,0},{4,7},{5,6},{6,5},{7,4},{8,11},{9,10},{10,... | collective-permute-start | bytes 2875400 | tf_op jit(solution)/shard_map/ppermute | solution.py:55
  388.7 42.0 %collective-permute-start.55 = (bf16[416,1152]{1,0:T(8,128)(2,1)}, bf16[416,1152]{1,0:T(8,128)(2,1)S(1)}, u32[]{:S(2)}, u32[]{:S(2)}) collective-permute-start(bf16[416,1152]{1,0:T(8,128)(2,1)} %fence.15.refs_25_), channel_id=1, source_target_pairs={{0,2},{1,3},{2,0},{3,1},{4,6},{5,7},{6,4},{7,5},{8,10},{9,11},{10,... | collective-permute-start | bytes 2875400 | tf_op jit(solution)/shard_map/ppermute | solution.py:55
  400.2 46.0 %collective-permute-start.64 = (bf16[8,17,8,768]{3,2,1,0:T(8,128)(2,1)S(1)}, bf16[8,17,8,768]{3,2,1,0:T(8,128)(2,1)S(1)}, u32[]{:S(2)}, u32[]{:S(2)}) collective-permute-start(bf16[8,17,8,768]{3,2,1,0:T(8,128)(2,1)S(1)} %theirs.3), channel_id=1, source_target_pairs={{0,8},{8,0},{16,24},{24,16},{32,40},{40,32},{48,56},{56,48},{64,72... | collective-permute-start | bytes 5013512 | tf_op jit(solution)/shard_map/ppermute | solution.py:59
  433.3 56.1 %collective-permute-start.56 = (bf16[208,1152]{1,0:T(8,128)(2,1)}, bf16[208,1152]{1,0:T(8,128)(2,1)S(1)}, u32[]{:S(2)}, u32[]{:S(2)}) collective-permute-start(bf16[208,1152]{1,0:T(8,128)(2,1)} %slice.694), channel_id=1, source_target_pairs={{0,4},{1,5},{2,6},{3,7},{4,0},{5,1},{6,2},{7,3},{8,12},{9,13},{10,... | collective-permute-start | bytes 1437704 | tf_op jit(solution)/shard_map/ppermute | solution.py:55
  442.0 70.4 %collective-permute-start.61 = (bf16[528,1024]{1,0:T(8,128)(2,1)S(1)}, bf16[528,1024]{1,0:T(8,128)(2,1)S(1)}, u32[]{:S(2)}, u32[]{:S(2)}) collective-permute-start(bf16[528,1024]{1,0:T(8,128)(2,1)S(1)} %bitcast.204), channel_id=1, source_target_pairs={{0,1},{1,0},{2,3},{3,2},{4,5},{5,4},{6,7},{7,6},{8,9},{9,8},{10,11... | collective-permute-start | bytes 3244040 | tf_op jit(solution)/shard_map/ppermute | solution.py:55
  442.1 70.3 %collective-permute-start.62 = (bf16[528,1024]{1,0:T(8,128)(2,1)S(1)}, bf16[528,1024]{1,0:T(8,128)(2,1)S(1)}, u32[]{:S(2)}, u32[]{:S(2)}) collective-permute-start(bf16[528,1024]{1,0:T(8,128)(2,1)S(1)} %bitcast.202), channel_id=1, source_target_pairs={{0,3},{1,2},{2,1},{3,0},{4,7},{5,6},{6,5},{7,4},{8,11},{9,10},{10,... | collective-permute-start | bytes 3244040 | tf_op jit(solution)/shard_map/ppermute | solution.py:55
  444.8 67.6 %collective-permute-start.63 = (bf16[528,1024]{1,0:T(8,128)(2,1)S(1)}, bf16[528,1024]{1,0:T(8,128)(2,1)S(1)}, u32[]{:S(2)}, u32[]{:S(2)}) collective-permute-start(bf16[528,1024]{1,0:T(8,128)(2,1)S(1)} %bitcast.200), channel_id=1, source_target_pairs={{0,2},{1,3},{2,0},{3,1},{4,6},{5,7},{6,4},{7,5},{8,10},{9,11},{10,... | collective-permute-start | bytes 3244040 | tf_op jit(solution)/shard_map/ppermute | solution.py:55
  448.4 49.9 %collective-permute-start.65 = (bf16[272,768]{1,0:T(8,128)(2,1)S(1)}, bf16[272,768]{1,0:T(8,128)(2,1)S(1)}, u32[]{:S(2)}, u32[]{:S(2)}) collective-permute-start(bf16[272,768]{1,0:T(8,128)(2,1)S(1)} %bitcast.216), channel_id=1, source_target_pairs={{0,1},{1,0},{2,3},{3,2},{4,5},{5,4},{6,7},{7,6},{8,9},{9,8},{10,11... | collective-permute-start | bytes 1253384 | tf_op jit(solution)/shard_map/ppermute | solution.py:55
  526.8 25.3 %collective-permute-start.70 = (bf16[264,1024]{1,0:T(8,128)(2,1)}, bf16[264,1024]{1,0:T(8,128)(2,1)}, u32[]{:S(2)}, u32[]{:S(2)}) collective-permute-start(bf16[264,1024]{1,0:T(8,128)(2,1)} %fence.16.refs_1_), channel_id=1, source_target_pairs={{0,4},{1,5},{2,6},{3,7},{4,0},{5,1},{6,2},{7,3},{8,12},{9,13},{10,... | collective-permute-start | bytes 1622024 | tf_op jit(solution)/shard_map/ppermute | solution.py:55
  (190 other events, 2132.2 us)
Sparse Core Ops, SparseCore 0:
  306.8 180.9 all-reduce.19

commit v10 on v8

--- a/solution.py
+++ b/solution.py
@@ -1055,7 +1055,7 @@
         [unrotate(kv_sum[:, :HD], own_cos, own_sin), kv_sum[:, HD:]], axis=1
     ).astype(bf16)
 
-    out = pair_sum(out, mp_swap, tuple(last_sent))
+    out = pair_sum(out, mp_swap, (grads[0],))
     prefix_output = (hidden_d + out[:PREF]).astype(bf16)[None]
     action_output = (hidden_a + out[PREF:, :DA])[:ACT].astype(bf16)[None]
 

time: 557 us -> 553 us (level)
  waiting for transfers between devices: 175 us -> 159 us
    ppermute x52, waiting for transfers between devices: 156 us -> 145 us  [mp_swap(): return lax.ppermute(array, 'mp', [(i, i ^ step) for i in range(N_MP)])]
    unnamed x315 -> x291, local copies, waits for them, and re-layouts: 30.4 us -> 29.2 us
  transfers between devices with their start and end apart: 76 -> 76, of which waited for: 29 -> 25; matrix products, arithmetic and copies ran while one was open for 21% -> 25% of each run, Pallas kernels for 15% -> 16%
where the time goes in v10:
time: 553 us; the launch traced here: 543 us
  waiting for transfers between devices  159 us (29%)
  Pallas kernels  103 us (19%)
  starting transfers between devices  93.4 us (17%)
  other arithmetic  70.6 us (13%)
  matrix products  51.5 us (9%)
  local copies, waits for them, and re-layouts  47.5 us (9%)
  between operations  17.5 us (3%)
    ppermute x52, waiting for transfers between devices, mp_swap(): return lax.ppermute(array, 'mp', [(i, i ^ step) for i in range(N_MP)])  145 us
    ppermute x52, starting transfers between devices, mp_swap(): return lax.ppermute(array, 'mp', [(i, i ^ step) for i in range(N_MP)])  69.5 us
    pallas_call x3, Pallas kernels, feed(): pl.pallas_call(functools.partial(feed_kernel, layout), grid=(1,), in_spec...  44 us
    dot_general x12, matrix products, t_dot(): lax.dot_general(a, b, (((0,), (0,)), ((), ())), preferred_element_type=f32)  32.6 us
    unnamed x291, local copies, waits for them, and re-layouts  29.2 us
    ppermute x23, starting transfers between devices, dp_swap(): return lax.ppermute(array, 'dp', [(i, i ^ step) for i in range(16)])  23.8 us
    ppermute x23, waiting for transfers between devices, dp_swap(): return lax.ppermute(array, 'dp', [(i, i ^ step) for i in range(16)])  14 us
    pallas_call x1, Pallas kernels, attend_back(): pl.pallas_call(attend_back_kernel, in_specs=[VMEM] * len(given) + [ANY] *...  12.9 us
  transfers between devices with their start and end apart: 76, of which 25 were waited for; matrix products, arithmetic and copies ran while one was open for 25% of the time, Pallas kernels for 16%

profile of v10, /device:TPU:0, one launch (start us, length us, event | category | flops | bytes accessed | tf_op | source)
XLA Modules:
  0.0 543.1 jit_solution(12223324194236412598)
XLA Ops:
  23.0 7.4 %collective-permute-done.1 = bf16[2,8,5760]{2,1,0:T(8,128)(2,1)S(1)} collective-permute-done((bf16[2,8,5760]{2,1,0:T(8,128)(2,1)S(1)}, bf16[2,8,5760]{2,1,0:T(8,128)(2,1)S(1)}, u32[]{:S(2)}, u32[]{:S(2)}) %collective-permute-start.1) | collective-permute-done | bytes 184352 | tf_op jit(solution)/shard_map/ppermute | solution.py:55
  35.8 3.6 collective-permute-start.14
  49.3 5.8 %collective-permute-done.5.refs_1_.refs_4_.refs_2_ = bf16[208,1152]{1,0:T(8,128)(2,1)S(1)} collective-permute-done((bf16[208,1152]{1,0:T(8,128)(2,1)S(1)}, bf16[208,1152]{1,0:T(8,128)(2,1)S(1)}, u32[]{:S(2)}, u32[]{:S(2)}) %collective-permute-start.5) | collective-permute-done | bytes 479264 | tf_op jit(solution)/shard_map/ppermute | solution.py:55
  59.5 6.2 %collective-permute-done.14.refs_2_ = bf16[400,1024]{1,0:T(8,128)(2,1)S(1)} collective-permute-done((bf16[400,1024]{1,0:T(8,128)(2,1)}, bf16[400,1024]{1,0:T(8,128)(2,1)S(1)}, u32[]{:S(2)}, u32[]{:S(2)}) %collective-permute-start.14) | collective-permute-done | bytes 819232 | tf_op jit(solution)/shard_map/ppermute | solution.py:59
  68.7 4.2 multiply_sine_fusion
  78.6 6.6 %collective-permute-done.9.refs_4_.refs_6_ = bf16[224,1152]{1,0:T(8,128)(2,1)S(1)} collective-permute-done((bf16[224,1152]{1,0:T(8,128)(2,1)}, bf16[224,1152]{1,0:T(8,128)(2,1)S(1)}, u32[]{:S(2)}, u32[]{:S(2)}) %collective-permute-start.9) | collective-permute-done | bytes 516128 | tf_op jit(solution)/shard_map/ppermute | solution.py:55
  109.3 3.7 collective-permute-done.19
  138.7 8.5 %assemble.1 = (bf16[8,2,8,8,1024]{4,3,2,1,0:T(8,128)(2,1)}, bf16[8,2,8,8,1024]{4,3,2,1,0:T(8,128)(2,1)}, bf16[8,2,8,8,512]{4,3,2,1,0:T(8,128)(2,1)}, bf16[8,2,8,...) custom-call(s32[2]{0:T(128)S(1)} %pad_add_fusion.2.place_ref, ...), custom_call_target="tpu_custom_call" | custom-call | tf_op jit(solution)/shard_map/assemble/pallas_call | solution.py:242
  151.3 6.3 %keys_of.1 = (bf16[384,1152]{1,0:T(8,128)(2,1)}, bf16[32,1024]{1,0:T(8,128)(2,1)S(1)}, bf16[1664,256]{1,0:T(8,128)(2,1)}, bf16[1664,256]{1,0:T(8,128)(2,1)}) custom-call(bf16[208,1152]{1,0:T(8,128)(2,1)S(1)} %copy-done.10, bf16[208,1152]{1,0:T(8,128)(2,1)S(1)} %collective-permute-done.4.refs_0_.refs_3_.refs_1_, ...), custom_call_target="tpu_custom_call" | custom-call | flops 1962934272 | bytes 8388608 | tf_op jit(solution)/shard_map/keys_of/pallas_call | solution.py:292
  157.6 11.3 %attend.1 = (bf16[832,256]{1,0:T(8,128)(2,1)S(1)}, bf16[208,1024]{1,0:T(8,128)(2,1)S(1)}, f32[832,1]{1,0:T(8,128)S(1)}, f32[832,1]{1,0:T(8,128)S(1)}, f32[192,11...) custom-call(bf16[384,1152]{1,0:T(8,128)(2,1)} %get-tuple-element.149.refs_0_, ...), custom_call_target="tpu_custom_call" | custom-call | flops 2399141888 | bytes 20971520 | tf_op jit(solution)/shard_map/attend/pallas_call | solution.py:508
  176.9 10.0 %feed.3 = (bf16[1536,896]{1,0:T(8,128)(2,1)}, bf16[1536,1792]{1,0:T(8,128)(2,1)}, bf16[1536,1152]{1,0:T(8,128)(2,1)}, bf16[1536,1152]{1,0:T(8,128)(2,1)}, bf16[1...) custom-call(bf16[208,1152]{1,0:T(8,128)(2,1)S(1)} %copy-done.11, ...), custom_call_target="tpu_custom_call" | custom-call | flops 2078801920 | bytes 12263424 | tf_op jit(solution)/shard_map/feed/pallas_call | solution.py:436
  194.3 15.5 %feed.4 = (bf16[1536,896]{1,0:T(8,128)(2,1)}, bf16[1536,1792]{1,0:T(8,128)(2,1)}, bf16[1536,1152]{1,0:T(8,128)(2,1)}, bf16[1536,1152]{1,0:T(8,128)(2,1)}, bf16[1...) custom-call(bf16[208,1152]{1,0:T(8,128)(2,1)S(1)} %collective-permut, ...), custom_call_target="tpu_custom_call", output_to_operand_aliasing={{0}: (13, {}), {1}: (14, {}), {2}: (15, {}), {3}: (16, {}),... | custom-call | flops 6236405760 | bytes 12263424 | tf_op jit(solution)/shard_map/feed/pallas_call | solution.py:436
  221.4 18.4 %feed.5 = (bf16[1536,896]{1,0:T(8,128)(2,1)}, bf16[1536,1792]{1,0:T(8,128)(2,1)}, bf16[1536,1152]{1,0:T(8,128)(2,1)}, bf16[1536,1152]{1,0:T(8,128)(2,1)}, bf16[1...) custom-call(bf16[192,1152]{1,0:T(8,128)(2,1)S(1)} %collective-permut, ...), custom_call_target="tpu_custom_call", output_to_operand_aliasing={{0}: (17, {}), {1}: (18, {}), {2}: (19, {}), {3}: (20, {}),... | custom-call | flops 8315207680 | bytes 12263424 | tf_op jit(solution)/shard_map/feed/pallas_call | solution.py:436
  244.0 8.2 %convolution_convert_fusion.5 = bf16[896,1152]{1,0:T(8,128)(2,1)} fusion(bf16[1536,896]{1,0:T(8,128)(2,1)} %get-tuple-element.185, bf16[1536,1152]{1,0:T(8,128)(2,1)} %get-tuple-element.238), kind=kOutput, calls=%fused_computation.14 | convolution fusion | flops 3171926016 | bytes 8355840 | tf_op jit(solution)/shard_map/dot_general | solution.py:710
  252.2 9.1 %convolution_convert_fusion = bf16[1792,1152]{1,0:T(8,128)(2,1)} fusion(bf16[1536,1792]{1,0:T(8,128)(2,1)S(1)} %bitcast.210, bf16[1536,1152]{1,0:T(8,128)(2,1)S(1)} %copy-done.71), kind=kOutput, calls=%fused_computation | convolution fusion | flops 6343852032 | bytes 13172736 | tf_op jit(solution)/shard_map/dot_general | solution.py:710
  261.3 4.4 convolution_convert_fusion.1
  269.1 5.0 collective-permute-done.46
  283.9 3.3 convolution_convert_fusion.4
  296.2 12.9 %attend_back.1 = (f32[192,1152]{1,0:T(8,128)}, f32[16,1024]{1,0:T(8,128)S(1)}, bf16[208,1152]{1,0:T(8,128)(2,1)}, bf16[192,1152]{1,0:T(8,128)(2,1)}, bf16[16,102...) custom-call(bf16[96,1152]{1,0:T(8,128)(2,1)S(1)} %get-tuple-element., ...), custom_call_target="tpu_custom_call" | custom-call | flops 425984 | bytes 832 | tf_op jit(solution)/shard_map/attend_back/pallas_call | solution.py:597
  330.1 3.5 convolution_convert_fusion.7
  336.8 8.7 %collective-permute-done.58 = bf16[416,512]{1,0:T(8,128)(2,1)} collective-permute-done((bf16[416,512]{1,0:T(8,128)(2,1)}, bf16[416,512]{1,0:T(8,128)(2,1)}, u32[]{:S(2)}, u32[]{:S(2)}) %collective-permute-start.58) | collective-permute-done | bytes 426016 | tf_op jit(solution)/shard_map/ppermute | solution.py:55
  352.4 5.6 %near.2 = (bf16[66,8,1024]{2,1,0:T(8,128)(2,1)S(1)}, bf16[66,8,1024]{2,1,0:T(8,128)(2,1)S(1)}, bf16[66,8,1024]{2,1,0:T(8,128)(2,1)}, bf16[66,8,1024]{2,1,0:T(8,128)(2,1)S(1)}) custom-call(s32[2]{0:T(128)S(1)} %pad_add_fusion.3.place_ref, bf16[2,8,8,8,1024]{4,3,2,1,0:T(8,128)(2,1)S(1)} %bitcast.170, bf16[2,8,8,8,1024]{4,3,2,1,0:T(8,128)(2,1)S(1)} %bitcast.172, ...), custom_call_target="tpu_custom_call" | custom-call | tf_op jit(solution)/shard_map/near/pallas_call | solution.py:660
  367.8 35.5 %collective-permute-done.64 = bf16[272,768]{1,0:T(8,128)(2,1)} collective-permute-done((bf16[272,768]{1,0:T(8,128)(2,1)S(1)}, bf16[272,768]{1,0:T(8,128)(2,1)}, u32[]{:S(2)}, u32[]{:S(2)}) %collective-permute-start.64) | collective-permute-done | bytes 417824 | tf_op jit(solution)/shard_map/ppermute | solution.py:55
  408.6 3.6 fusion.85
  417.5 15.9 %collective-permute-done.69 = bf16[528,1024]{1,0:T(8,128)(2,1)S(1)} collective-permute-done((bf16[528,1024]{1,0:T(8,128)(2,1)}, bf16[528,1024]{1,0:T(8,128)(2,1)S(1)}, u32[]{:S(2)}, u32[]{:S(2)}) %collective-permute-start.69) | collective-permute-done | bytes 1081376 | tf_op jit(solution)/shard_map/ppermute | solution.py:55
  437.6 15.8 %collective-permute-done.53 = bf16[416,1152]{1,0:T(8,128)(2,1)S(1)} collective-permute-done((bf16[416,1152]{1,0:T(8,128)(2,1)}, bf16[416,1152]{1,0:T(8,128)(2,1)S(1)}, u32[]{:S(2)}, u32[]{:S(2)}) %collective-permute-start.53) | collective-permute-done | bytes 958496 | tf_op jit(solution)/shard_map/ppermute | solution.py:55
  453.4 19.4 %collective-permute-done.55 = bf16[416,1152]{1,0:T(8,128)(2,1)S(1)} collective-permute-done((bf16[416,1152]{1,0:T(8,128)(2,1)}, bf16[416,1152]{1,0:T(8,128)(2,1)S(1)}, u32[]{:S(2)}, u32[]{:S(2)}) %collective-permute-start.55) | collective-permute-done | bytes 958496 | tf_op jit(solution)/shard_map/ppermute | solution.py:55
  474.9 3.8 collective-permute-done.70
  487.6 5.9 %convert_bitcast_fusion = (f32[1152,864]{0,1:T(8,128)}, f32[1152,864]{0,1:T(8,128)}) fusion(bf16[1792,1152]{1,0:T(8,128)(2,1)} %get-tuple-element.246.refs_1_.refs_4_), kind=kLoop, calls=%fused_computation.9 | loop fusion | flops 1990656 | bytes 11943936 | tf_op jit(solution)/shard_map/transpose | solution.py:1120
  494.4 3.7 slice_convert_fusion
  500.0 6.0 %collective-permute-start.73 = (bf16[2,8,5760]{2,1,0:T(8,128)(2,1)}, bf16[2,8,5760]{2,1,0:T(8,128)(2,1)}, u32[]{:S(2)}, u32[]{:S(2)}) collective-permute-start(bf16[2,8,5760]{2,1,0:T(8,128)(2,1)} %get-tuple-element.279), channel_id=1, source_target_pairs={{0,32},{8,40},{16,48},{24,56},{32,0},{40,8},{48,16},{56,24},{64,96... | collective-permute-start | bytes 552968 | tf_op jit(solution)/shard_map/ppermute | solution.py:59
  506.0 6.8 %fusion.13 = (f32[1,1024,1024]{2,1,0:T(8,128)}, f32[1,1024,1024]{2,1,0:T(8,128)}) fusion(bf16[1024,2048]{1,0:T(8,128)(2,1)} %get-tuple-element.248), kind=kLoop, calls=%fused_computation.30 | loop fusion | flops 2097152 | bytes 12582912 | tf_op jit(solution)/shard_map/broadcast_in_dim | solution.py:1123
  (595 shorter events, 240.9 us)
Async XLA Ops:
  7.2 480.4 %all-reduce.20.cloned.1.call-start = ((), (), s32[]{:S(2)}) async-start(), calls=%async_computation | async-start | bytes 24969216 | tf_op jit(solution)/shard_map/psum | solution.py:953
  35.8 29.9 %collective-permute-start.14 = (bf16[400,1024]{1,0:T(8,128)(2,1)}, bf16[400,1024]{1,0:T(8,128)(2,1)S(1)}, u32[]{:S(2)}, u32[]{:S(2)}) collective-permute-start(bf16[400,1024]{1,0:T(8,128)(2,1)} %fusion.91), channel_id=1, source_target_pairs={{0,64},{8,72},{16,80},{24,88},{32,96},{40,104},{48,112},{56,120},{... | collective-permute-start | bytes 2457608 | tf_op jit(solution)/shard_map/ppermute | solution.py:59
  39.4 26.3 %collective-permute-start.13 = (bf16[400,1024]{1,0:T(8,128)(2,1)}, bf16[400,1024]{1,0:T(8,128)(2,1)S(1)}, u32[]{:S(2)}, u32[]{:S(2)}) collective-permute-start(bf16[400,1024]{1,0:T(8,128)(2,1)} %fusion.91), channel_id=1, source_target_pairs={{0,48},{8,56},{16,32},{24,40},{32,16},{40,24},{48,0},{56,8},{64,11... | collective-permute-start | bytes 2457608 | tf_op jit(solution)/shard_map/ppermute | solution.py:59
  42.4 23.3 %collective-permute-start.12 = (bf16[400,1024]{1,0:T(8,128)(2,1)}, bf16[400,1024]{1,0:T(8,128)(2,1)S(1)}, u32[]{:S(2)}, u32[]{:S(2)}) collective-permute-start(bf16[400,1024]{1,0:T(8,128)(2,1)} %fusion.91), channel_id=1, source_target_pairs={{0,16},{8,24},{16,0},{24,8},{32,48},{40,56},{48,32},{56,40},{64,80... | collective-permute-start | bytes 2457608 | tf_op jit(solution)/shard_map/ppermute | solution.py:59
  67.1 23.4 %collective-permute-start.15 = (bf16[384,1024]{1,0:T(8,128)(2,1)}, bf16[384,1024]{1,0:T(8,128)(2,1)}, u32[]{:S(2)}, u32[]{:S(2)}) collective-permute-start(bf16[384,1024]{1,0:T(8,128)(2,1)} %get-tuple-element.137), channel_id=1, source_target_pairs={{0,64},{8,72},{16,80},{24,88},{32,96},{40,104},{48,112},{56,120},{... | collective-permute-start | bytes 2359304 | tf_op jit(solution)/shard_map/ppermute | solution.py:59
  67.2 23.4 %collective-permute-start.16 = (bf16[400,1024]{1,0:T(8,128)(2,1)}, bf16[400,1024]{1,0:T(8,128)(2,1)}, u32[]{:S(2)}, u32[]{:S(2)}) collective-permute-start(bf16[400,1024]{1,0:T(8,128)(2,1)} %get-tuple-element.138), channel_id=1, source_target_pairs={{0,16},{8,24},{16,0},{24,8},{32,48},{40,56},{48,32},{56,40},{64,80... | collective-permute-start | bytes 2457608 | tf_op jit(solution)/shard_map/ppermute | solution.py:59
  76.0 20.8 %collective-permute-start.23 = (bf16[400,1024]{1,0:T(8,128)(2,1)}, bf16[400,1024]{1,0:T(8,128)(2,1)S(1)}, u32[]{:S(2)}, u32[]{:S(2)}) collective-permute-start(bf16[400,1024]{1,0:T(8,128)(2,1)} %copy-done.13), channel_id=1, source_target_pairs={{0,8},{8,0},{16,24},{24,16},{32,40},{40,32},{48,56},{56,48},{64,72... | collective-permute-start | bytes 2457608 | tf_op jit(solution)/shard_map/ppermute | solution.py:59
  85.2 23.5 %collective-permute-start.17 = (bf16[416,1024]{1,0:T(8,128)(2,1)}, bf16[416,1024]{1,0:T(8,128)(2,1)}, u32[]{:S(2)}, u32[]{:S(2)}) collective-permute-start(bf16[416,1024]{1,0:T(8,128)(2,1)} %copy-done.67), channel_id=1, source_target_pairs={{0,48},{8,56},{16,32},{24,40},{32,16},{40,24},{48,0},{56,8},{64,11... | collective-permute-start | bytes 2555912 | tf_op jit(solution)/shard_map/ppermute | solution.py:59
  126.8 20.4 %collective-permute-start.33 = (bf16[208,1152]{1,0:T(8,128)(2,1)}, bf16[208,1152]{1,0:T(8,128)(2,1)}, u32[]{:S(2)}, u32[]{:S(2)}) collective-permute-start(bf16[208,1152]{1,0:T(8,128)(2,1)} %get-tuple-element.147.refs_16_), channel_id=1, source_target_pairs={{0,1},{1,0},{2,3},{3,2},{4,5},{5,4},{6,7},{7,6},{8,9},{9,8},{10,11... | collective-permute-start | bytes 1437704 | tf_op jit(solution)/shard_map/ppermute | solution.py:55
  128.2 23.1 %collective-permute-start.11 = (bf16[112,1152]{1,0:T(8,128)(2,1)S(1)}, bf16[112,1152]{1,0:T(8,128)(2,1)S(1)}, u32[]{:S(2)}, u32[]{:S(2)}) collective-permute-start(bf16[112,1152]{1,0:T(8,128)(2,1)S(1)} %get-tuple-element.136), channel_id=1, source_target_pairs={{0,3},{1,2},{2,1},{3,0},{4,7},{5,6},{6,5},{7,4},{8,11},{9,10},{10,... | collective-permute-start | bytes 774152 | tf_op jit(solution)/shard_map/ppermute | solution.py:55
  132.3 84.0 %collective-permute-start.43 = (bf16[224,1152]{1,0:T(8,128)(2,1)}, bf16[224,1152]{1,0:T(8,128)(2,1)}, u32[]{:S(2)}, u32[]{:S(2)}) collective-permute-start(bf16[224,1152]{1,0:T(8,128)(2,1)} %copy-done.41), channel_id=1, source_target_pairs={{0,3},{1,2},{2,1},{3,0},{4,7},{5,6},{6,5},{7,4},{8,11},{9,10},{10,... | collective-permute-start | bytes 1548296 | tf_op jit(solution)/shard_map/ppermute | solution.py:55
  148.5 23.5 %collective-permute-start.34 = (bf16[112,1152]{1,0:T(8,128)(2,1)S(1)}, bf16[112,1152]{1,0:T(8,128)(2,1)}, u32[]{:S(2)}, u32[]{:S(2)}) collective-permute-start(bf16[112,1152]{1,0:T(8,128)(2,1)S(1)} %get-tuple-element.159.refs_18_), channel_id=1, source_target_pairs={{0,3},{1,2},{2,1},{3,0},{4,7},{5,6},{6,5},{7,4},{8,11},{9,10},{10,... | collective-permute-start | bytes 774152 | tf_op jit(solution)/shard_map/ppermute | solution.py:55
  188.6 21.3 %collective-permute-start.38 = (bf16[192,1152]{1,0:T(8,128)(2,1)S(1)}, bf16[192,1152]{1,0:T(8,128)(2,1)S(1)}, u32[]{:S(2)}, u32[]{:S(2)}) collective-permute-start(bf16[192,1152]{1,0:T(8,128)(2,1)S(1)} %get-tuple-element.163.refs_21_), channel_id=1, source_target_pairs={{0,4},{1,5},{2,6},{3,7},{4,0},{5,1},{6,2},{7,3},{8,12},{9,13},{10,... | collective-permute-start | bytes 1327112 | tf_op jit(solution)/shard_map/ppermute | solution.py:55
  189.5 20.4 %collective-permute-start.39 = (bf16[208,1152]{1,0:T(8,128)(2,1)S(1)}, bf16[208,1152]{1,0:T(8,128)(2,1)S(1)}, u32[]{:S(2)}, u32[]{:S(2)}) collective-permute-start(bf16[208,1152]{1,0:T(8,128)(2,1)S(1)} %get-tuple-element.164.refs_22_), channel_id=1, source_target_pairs={{0,1},{1,0},{2,3},{3,2},{4,5},{5,4},{6,7},{7,6},{8,9},{9,8},{10,11... | collective-permute-start | bytes 1437704 | tf_op jit(solution)/shard_map/ppermute | solution.py:55
  191.5 27.5 %collective-permute-start.40 = (bf16[224,1152]{1,0:T(8,128)(2,1)S(1)}, bf16[224,1152]{1,0:T(8,128)(2,1)S(1)}, u32[]{:S(2)}, u32[]{:S(2)}) collective-permute-start(bf16[224,1152]{1,0:T(8,128)(2,1)S(1)} %get-tuple-element.165.refs_23_), channel_id=1, source_target_pairs={{0,3},{1,2},{2,1},{3,0},{4,7},{5,6},{6,5},{7,4},{8,11},{9,10},{10,... | collective-permute-start | bytes 1548296 | tf_op jit(solution)/shard_map/ppermute | solution.py:55
  239.8 25.9 %collective-permute-start.45 = (bf16[96,1152]{1,0:T(8,128)(2,1)S(1)}, bf16[96,1152]{1,0:T(8,128)(2,1)S(1)}, u32[]{:S(2)}, u32[]{:S(2)}) collective-permute-start(bf16[96,1152]{1,0:T(8,128)(2,1)S(1)} %get-tuple-element.189), channel_id=1, source_target_pairs={{0,1},{1,0},{2,3},{3,2},{4,5},{5,4},{6,7},{7,6},{8,9},{9,8},{10,11... | collective-permute-start | bytes 663560 | tf_op jit(solution)/shard_map/ppermute | solution.py:55
  240.2 26.6 %collective-permute-start.49 = (bf16[112,1152]{1,0:T(8,128)(2,1)S(1)}, bf16[112,1152]{1,0:T(8,128)(2,1)S(1)}, u32[]{:S(2)}, u32[]{:S(2)}) collective-permute-start(bf16[112,1152]{1,0:T(8,128)(2,1)S(1)} %get-tuple-element.196), channel_id=1, source_target_pairs={{0,3},{1,2},{2,1},{3,0},{4,7},{5,6},{6,5},{7,4},{8,11},{9,10},{10,... | collective-permute-start | bytes 774152 | tf_op jit(solution)/shard_map/ppermute | solution.py:55
  242.6 36.6 %collective-permute-start.47 = (bf16[224,1152]{1,0:T(8,128)(2,1)S(1)}, bf16[224,1152]{1,0:T(8,128)(2,1)S(1)}, u32[]{:S(2)}, u32[]{:S(2)}) collective-permute-start(bf16[224,1152]{1,0:T(8,128)(2,1)S(1)} %pad_maximum_fusion), channel_id=1, source_target_pairs={{0,3},{1,2},{2,1},{3,0},{4,7},{5,6},{6,5},{7,4},{8,11},{9,10},{10,... | collective-permute-start | bytes 1548296 | tf_op jit(solution)/shard_map/ppermute | solution.py:55
  317.0 33.8 %collective-permute-start.61 = (bf16[8,33,8,1024]{3,2,1,0:T(8,128)(2,1)}, bf16[8,33,8,1024]{3,2,1,0:T(8,128)(2,1)}, u32[]{:S(2)}, u32[]{:S(2)}) collective-permute-start(bf16[8,33,8,1024]{3,2,1,0:T(8,128)(2,1)} %theirs.3), channel_id=1, source_target_pairs={{0,8},{8,0},{16,24},{24,16},{32,40},{40,32},{48,56},{56,48},{64,72... | collective-permute-start | bytes 12976136 | tf_op jit(solution)/shard_map/ppermute | solution.py:59
  325.2 20.3 %collective-permute-start.58 = (bf16[416,512]{1,0:T(8,128)(2,1)}, bf16[416,512]{1,0:T(8,128)(2,1)}, u32[]{:S(2)}, u32[]{:S(2)}) collective-permute-start(bf16[416,512]{1,0:T(8,128)(2,1)} %pad_maximum_fusion.8), channel_id=1, source_target_pairs={{0,3},{1,2},{2,1},{3,0},{4,7},{5,6},{6,5},{7,4},{8,11},{9,10},{10,... | collective-permute-start | bytes 1277960 | tf_op jit(solution)/shard_map/ppermute | solution.py:55
  358.0 49.6 %collective-permute-start.68 = (bf16[528,1024]{1,0:T(8,128)(2,1)}, bf16[528,1024]{1,0:T(8,128)(2,1)}, u32[]{:S(2)}, u32[]{:S(2)}) collective-permute-start(bf16[528,1024]{1,0:T(8,128)(2,1)} %bitcast.70.refs_7_), channel_id=1, source_target_pairs={{0,3},{1,2},{2,1},{3,0},{4,7},{5,6},{6,5},{7,4},{8,11},{9,10},{10,... | collective-permute-start | bytes 3244040 | tf_op jit(solution)/shard_map/ppermute | solution.py:55
  362.8 40.5 %collective-permute-start.64 = (bf16[272,768]{1,0:T(8,128)(2,1)S(1)}, bf16[272,768]{1,0:T(8,128)(2,1)}, u32[]{:S(2)}, u32[]{:S(2)}) collective-permute-start(bf16[272,768]{1,0:T(8,128)(2,1)S(1)} %bitcast.204), channel_id=1, source_target_pairs={{0,3},{1,2},{2,1},{3,0},{4,7},{5,6},{6,5},{7,4},{8,11},{9,10},{10,... | collective-permute-start | bytes 1253384 | tf_op jit(solution)/shard_map/ppermute | solution.py:55
  364.9 39.3 %collective-permute-start.63 = (bf16[272,768]{1,0:T(8,128)(2,1)S(1)}, bf16[272,768]{1,0:T(8,128)(2,1)}, u32[]{:S(2)}, u32[]{:S(2)}) collective-permute-start(bf16[272,768]{1,0:T(8,128)(2,1)S(1)} %bitcast.202), channel_id=1, source_target_pairs={{0,1},{1,0},{2,3},{3,2},{4,5},{5,4},{6,7},{7,6},{8,9},{9,8},{10,11... | collective-permute-start | bytes 1253384 | tf_op jit(solution)/shard_map/ppermute | solution.py:55
  364.9 40.5 %collective-permute-start.65 = (bf16[272,768]{1,0:T(8,128)(2,1)}, bf16[272,768]{1,0:T(8,128)(2,1)}, u32[]{:S(2)}, u32[]{:S(2)}) collective-permute-start(bf16[272,768]{1,0:T(8,128)(2,1)} %bitcast.74.refs_3_), channel_id=1, source_target_pairs={{0,2},{1,3},{2,0},{3,1},{4,6},{5,7},{6,4},{7,5},{8,10},{9,11},{10,... | collective-permute-start | bytes 1253384 | tf_op jit(solution)/shard_map/ppermute | solution.py:55
  367.7 48.0 %collective-permute-start.67 = (bf16[528,1024]{1,0:T(8,128)(2,1)}, bf16[528,1024]{1,0:T(8,128)(2,1)S(1)}, u32[]{:S(2)}, u32[]{:S(2)}) collective-permute-start(bf16[528,1024]{1,0:T(8,128)(2,1)} %bitcast.195), channel_id=1, source_target_pairs={{0,1},{1,0},{2,3},{3,2},{4,5},{5,4},{6,7},{7,6},{8,9},{9,8},{10,11... | collective-permute-start | bytes 3244040 | tf_op jit(solution)/shard_map/ppermute | solution.py:55
  403.2 30.2 %collective-permute-start.69 = (bf16[528,1024]{1,0:T(8,128)(2,1)}, bf16[528,1024]{1,0:T(8,128)(2,1)S(1)}, u32[]{:S(2)}, u32[]{:S(2)}) collective-permute-start(bf16[528,1024]{1,0:T(8,128)(2,1)} %bitcast.193), channel_id=1, source_target_pairs={{0,2},{1,3},{2,0},{3,1},{4,6},{5,7},{6,4},{7,5},{8,10},{9,11},{10,... | collective-permute-start | bytes 3244040 | tf_op jit(solution)/shard_map/ppermute | solution.py:55
  404.2 49.2 %collective-permute-start.53 = (bf16[416,1152]{1,0:T(8,128)(2,1)}, bf16[416,1152]{1,0:T(8,128)(2,1)S(1)}, u32[]{:S(2)}, u32[]{:S(2)}) collective-permute-start(bf16[416,1152]{1,0:T(8,128)(2,1)} %fence.13.refs_24_), channel_id=1, source_target_pairs={{0,1},{1,0},{2,3},{3,2},{4,5},{5,4},{6,7},{7,6},{8,9},{9,8},{10,11... | collective-permute-start | bytes 2875400 | tf_op jit(solution)/shard_map/ppermute | solution.py:55
  405.4 48.0 %collective-permute-start.54 = (bf16[416,1152]{1,0:T(8,128)(2,1)}, bf16[416,1152]{1,0:T(8,128)(2,1)S(1)}, u32[]{:S(2)}, u32[]{:S(2)}) collective-permute-start(bf16[416,1152]{1,0:T(8,128)(2,1)} %fence.14.refs_26_), channel_id=1, source_target_pairs={{0,3},{1,2},{2,1},{3,0},{4,7},{5,6},{6,5},{7,4},{8,11},{9,10},{10,... | collective-permute-start | bytes 2875400 | tf_op jit(solution)/shard_map/ppermute | solution.py:55
  407.6 65.3 %collective-permute-start.55 = (bf16[416,1152]{1,0:T(8,128)(2,1)}, bf16[416,1152]{1,0:T(8,128)(2,1)S(1)}, u32[]{:S(2)}, u32[]{:S(2)}) collective-permute-start(bf16[416,1152]{1,0:T(8,128)(2,1)} %fence.15.refs_25_), channel_id=1, source_target_pairs={{0,2},{1,3},{2,0},{3,1},{4,6},{5,7},{6,4},{7,5},{8,10},{9,11},{10,... | collective-permute-start | bytes 2875400 | tf_op jit(solution)/shard_map/ppermute | solution.py:55
  415.7 58.4 %collective-permute-start.66 = (bf16[136,768]{1,0:T(8,128)(2,1)S(1)}, bf16[136,768]{1,0:T(8,128)(2,1)S(1)}, u32[]{:S(2)}, u32[]{:S(2)}) collective-permute-start(bf16[136,768]{1,0:T(8,128)(2,1)S(1)} %slice.695), channel_id=1, source_target_pairs={{0,4},{1,5},{2,6},{3,7},{4,0},{5,1},{6,2},{7,3},{8,12},{9,13},{10,... | collective-permute-start | bytes 626696 | tf_op jit(solution)/shard_map/ppermute | solution.py:55
  435.7 43.0 %collective-permute-start.70 = (bf16[264,1024]{1,0:T(8,128)(2,1)S(1)}, bf16[264,1024]{1,0:T(8,128)(2,1)S(1)}, u32[]{:S(2)}, u32[]{:S(2)}) collective-permute-start(bf16[264,1024]{1,0:T(8,128)(2,1)S(1)} %slice.693), channel_id=1, source_target_pairs={{0,4},{1,5},{2,6},{3,7},{4,0},{5,1},{6,2},{7,3},{8,12},{9,13},{10,... | collective-permute-start | bytes 1622024 | tf_op jit(solution)/shard_map/ppermute | solution.py:55
  493.5 39.6 %collective-permute-start.56 = (bf16[208,1152]{1,0:T(8,128)(2,1)}, bf16[208,1152]{1,0:T(8,128)(2,1)}, u32[]{:S(2)}, u32[]{:S(2)}) collective-permute-start(bf16[208,1152]{1,0:T(8,128)(2,1)} %fence.16), channel_id=1, source_target_pairs={{0,4},{1,5},{2,6},{3,7},{4,0},{5,1},{6,2},{7,3},{8,12},{9,13},{10,... | collective-permute-start | bytes 1437704 | tf_op jit(solution)/shard_map/ppermute | solution.py:55
  (181 other events, 1914.2 us)
Sparse Core Ops, SparseCore 0:
  289.1 182.0 all-reduce.19
